TPU v7x, 32 devices: a whole 2x2x4 slice. The times are simulated.
32 devices in a mesh: section: 8 (over z, x), tensor: 4 (over y, core).
Axes of the slice: x: 2, y: 2, z: 4, core: 2. Of those that a mesh axis runs over, the one named last changes fastest.
Arguments:
- trainer_tiles: bfloat16 [49152, 6144], P(('section', 'tensor')), may hold values from -0.09375 to 0.09375
- tile_lengths: int32 [32], replicated, may hold values from 1 to 24, 512 in all
- wo_rollout: bfloat16 [8, 4096, 4096], P('section', 'tensor'), may hold values from -0.1875 to 0.1875
- cache_keys: bfloat16 [8, 32, 64, 1024], P('section', None, None, 'tensor')
- cache_values: bfloat16 [8, 32, 64, 1024], P('section', None, None, 'tensor'), may hold values from -6 to 6
- cache_lengths: int32 [32], replicated, may hold values from 1 to 64, as said below
- norm_gain: float32 [8, 4096], P('section'), may hold values from 0.1 to 1.9
- step_inputs: bfloat16 [3, 32, 4096], replicated, may hold values from -3 to 3
Outputs:
- hidden: float32 [8, 3, 32, 4096], P('section', None, None, 'tensor')
Inputs may be any that keep to these rules, and one draw needn't show every extreme that they name: `tile_lengths`: the lengths of all tiles sum to 512; some tile holds exactly 24 blocks. `cache_lengths`: some sequence uses all 64 positions.
All inputs are finite; a program needn't handle non-finite values.
Results may differ from a plain program's by a relative error of at most 0.03.
Values may be sent and summed in bfloat16 or wider, within the bound.
No kernel may reach another device: no remote copies, remote signals or barrier semaphores. Data moves between devices by JAX's collectives and lax.ppermute only.
A program may use at most 192 MiB of HBM per device.

v0:
```python
import jax
import jax.numpy as jnp
from jax import lax
from jax.sharding import PartitionSpec as P

HDIM = 128
FB = 8


def from_behind(value, axis, steps):
    count = lax.axis_size(axis)
    leading, last = (max(0, -steps), min(count, count - steps))
    return lax.ppermute(value, axis, [(source, source + steps) for source in range(leading, last)])


def per_device(
    trainer_tiles,
    tile_lengths,
    wo_rollout,
    cache_keys,
    cache_values,
    cache_lengths,
    norm_gain,
    step_inputs,
):
    n_section = lax.axis_size("section")
    n_tensor = lax.axis_size("tensor")
    devices = n_section * n_tensor
    cdev = trainer_tiles.shape[1] // n_tensor
    slab = trainer_tiles.shape[0] // n_section
    slots = slab // FB
    width = wo_rollout.shape[2]
    qdim = wo_rollout.shape[1]
    kvdim = cache_keys.shape[3]
    kvlocal = kvdim // HDIM
    groups = qdim // HDIM // kvlocal
    ends = jnp.cumsum(tile_lengths)
    starts = ends - tile_lengths
    blocks = jnp.arange(width // FB, dtype=jnp.int32)
    owner = jnp.sum((ends[None, :] <= blocks[:, None]).astype(jnp.int32), axis=1)
    inner = blocks - starts[owner]
    feats = jnp.arange(width, dtype=jnp.int32)
    owner_f = owner[feats // FB]
    inner_f = inner[feats // FB]
    outgoing = trainer_tiles.reshape(slab, devices, cdev)
    arrived = lax.all_to_all(
        outgoing, ("section", "tensor"), split_axis=1, concat_axis=0, tiled=True
    )
    picks = (owner_f * slots + inner_f) * FB + feats % FB
    weights = arrived.reshape(-1, cdev)[picks]
    section = lax.axis_index("section")
    tpos = lax.axis_index("tensor")
    steps = step_inputs.shape[0]
    seqs = cache_keys.shape[1]
    length = cache_keys.shape[2]
    nblock = 4
    brow = seqs // nblock
    items = steps * nblock
    ticks = items + n_section - 1
    shard = width // n_tensor
    scale = 1.0 / HDIM**0.5
    wo_local = wo_rollout[0]
    keys_local = cache_keys[0]
    values_local = cache_values[0]
    gain = norm_gain[0]

    def run_tick(tick, carry):
        current, newk, newv, record = carry
        item = tick - section
        valid = (item >= 0) & (item < items)
        item_c = jnp.clip(item, 0, items - 1)
        step = item_c // nblock
        first = item_c % nblock * brow
        fresh = lax.dynamic_slice(step_inputs, (step, first, 0), (1, brow, width))[0]
        resid = jnp.where(section == 0, fresh, current)
        states = resid.astype(jnp.float32)
        normed = (
            states * lax.rsqrt(jnp.mean(states * states, axis=-1, keepdims=True) + 1e-06) * gain
        ).astype(jnp.bfloat16)
        qkv = jnp.dot(normed, weights, preferred_element_type=jnp.float32).astype(jnp.bfloat16)
        query = qkv[:, :qdim].reshape(brow, kvlocal, groups, HDIM)
        kpart = qkv[:, qdim : qdim + kvdim]
        vpart = qkv[:, qdim + kvdim :]
        newk = jnp.where(valid, lax.dynamic_update_slice(newk, kpart[None], (step, first, 0)), newk)
        newv = jnp.where(valid, lax.dynamic_update_slice(newv, vpart[None], (step, first, 0)), newv)
        block_k = lax.dynamic_slice(newk, (0, first, 0), (steps, brow, kvdim)).reshape(
            steps, brow, kvlocal, HDIM
        )
        block_v = lax.dynamic_slice(newv, (0, first, 0), (steps, brow, kvdim)).reshape(
            steps, brow, kvlocal, HDIM
        )
        ckeys = lax.dynamic_slice_in_dim(keys_local, first, brow, 0).reshape(
            brow, length, kvlocal, HDIM
        )
        cvals = lax.dynamic_slice_in_dim(values_local, first, brow, 0).reshape(
            brow, length, kvlocal, HDIM
        )
        spans = lax.dynamic_slice_in_dim(cache_lengths, first, brow)
        cmask = (jnp.arange(length)[None, :] < spans[:, None])[:, None, None, :]
        nmask = (jnp.arange(steps) <= step)[None, None, None, :]
        scache = (
            jnp.einsum("bkgd,blkd->bkgl", query, ckeys, preferred_element_type=jnp.float32) * scale
        )
        snew = (
            jnp.einsum("bkgd,tbkd->bkgt", query, block_k, preferred_element_type=jnp.float32)
            * scale
        )
        scache = jnp.where(cmask, scache, -1e30)
        snew = jnp.where(nmask, snew, -1e30)
        top = jnp.maximum(jnp.max(scache, axis=-1), jnp.max(snew, axis=-1))[..., None]
        ecache = jnp.where(cmask, jnp.exp(scache - top), 0.0)
        enew = jnp.where(nmask, jnp.exp(snew - top), 0.0)
        total = (jnp.sum(ecache, axis=-1) + jnp.sum(enew, axis=-1))[..., None]
        wcache = (ecache / total).astype(jnp.bfloat16)
        wnew = (enew / total).astype(jnp.bfloat16)
        mixed = jnp.einsum("bkgl,blkd->bkgd", wcache, cvals, preferred_element_type=jnp.float32)
        mixed = mixed + jnp.einsum(
            "bkgt,tbkd->bkgd", wnew, block_v, preferred_element_type=jnp.float32
        )
        attn = mixed.astype(jnp.bfloat16).reshape(brow, qdim)
        partial_value = jnp.dot(attn, wo_local, preferred_element_type=jnp.float32)
        summed = lax.psum(partial_value.astype(jnp.bfloat16), "tensor").astype(jnp.float32)
        wide = states + summed
        local = lax.dynamic_slice_in_dim(wide, tpos * shard, shard, 1)
        after = wide.astype(jnp.bfloat16)
        record = jnp.where(
            valid, lax.dynamic_update_slice(record, local[None], (step, first, 0)), record
        )
        current = from_behind(after, "section", 1)
        return (current, newk, newv, record)

    start_rows = jnp.zeros((brow, width), jnp.bfloat16)
    start_keys = jnp.zeros((steps, seqs, kvdim), jnp.bfloat16)
    start_record = jnp.zeros((steps, seqs, shard), jnp.float32)
    final = lax.fori_loop(0, ticks, run_tick, (start_rows, start_keys, start_keys, start_record))
    return final[3][None]


def solution(mesh):
    placed = (
        P(("section", "tensor"), None),
        P(),
        P("section", "tensor", None),
        P("section", None, None, "tensor"),
        P("section", None, None, "tensor"),
        P(),
        P("section", None),
        P(),
    )
    return jax.shard_map(
        per_device,
        mesh=mesh,
        in_specs=placed,
        out_specs=P("section", None, None, "tensor"),
        check_vma=False,
    )
```

profile of v0, /device:TPU:0, one launch (start us, length us, event | category | flops | bytes accessed | tf_op | source)
XLA Modules:
  0.0 1544.7 jit_solution(16018685016950284330)
XLA Ops:
  6.5 28.7 %reshape.250 = bf16[192,32,1536]{2,1,0:T(8,128)(2,1)} reshape(bf16[1536,6144]{1,0:T(8,128)(2,1)} %param.10) | data formatting | bytes 37748736 | tf_op jit(solution)/shard_map/reshape | solution.py:45
  63.7 25.9 %gather_fusion = s32[4096]{0:T(1024)S(1)} fusion(s32[512]{0:T(512)S(1)} %convert_reduce_fusion, s32[4096]{0:T(1024)S(1)} %broadcast_clamp_fusion.1), kind=kCustom, calls=%fused_computation | custom fusion | bytes 49152 | tf_op jit(solution)/shard_map/gather | solution.py:43
  137.3 336.8 %all-to-all-done = bf16[192,32,1536]{2,0,1:T(8,128)(2,1)} async-done(((bf16[192,32,1536]{2,0,1:T(8,128)(2,1)}), bf16[192,32,1536]{2,0,1:T(8,128)(2,1)}, u32[]{:S(2)}, u32[]{:S(2)}) %all-to-all-start) | async-done | bytes 18874400 | tf_op jit(solution)/shard_map/all_to_all | solution.py:46
  474.1 34.2 %gather_fusion.2 = bf16[4096,1536]{1,0:T(8,128)(2,1)} fusion(bf16[6144,1536]{1,0:T(8,128)(2,1)} %bitcast.10, s32[4096]{0:T(1024)S(1)} %broadcast_clamp_fusion), kind=kCustom, calls=%fused_computation.2 | custom fusion | bytes 25182208 | tf_op jit(solution)/shard_map/gather | solution.py:50
  508.4 1029.1 %while.21 = (s32[]{:T(128)}, bf16[8,4096]{1,0:T(8,128)(2,1)S(1)}, bf16[3,32,256]{2,1,0:T(8,128)(2,1)S(1)}, bf16[3,32,256]{2,1,0:T(8,128)(2,1)S(1)}, f32[3,32,102...) while((s32[]{:T(128)}, bf16[8,4096]{1,0:T(8,128)(2,1)S(1)}, ...), condition=%wide.region_9.10_spmd, body=%wide.region_2.9_spmd.sunk | while | flops 170510624 | bytes 24347716 | solution.py:135
  523.7 45.0 %all-reduce.2.cloned.1.call-done = bf16[8,4096]{1,0:T(8,128)(2,1)} async-done(((bf16[8,4096]{1,0:T(8,128)(2,1)}), bf16[8,4096]{1,0:T(8,128)(2,1)}) %all-reduce.2.cloned.1.call-update) | async-done | bytes 65552 | tf_op jit(solution)/shard_map/while/body/eval_jaxpr/psum | solution.py:122
  590.0 32.1 %all-reduce.2.cloned.1.call-done = bf16[8,4096]{1,0:T(8,128)(2,1)} async-done(((bf16[8,4096]{1,0:T(8,128)(2,1)}), bf16[8,4096]{1,0:T(8,128)(2,1)}) %all-reduce.2.cloned.1.call-update) | async-done | bytes 65552 | tf_op jit(solution)/shard_map/while/body/eval_jaxpr/psum | solution.py:122
  643.5 32.1 %all-reduce.2.cloned.1.call-done = bf16[8,4096]{1,0:T(8,128)(2,1)} async-done(((bf16[8,4096]{1,0:T(8,128)(2,1)}), bf16[8,4096]{1,0:T(8,128)(2,1)}) %all-reduce.2.cloned.1.call-update) | async-done | bytes 65552 | tf_op jit(solution)/shard_map/while/body/eval_jaxpr/psum | solution.py:122
  697.0 32.1 %all-reduce.2.cloned.1.call-done = bf16[8,4096]{1,0:T(8,128)(2,1)} async-done(((bf16[8,4096]{1,0:T(8,128)(2,1)}), bf16[8,4096]{1,0:T(8,128)(2,1)}) %all-reduce.2.cloned.1.call-update) | async-done | bytes 65552 | tf_op jit(solution)/shard_map/while/body/eval_jaxpr/psum | solution.py:122
  750.5 32.1 %all-reduce.2.cloned.1.call-done = bf16[8,4096]{1,0:T(8,128)(2,1)} async-done(((bf16[8,4096]{1,0:T(8,128)(2,1)}), bf16[8,4096]{1,0:T(8,128)(2,1)}) %all-reduce.2.cloned.1.call-update) | async-done | bytes 65552 | tf_op jit(solution)/shard_map/while/body/eval_jaxpr/psum | solution.py:122
  803.9 32.1 %all-reduce.2.cloned.1.call-done = bf16[8,4096]{1,0:T(8,128)(2,1)} async-done(((bf16[8,4096]{1,0:T(8,128)(2,1)}), bf16[8,4096]{1,0:T(8,128)(2,1)}) %all-reduce.2.cloned.1.call-update) | async-done | bytes 65552 | tf_op jit(solution)/shard_map/while/body/eval_jaxpr/psum | solution.py:122
  857.4 32.1 %all-reduce.2.cloned.1.call-done = bf16[8,4096]{1,0:T(8,128)(2,1)} async-done(((bf16[8,4096]{1,0:T(8,128)(2,1)}), bf16[8,4096]{1,0:T(8,128)(2,1)}) %all-reduce.2.cloned.1.call-update) | async-done | bytes 65552 | tf_op jit(solution)/shard_map/while/body/eval_jaxpr/psum | solution.py:122
  910.9 32.1 %all-reduce.2.cloned.1.call-done = bf16[8,4096]{1,0:T(8,128)(2,1)} async-done(((bf16[8,4096]{1,0:T(8,128)(2,1)}), bf16[8,4096]{1,0:T(8,128)(2,1)}) %all-reduce.2.cloned.1.call-update) | async-done | bytes 65552 | tf_op jit(solution)/shard_map/while/body/eval_jaxpr/psum | solution.py:122
  964.4 32.1 %all-reduce.2.cloned.1.call-done = bf16[8,4096]{1,0:T(8,128)(2,1)} async-done(((bf16[8,4096]{1,0:T(8,128)(2,1)}), bf16[8,4096]{1,0:T(8,128)(2,1)}) %all-reduce.2.cloned.1.call-update) | async-done | bytes 65552 | tf_op jit(solution)/shard_map/while/body/eval_jaxpr/psum | solution.py:122
  1017.9 32.1 %all-reduce.2.cloned.1.call-done = bf16[8,4096]{1,0:T(8,128)(2,1)} async-done(((bf16[8,4096]{1,0:T(8,128)(2,1)}), bf16[8,4096]{1,0:T(8,128)(2,1)}) %all-reduce.2.cloned.1.call-update) | async-done | bytes 65552 | tf_op jit(solution)/shard_map/while/body/eval_jaxpr/psum | solution.py:122
  1071.3 32.1 %all-reduce.2.cloned.1.call-done = bf16[8,4096]{1,0:T(8,128)(2,1)} async-done(((bf16[8,4096]{1,0:T(8,128)(2,1)}), bf16[8,4096]{1,0:T(8,128)(2,1)}) %all-reduce.2.cloned.1.call-update) | async-done | bytes 65552 | tf_op jit(solution)/shard_map/while/body/eval_jaxpr/psum | solution.py:122
  1124.8 32.1 %all-reduce.2.cloned.1.call-done = bf16[8,4096]{1,0:T(8,128)(2,1)} async-done(((bf16[8,4096]{1,0:T(8,128)(2,1)}), bf16[8,4096]{1,0:T(8,128)(2,1)}) %all-reduce.2.cloned.1.call-update) | async-done | bytes 65552 | tf_op jit(solution)/shard_map/while/body/eval_jaxpr/psum | solution.py:122
  1178.3 32.1 %all-reduce.2.cloned.1.call-done = bf16[8,4096]{1,0:T(8,128)(2,1)} async-done(((bf16[8,4096]{1,0:T(8,128)(2,1)}), bf16[8,4096]{1,0:T(8,128)(2,1)}) %all-reduce.2.cloned.1.call-update) | async-done | bytes 65552 | tf_op jit(solution)/shard_map/while/body/eval_jaxpr/psum | solution.py:122
  1231.8 32.1 %all-reduce.2.cloned.1.call-done = bf16[8,4096]{1,0:T(8,128)(2,1)} async-done(((bf16[8,4096]{1,0:T(8,128)(2,1)}), bf16[8,4096]{1,0:T(8,128)(2,1)}) %all-reduce.2.cloned.1.call-update) | async-done | bytes 65552 | tf_op jit(solution)/shard_map/while/body/eval_jaxpr/psum | solution.py:122
  1285.2 32.1 %all-reduce.2.cloned.1.call-done = bf16[8,4096]{1,0:T(8,128)(2,1)} async-done(((bf16[8,4096]{1,0:T(8,128)(2,1)}), bf16[8,4096]{1,0:T(8,128)(2,1)}) %all-reduce.2.cloned.1.call-update) | async-done | bytes 65552 | tf_op jit(solution)/shard_map/while/body/eval_jaxpr/psum | solution.py:122
  1338.7 32.1 %all-reduce.2.cloned.1.call-done = bf16[8,4096]{1,0:T(8,128)(2,1)} async-done(((bf16[8,4096]{1,0:T(8,128)(2,1)}), bf16[8,4096]{1,0:T(8,128)(2,1)}) %all-reduce.2.cloned.1.call-update) | async-done | bytes 65552 | tf_op jit(solution)/shard_map/while/body/eval_jaxpr/psum | solution.py:122
  1392.2 32.1 %all-reduce.2.cloned.1.call-done = bf16[8,4096]{1,0:T(8,128)(2,1)} async-done(((bf16[8,4096]{1,0:T(8,128)(2,1)}), bf16[8,4096]{1,0:T(8,128)(2,1)}) %all-reduce.2.cloned.1.call-update) | async-done | bytes 65552 | tf_op jit(solution)/shard_map/while/body/eval_jaxpr/psum | solution.py:122
  1445.7 32.1 %all-reduce.2.cloned.1.call-done = bf16[8,4096]{1,0:T(8,128)(2,1)} async-done(((bf16[8,4096]{1,0:T(8,128)(2,1)}), bf16[8,4096]{1,0:T(8,128)(2,1)}) %all-reduce.2.cloned.1.call-update) | async-done | bytes 65552 | tf_op jit(solution)/shard_map/while/body/eval_jaxpr/psum | solution.py:122
  1499.2 32.1 %all-reduce.2.cloned.1.call-done = bf16[8,4096]{1,0:T(8,128)(2,1)} async-done(((bf16[8,4096]{1,0:T(8,128)(2,1)}), bf16[8,4096]{1,0:T(8,128)(2,1)}) %all-reduce.2.cloned.1.call-update) | async-done | bytes 65552 | tf_op jit(solution)/shard_map/while/body/eval_jaxpr/psum | solution.py:122
  (524 shorter events, 481.1 us)
Async XLA Ops:
  55.8 418.3 %all-to-all-start = ((bf16[192,32,1536]{2,0,1:T(8,128)(2,1)}), bf16[192,32,1536]{2,0,1:T(8,128)(2,1)}, u32[]{:S(2)}, u32[]{:S(2)}) async-start(bf16[192,32,1536]{2,0,1:T(8,128)(2,1)} %copy.30), calls=%async_computation | async-start | bytes 37748736 | tf_op jit(solution)/shard_map/all_to_all | solution.py:46
  508.4 60.3 %all-reduce.2.cloned.1.call-start = ((), (), s32[]{:S(2)}) async-start(), calls=%async_computation.1 | async-start | bytes 131072 | tf_op jit(solution)/shard_map/while/body/eval_jaxpr/psum | solution.py:122
  574.8 47.4 %all-reduce.2.cloned.1.call-start = ((), (), s32[]{:S(2)}) async-start(), calls=%async_computation.1 | async-start | bytes 131072 | tf_op jit(solution)/shard_map/while/body/eval_jaxpr/psum | solution.py:122
  623.0 5.3 collective-permute-start
  628.3 47.3 %all-reduce.2.cloned.1.call-start = ((), (), s32[]{:S(2)}) async-start(), calls=%async_computation.1 | async-start | bytes 131072 | tf_op jit(solution)/shard_map/while/body/eval_jaxpr/psum | solution.py:122
  681.7 47.4 %all-reduce.2.cloned.1.call-start = ((), (), s32[]{:S(2)}) async-start(), calls=%async_computation.1 | async-start | bytes 131072 | tf_op jit(solution)/shard_map/while/body/eval_jaxpr/psum | solution.py:122
  735.2 47.3 %all-reduce.2.cloned.1.call-start = ((), (), s32[]{:S(2)}) async-start(), calls=%async_computation.1 | async-start | bytes 131072 | tf_op jit(solution)/shard_map/while/body/eval_jaxpr/psum | solution.py:122
  788.7 47.4 %all-reduce.2.cloned.1.call-start = ((), (), s32[]{:S(2)}) async-start(), calls=%async_computation.1 | async-start | bytes 131072 | tf_op jit(solution)/shard_map/while/body/eval_jaxpr/psum | solution.py:122
  842.2 47.3 %all-reduce.2.cloned.1.call-start = ((), (), s32[]{:S(2)}) async-start(), calls=%async_computation.1 | async-start | bytes 131072 | tf_op jit(solution)/shard_map/while/body/eval_jaxpr/psum | solution.py:122
  895.7 47.4 %all-reduce.2.cloned.1.call-start = ((), (), s32[]{:S(2)}) async-start(), calls=%async_computation.1 | async-start | bytes 131072 | tf_op jit(solution)/shard_map/while/body/eval_jaxpr/psum | solution.py:122
  943.9 5.3 collective-permute-start
  949.1 47.3 %all-reduce.2.cloned.1.call-start = ((), (), s32[]{:S(2)}) async-start(), calls=%async_computation.1 | async-start | bytes 131072 | tf_op jit(solution)/shard_map/while/body/eval_jaxpr/psum | solution.py:122
  1002.6 47.4 %all-reduce.2.cloned.1.call-start = ((), (), s32[]{:S(2)}) async-start(), calls=%async_computation.1 | async-start | bytes 131072 | tf_op jit(solution)/shard_map/while/body/eval_jaxpr/psum | solution.py:122
  1050.8 5.3 collective-permute-start
  1056.1 47.3 %all-reduce.2.cloned.1.call-start = ((), (), s32[]{:S(2)}) async-start(), calls=%async_computation.1 | async-start | bytes 131072 | tf_op jit(solution)/shard_map/while/body/eval_jaxpr/psum | solution.py:122
  1109.6 47.4 %all-reduce.2.cloned.1.call-start = ((), (), s32[]{:S(2)}) async-start(), calls=%async_computation.1 | async-start | bytes 131072 | tf_op jit(solution)/shard_map/while/body/eval_jaxpr/psum | solution.py:122
  1163.1 47.3 %all-reduce.2.cloned.1.call-start = ((), (), s32[]{:S(2)}) async-start(), calls=%async_computation.1 | async-start | bytes 131072 | tf_op jit(solution)/shard_map/while/body/eval_jaxpr/psum | solution.py:122
  1216.5 47.4 %all-reduce.2.cloned.1.call-start = ((), (), s32[]{:S(2)}) async-start(), calls=%async_computation.1 | async-start | bytes 131072 | tf_op jit(solution)/shard_map/while/body/eval_jaxpr/psum | solution.py:122
  1270.0 47.3 %all-reduce.2.cloned.1.call-start = ((), (), s32[]{:S(2)}) async-start(), calls=%async_computation.1 | async-start | bytes 131072 | tf_op jit(solution)/shard_map/while/body/eval_jaxpr/psum | solution.py:122
  1323.5 47.4 %all-reduce.2.cloned.1.call-start = ((), (), s32[]{:S(2)}) async-start(), calls=%async_computation.1 | async-start | bytes 131072 | tf_op jit(solution)/shard_map/while/body/eval_jaxpr/psum | solution.py:122
  1371.7 5.3 collective-permute-start
  1377.0 47.3 %all-reduce.2.cloned.1.call-start = ((), (), s32[]{:S(2)}) async-start(), calls=%async_computation.1 | async-start | bytes 131072 | tf_op jit(solution)/shard_map/while/body/eval_jaxpr/psum | solution.py:122
  1430.5 47.4 %all-reduce.2.cloned.1.call-start = ((), (), s32[]{:S(2)}) async-start(), calls=%async_computation.1 | async-start | bytes 131072 | tf_op jit(solution)/shard_map/while/body/eval_jaxpr/psum | solution.py:122
  1483.9 47.3 %all-reduce.2.cloned.1.call-start = ((), (), s32[]{:S(2)}) async-start(), calls=%async_computation.1 | async-start | bytes 131072 | tf_op jit(solution)/shard_map/while/body/eval_jaxpr/psum | solution.py:122
  (19 other events, 155.7 us)
Sparse Core Ops, SparseCore 0:
  523.8 44.7 all-reduce.1
  590.1 31.9 all-reduce.1
  643.6 31.9 all-reduce.1
  697.1 31.9 all-reduce.1
  750.6 31.9 all-reduce.1
  804.1 31.9 all-reduce.1
  857.5 31.9 all-reduce.1
  911.0 31.9 all-reduce.1
  964.5 31.9 all-reduce.1
  1018.0 31.9 all-reduce.1
  1071.5 31.9 all-reduce.1
  1124.9 31.9 all-reduce.1
  1178.4 31.9 all-reduce.1
  1231.9 31.9 all-reduce.1
  1285.4 31.9 all-reduce.1
  1338.8 31.9 all-reduce.1
  1392.3 31.9 all-reduce.1
  1445.8 31.9 all-reduce.1
  1499.3 31.9 all-reduce.1
where the time goes:
time: 1550 us; the launch traced here: 1540 us
  waiting for transfers between devices  996 us (64%)
  matrix products  239 us (15%)
  local copies, waits for them, and re-layouts  160 us (10%)
  starting transfers between devices  71.6 us (5%)
  other arithmetic  63.6 us (4%)
    psum x19, waiting for transfers between devices, run_tick(): lax.psum(partial_value.astype(jnp.bfloat16), 'tensor').astype(jnp.float32)  623 us
    all_to_all x1, waiting for transfers between devices, per_device(): lax.all_to_all(outgoing, ('section', 'tensor'), split_axis=1, concat_axis...  337 us
    dot_general x19, matrix products, run_tick(): jnp.dot(normed, weights, preferred_element_type=jnp.float32)  120 us
    dot_general x19, matrix products, run_tick(): partial_value = jnp.dot(attn, wo_local, preferred_element_type=jnp.float32)  99 us
    ppermute x19, starting transfers between devices, from_behind(): lax.ppermute(value, axis, [(source, source + steps) for source in range(l...  64.1 us
    reshape x2, local copies, waits for them, and re-layouts, per_device(): outgoing = trainer_tiles.reshape(slab, devices, cdev)  49.3 us
    ppermute x19, waiting for transfers between devices, from_behind(): lax.ppermute(value, axis, [(source, source + steps) for source in range(l...  35.3 us
    gather x1, local copies, waits for them, and re-layouts, per_device(): weights = arrived.reshape(-1, cdev)[picks]  34.2 us
  transfers between devices with their start and end apart: 39, of which 39 were waited for; matrix products, arithmetic and copies ran while one was open for 5% of the time, Pallas kernels for 0%

commit v1 on v0

v1 whole, which is shorter than its diff:
```python
import jax
import jax.numpy as jnp
from jax import lax
from jax.sharding import PartitionSpec as P

HDIM = 128
FB = 8


def from_behind(value, axis, steps):
    count = lax.axis_size(axis)
    leading, last = (max(0, -steps), min(count, count - steps))
    return lax.ppermute(value, axis, [(source, source + steps) for source in range(leading, last)])


def per_device(
    trainer_tiles,
    tile_lengths,
    wo_rollout,
    cache_keys,
    cache_values,
    cache_lengths,
    norm_gain,
    step_inputs,
):
    n_section = lax.axis_size("section")
    n_tensor = lax.axis_size("tensor")
    devices = n_section * n_tensor
    cdev = trainer_tiles.shape[1] // n_tensor
    slab = trainer_tiles.shape[0] // n_section
    slots = slab // FB
    width = wo_rollout.shape[2]
    qdim = wo_rollout.shape[1]
    kvdim = cache_keys.shape[3]
    kvlocal = kvdim // HDIM
    groups = qdim // HDIM // kvlocal
    ends = jnp.cumsum(tile_lengths)
    starts = ends - tile_lengths
    blocks = jnp.arange(width // FB, dtype=jnp.int32)
    owner = jnp.sum((ends[None, :] <= blocks[:, None]).astype(jnp.int32), axis=1)
    inner = blocks - starts[owner]
    feats = jnp.arange(width, dtype=jnp.int32)
    owner_f = owner[feats // FB]
    inner_f = inner[feats // FB]
    outgoing = trainer_tiles.reshape(slab, devices, cdev)
    arrived = lax.all_to_all(
        outgoing, ("section", "tensor"), split_axis=1, concat_axis=0, tiled=True
    )
    picks = (owner_f * slots + inner_f) * FB + feats % FB
    weights = arrived.reshape(-1, cdev)[picks]
    section = lax.axis_index("section")
    tpos = lax.axis_index("tensor")
    steps = step_inputs.shape[0]
    seqs = cache_keys.shape[1]
    length = cache_keys.shape[2]
    nblock = 4
    brow = seqs // nblock
    rows = steps * brow
    ticks = nblock + n_section - 1
    shard = width // n_tensor
    scale = 1.0 / HDIM**0.5
    wo_local = wo_rollout[0]
    keys_local = cache_keys[0]
    values_local = cache_values[0]
    gain = norm_gain[0]
    nmask = (jnp.arange(steps)[None, :] <= jnp.arange(steps)[:, None])[:, None, None, None, :]
    along_core = [(t, t ^ 1) for t in range(n_tensor)]
    record = jnp.zeros((steps, seqs, shard), jnp.float32)
    current = jnp.zeros((rows, shard), jnp.bfloat16)

    for tick in range(ticks):
        item = tick - section
        valid = (item >= 0) & (item < nblock)
        first = jnp.clip(item, 0, nblock - 1) * brow
        fresh = lax.dynamic_slice(step_inputs, (0, first, 0), (steps, brow, width)).reshape(rows, width)
        if tick:
            halves = jnp.stack([current, lax.ppermute(current, "tensor", along_core)])
            even = jnp.where(tpos % 2 == 0, halves[0], halves[1])
            odd = jnp.where(tpos % 2 == 0, halves[1], halves[0])
            pair = jnp.concatenate([even, odd], axis=1)
            chips = n_tensor // 2
            gathered = [None] * chips
            parts = [pair]
            for hop in range(1, chips):
                moved = lax.ppermute(
                    pair, "tensor", [(t, (t + 2 * hop) % n_tensor) for t in range(n_tensor)]
                )
                parts.append(moved)
            stacked = jnp.stack(parts)
            order = (tpos // 2 - jnp.arange(chips)) % chips
            placed = jnp.concatenate([stacked[order[c]] for c in range(chips)], axis=1)
            resid = jnp.where(section == 0, fresh, placed)
        else:
            resid = fresh
        states = resid.astype(jnp.float32)
        normed = (
            states * lax.rsqrt(jnp.mean(states * states, axis=-1, keepdims=True) + 1e-06) * gain
        ).astype(jnp.bfloat16)
        qkv = jnp.dot(normed, weights, preferred_element_type=jnp.float32).astype(jnp.bfloat16)
        query = qkv[:, :qdim].reshape(steps, brow, kvlocal, groups, HDIM)
        block_k = qkv[:, qdim : qdim + kvdim].reshape(steps, brow, kvlocal, HDIM)
        block_v = qkv[:, qdim + kvdim :].reshape(steps, brow, kvlocal, HDIM)
        ckeys = lax.dynamic_slice_in_dim(keys_local, first, brow, 0).reshape(
            brow, length, kvlocal, HDIM
        )
        cvals = lax.dynamic_slice_in_dim(values_local, first, brow, 0).reshape(
            brow, length, kvlocal, HDIM
        )
        spans = lax.dynamic_slice_in_dim(cache_lengths, first, brow)
        cmask = (jnp.arange(length)[None, :] < spans[:, None])[None, :, None, None, :]
        scache = (
            jnp.einsum("sbkgd,blkd->sbkgl", query, ckeys, preferred_element_type=jnp.float32)
            * scale
        )
        snew = (
            jnp.einsum("sbkgd,tbkd->sbkgt", query, block_k, preferred_element_type=jnp.float32)
            * scale
        )
        scache = jnp.where(cmask, scache, -1e30)
        snew = jnp.where(nmask, snew, -1e30)
        top = jnp.maximum(jnp.max(scache, axis=-1), jnp.max(snew, axis=-1))[..., None]
        ecache = jnp.where(cmask, jnp.exp(scache - top), 0.0)
        enew = jnp.where(nmask, jnp.exp(snew - top), 0.0)
        total = (jnp.sum(ecache, axis=-1) + jnp.sum(enew, axis=-1))[..., None]
        wcache = (ecache / total).astype(jnp.bfloat16)
        wnew = (enew / total).astype(jnp.bfloat16)
        mixed = jnp.einsum("sbkgl,blkd->sbkgd", wcache, cvals, preferred_element_type=jnp.float32)
        mixed = mixed + jnp.einsum(
            "sbkgt,tbkd->sbkgd", wnew, block_v, preferred_element_type=jnp.float32
        )
        attn = mixed.astype(jnp.bfloat16).reshape(rows, qdim)
        partial_value = jnp.dot(attn, wo_local, preferred_element_type=jnp.float32).astype(
            jnp.bfloat16
        )
        pieces = partial_value.reshape(rows, n_tensor, shard).swapaxes(0, 1)
        swapped = lax.all_to_all(pieces, "tensor", split_axis=0, concat_axis=0, tiled=True)
        summed = jnp.sum(swapped.astype(jnp.float32), axis=0)
        wide = lax.dynamic_slice_in_dim(states, tpos * shard, shard, 1) + summed
        record = jnp.where(
            valid,
            lax.dynamic_update_slice(record, wide.reshape(steps, brow, shard), (0, first, 0)),
            record,
        )
        if tick < ticks - 1:
            current = from_behind(wide.astype(jnp.bfloat16), "section", 1)
    return record[None]


def solution(mesh):
    placed = (
        P(("section", "tensor"), None),
        P(),
        P("section", "tensor", None),
        P("section", None, None, "tensor"),
        P("section", None, None, "tensor"),
        P(),
        P("section", None),
        P(),
    )
    return jax.shard_map(
        per_device,
        mesh=mesh,
        in_specs=placed,
        out_specs=P("section", None, None, "tensor"),
        check_vma=False,
    )
```

time: 1550 us -> 914 us (0.59)
  waiting for transfers between devices: 996 us -> 405 us
  matrix products: 239 us -> 138 us
  blocking collectives: 0 us -> 54.3 us
  other arithmetic: 63.6 us -> 45.3 us
  starting transfers between devices: 71.6 us -> 88.5 us
    psum x19 -> x0, waiting for transfers between devices: 623 us -> none  [run_tick(): lax.psum(partial_value.astype(jnp.bfloat16), 'tensor').astype(jnp.float32)]
    dot_general x114 -> x66, matrix products: 239 us -> 138 us  [the longest x11 70.8 us: per_device(): jnp.dot(normed, weights, preferred_element_type=jnp.float32)]
    all_to_all x0 -> x7, blocking collectives: none -> 54.3 us  [per_device(): lax.all_to_all(pieces, 'tensor', split_axis=0, concat_axis=0, tiled=True)]
    ppermute x0 -> x20, waiting for transfers between devices: none -> 38 us  [the longest x10 27.9 us: per_device(): lax.ppermute(pair, 'tensor', [(t, (t + 2 * hop) % n_tensor) for t in rang...]
    reshape x38 -> x44, local copies, waits for them, and re-layouts: 0.6 us -> 25.3 us  [the longest x11 12.1 us: per_device(): lax.dynamic_slice_in_dim(keys_local, first, brow, 0)]
    all_to_all x0 -> x4, starting transfers between devices: none -> 23.1 us  [per_device(): lax.all_to_all(pieces, 'tensor', split_axis=0, concat_axis=0, tiled=True)]
    all_to_all x0 -> x4, waiting for transfers between devices: none -> 20.4 us  [per_device(): lax.all_to_all(pieces, 'tensor', split_axis=0, concat_axis=0, tiled=True)]
    while x19 -> x0, local copies, waits for them, and re-layouts: 20.4 us -> none
  transfers between devices with their start and end apart: 39 -> 35, of which waited for: 39 -> 33; matrix products, arithmetic and copies ran while one was open for 5% -> 12% of each run, Pallas kernels for 0% -> 0%
where the time goes in v1:
time: 914 us; the launch traced here: 906 us
  waiting for transfers between devices  405 us (44%)
  local copies, waits for them, and re-layouts  170 us (19%)
  matrix products  138 us (15%)
  starting transfers between devices  88.5 us (10%)
  blocking collectives  54.3 us (6%)
  other arithmetic  45.3 us (5%)
    all_to_all x1, waiting for transfers between devices, per_device(): lax.all_to_all(outgoing, ('section', 'tensor'), split_axis=1, concat_axis...  331 us
    dot_general x11, matrix products, per_device(): jnp.dot(normed, weights, preferred_element_type=jnp.float32)  70.8 us
    all_to_all x7, blocking collectives, per_device(): lax.all_to_all(pieces, 'tensor', split_axis=0, concat_axis=0, tiled=True)  54.3 us
    ppermute x10, starting transfers between devices, from_behind(): lax.ppermute(value, axis, [(source, source + steps) for source in range(l...  53.8 us
    dot_general x11, matrix products, per_device(): jnp.dot(attn, wo_local, preferred_element_type=jnp.float32)  50.5 us
    reshape x2, local copies, waits for them, and re-layouts, per_device(): outgoing = trainer_tiles.reshape(slab, devices, cdev)  49.3 us
    gather x1, local copies, waits for them, and re-layouts, per_device(): weights = arrived.reshape(-1, cdev)[picks]  34.1 us
    ppermute x10, waiting for transfers between devices, per_device(): lax.ppermute(pair, 'tensor', [(t, (t + 2 * hop) % n_tensor) for t in rang...  27.9 us
  transfers between devices with their start and end apart: 35, of which 33 were waited for; matrix products, arithmetic and copies ran while one was open for 12% of the time, Pallas kernels for 0%

profile of v1, /device:TPU:0, one launch (start us, length us, event | category | flops | bytes accessed | tf_op | source)
XLA Modules:
  0.0 906.2 jit_solution(9881445877012312534)
XLA Ops:
  0.0 28.7 %reshape.1028 = bf16[192,32,1536]{2,1,0:T(8,128)(2,1)} reshape(bf16[1536,6144]{1,0:T(8,128)(2,1)} %param.8) | data formatting | bytes 37748736 | tf_op jit(solution)/shard_map/reshape | solution.py:45
  28.7 20.6 %copy.257 = bf16[192,32,1536]{2,0,1:T(8,128)(2,1)} copy(bf16[192,32,1536]{2,1,0:T(8,128)(2,1)} %reshape.1028) | data formatting | bytes 37748736 | tf_op jit(solution)/shard_map/reshape | solution.py:45
  49.3 7.6 all-to-all-start
  57.4 25.9 %gather_fusion = s32[4096]{0:T(1024)S(1)} fusion(s32[512]{0:T(512)S(1)} %convert_reduce_fusion.11, s32[4096]{0:T(1024)S(1)} %broadcast_clamp_fusion.1), kind=kCustom, calls=%fused_computation | custom fusion | bytes 49152 | tf_op jit(solution)/shard_map/gather | solution.py:43
  89.4 15.7 %select_subtract_fusion = s32[512]{0:T(512)S(1)} fusion(pred[512]{0:T(512)(128)(4,1)S(1)} %get-tuple-element.29, pred[512]{0:T(512)(128)(4,1)S(1)} %get-tuple-element.28, pred[512]{0:T(512)(128)(4,1)S(1)} %get-tuple-element.27, pred[512]{0:T(512)(128)(4,1)S(1)} %get-tuple-element.26, pred[512]{0:T(512)(128)(4,1)S(1)} %get-tuple-element.25, ...), kind=kLoop, calls=%fused_computation.709 | loop fusion | flops 13312 | bytes 16996 | tf_op jit(solution)/shard_map/sub | solution.py:41
  105.1 25.9 %gather_fusion.1 = s32[4096]{0:T(1024)S(1)} fusion(s32[512]{0:T(512)S(1)} %select_subtract_fusion, s32[4096]{0:T(1024)S(1)} %broadcast_clamp_fusion.1), kind=kCustom, calls=%fused_computation.1 | custom fusion | bytes 49152 | tf_op jit(solution)/shard_map/gather | solution.py:44
  136.4 331.3 %all-to-all-done = bf16[192,32,1536]{2,0,1:T(8,128)(2,1)} async-done(((bf16[192,32,1536]{2,0,1:T(8,128)(2,1)}), bf16[192,32,1536]{2,0,1:T(8,128)(2,1)}, u32[]{:S(2)}, u32[]{:S(2)}) %all-to-all-start) | async-done | bytes 18874400 | tf_op jit(solution)/shard_map/all_to_all | solution.py:46
  467.7 34.1 %gather_fusion.2 = bf16[4096,1536]{1,0:T(8,128)(2,1)} fusion(bf16[6144,1536]{1,0:T(8,128)(2,1)} %bitcast.6, s32[4096]{0:T(1024)S(1)} %broadcast_clamp_fusion), kind=kCustom, calls=%fused_computation.2 | custom fusion | bytes 25182208 | tf_op jit(solution)/shard_map/gather | solution.py:50
  515.5 12.4 %all-to-all-start.1 = ((bf16[4,24,1024]{2,1,0:T(8,128)(2,1)}), bf16[4,24,1024]{2,1,0:T(8,128)(2,1)S(1)}, u32[]{:S(2)}, u32[]{:S(2)}) async-start(bf16[4,24,1024]{2,1,0:T(8,128)(2,1)} %bitcast.633), calls=%async_computation.1 | async-start | bytes 393216 | tf_op jit(solution)/shard_map/all_to_all | solution.py:136
  533.2 9.6 %collective-permute-start = (bf16[24,1024]{1,0:T(8,128)(2,1)S(1)}, bf16[24,1024]{1,0:T(8,128)(2,1)S(1)}, u32[]{:S(2)}, u32[]{:S(2)}) collective-permute-start(bf16[24,1024]{1,0:T(8,128)(2,1)S(1)} %fusion.348), channel_id=1, source_target_pairs={{0,4},{4,8},{8,12},{12,16},{16,20},{20,24},{24,28},{1,5},{5,9},{9,... | collective-permute-start | bytes 147464 | tf_op jit(solution)/shard_map/ppermute | solution.py:13
  551.2 6.4 convolution_convert_fusion.9
  564.1 8.1 all_to_all.70
  597.8 7.7 all_to_all.71
  618.1 6.4 convolution_convert_fusion.7
  631.1 7.7 all_to_all.72
  653.9 6.4 convolution_convert_fusion.6
  666.9 7.7 all_to_all.73
  689.5 6.4 convolution_convert_fusion.5
  702.4 7.7 all_to_all.74
  727.4 6.5 convolution_convert_fusion.4
  740.4 7.7 all_to_all.75
  764.0 6.5 convolution_convert_fusion.3
  777.0 7.7 all_to_all.76
  807.5 6.5 convolution_convert_fusion.2
  (468 shorter events, 288.8 us)
Async XLA Ops:
  49.3 418.4 %all-to-all-start = ((bf16[192,32,1536]{2,0,1:T(8,128)(2,1)}), bf16[192,32,1536]{2,0,1:T(8,128)(2,1)}, u32[]{:S(2)}, u32[]{:S(2)}) async-start(bf16[192,32,1536]{2,0,1:T(8,128)(2,1)} %copy.257), calls=%async_computation | async-start | bytes 37748736 | tf_op jit(solution)/shard_map/all_to_all | solution.py:46
  515.5 17.7 %all-to-all-start.1 = ((bf16[4,24,1024]{2,1,0:T(8,128)(2,1)}), bf16[4,24,1024]{2,1,0:T(8,128)(2,1)S(1)}, u32[]{:S(2)}, u32[]{:S(2)}) async-start(bf16[4,24,1024]{2,1,0:T(8,128)(2,1)} %bitcast.633), calls=%async_computation.1 | async-start | bytes 393216 | tf_op jit(solution)/shard_map/all_to_all | solution.py:136
  533.2 11.1 %collective-permute-start = (bf16[24,1024]{1,0:T(8,128)(2,1)S(1)}, bf16[24,1024]{1,0:T(8,128)(2,1)S(1)}, u32[]{:S(2)}, u32[]{:S(2)}) collective-permute-start(bf16[24,1024]{1,0:T(8,128)(2,1)S(1)} %fusion.348), channel_id=1, source_target_pairs={{0,4},{4,8},{8,12},{12,16},{16,20},{20,24},{24,28},{1,5},{5,9},{9,... | collective-permute-start | bytes 147464 | tf_op jit(solution)/shard_map/ppermute | solution.py:13
  545.6 5.2 collective-permute-start.2
  572.3 6.0 collective-permute-start.3
  579.5 4.9 collective-permute-start.5
  605.5 6.0 collective-permute-start.6
  638.9 6.0 collective-permute-start.9
  646.8 5.1 collective-permute-start.11
  674.6 6.4 collective-permute-start.12
  682.9 5.2 collective-permute-start.14
  710.2 6.9 collective-permute-start.15
  719.0 5.2 collective-permute-start.17
  748.8 6.9 collective-permute-start.18
  785.4 6.9 collective-permute-start.21
  792.3 9.5 %collective-permute-start.22 = (bf16[24,1024]{1,0:T(8,128)(2,1)S(1)}, bf16[24,1024]{1,0:T(8,128)(2,1)S(1)}, u32[]{:S(2)}, u32[]{:S(2)}) collective-permute-start(bf16[24,1024]{1,0:T(8,128)(2,1)S(1)} %collective-permute-done.21), channel_id=1, source_target_pairs={{0,1},{1,0},{2,3},{3,2},{4,5},{5,4},{6,7},{7,6},{8,9},{9,8},{10,11... | collective-permute-start | bytes 147464 | tf_op jit(solution)/shard_map/ppermute | solution.py:77
  801.8 5.3 collective-permute-start.23
  821.2 9.4 %all-to-all-start.9 = ((bf16[4,24,1024]{2,1,0:T(8,128)(2,1)}), bf16[4,24,1024]{2,1,0:T(8,128)(2,1)}, u32[]{:S(2)}, u32[]{:S(2)}) async-start(bf16[4,24,1024]{2,1,0:T(8,128)(2,1)} %bitcast.658), calls=%async_computation.9 | async-start | bytes 393216 | tf_op jit(solution)/shard_map/all_to_all | solution.py:136
  832.5 6.9 collective-permute-start.24
  840.7 4.9 collective-permute-start.26
  860.6 8.7 all-to-all-start.10
  869.3 7.0 collective-permute-start.27
  877.6 5.0 collective-permute-start.29
  896.6 8.7 all-to-all-start.11
  (61 other events, 952.1 us)

commit v2 on v0

v2 whole, which is shorter than its diff:
```python
import functools

import jax
import jax.numpy as jnp
import numpy as np
from jax import lax
from jax.experimental import pallas as pl
from jax.experimental.pallas import tpu as pltpu
from jax.sharding import Mesh, PartitionSpec as P

HDIM = 128
FB = 8
STREAMS = 2
ITEMS = 2
ROWBLOCK = 256
CHUNK = 384
WINDOW = 512
VMEM = 48 * 1024 * 1024


def sort_kernel(first, layers, kept, slab, out):
    feats = ROWBLOCK // layers
    row = lax.broadcasted_iota(jnp.int32, (kept * feats, ROWBLOCK), 0)
    col = lax.broadcasted_iota(jnp.int32, (kept * feats, ROWBLOCK), 1)
    source = row % feats * layers + first + row // feats
    order = jnp.where(col == source, 1.0, 0.0).astype(jnp.bfloat16)
    moved = jnp.dot(order, slab[...], preferred_element_type=jnp.float32).astype(jnp.bfloat16)
    for layer in range(kept):
        out[layer, 0] = moved[layer * feats : (layer + 1) * feats]


def sort_slab(slab, phase, layers, n_tensor):
    rows, columns = slab.shape
    kept = layers // 2
    cdev = columns // n_tensor
    feats = ROWBLOCK // layers
    return pl.pallas_call(
        functools.partial(sort_kernel, phase * kept, layers, kept),
        grid=(n_tensor, rows // ROWBLOCK),
        in_specs=[pl.BlockSpec((ROWBLOCK, cdev), lambda t, i: (i, t))],
        out_specs=pl.BlockSpec((kept, 1, feats, cdev), lambda t, i: (0, t, i, 0)),
        out_shape=jax.ShapeDtypeStruct((kept, n_tensor, rows // layers, cdev), jnp.bfloat16),
        compiler_params=pltpu.CompilerParams(vmem_limit_bytes=VMEM),
        cost_estimate=pl.CostEstimate(
            flops=rows * columns * ROWBLOCK, bytes_accessed=3 * rows * columns, transcendentals=0
        ),
    )(slab)


def project_kernel(tick, tiles, tilew, n_y, use, scalars, mine, other, gains, *rest):
    weights, (out, normed, acc) = rest[: len(use)], rest[len(use) :]
    j = pl.program_id(0)
    rows, half = mine.shape
    width = 2 * half
    shard = half // n_y
    core, phase = scalars[0], scalars[1 + tick]

    @pl.when(j == 0)
    def _():
        here = mine[...].astype(jnp.float32)
        there = other[...].astype(jnp.float32)
        total = jnp.sum(here * here, axis=1, keepdims=True)
        total = total + jnp.sum(there * there, axis=1, keepdims=True)
        inverse = lax.rsqrt(total / width + 1e-06)
        gain = jnp.where(phase == 0, gains[0:1], gains[1:2])
        low = jnp.where(core == 0, here, there) * inverse
        high = jnp.where(core == 0, there, here) * inverse
        for y in range(n_y):
            at = 2 * y * shard
            piece = slice(y * shard, (y + 1) * shard)
            normed[:, at : at + shard] = low[:, piece] * gain[:, at : at + shard]
            at = at + shard
            normed[:, at : at + shard] = high[:, piece] * gain[:, at : at + shard]
        normed[:, width:] = jnp.zeros((rows, WINDOW), jnp.float32)
        acc[...] = jnp.zeros_like(acc)

    per = CHUNK // tilew
    base = scalars.shape[0] - 2 * tiles
    lane = lax.broadcasted_iota(jnp.int32, (rows, CHUNK), 1)
    spread = jnp.zeros((rows, CHUNK), jnp.float32)
    for a in range(per):
        start = scalars[base + j * per + a] * FB
        count = scalars[base + tiles + j * per + a] * FB
        aligned = start // 128 * 128
        window = normed[:, pl.ds(pl.multiple_of(aligned, 128), WINDOW)]
        put = a * tilew
        shift = (put - (start - aligned) + WINDOW) % WINDOW
        rolled = pltpu.roll(window, shift, 1)[:, :CHUNK]
        spread = jnp.where((lane >= put) & (lane < put + count), rolled, spread)
    spread = spread.astype(jnp.bfloat16)
    if len(use) == 1:
        acc[...] += jnp.dot(spread, weights[0][...], preferred_element_type=jnp.float32)
    else:

        @pl.when(phase == 0)
        def _():
            acc[...] += jnp.dot(spread, weights[0][...], preferred_element_type=jnp.float32)

        @pl.when(phase == 1)
        def _():
            acc[...] += jnp.dot(spread, weights[1][...], preferred_element_type=jnp.float32)

    @pl.when(j == pl.num_programs(0) - 1)
    def _():
        out[...] = acc[...].astype(jnp.bfloat16)


def project(tick, use, tiles, tilew, n_y, scalars, mine, other, gains, weights):
    rows, half = mine.shape
    depth, cdev = weights[0].shape
    if len(use) == 1:
        maps = [lambda j, s: (j, 0)]
    else:
        maps = [
            lambda j, s: (jnp.where(s[1 + tick] == 0, j, 0), 0),
            lambda j, s: (jnp.where(s[1 + tick] == 1, j, 0), 0),
        ]
    whole = lambda j, s: (0, 0)
    return pl.pallas_call(
        functools.partial(project_kernel, tick, tiles, tilew, n_y, use),
        grid_spec=pltpu.PrefetchScalarGridSpec(
            num_scalar_prefetch=1,
            grid=(depth // CHUNK,),
            in_specs=[
                pl.BlockSpec((rows, half), whole),
                pl.BlockSpec((rows, half), whole),
                pl.BlockSpec(gains.shape, whole),
            ]
            + [pl.BlockSpec((CHUNK, cdev), m) for m in maps],
            out_specs=pl.BlockSpec((rows, cdev), whole),
            scratch_shapes=[
                pltpu.VMEM((rows, 2 * half + WINDOW), jnp.float32),
                pltpu.VMEM((rows, cdev), jnp.float32),
            ],
        ),
        out_shape=jax.ShapeDtypeStruct((rows, cdev), jnp.bfloat16),
        compiler_params=pltpu.CompilerParams(vmem_limit_bytes=VMEM),
        cost_estimate=pl.CostEstimate(
            flops=2 * rows * depth * cdev, bytes_accessed=2 * depth * cdev, transcendentals=0
        ),
    )(scalars, mine, other, gains, *weights)


def attend_kernel(steps, brow, kvlocal, groups, n_y, scalars, own, sent, span, ckeys, cvals, wo, theirs, ours, attn):
    k = pl.program_id(0)
    rows = steps * brow
    length = ckeys.shape[1]
    scale = 1.0 / HDIM**0.5
    qdim = kvlocal * groups * HDIM
    kvdim = kvlocal * HDIM

    @pl.when(k == 0)
    def _():
        qkv = (own[...].astype(jnp.float32) + sent[...].astype(jnp.float32)).astype(jnp.bfloat16)
        qkv = qkv.astype(jnp.float32)
        keys = ckeys[...].reshape(brow * length, kvdim)
        values = cvals[...].reshape(brow * length, kvdim)
        tall = groups * rows
        at = lax.broadcasted_iota(jnp.int32, (tall, brow * length), 0)
        col = lax.broadcasted_iota(jnp.int32, (tall, brow * length), 1)
        cmask = (at % brow == col // length) & (col % length < span[0])
        at = lax.broadcasted_iota(jnp.int32, (tall, rows), 0)
        col = lax.broadcasted_iota(jnp.int32, (tall, rows), 1)
        nmask = (at % brow == col % brow) & (col // brow <= at % rows // brow)
        contract = (((1,), (1,)), ((), ()))
        for head in range(kvlocal):
            lanes = slice(head * HDIM, (head + 1) * HDIM)
            first = head * groups * HDIM
            query = jnp.concatenate(
                [qkv[:, first + g * HDIM : first + (g + 1) * HDIM] for g in range(groups)], axis=0
            ).astype(jnp.bfloat16)
            at = qdim + head * HDIM
            knew = qkv[:, at : at + HDIM].astype(jnp.bfloat16)
            at = at + kvdim
            vnew = qkv[:, at : at + HDIM].astype(jnp.bfloat16)
            scache = scale * lax.dot_general(
                query, keys[:, lanes], contract, preferred_element_type=jnp.float32
            )
            snew = scale * lax.dot_general(
                query, knew, contract, preferred_element_type=jnp.float32
            )
            scache = jnp.where(cmask, scache, -1e30)
            snew = jnp.where(nmask, snew, -1e30)
            top = jnp.maximum(
                jnp.max(scache, axis=1, keepdims=True), jnp.max(snew, axis=1, keepdims=True)
            )
            ecache = jnp.where(cmask, jnp.exp(scache - top), 0.0)
            enew = jnp.where(nmask, jnp.exp(snew - top), 0.0)
            total = jnp.sum(ecache, axis=1, keepdims=True) + jnp.sum(enew, axis=1, keepdims=True)
            inverse = 1.0 / total
            wcache = (ecache * inverse).astype(jnp.bfloat16)
            wnew = (enew * inverse).astype(jnp.bfloat16)
            mixed = jnp.dot(wcache, values[:, lanes], preferred_element_type=jnp.float32)
            mixed = mixed + jnp.dot(wnew, vnew, preferred_element_type=jnp.float32)
            for g in range(groups):
                attn[:, first + g * HDIM : first + (g + 1) * HDIM] = mixed[
                    g * rows : (g + 1) * rows
                ].astype(jnp.bfloat16)

    product = jnp.dot(attn[...], wo[0], preferred_element_type=jnp.float32).astype(jnp.bfloat16)

    @pl.when(k < n_y)
    def _():
        theirs[...] = product

    @pl.when(k >= n_y)
    def _():
        ours[...] = product


def attend(item_at, steps, brow, n_y, scalars, own, sent, spans, keys, values, wo):
    rows, cdev = own.shape
    _, qdim, width = wo.shape
    length, kvdim = keys.shape[1:]
    kvlocal = kvdim // HDIM
    groups = qdim // kvdim
    shard = width // (2 * n_y)
    whole = lambda k, s: (0, 0)
    return pl.pallas_call(
        functools.partial(attend_kernel, steps, brow, kvlocal, groups, n_y),
        grid_spec=pltpu.PrefetchScalarGridSpec(
            num_scalar_prefetch=1,
            grid=(2 * n_y,),
            in_specs=[
                pl.BlockSpec((rows, cdev), whole),
                pl.BlockSpec((rows, cdev), whole),
                pl.BlockSpec((1, 1, brow * length), lambda k, s: (s[item_at], 0, 0)),
                pl.BlockSpec((brow, length, kvdim), lambda k, s: (s[item_at], 0, 0)),
                pl.BlockSpec((brow, length, kvdim), lambda k, s: (s[item_at], 0, 0)),
                pl.BlockSpec(
                    (1, qdim, shard),
                    lambda k, s: (0, 0, k % n_y * 2 + jnp.where(k < n_y, 1 - s[0], s[0])),
                ),
            ],
            out_specs=[
                pl.BlockSpec((rows, shard), lambda k, s: (0, jnp.minimum(k, n_y - 1))),
                pl.BlockSpec((rows, shard), lambda k, s: (0, jnp.maximum(k - n_y, 0))),
            ],
            scratch_shapes=[pltpu.VMEM((rows, qdim), jnp.bfloat16)],
        ),
        out_shape=[jax.ShapeDtypeStruct((rows, shard * n_y), jnp.bfloat16)] * 2,
        compiler_params=pltpu.CompilerParams(vmem_limit_bytes=VMEM),
        cost_estimate=pl.CostEstimate(
            flops=2 * rows * qdim * width, bytes_accessed=2 * qdim * width, transcendentals=0
        ),
    )(scalars, own, sent, spans, keys, values, wo)


def per_device(
    trainer_tiles,
    tile_lengths,
    wo_rollout,
    cache_keys,
    cache_values,
    cache_lengths,
    norm_gain,
    step_inputs,
):
    n_zone = lax.axis_size("zone")
    n_spot = lax.axis_size("spot")
    n_tensor = lax.axis_size("tensor")
    layers = n_zone * n_spot
    tiles = n_spot * n_tensor
    n_y = n_tensor // 2
    slab, columns = trainer_tiles.shape
    cdev = columns // n_tensor
    tilew = slab // layers
    width = wo_rollout.shape[2]
    shard = width // n_tensor
    half = n_y * shard
    steps = step_inputs.shape[0]
    seqs, length = cache_keys.shape[1:3]
    n_item = STREAMS * ITEMS
    brow = seqs // n_item
    rows = steps * brow
    ticks = layers + ITEMS - 1
    zone = lax.axis_index("zone")
    spot = lax.axis_index("spot")
    tpos = lax.axis_index("tensor")
    core = tpos % 2
    layer = zone * n_spot + spot

    weights = []
    for phase in range(2):
        ordered = sort_slab(trainer_tiles, phase, layers, n_tensor)
        arrived = lax.all_to_all(
            ordered.reshape(tiles, tilew, cdev),
            ("spot", "tensor"),
            split_axis=0,
            concat_axis=0,
            tiled=True,
        )
        weights.append(arrived.reshape(tiles * tilew, cdev))

    ends = jnp.cumsum(tile_lengths)
    starts = lax.dynamic_slice_in_dim(ends - tile_lengths, zone * tiles, tiles)
    counts = lax.dynamic_slice_in_dim(tile_lengths, zone * tiles, tiles)
    tick_ids = jnp.arange(ticks, dtype=jnp.int32)
    phases = (tick_ids >= spot + n_spot).astype(jnp.int32)
    turns = jnp.clip(tick_ids - layer, 0, ITEMS - 1)
    turns = jnp.concatenate([turns + stream * ITEMS for stream in range(STREAMS)])
    scalars = jnp.concatenate([core[None], phases, turns, starts, counts]).astype(jnp.int32)
    flip = [(z, 1 - z) for z in range(2)]
    swapped = lax.ppermute(norm_gain, "zone", flip)
    gains = jnp.concatenate(
        [jnp.where(zone == 0, norm_gain, swapped), jnp.where(zone == 0, swapped, norm_gain)]
    )
    spans = jnp.repeat(cache_lengths, length).reshape(n_item, 1, brow * length)
    axes = ("zone", "spot", "tensor")

    def device(z, s, t):
        return (z * n_spot + s) * n_tensor + t

    def split(pairs, value):
        return lax.ppermute(value, axes, pairs)

    def active(tick):
        return [l for l in range(layers) if 0 <= tick - l < ITEMS]

    across = [(t, t ^ 1) for t in range(n_tensor)]
    shown = step_inputs.reshape(steps, n_item, brow, n_y, 2, shard)
    records = []
    for stream in range(STREAMS):
        arrived, record = None, []
        for tick in range(ticks):
            busy = active(tick)
            if tick < ITEMS:
                item = stream * ITEMS + tick
                fresh = shown[:, item].reshape(rows, n_y, 2, shard)
                mine = lax.dynamic_index_in_dim(fresh, core, 2, False).reshape(rows, half)
                mine = jnp.where(spot == 0, mine, 0)
                if tick:
                    mine = mine + arrived
            else:
                mine = arrived
            if tick:
                other = lax.ppermute(mine, "tensor", across)
            else:
                other = lax.dynamic_index_in_dim(fresh, 1 - core, 2, False).reshape(rows, half)
            use = sorted({l // n_spot for l in busy})
            own = project(
                tick, use, tiles, tilew, n_y, scalars, mine, other, gains, [weights[p] for p in use]
            )
            pairs = [
                (device(1 - l // n_spot, l % n_spot, t), device(l // n_spot, l % n_spot, t))
                for l in busy
                for t in range(n_tensor)
            ]
            sent = split(pairs, own)
            item_at = 1 + ticks + stream * ticks + tick
            theirs, ours = attend(
                item_at, steps, brow, n_y, scalars, own, sent, spans, cache_keys[0], cache_values[0], wo_rollout
            )
            part = ours.astype(jnp.float32) + lax.ppermute(theirs, "tensor", across).astype(
                jnp.float32
            )
            bit = 2
            while bit < n_tensor:
                part = part.astype(jnp.bfloat16)
                moved = lax.ppermute(part, "tensor", [(t, t ^ bit) for t in range(n_tensor)])
                part = part.astype(jnp.float32) + moved.astype(jnp.float32)
                bit = bit * 2
            wide = mine.astype(jnp.float32) + part
            record.append(lax.dynamic_slice_in_dim(wide, tpos // 2 * shard, shard, 1))
            after = wide.astype(jnp.bfloat16)
            going = [l for l in busy if l + 1 < layers]
            if tick + 1 < ticks:
                arrived = 0
                for turn in range(2):
                    pairs = []
                    for l in going:
                        home = l // n_spot
                        for t in range(n_tensor):
                            source = device(home, l % n_spot, t)
                            pairs.append((source, device(home ^ turn, (l + 1) % n_spot, t)))
                    arrived = arrived + split(pairs, after)
        record = jnp.stack(record)
        record = lax.dynamic_slice_in_dim(record, layer, ITEMS, 0)
        record = record.reshape(ITEMS, steps, brow, shard).swapaxes(0, 1)
        records.append(record.reshape(steps, ITEMS * brow, shard))
    return jnp.concatenate(records, axis=1)[None]


def solution(mesh):
    n_section, n_tensor = mesh.devices.shape
    fine = Mesh(mesh.devices.reshape(2, n_section // 2, n_tensor), ("zone", "spot", "tensor"))
    section = ("zone", "spot")
    placed = (
        P(("zone", "spot", "tensor"), None),
        P(),
        P(section, "tensor", None),
        P(section, None, None, "tensor"),
        P(section, None, None, "tensor"),
        P(),
        P(section, None),
        P(),
    )
    return jax.shard_map(
        per_device,
        mesh=fine,
        in_specs=placed,
        out_specs=P(section, None, None, "tensor"),
        check_vma=False,
    )
```

time: 1550 us -> 860 us (0.55)
  waiting for transfers between devices: 996 us -> 312 us
  Pallas kernels: 0 us -> 303 us
  matrix products: 239 us -> 0 us
  local copies, waits for them, and re-layouts: 160 us -> 3.12 us
  starting transfers between devices: 71.6 us -> 221 us
  other arithmetic: 63.6 us -> 5.11 us
    psum x19 -> x0, waiting for transfers between devices: 623 us -> none  [run_tick(): lax.psum(partial_value.astype(jnp.bfloat16), 'tensor').astype(jnp.float32)]
    pallas_call x0 -> x38, Pallas kernels: none -> 303 us  [the longest x18 144 us: project(): pl.pallas_call(functools.partial(project_kernel, tick, tiles, tilew, n_y,...]
    dot_general x114 -> x0, matrix products: 239 us -> none  [the longest x19 120 us: run_tick(): jnp.dot(normed, weights, preferred_element_type=jnp.float32)]
    all_to_all x1 -> x2, waiting for transfers between devices: 337 us -> 117 us  [per_device(): lax.all_to_all(ordered.reshape(tiles, tilew, cdev), ('spot', 'tensor'), s...]
    ppermute x19 -> x103, waiting for transfers between devices: 35.3 us -> 194 us  [the longest x1 131 us: per_device(): swapped = lax.ppermute(norm_gain, 'zone', flip)]
    ppermute x19 -> x103, starting transfers between devices: 64.1 us -> 209 us  [the longest x50 174 us: split(): return lax.ppermute(value, axes, pairs)]
    gather x5 -> x0, local copies, waits for them, and re-layouts: 87.3 us -> none  [the longest x1 34.2 us: per_device(): weights = arrived.reshape(-1, cdev)[picks]]
    reshape x40 -> x2, local copies, waits for them, and re-layouts: 49.9 us -> 0.05 us  [per_device(): records.append(record.reshape(steps, ITEMS * brow, shard))]
  transfers between devices with their start and end apart: 39 -> 105, of which waited for: 39 -> 29; matrix products, arithmetic and copies ran while one was open for 5% -> 1% of each run, Pallas kernels for 0% -> 33%
where the time goes in v2:
time: 860 us; the launch traced here: 846 us
  waiting for transfers between devices  312 us (36%)
  Pallas kernels  303 us (35%)
  starting transfers between devices  221 us (26%)
    ppermute x50, starting transfers between devices, split(): return lax.ppermute(value, axes, pairs)  174 us
    pallas_call x18, Pallas kernels, project(): pl.pallas_call(functools.partial(project_kernel, tick, tiles, tilew, n_y,...  144 us
    ppermute x1, waiting for transfers between devices, per_device(): swapped = lax.ppermute(norm_gain, 'zone', flip)  131 us
    all_to_all x2, waiting for transfers between devices, per_device(): lax.all_to_all(ordered.reshape(tiles, tilew, cdev), ('spot', 'tensor'), s...  117 us
    pallas_call x18, Pallas kernels, attend(): pl.pallas_call(functools.partial(attend_kernel, steps, brow, kvlocal, gro...  117 us
    pallas_call x2, Pallas kernels, sort_slab(): pl.pallas_call(functools.partial(sort_kernel, phase * kept, layers, kept)...  41.5 us
    ppermute x18, waiting for transfers between devices, per_device(): lax.ppermute(part, 'tensor', [(t, t ^ bit) for t in range(n_tensor)])  29.2 us
    ppermute x50, waiting for transfers between devices, split(): return lax.ppermute(value, axes, pairs)  28.6 us
  transfers between devices with their start and end apart: 105, of which 29 were waited for; matrix products, arithmetic and copies ran while one was open for 1% of the time, Pallas kernels for 33%

profile of v2, /device:TPU:0, one launch (start us, length us, event | category | flops | bytes accessed | tf_op | source)
XLA Modules:
  0.0 845.8 jit_solution(16407880007983980941)
XLA Ops:
  0.0 20.7 %shard_map.82 = bf16[4,4,192,1536]{3,2,1,0:T(8,128)(2,1)} custom-call(bf16[1536,6144]{1,0:T(8,128)(2,1)} %slab.3), custom_call_target="tpu_custom_call" | custom-call | flops 2415919104 | bytes 28311552 | tf_op jit(solution)/shard_map/pallas_call | solution.py:37
  27.1 20.8 %shard_map.91 = bf16[4,4,192,1536]{3,2,1,0:T(8,128)(2,1)} custom-call(bf16[1536,6144]{1,0:T(8,128)(2,1)} %slab.3), custom_call_target="tpu_custom_call" | custom-call | flops 2415919104 | bytes 28311552 | tf_op jit(solution)/shard_map/pallas_call | solution.py:37
  47.9 117.1 %all-to-all-done = bf16[16,192,1536]{2,1,0:T(8,128)(2,1)} async-done(((bf16[16,192,1536]{2,1,0:T(8,128)(2,1)}), bf16[16,192,1536]{2,1,0:T(8,128)(2,1)}, u32[]{:S(2)}, u32[]{:S(2)}) %all-to-all-start) | async-done | bytes 9437216 | tf_op jit(solution)/shard_map/all_to_all | solution.py:286
  177.9 130.8 %collective-permute-done = f32[1,4096]{1,0:T(1,128)S(1)} collective-permute-done((f32[1,4096]{1,0:T(1,128)S(1)}, f32[1,4096]{1,0:T(1,128)S(1)}, u32[]{:S(2)}, u32[]{:S(2)}) %collective-permute-start) | collective-permute-done | bytes 16416 | tf_op jit(solution)/shard_map/ppermute | solution.py:304
  308.9 8.0 shard_map.83.own
  319.1 8.0 shard_map.102.own
  355.6 8.0 shard_map.85.own
  377.6 8.0 shard_map.104.own
  416.6 8.0 shard_map.87.own
  432.3 8.0 shard_map.106.own
  459.0 8.0 shard_map.89.own
  466.9 25.5 %collective-permute-start.19 = (bf16[24,1536]{1,0:T(8,128)(2,1)S(1)}, bf16[24,1536]{1,0:T(8,128)(2,1)S(1)}, u32[]{:S(2)}, u32[]{:S(2)}) collective-permute-start(bf16[24,1536]{1,0:T(8,128)(2,1)S(1)} %shard_map.89.own), channel_id=1, source_target_pairs={{24,8},{25,9},{26,10},{27,11},{28,12},{29,13},{30,14},{31,15}} | collective-permute-start | bytes 221192 | tf_op jit(solution)/shard_map/ppermute | solution.py:315
  492.5 8.0 shard_map.108.own
  551.5 8.5 %shard_map.92.own = bf16[24,1536]{1,0:T(8,128)(2,1)S(1)} custom-call(s32[60]{0:T(128)S(1)} %concatenate.9.scalars, bf16[24,2048]{1,0:T(8,128)(2,1)S(1)} %add.294.mine, bf16[24,2048]{1,0:T(8,128)(2,1)S(1)} %collective-permute-done.24.other, f32[2,4096]{1,0:T(2,128)S(1)} %pad_maximum_fusion.gains, bf16[3072,1536]{1,0:T(8,128)(2,1)} %bitcast.5.rest_0_, ...), custom_call_target="tpu_custom_call" | custom-call | flops 226492416 | bytes 9437184 | tf_op jit(solution)/shard_map/pallas_call | solution.py:119
  561.5 8.5 %shard_map.110.own = bf16[24,1536]{1,0:T(8,128)(2,1)S(1)} custom-call(s32[60]{0:T(128)S(1)} %concatenate.9.scalars, bf16[24,2048]{1,0:T(8,128)(2,1)S(1)} %add.331.mine, bf16[24,2048]{1,0:T(8,128)(2,1)S(1)} %collective-permute-done.75.other, f32[2,4096]{1,0:T(2,128)S(1)} %pad_maximum_fusion.gains, bf16[3072,1536]{1,0:T(8,128)(2,1)} %bitcast.5.rest_0_, ...), custom_call_target="tpu_custom_call" | custom-call | flops 226492416 | bytes 9437184 | tf_op jit(solution)/shard_map/pallas_call | solution.py:119
  623.0 8.0 shard_map.94.own
  632.5 8.0 shard_map.112.own
  686.2 8.0 shard_map.96.own
  694.9 8.0 shard_map.114.own
  723.0 11.7 %collective-permute-start.41 = (bf16[24,2048]{1,0:T(8,128)(2,1)S(1)}, bf16[24,2048]{1,0:T(8,128)(2,1)S(1)}, u32[]{:S(2)}, u32[]{:S(2)}) collective-permute-start(bf16[24,2048]{1,0:T(8,128)(2,1)S(1)} %get-tuple-element.79), channel_id=1, source_target_pairs={{20,8},{21,9},{22,10},{23,11},{24,12},{25,13},{26,14},{27,15}} | collective-permute-start | bytes 294920 | tf_op jit(solution)/shard_map/ppermute | solution.py:315
  764.0 8.0 shard_map.116.own
  771.9 11.1 %collective-permute-start.94 = (bf16[24,1536]{1,0:T(8,128)(2,1)S(1)}, bf16[24,1536]{1,0:T(8,128)(2,1)S(1)}, u32[]{:S(2)}, u32[]{:S(2)}) collective-permute-start(bf16[24,1536]{1,0:T(8,128)(2,1)S(1)} %shard_map.116.own), channel_id=1, source_target_pairs={{8,24},{9,25},{10,26},{11,27},{12,28},{13,29},{14,30},{15,31}} | collective-permute-start | bytes 221192 | tf_op jit(solution)/shard_map/ppermute | solution.py:315
  806.9 8.0 shard_map.100.own
  815.5 8.0 shard_map.118.own
  (345 shorter events, 369.5 us)
Async XLA Ops:
  20.7 144.2 %all-to-all-start = ((bf16[16,192,1536]{2,1,0:T(8,128)(2,1)}), bf16[16,192,1536]{2,1,0:T(8,128)(2,1)}, u32[]{:S(2)}, u32[]{:S(2)}) async-start(bf16[16,192,1536]{2,1,0:T(8,128)(2,1)} %bitcast.132), calls=%async_computation | async-start | bytes 18874368 | tf_op jit(solution)/shard_map/all_to_all | solution.py:286
  164.9 386.5 %all-to-all-start.1 = ((bf16[16,192,1536]{2,1,0:T(8,128)(2,1)}), bf16[16,192,1536]{2,1,0:T(8,128)(2,1)}, u32[]{:S(2)}, u32[]{:S(2)}) async-start(bf16[16,192,1536]{2,1,0:T(8,128)(2,1)} %bitcast.131), calls=%async_computation.1 | async-start | bytes 18874368 | tf_op jit(solution)/shard_map/all_to_all | solution.py:286
  170.7 138.1 %collective-permute-start = (f32[1,4096]{1,0:T(1,128)S(1)}, f32[1,4096]{1,0:T(1,128)S(1)}, u32[]{:S(2)}, u32[]{:S(2)}) collective-permute-start(f32[1,4096]{1,0:T(1,128)S(1)} %copy-done.8), channel_id=1, source_target_pairs={{0,16},{16,0},{1,17},{17,1},{2,18},{18,2},{3,19},{19,3},{4,20},{20... | collective-permute-start | bytes 49160 | tf_op jit(solution)/shard_map/ppermute | solution.py:304
  355.5 22.1 %collective-permute-start.57 = (bf16[24,2048]{1,0:T(8,128)(2,1)S(1)}, bf16[24,2048]{1,0:T(8,128)(2,1)S(1)}, u32[]{:S(2)}, u32[]{:S(2)}) collective-permute-start(bf16[24,2048]{1,0:T(8,128)(2,1)S(1)} %add_add_fusion.16.mine), channel_id=1, source_target_pairs={{0,1},{1,0},{2,3},{3,2},{4,5},{5,4},{6,7},{7,6},{8,9},{9,8},{10,11... | collective-permute-start | bytes 294920 | tf_op jit(solution)/shard_map/ppermute | solution.py:337
  377.5 22.1 %collective-permute-start.8 = (bf16[24,2048]{1,0:T(8,128)(2,1)S(1)}, bf16[24,2048]{1,0:T(8,128)(2,1)S(1)}, u32[]{:S(2)}, u32[]{:S(2)}) collective-permute-start(bf16[24,2048]{1,0:T(8,128)(2,1)S(1)} %get-tuple-element.44), channel_id=1, source_target_pairs={{0,1},{1,0},{2,3},{3,2},{4,5},{5,4},{6,7},{7,6},{8,9},{9,8},{10,11... | collective-permute-start | bytes 294920 | tf_op jit(solution)/shard_map/ppermute | solution.py:354
  416.5 15.8 %collective-permute-start.63 = (bf16[24,2048]{1,0:T(8,128)(2,1)S(1)}, bf16[24,2048]{1,0:T(8,128)(2,1)S(1)}, u32[]{:S(2)}, u32[]{:S(2)}) collective-permute-start(bf16[24,2048]{1,0:T(8,128)(2,1)S(1)} %add.323.mine), channel_id=1, source_target_pairs={{0,1},{1,0},{2,3},{3,2},{4,5},{5,4},{6,7},{7,6},{8,9},{9,8},{10,11... | collective-permute-start | bytes 294920 | tf_op jit(solution)/shard_map/ppermute | solution.py:337
  431.8 16.0 %collective-permute-start.14 = (bf16[24,2048]{1,0:T(8,128)(2,1)S(1)}, bf16[24,2048]{1,0:T(8,128)(2,1)S(1)}, u32[]{:S(2)}, u32[]{:S(2)}) collective-permute-start(bf16[24,2048]{1,0:T(8,128)(2,1)S(1)} %get-tuple-element.46), channel_id=1, source_target_pairs={{0,1},{1,0},{2,3},{3,2},{4,5},{5,4},{6,7},{7,6},{8,9},{9,8},{10,11... | collective-permute-start | bytes 294920 | tf_op jit(solution)/shard_map/ppermute | solution.py:354
  457.7 34.7 %collective-permute-start.69 = (bf16[24,2048]{1,0:T(8,128)(2,1)S(1)}, bf16[24,2048]{1,0:T(8,128)(2,1)S(1)}, u32[]{:S(2)}, u32[]{:S(2)}) collective-permute-start(bf16[24,2048]{1,0:T(8,128)(2,1)S(1)} %add.327.mine), channel_id=1, source_target_pairs={{0,1},{1,0},{2,3},{3,2},{4,5},{5,4},{6,7},{7,6},{8,9},{9,8},{10,11... | collective-permute-start | bytes 294920 | tf_op jit(solution)/shard_map/ppermute | solution.py:337
  466.9 40.5 %collective-permute-start.19 = (bf16[24,1536]{1,0:T(8,128)(2,1)S(1)}, bf16[24,1536]{1,0:T(8,128)(2,1)S(1)}, u32[]{:S(2)}, u32[]{:S(2)}) collective-permute-start(bf16[24,1536]{1,0:T(8,128)(2,1)S(1)} %shard_map.89.own), channel_id=1, source_target_pairs={{24,8},{25,9},{26,10},{27,11},{28,12},{29,13},{30,14},{31,15}} | collective-permute-start | bytes 221192 | tf_op jit(solution)/shard_map/ppermute | solution.py:315
  500.5 14.6 %collective-permute-start.70 = (bf16[24,1536]{1,0:T(8,128)(2,1)S(1)}, bf16[24,1536]{1,0:T(8,128)(2,1)S(1)}, u32[]{:S(2)}, u32[]{:S(2)}) collective-permute-start(bf16[24,1536]{1,0:T(8,128)(2,1)S(1)} %shard_map.108.own), channel_id=1, source_target_pairs={{24,8},{25,9},{26,10},{27,11},{28,12},{29,13},{30,14},{31,15}} | collective-permute-start | bytes 221192 | tf_op jit(solution)/shard_map/ppermute | solution.py:315
  528.2 16.0 %collective-permute-start.23 = (bf16[24,2048]{1,0:T(8,128)(2,1)S(1)}, bf16[24,2048]{1,0:T(8,128)(2,1)S(1)}, u32[]{:S(2)}, u32[]{:S(2)}) collective-permute-start(bf16[24,2048]{1,0:T(8,128)(2,1)S(1)} %get-tuple-element.85), channel_id=1, source_target_pairs={{8,28},{9,29},{10,30},{11,31},{12,16},{13,17},{14,18},{15,19}} | collective-permute-start | bytes 294920 | tf_op jit(solution)/shard_map/ppermute | solution.py:315
  586.8 16.8 %collective-permute-start.78 = (bf16[24,2048]{1,0:T(8,128)(2,1)S(1)}, bf16[24,2048]{1,0:T(8,128)(2,1)S(1)}, u32[]{:S(2)}, u32[]{:S(2)}) collective-permute-start(bf16[24,2048]{1,0:T(8,128)(2,1)S(1)} %add_convert_fusion.4), channel_id=1, source_target_pairs={{0,2},{1,3},{2,0},{3,1},{4,6},{5,7},{6,4},{7,5},{8,10},{9,11},{10,... | collective-permute-start | bytes 294920 | tf_op jit(solution)/shard_map/ppermute | solution.py:360
  590.9 25.4 %collective-permute-start.29 = (bf16[24,2048]{1,0:T(8,128)(2,1)S(1)}, bf16[24,2048]{1,0:T(8,128)(2,1)S(1)}, u32[]{:S(2)}, u32[]{:S(2)}) collective-permute-start(bf16[24,2048]{1,0:T(8,128)(2,1)S(1)} %get-tuple-element.83), channel_id=1, source_target_pairs={{12,16},{13,17},{14,18},{15,19},{16,4},{17,5},{18,6},{19,7}} | collective-permute-start | bytes 294920 | tf_op jit(solution)/shard_map/ppermute | solution.py:315
  597.2 19.2 %collective-permute-start.28 = (bf16[24,2048]{1,0:T(8,128)(2,1)S(1)}, bf16[24,2048]{1,0:T(8,128)(2,1)S(1)}, u32[]{:S(2)}, u32[]{:S(2)}) collective-permute-start(bf16[24,2048]{1,0:T(8,128)(2,1)S(1)} %get-tuple-element.83), channel_id=1, source_target_pairs={{12,0},{13,1},{14,2},{15,3},{16,20},{17,21},{18,22},{19,23}} | collective-permute-start | bytes 294920 | tf_op jit(solution)/shard_map/ppermute | solution.py:315
  657.3 14.7 %collective-permute-start.84 = (bf16[24,2048]{1,0:T(8,128)(2,1)S(1)}, bf16[24,2048]{1,0:T(8,128)(2,1)S(1)}, u32[]{:S(2)}, u32[]{:S(2)}) collective-permute-start(bf16[24,2048]{1,0:T(8,128)(2,1)S(1)} %add_convert_fusion.3), channel_id=1, source_target_pairs={{0,2},{1,3},{2,0},{3,1},{4,6},{5,7},{6,4},{7,5},{8,10},{9,11},{10,... | collective-permute-start | bytes 294920 | tf_op jit(solution)/shard_map/ppermute | solution.py:360
  661.4 23.4 %collective-permute-start.35 = (bf16[24,2048]{1,0:T(8,128)(2,1)S(1)}, bf16[24,2048]{1,0:T(8,128)(2,1)S(1)}, u32[]{:S(2)}, u32[]{:S(2)}) collective-permute-start(bf16[24,2048]{1,0:T(8,128)(2,1)S(1)} %get-tuple-element.81), channel_id=1, source_target_pairs={{16,4},{17,5},{18,6},{19,7},{20,8},{21,9},{22,10},{23,11}} | collective-permute-start | bytes 294920 | tf_op jit(solution)/shard_map/ppermute | solution.py:315
  665.6 19.2 %collective-permute-start.34 = (bf16[24,2048]{1,0:T(8,128)(2,1)S(1)}, bf16[24,2048]{1,0:T(8,128)(2,1)S(1)}, u32[]{:S(2)}, u32[]{:S(2)}) collective-permute-start(bf16[24,2048]{1,0:T(8,128)(2,1)S(1)} %get-tuple-element.81), channel_id=1, source_target_pairs={{16,20},{17,21},{18,22},{19,23},{20,24},{21,25},{22,26},{23,27}} | collective-permute-start | bytes 294920 | tf_op jit(solution)/shard_map/ppermute | solution.py:315
  672.0 13.2 %collective-permute-start.86 = (bf16[24,2048]{1,0:T(8,128)(2,1)S(1)}, bf16[24,2048]{1,0:T(8,128)(2,1)S(1)}, u32[]{:S(2)}, u32[]{:S(2)}) collective-permute-start(bf16[24,2048]{1,0:T(8,128)(2,1)S(1)} %get-tuple-element.97), channel_id=1, source_target_pairs={{16,4},{17,5},{18,6},{19,7},{20,8},{21,9},{22,10},{23,11}} | collective-permute-start | bytes 294920 | tf_op jit(solution)/shard_map/ppermute | solution.py:315
  719.2 21.9 %collective-permute-start.90 = (bf16[24,2048]{1,0:T(8,128)(2,1)S(1)}, bf16[24,2048]{1,0:T(8,128)(2,1)S(1)}, u32[]{:S(2)}, u32[]{:S(2)}) collective-permute-start(bf16[24,2048]{1,0:T(8,128)(2,1)S(1)} %add_convert_fusion.2), channel_id=1, source_target_pairs={{0,2},{1,3},{2,0},{3,1},{4,6},{5,7},{6,4},{7,5},{8,10},{9,11},{10,... | collective-permute-start | bytes 294920 | tf_op jit(solution)/shard_map/ppermute | solution.py:360
  723.0 30.9 %collective-permute-start.41 = (bf16[24,2048]{1,0:T(8,128)(2,1)S(1)}, bf16[24,2048]{1,0:T(8,128)(2,1)S(1)}, u32[]{:S(2)}, u32[]{:S(2)}) collective-permute-start(bf16[24,2048]{1,0:T(8,128)(2,1)S(1)} %get-tuple-element.79), channel_id=1, source_target_pairs={{20,8},{21,9},{22,10},{23,11},{24,12},{25,13},{26,14},{27,15}} | collective-permute-start | bytes 294920 | tf_op jit(solution)/shard_map/ppermute | solution.py:315
  734.7 19.2 %collective-permute-start.40 = (bf16[24,2048]{1,0:T(8,128)(2,1)S(1)}, bf16[24,2048]{1,0:T(8,128)(2,1)S(1)}, u32[]{:S(2)}, u32[]{:S(2)}) collective-permute-start(bf16[24,2048]{1,0:T(8,128)(2,1)S(1)} %get-tuple-element.79), channel_id=1, source_target_pairs={{20,24},{21,25},{22,26},{23,27},{24,28},{25,29},{26,30},{27,31}} | collective-permute-start | bytes 294920 | tf_op jit(solution)/shard_map/ppermute | solution.py:315
  741.1 13.2 %collective-permute-start.92 = (bf16[24,2048]{1,0:T(8,128)(2,1)S(1)}, bf16[24,2048]{1,0:T(8,128)(2,1)S(1)}, u32[]{:S(2)}, u32[]{:S(2)}) collective-permute-start(bf16[24,2048]{1,0:T(8,128)(2,1)S(1)} %get-tuple-element.95), channel_id=1, source_target_pairs={{20,8},{21,9},{22,10},{23,11},{24,12},{25,13},{26,14},{27,15}} | collective-permute-start | bytes 294920 | tf_op jit(solution)/shard_map/ppermute | solution.py:315
  763.3 19.8 %collective-permute-start.43 = (bf16[24,1536]{1,0:T(8,128)(2,1)S(1)}, bf16[24,1536]{1,0:T(8,128)(2,1)S(1)}, u32[]{:S(2)}, u32[]{:S(2)}) collective-permute-start(bf16[24,1536]{1,0:T(8,128)(2,1)S(1)} %shard_map.98.own), channel_id=1, source_target_pairs={{8,24},{9,25},{10,26},{11,27},{12,28},{13,29},{14,30},{15,31}} | collective-permute-start | bytes 221192 | tf_op jit(solution)/shard_map/ppermute | solution.py:315
  771.9 18.1 %collective-permute-start.94 = (bf16[24,1536]{1,0:T(8,128)(2,1)S(1)}, bf16[24,1536]{1,0:T(8,128)(2,1)S(1)}, u32[]{:S(2)}, u32[]{:S(2)}) collective-permute-start(bf16[24,1536]{1,0:T(8,128)(2,1)S(1)} %shard_map.116.own), channel_id=1, source_target_pairs={{8,24},{9,25},{10,26},{11,27},{12,28},{13,29},{14,30},{15,31}} | collective-permute-start | bytes 221192 | tf_op jit(solution)/shard_map/ppermute | solution.py:315
  (92 other events, 819.6 us)

commit v3 on v2

v3 whole, which is shorter than its diff:
```python
import functools

import jax
import jax.numpy as jnp
import numpy as np
from jax import lax
from jax.experimental import pallas as pl
from jax.experimental.pallas import tpu as pltpu
from jax.sharding import Mesh, PartitionSpec as P

HDIM = 128
FB = 8
STREAMS = 2
ITEMS = 2
ROWBLOCK = 256
CHUNK = 384
WINDOW = 512
VMEM = 48 * 1024 * 1024


def sort_kernel(first, layers, kept, slab, out):
    feats = ROWBLOCK // layers
    row = lax.broadcasted_iota(jnp.int32, (kept * feats, ROWBLOCK), 0)
    col = lax.broadcasted_iota(jnp.int32, (kept * feats, ROWBLOCK), 1)
    source = row % feats * layers + first + row // feats
    order = jnp.where(col == source, 1.0, 0.0).astype(jnp.bfloat16)
    moved = jnp.dot(order, slab[...], preferred_element_type=jnp.float32).astype(jnp.bfloat16)
    for layer in range(kept):
        out[layer, 0] = moved[layer * feats : (layer + 1) * feats]


def sort_slab(slab, phase, layers, n_tensor):
    rows, columns = slab.shape
    kept = layers // 2
    cdev = columns // n_tensor
    feats = ROWBLOCK // layers
    return pl.pallas_call(
        functools.partial(sort_kernel, phase * kept, layers, kept),
        grid=(n_tensor, rows // ROWBLOCK),
        in_specs=[pl.BlockSpec((ROWBLOCK, cdev), lambda t, i: (i, t))],
        out_specs=pl.BlockSpec((kept, 1, feats, cdev), lambda t, i: (0, t, i, 0)),
        out_shape=jax.ShapeDtypeStruct((kept, n_tensor, rows // layers, cdev), jnp.bfloat16),
        compiler_params=pltpu.CompilerParams(vmem_limit_bytes=VMEM),
        cost_estimate=pl.CostEstimate(
            flops=rows * columns * ROWBLOCK, bytes_accessed=3 * rows * columns, transcendentals=0
        ),
    )(slab)


def project_kernel(tick, tiles, tilew, n_y, use, scalars, mine, other, gains, *rest):
    weights, (out, normed, held, sems) = rest[: len(use)], rest[len(use) :]
    rows, half = mine.shape
    width = 2 * half
    shard = half // n_y
    chunks, size, cdev = held.shape
    core, phase = scalars[0], scalars[1 + tick]

    def fetch(source, j):
        return pltpu.make_async_copy(source.at[pl.ds(j * size, size)], held.at[j], sems.at[j])

    if len(use) == 1:
        for j in range(chunks):
            fetch(weights[0], j).start()
    else:
        for p in range(2):

            @pl.when(phase == p)
            def _():
                for j in range(chunks):
                    fetch(weights[p], j).start()

    here = mine[...].astype(jnp.float32)
    there = other[...].astype(jnp.float32)
    total = jnp.sum(here * here, axis=1, keepdims=True)
    total = total + jnp.sum(there * there, axis=1, keepdims=True)
    inverse = lax.rsqrt(total / width + 1e-06)
    gain = jnp.where(phase == 0, gains[0:1], gains[1:2])
    low = jnp.where(core == 0, here, there) * inverse
    high = jnp.where(core == 0, there, here) * inverse
    for y in range(n_y):
        at = 2 * y * shard
        piece = slice(y * shard, (y + 1) * shard)
        normed[:, at : at + shard] = low[:, piece] * gain[:, at : at + shard]
        at = at + shard
        normed[:, at : at + shard] = high[:, piece] * gain[:, at : at + shard]
    normed[:, width:] = jnp.zeros((rows, WINDOW), jnp.float32)

    per = CHUNK // tilew
    base = scalars.shape[0] - 2 * tiles
    lane = lax.broadcasted_iota(jnp.int32, (rows, CHUNK), 1)

    def spread(j):
        value = jnp.zeros((rows, CHUNK), jnp.float32)
        for a in range(per):
            start = scalars[base + j * per + a] * FB
            count = scalars[base + tiles + j * per + a] * FB
            aligned = start // 128 * 128
            window = normed[:, pl.ds(pl.multiple_of(aligned, 128), WINDOW)]
            put = a * tilew
            shift = (put - (start - aligned) + WINDOW) % WINDOW
            rolled = pltpu.roll(window, shift, 1)[:, :CHUNK]
            value = jnp.where((lane >= put) & (lane < put + count), rolled, value)
        return value.astype(jnp.bfloat16)

    acc = jnp.zeros((rows, cdev), jnp.float32)
    for j in range(chunks):
        parts = [spread(j * (size // CHUNK) + i) for i in range(size // CHUNK)]
        fetch(weights[0], j).wait()
        acc = acc + jnp.dot(
            jnp.concatenate(parts, axis=1), held[j], preferred_element_type=jnp.float32
        )
    out[...] = acc.astype(jnp.bfloat16)


def project(tick, use, tiles, tilew, n_y, scalars, mine, other, gains, weights):
    rows, half = mine.shape
    depth, cdev = weights[0].shape
    size = 2 * CHUNK
    vmem = pl.BlockSpec(memory_space=pltpu.VMEM)
    return pl.pallas_call(
        functools.partial(project_kernel, tick, tiles, tilew, n_y, use),
        in_specs=[pl.BlockSpec(memory_space=pltpu.SMEM)]
        + [vmem] * 3
        + [pl.BlockSpec(memory_space=pl.ANY)] * len(use),
        out_specs=vmem,
        scratch_shapes=[
            pltpu.VMEM((rows, 2 * half + WINDOW), jnp.float32),
            pltpu.VMEM((depth // size, size, cdev), jnp.bfloat16),
            pltpu.SemaphoreType.DMA((depth // size,)),
        ],
        out_shape=jax.ShapeDtypeStruct((rows, cdev), jnp.bfloat16),
        compiler_params=pltpu.CompilerParams(vmem_limit_bytes=VMEM),
        cost_estimate=pl.CostEstimate(
            flops=2 * rows * depth * cdev, bytes_accessed=2 * depth * cdev, transcendentals=0
        ),
    )(scalars, mine, other, gains, *weights)


def attend_kernel(steps, brow, kvlocal, groups, n_y, item_at, scalars, own, sent, spans, ckeys, cvals, wo, theirs, ours, attn, kheld, vheld, held, sems):
    rows = steps * brow
    length = ckeys.shape[1]
    scale = 1.0 / HDIM**0.5
    qdim = kvlocal * groups * HDIM
    kvdim = kvlocal * HDIM
    shard = held.shape[2]
    core = scalars[0]
    item = scalars[item_at]
    first = pl.multiple_of(item * brow, brow)
    gets = [
        pltpu.make_async_copy(ckeys.at[pl.ds(first, brow)], kheld, sems.at[2 * n_y]),
        pltpu.make_async_copy(cvals.at[pl.ds(first, brow)], vheld, sems.at[2 * n_y + 1]),
    ]
    for k in range(2 * n_y):
        side = 1 - core if k < n_y else core
        at = pl.multiple_of((k % n_y * 2 + side) * shard, shard)
        gets.append(
            pltpu.make_async_copy(wo.at[0, :, pl.ds(at, shard)], held.at[k], sems.at[k])
        )
    for get in gets:
        get.start()
    gets[0].wait()
    gets[1].wait()
    span = spans[item]

    qkv = (own[...].astype(jnp.float32) + sent[...].astype(jnp.float32)).astype(jnp.bfloat16)
    qkv = qkv.astype(jnp.float32)
    keys = kheld[...].reshape(brow * length, kvdim)
    values = vheld[...].reshape(brow * length, kvdim)
    tall = groups * rows
    at = lax.broadcasted_iota(jnp.int32, (tall, brow * length), 0)
    col = lax.broadcasted_iota(jnp.int32, (tall, brow * length), 1)
    cmask = (at % brow == col // length) & (col % length < span)
    at = lax.broadcasted_iota(jnp.int32, (tall, rows), 0)
    col = lax.broadcasted_iota(jnp.int32, (tall, rows), 1)
    nmask = (at % brow == col % brow) & (col // brow <= at % rows // brow)
    contract = (((1,), (1,)), ((), ()))
    for head in range(kvlocal):
        lanes = slice(head * HDIM, (head + 1) * HDIM)
        first = head * groups * HDIM
        query = jnp.concatenate(
            [qkv[:, first + g * HDIM : first + (g + 1) * HDIM] for g in range(groups)], axis=0
        ).astype(jnp.bfloat16)
        at = qdim + head * HDIM
        knew = qkv[:, at : at + HDIM].astype(jnp.bfloat16)
        at = at + kvdim
        vnew = qkv[:, at : at + HDIM].astype(jnp.bfloat16)
        scache = scale * lax.dot_general(
            query, keys[:, lanes], contract, preferred_element_type=jnp.float32
        )
        snew = scale * lax.dot_general(
            query, knew, contract, preferred_element_type=jnp.float32
        )
        scache = jnp.where(cmask, scache, -1e30)
        snew = jnp.where(nmask, snew, -1e30)
        top = jnp.maximum(
            jnp.max(scache, axis=1, keepdims=True), jnp.max(snew, axis=1, keepdims=True)
        )
        ecache = jnp.where(cmask, jnp.exp(scache - top), 0.0)
        enew = jnp.where(nmask, jnp.exp(snew - top), 0.0)
        total = jnp.sum(ecache, axis=1, keepdims=True) + jnp.sum(enew, axis=1, keepdims=True)
        inverse = 1.0 / total
        wcache = (ecache * inverse).astype(jnp.bfloat16)
        wnew = (enew * inverse).astype(jnp.bfloat16)
        mixed = jnp.dot(wcache, values[:, lanes], preferred_element_type=jnp.float32)
        mixed = mixed + jnp.dot(wnew, vnew, preferred_element_type=jnp.float32)
        for g in range(groups):
            attn[:, first + g * HDIM : first + (g + 1) * HDIM] = mixed[
                g * rows : (g + 1) * rows
            ].astype(jnp.bfloat16)

    for k in range(2 * n_y):
        gets[2 + k].wait()
        product = jnp.dot(attn[...], held[k], preferred_element_type=jnp.float32)
        target = theirs if k < n_y else ours
        at = k % n_y * shard
        target[:, at : at + shard] = product.astype(jnp.bfloat16)


def attend(item_at, steps, brow, n_y, scalars, own, sent, spans, keys, values, wo):
    rows, cdev = own.shape
    _, qdim, width = wo.shape
    length, kvdim = keys.shape[1:]
    kvlocal = kvdim // HDIM
    groups = qdim // kvdim
    shard = width // (2 * n_y)
    vmem = pl.BlockSpec(memory_space=pltpu.VMEM)
    return pl.pallas_call(
        functools.partial(attend_kernel, steps, brow, kvlocal, groups, n_y, item_at),
        in_specs=[pl.BlockSpec(memory_space=pltpu.SMEM)]
        + [vmem] * 3
        + [pl.BlockSpec(memory_space=pl.ANY)] * 3,
        out_specs=[vmem] * 2,
        scratch_shapes=[
            pltpu.VMEM((rows, qdim), jnp.bfloat16),
            pltpu.VMEM((brow, length, kvdim), jnp.bfloat16),
            pltpu.VMEM((brow, length, kvdim), jnp.bfloat16),
            pltpu.VMEM((2 * n_y, qdim, shard), jnp.bfloat16),
            pltpu.SemaphoreType.DMA((2 * n_y + 2,)),
        ],
        out_shape=[jax.ShapeDtypeStruct((rows, shard * n_y), jnp.bfloat16)] * 2,
        compiler_params=pltpu.CompilerParams(vmem_limit_bytes=VMEM),
        cost_estimate=pl.CostEstimate(
            flops=2 * rows * qdim * width, bytes_accessed=2 * qdim * width, transcendentals=0
        ),
    )(scalars, own, sent, spans, keys, values, wo)


def per_device(
    trainer_tiles,
    tile_lengths,
    wo_rollout,
    cache_keys,
    cache_values,
    cache_lengths,
    norm_gain,
    step_inputs,
):
    n_zone = lax.axis_size("zone")
    n_spot = lax.axis_size("spot")
    n_tensor = lax.axis_size("tensor")
    layers = n_zone * n_spot
    tiles = n_spot * n_tensor
    n_y = n_tensor // 2
    slab, columns = trainer_tiles.shape
    cdev = columns // n_tensor
    tilew = slab // layers
    width = wo_rollout.shape[2]
    shard = width // n_tensor
    half = n_y * shard
    steps = step_inputs.shape[0]
    seqs, length = cache_keys.shape[1:3]
    n_item = STREAMS * ITEMS
    brow = seqs // n_item
    rows = steps * brow
    ticks = layers + ITEMS - 1
    zone = lax.axis_index("zone")
    spot = lax.axis_index("spot")
    tpos = lax.axis_index("tensor")
    core = tpos % 2
    layer = zone * n_spot + spot

    weights = []
    for phase in range(2):
        ordered = sort_slab(trainer_tiles, phase, layers, n_tensor)
        arrived = lax.all_to_all(
            ordered.reshape(tiles, tilew, cdev),
            ("spot", "tensor"),
            split_axis=0,
            concat_axis=0,
            tiled=True,
        )
        weights.append(arrived.reshape(tiles * tilew, cdev))

    ends = jnp.cumsum(tile_lengths)
    starts = lax.dynamic_slice_in_dim(ends - tile_lengths, zone * tiles, tiles)
    counts = lax.dynamic_slice_in_dim(tile_lengths, zone * tiles, tiles)
    tick_ids = jnp.arange(ticks, dtype=jnp.int32)
    phases = (tick_ids >= spot + n_spot).astype(jnp.int32)
    turns = jnp.clip(tick_ids - layer, 0, ITEMS - 1)
    turns = jnp.concatenate([turns + stream * ITEMS for stream in range(STREAMS)])
    scalars = jnp.concatenate([core[None], phases, turns, starts, counts]).astype(jnp.int32)
    flip = [(z, 1 - z) for z in range(2)]
    swapped = lax.ppermute(norm_gain, "zone", flip)
    gains = jnp.concatenate(
        [jnp.where(zone == 0, norm_gain, swapped), jnp.where(zone == 0, swapped, norm_gain)]
    )
    spans = jnp.repeat(cache_lengths, length).reshape(n_item, 1, brow * length)
    axes = ("zone", "spot", "tensor")

    flat = [(z, s) for z in range(n_zone) for s in range(n_spot)]

    def shifted(turn):
        pairs = []
        for z, s in flat:
            nearby = (s + 1) % n_spot
            ahead = z if s + 1 < n_spot else 1 - z
            pairs.append((z * n_spot + s, (ahead ^ turn) * n_spot + nearby))
        return pairs

    hops = [shifted(turn) for turn in range(2)]

    def active(tick):
        return [l for l in range(layers) if 0 <= tick - l < ITEMS]

    across = [(t, t ^ 1) for t in range(n_tensor)]
    shown = step_inputs.reshape(steps, n_item, brow, n_y, 2, shard)
    records = []
    for stream in range(STREAMS):
        arrived, record = None, []
        for tick in range(ticks):
            busy = active(tick)
            if tick < ITEMS:
                item = stream * ITEMS + tick
                fresh = shown[:, item].reshape(rows, n_y, 2, shard)
                mine = lax.dynamic_index_in_dim(fresh, core, 2, False).reshape(rows, half)
                mine = jnp.where(spot == 0, mine, arrived if tick else 0)
            else:
                mine = arrived
            if tick:
                other = lax.ppermute(mine, "tensor", across)
            else:
                other = lax.dynamic_index_in_dim(fresh, 1 - core, 2, False).reshape(rows, half)
            use = sorted({l // n_spot for l in busy})
            own = project(
                tick, use, tiles, tilew, n_y, scalars, mine, other, gains, [weights[p] for p in use]
            )
            sent = lax.ppermute(own, "zone", flip)
            item_at = 1 + ticks + stream * ticks + tick
            theirs, ours = attend(
                item_at, steps, brow, n_y, scalars, own, sent, spans, cache_keys[0], cache_values[0], wo_rollout
            )
            part = ours.astype(jnp.float32) + lax.ppermute(theirs, "tensor", across).astype(
                jnp.float32
            )
            bit = 2
            while bit < n_tensor:
                part = part.astype(jnp.bfloat16)
                moved = lax.ppermute(part, "tensor", [(t, t ^ bit) for t in range(n_tensor)])
                part = part.astype(jnp.float32) + moved.astype(jnp.float32)
                bit = bit * 2
            wide = mine.astype(jnp.float32) + part
            record.append(lax.dynamic_slice_in_dim(wide, tpos // 2 * shard, shard, 1))
            after = wide.astype(jnp.bfloat16)
            if tick + 1 < ticks:
                at_home = phases[tick + 1] == zone
                near = lax.ppermute(after, ("zone", "spot"), hops[0])
                far = lax.ppermute(after, ("zone", "spot"), hops[1])
                arrived = jnp.where(at_home, near, far)
        record = jnp.stack(record)
        record = lax.dynamic_slice_in_dim(record, layer, ITEMS, 0)
        record = record.reshape(ITEMS, steps, brow, shard).swapaxes(0, 1)
        records.append(record.reshape(steps, ITEMS * brow, shard))
    return jnp.concatenate(records, axis=1)[None]


def solution(mesh):
    n_section, n_tensor = mesh.devices.shape
    fine = Mesh(mesh.devices.reshape(2, n_section // 2, n_tensor), ("zone", "spot", "tensor"))
    section = ("zone", "spot")
    placed = (
        P(("zone", "spot", "tensor"), None),
        P(),
        P(section, "tensor", None),
        P(section, None, None, "tensor"),
        P(section, None, None, "tensor"),
        P(),
        P(section, None),
        P(),
    )
    return jax.shard_map(
        per_device,
        mesh=fine,
        in_specs=placed,
        out_specs=P(section, None, None, "tensor"),
        check_vma=False,
    )
```

time: 860 us -> 690 us (0.80)
  starting transfers between devices: 221 us -> 107 us
  Pallas kernels: 303 us -> 214 us
  waiting for transfers between devices: 312 us -> 345 us
    ppermute x50, starting transfers between devices: 174 us -> 76 us  [the longest x16 41.7 us: per_device(): near = lax.ppermute(after, ('zone', 'spot'), hops[0])]
    pallas_call x18, Pallas kernels: 144 us -> 90.1 us  [project(): pl.pallas_call(functools.partial(project_kernel, tick, tiles, tilew, n_y,...]
    pallas_call x18, Pallas kernels: 117 us -> 82.8 us  [attend(): pl.pallas_call(functools.partial(attend_kernel, steps, brow, kvlocal, gro...]
    ppermute x50, waiting for transfers between devices: 28.6 us -> 54.1 us  [the longest x16 30.1 us: per_device(): near = lax.ppermute(after, ('zone', 'spot'), hops[0])]
  transfers between devices with their start and end apart: 105 -> 105, of which waited for: 29 -> 59; matrix products, arithmetic and copies ran while one was open for 1% -> 1% of each run, Pallas kernels for 33% -> 28%
where the time goes in v3:
time: 690 us; the launch traced here: 682 us
  waiting for transfers between devices  345 us (50%)
  Pallas kernels  214 us (31%)
  starting transfers between devices  107 us (16%)
  between operations  6.97 us (1%)
    ppermute x1, waiting for transfers between devices, per_device(): swapped = lax.ppermute(norm_gain, 'zone', flip)  134 us
    all_to_all x2, waiting for transfers between devices, per_device(): lax.all_to_all(ordered.reshape(tiles, tilew, cdev), ('spot', 'tensor'), s...  117 us
    pallas_call x18, Pallas kernels, project(): pl.pallas_call(functools.partial(project_kernel, tick, tiles, tilew, n_y,...  90.1 us
    pallas_call x18, Pallas kernels, attend(): pl.pallas_call(functools.partial(attend_kernel, steps, brow, kvlocal, gro...  82.8 us
    ppermute x16, starting transfers between devices, per_device(): near = lax.ppermute(after, ('zone', 'spot'), hops[0])  41.7 us
    pallas_call x2, Pallas kernels, sort_slab(): pl.pallas_call(functools.partial(sort_kernel, phase * kept, layers, kept)...  41.4 us
    ppermute x18, waiting for transfers between devices, per_device(): lax.ppermute(part, 'tensor', [(t, t ^ bit) for t in range(n_tensor)])  32.8 us
    ppermute x16, waiting for transfers between devices, per_device(): near = lax.ppermute(after, ('zone', 'spot'), hops[0])  30.1 us
  transfers between devices with their start and end apart: 105, of which 59 were waited for; matrix products, arithmetic and copies ran while one was open for 1% of the time, Pallas kernels for 28%

profile of v3, /device:TPU:0, one launch (start us, length us, event | category | flops | bytes accessed | tf_op | source)
XLA Modules:
  0.0 681.8 jit_solution(13078268177298141690)
XLA Ops:
  0.0 20.7 %shard_map.82 = bf16[4,4,192,1536]{3,2,1,0:T(8,128)(2,1)} custom-call(bf16[1536,6144]{1,0:T(8,128)(2,1)} %slab.3), custom_call_target="tpu_custom_call" | custom-call | flops 2415919104 | bytes 28311552 | tf_op jit(solution)/shard_map/pallas_call | solution.py:37
  20.7 6.3 all-to-all-start
  27.0 20.7 %shard_map.91 = bf16[4,4,192,1536]{3,2,1,0:T(8,128)(2,1)} custom-call(bf16[1536,6144]{1,0:T(8,128)(2,1)} %slab.3), custom_call_target="tpu_custom_call" | custom-call | flops 2415919104 | bytes 28311552 | tf_op jit(solution)/shard_map/pallas_call | solution.py:37
  47.8 117.1 %all-to-all-done = bf16[16,192,1536]{2,1,0:T(8,128)(2,1)} async-done(((bf16[16,192,1536]{2,1,0:T(8,128)(2,1)}), bf16[16,192,1536]{2,1,0:T(8,128)(2,1)}, u32[]{:S(2)}, u32[]{:S(2)}) %all-to-all-start) | async-done | bytes 9437216 | tf_op jit(solution)/shard_map/all_to_all | solution.py:285
  164.9 5.8 all-to-all-start.1
  175.1 133.6 %collective-permute-done = f32[1,4096]{1,0:T(1,128)S(1)} collective-permute-done((f32[1,4096]{1,0:T(1,128)S(1)}, f32[1,4096]{1,0:T(1,128)S(1)}, u32[]{:S(2)}, u32[]{:S(2)}) %collective-permute-start) | collective-permute-done | bytes 16416 | tf_op jit(solution)/shard_map/ppermute | solution.py:303
  308.8 5.0 shard_map.83.own
  323.5 5.0 shard_map.102.own
  358.5 5.0 shard_map.85.own
  364.9 5.0 shard_map.104.own
  399.9 5.0 shard_map.87.own
  407.9 5.0 shard_map.106.own
  443.4 5.0 shard_map.89.own
  449.8 5.0 shard_map.108.own
  485.1 5.0 shard_map.92.own
  491.4 5.0 shard_map.110.own
  526.0 5.0 shard_map.94.own
  532.7 5.0 shard_map.112.own
  567.3 5.0 shard_map.96.own
  573.8 5.0 shard_map.114.own
  608.4 5.0 shard_map.98.own
  615.1 5.0 shard_map.116.own
  649.6 5.0 shard_map.100.own
  656.4 5.0 shard_map.118.own
  (341 shorter events, 280.5 us)
Async XLA Ops:
  20.7 144.2 %all-to-all-start = ((bf16[16,192,1536]{2,1,0:T(8,128)(2,1)}), bf16[16,192,1536]{2,1,0:T(8,128)(2,1)}, u32[]{:S(2)}, u32[]{:S(2)}) async-start(bf16[16,192,1536]{2,1,0:T(8,128)(2,1)} %bitcast.140), calls=%async_computation | async-start | bytes 18874368 | tf_op jit(solution)/shard_map/all_to_all | solution.py:285
  164.9 320.2 %all-to-all-start.1 = ((bf16[16,192,1536]{2,1,0:T(8,128)(2,1)}), bf16[16,192,1536]{2,1,0:T(8,128)(2,1)}, u32[]{:S(2)}, u32[]{:S(2)}) async-start(bf16[16,192,1536]{2,1,0:T(8,128)(2,1)} %bitcast.139), calls=%async_computation.1 | async-start | bytes 18874368 | tf_op jit(solution)/shard_map/all_to_all | solution.py:285
  170.7 138.1 %collective-permute-start = (f32[1,4096]{1,0:T(1,128)S(1)}, f32[1,4096]{1,0:T(1,128)S(1)}, u32[]{:S(2)}, u32[]{:S(2)}) collective-permute-start(f32[1,4096]{1,0:T(1,128)S(1)} %copy-done.5), channel_id=1, source_target_pairs={{0,16},{16,0},{1,17},{17,1},{2,18},{18,2},{3,19},{19,3},{4,20},{20... | collective-permute-start | bytes 49160 | tf_op jit(solution)/shard_map/ppermute | solution.py:303
  313.8 14.8 %collective-permute-start.1 = (bf16[24,1536]{1,0:T(8,128)(2,1)S(1)}, bf16[24,1536]{1,0:T(8,128)(2,1)S(1)}, u32[]{:S(2)}, u32[]{:S(2)}) collective-permute-start(bf16[24,1536]{1,0:T(8,128)(2,1)S(1)} %shard_map.83.own), channel_id=1, source_target_pairs={{0,16},{16,0},{1,17},{17,1},{2,18},{18,2},{3,19},{19,3},{4,20},{20... | collective-permute-start | bytes 221192 | tf_op jit(solution)/shard_map/ppermute | solution.py:347
  340.6 8.7 %collective-permute-start.54 = (bf16[24,2048]{1,0:T(8,128)(2,1)S(1)}, bf16[24,2048]{1,0:T(8,128)(2,1)S(1)}, u32[]{:S(2)}, u32[]{:S(2)}) collective-permute-start(bf16[24,2048]{1,0:T(8,128)(2,1)S(1)} %add_convert_fusion.8), channel_id=1, source_target_pairs={{0,2},{1,3},{2,0},{3,1},{4,6},{5,7},{6,4},{7,5},{8,10},{9,11},{10,... | collective-permute-start | bytes 294920 | tf_op jit(solution)/shard_map/ppermute | solution.py:358
  345.1 9.6 %collective-permute-start.4 = (bf16[24,2048]{1,0:T(8,128)(2,1)S(1)}, bf16[24,2048]{1,0:T(8,128)(2,1)S(1)}, u32[]{:S(2)}, u32[]{:S(2)}) collective-permute-start(bf16[24,2048]{1,0:T(8,128)(2,1)S(1)} %get-tuple-element.91), channel_id=1, source_target_pairs={{0,4},{4,8},{8,12},{12,16},{16,20},{20,24},{24,28},{28,0},{1,5},{5... | collective-permute-start | bytes 294920 | tf_op jit(solution)/shard_map/ppermute | solution.py:366
  363.5 8.7 %collective-permute-start.7 = (bf16[24,1536]{1,0:T(8,128)(2,1)S(1)}, bf16[24,1536]{1,0:T(8,128)(2,1)S(1)}, u32[]{:S(2)}, u32[]{:S(2)}) collective-permute-start(bf16[24,1536]{1,0:T(8,128)(2,1)S(1)} %shard_map.85.own), channel_id=1, source_target_pairs={{0,16},{16,0},{1,17},{17,1},{2,18},{18,2},{3,19},{19,3},{4,20},{20... | collective-permute-start | bytes 221192 | tf_op jit(solution)/shard_map/ppermute | solution.py:347
  404.9 8.7 %collective-permute-start.13 = (bf16[24,1536]{1,0:T(8,128)(2,1)S(1)}, bf16[24,1536]{1,0:T(8,128)(2,1)S(1)}, u32[]{:S(2)}, u32[]{:S(2)}) collective-permute-start(bf16[24,1536]{1,0:T(8,128)(2,1)S(1)} %shard_map.87.own), channel_id=1, source_target_pairs={{0,16},{16,0},{1,17},{17,1},{2,18},{18,2},{3,19},{19,3},{4,20},{20... | collective-permute-start | bytes 221192 | tf_op jit(solution)/shard_map/ppermute | solution.py:347
  425.8 8.3 %collective-permute-start.66 = (bf16[24,2048]{1,0:T(8,128)(2,1)S(1)}, bf16[24,2048]{1,0:T(8,128)(2,1)S(1)}, u32[]{:S(2)}, u32[]{:S(2)}) collective-permute-start(bf16[24,2048]{1,0:T(8,128)(2,1)S(1)} %add_convert_fusion.6), channel_id=1, source_target_pairs={{0,2},{1,3},{2,0},{3,1},{4,6},{5,7},{6,4},{7,5},{8,10},{9,11},{10,... | collective-permute-start | bytes 294920 | tf_op jit(solution)/shard_map/ppermute | solution.py:358
  431.1 10.1 %collective-permute-start.16 = (bf16[24,2048]{1,0:T(8,128)(2,1)S(1)}, bf16[24,2048]{1,0:T(8,128)(2,1)S(1)}, u32[]{:S(2)}, u32[]{:S(2)}) collective-permute-start(bf16[24,2048]{1,0:T(8,128)(2,1)S(1)} %get-tuple-element.87), channel_id=1, source_target_pairs={{0,4},{4,8},{8,12},{12,16},{16,20},{20,24},{24,28},{28,0},{1,5},{5... | collective-permute-start | bytes 294920 | tf_op jit(solution)/shard_map/ppermute | solution.py:366
  434.5 8.8 %collective-permute-start.67 = (bf16[24,2048]{1,0:T(8,128)(2,1)S(1)}, bf16[24,2048]{1,0:T(8,128)(2,1)S(1)}, u32[]{:S(2)}, u32[]{:S(2)}) collective-permute-start(bf16[24,2048]{1,0:T(8,128)(2,1)S(1)} %get-tuple-element.103), channel_id=1, source_target_pairs={{0,4},{4,8},{8,12},{12,16},{16,20},{20,24},{24,28},{28,0},{1,5},{5... | collective-permute-start | bytes 294920 | tf_op jit(solution)/shard_map/ppermute | solution.py:366
  448.4 8.7 %collective-permute-start.19 = (bf16[24,1536]{1,0:T(8,128)(2,1)S(1)}, bf16[24,1536]{1,0:T(8,128)(2,1)S(1)}, u32[]{:S(2)}, u32[]{:S(2)}) collective-permute-start(bf16[24,1536]{1,0:T(8,128)(2,1)S(1)} %shard_map.89.own), channel_id=1, source_target_pairs={{0,16},{16,0},{1,17},{17,1},{2,18},{18,2},{3,19},{19,3},{4,20},{20... | collective-permute-start | bytes 221192 | tf_op jit(solution)/shard_map/ppermute | solution.py:347
  473.4 9.4 %collective-permute-start.22 = (bf16[24,2048]{1,0:T(8,128)(2,1)S(1)}, bf16[24,2048]{1,0:T(8,128)(2,1)S(1)}, u32[]{:S(2)}, u32[]{:S(2)}) collective-permute-start(bf16[24,2048]{1,0:T(8,128)(2,1)S(1)} %get-tuple-element.85), channel_id=1, source_target_pairs={{0,4},{4,8},{8,12},{12,16},{16,20},{20,24},{24,28},{28,0},{1,5},{5... | collective-permute-start | bytes 294920 | tf_op jit(solution)/shard_map/ppermute | solution.py:366
  490.1 8.1 %collective-permute-start.25 = (bf16[24,1536]{1,0:T(8,128)(2,1)S(1)}, bf16[24,1536]{1,0:T(8,128)(2,1)S(1)}, u32[]{:S(2)}, u32[]{:S(2)}) collective-permute-start(bf16[24,1536]{1,0:T(8,128)(2,1)S(1)} %shard_map.92.own), channel_id=1, source_target_pairs={{0,16},{16,0},{1,17},{17,1},{2,18},{18,2},{3,19},{19,3},{4,20},{20... | collective-permute-start | bytes 221192 | tf_op jit(solution)/shard_map/ppermute | solution.py:347
  514.3 9.0 %collective-permute-start.28 = (bf16[24,2048]{1,0:T(8,128)(2,1)S(1)}, bf16[24,2048]{1,0:T(8,128)(2,1)S(1)}, u32[]{:S(2)}, u32[]{:S(2)}) collective-permute-start(bf16[24,2048]{1,0:T(8,128)(2,1)S(1)} %get-tuple-element.83), channel_id=1, source_target_pairs={{0,4},{4,8},{8,12},{12,16},{16,20},{20,24},{24,28},{28,0},{1,5},{5... | collective-permute-start | bytes 294920 | tf_op jit(solution)/shard_map/ppermute | solution.py:366
  517.7 8.2 %collective-permute-start.79 = (bf16[24,2048]{1,0:T(8,128)(2,1)S(1)}, bf16[24,2048]{1,0:T(8,128)(2,1)S(1)}, u32[]{:S(2)}, u32[]{:S(2)}) collective-permute-start(bf16[24,2048]{1,0:T(8,128)(2,1)S(1)} %get-tuple-element.99), channel_id=1, source_target_pairs={{0,4},{4,8},{8,12},{12,16},{16,20},{20,24},{24,28},{28,0},{1,5},{5... | collective-permute-start | bytes 294920 | tf_op jit(solution)/shard_map/ppermute | solution.py:366
  555.2 9.3 %collective-permute-start.34 = (bf16[24,2048]{1,0:T(8,128)(2,1)S(1)}, bf16[24,2048]{1,0:T(8,128)(2,1)S(1)}, u32[]{:S(2)}, u32[]{:S(2)}) collective-permute-start(bf16[24,2048]{1,0:T(8,128)(2,1)S(1)} %get-tuple-element.81), channel_id=1, source_target_pairs={{0,4},{4,8},{8,12},{12,16},{16,20},{20,24},{24,28},{28,0},{1,5},{5... | collective-permute-start | bytes 294920 | tf_op jit(solution)/shard_map/ppermute | solution.py:366
  558.6 8.6 %collective-permute-start.85 = (bf16[24,2048]{1,0:T(8,128)(2,1)S(1)}, bf16[24,2048]{1,0:T(8,128)(2,1)S(1)}, u32[]{:S(2)}, u32[]{:S(2)}) collective-permute-start(bf16[24,2048]{1,0:T(8,128)(2,1)S(1)} %get-tuple-element.97), channel_id=1, source_target_pairs={{0,4},{4,8},{8,12},{12,16},{16,20},{20,24},{24,28},{28,0},{1,5},{5... | collective-permute-start | bytes 294920 | tf_op jit(solution)/shard_map/ppermute | solution.py:366
  572.3 8.1 %collective-permute-start.37 = (bf16[24,1536]{1,0:T(8,128)(2,1)S(1)}, bf16[24,1536]{1,0:T(8,128)(2,1)S(1)}, u32[]{:S(2)}, u32[]{:S(2)}) collective-permute-start(bf16[24,1536]{1,0:T(8,128)(2,1)S(1)} %shard_map.96.own), channel_id=1, source_target_pairs={{0,16},{16,0},{1,17},{17,1},{2,18},{18,2},{3,19},{19,3},{4,20},{20... | collective-permute-start | bytes 221192 | tf_op jit(solution)/shard_map/ppermute | solution.py:347
  596.3 9.3 %collective-permute-start.40 = (bf16[24,2048]{1,0:T(8,128)(2,1)S(1)}, bf16[24,2048]{1,0:T(8,128)(2,1)S(1)}, u32[]{:S(2)}, u32[]{:S(2)}) collective-permute-start(bf16[24,2048]{1,0:T(8,128)(2,1)S(1)} %get-tuple-element.79), channel_id=1, source_target_pairs={{0,4},{4,8},{8,12},{12,16},{16,20},{20,24},{24,28},{28,0},{1,5},{5... | collective-permute-start | bytes 294920 | tf_op jit(solution)/shard_map/ppermute | solution.py:366
  599.8 8.5 %collective-permute-start.91 = (bf16[24,2048]{1,0:T(8,128)(2,1)S(1)}, bf16[24,2048]{1,0:T(8,128)(2,1)S(1)}, u32[]{:S(2)}, u32[]{:S(2)}) collective-permute-start(bf16[24,2048]{1,0:T(8,128)(2,1)S(1)} %get-tuple-element.95), channel_id=1, source_target_pairs={{0,4},{4,8},{8,12},{12,16},{16,20},{20,24},{24,28},{28,0},{1,5},{5... | collective-permute-start | bytes 294920 | tf_op jit(solution)/shard_map/ppermute | solution.py:366
  613.4 8.1 %collective-permute-start.43 = (bf16[24,1536]{1,0:T(8,128)(2,1)S(1)}, bf16[24,1536]{1,0:T(8,128)(2,1)S(1)}, u32[]{:S(2)}, u32[]{:S(2)}) collective-permute-start(bf16[24,1536]{1,0:T(8,128)(2,1)S(1)} %shard_map.98.own), channel_id=1, source_target_pairs={{0,16},{16,0},{1,17},{17,1},{2,18},{18,2},{3,19},{19,3},{4,20},{20... | collective-permute-start | bytes 221192 | tf_op jit(solution)/shard_map/ppermute | solution.py:347
  637.6 9.2 %collective-permute-start.46 = (bf16[24,2048]{1,0:T(8,128)(2,1)S(1)}, bf16[24,2048]{1,0:T(8,128)(2,1)S(1)}, u32[]{:S(2)}, u32[]{:S(2)}) collective-permute-start(bf16[24,2048]{1,0:T(8,128)(2,1)S(1)} %get-tuple-element.77), channel_id=1, source_target_pairs={{0,4},{4,8},{8,12},{12,16},{16,20},{20,24},{24,28},{28,0},{1,5},{5... | collective-permute-start | bytes 294920 | tf_op jit(solution)/shard_map/ppermute | solution.py:366
  641.0 8.6 %collective-permute-start.97 = (bf16[24,2048]{1,0:T(8,128)(2,1)S(1)}, bf16[24,2048]{1,0:T(8,128)(2,1)S(1)}, u32[]{:S(2)}, u32[]{:S(2)}) collective-permute-start(bf16[24,2048]{1,0:T(8,128)(2,1)S(1)} %get-tuple-element.93), channel_id=1, source_target_pairs={{0,4},{4,8},{8,12},{12,16},{16,20},{20,24},{24,28},{28,0},{1,5},{5... | collective-permute-start | bytes 294920 | tf_op jit(solution)/shard_map/ppermute | solution.py:366
  (89 other events, 694.2 us)

commit v4 on v3

--- a/solution.py
+++ b/solution.py
@@ -10,7 +10,7 @@
 
 HDIM = 128
 FB = 8
-STREAMS = 2
+STREAMS = 1
 ITEMS = 2
 ROWBLOCK = 256
 CHUNK = 384
@@ -326,7 +326,7 @@
     shown = step_inputs.reshape(steps, n_item, brow, n_y, 2, shard)
     records = []
     for stream in range(STREAMS):
-        arrived, record = None, []
+        arrived, record = None, [jnp.zeros((rows, half), jnp.float32)] * ITEMS
         for tick in range(ticks):
             busy = active(tick)
             if tick < ITEMS:
@@ -359,17 +359,17 @@
                 part = part.astype(jnp.float32) + moved.astype(jnp.float32)
                 bit = bit * 2
             wide = mine.astype(jnp.float32) + part
-            record.append(lax.dynamic_slice_in_dim(wide, tpos // 2 * shard, shard, 1))
+            for item in range(ITEMS):
+                record[item] = jnp.where(layer == tick - item, wide, record[item])
             after = wide.astype(jnp.bfloat16)
             if tick + 1 < ticks:
                 at_home = phases[tick + 1] == zone
                 near = lax.ppermute(after, ("zone", "spot"), hops[0])
                 far = lax.ppermute(after, ("zone", "spot"), hops[1])
                 arrived = jnp.where(at_home, near, far)
-        record = jnp.stack(record)
-        record = lax.dynamic_slice_in_dim(record, layer, ITEMS, 0)
-        record = record.reshape(ITEMS, steps, brow, shard).swapaxes(0, 1)
-        records.append(record.reshape(steps, ITEMS * brow, shard))
+        for value in record:
+            value = lax.dynamic_slice_in_dim(value, tpos // 2 * shard, shard, 1)
+            records.append(value.reshape(steps, brow, shard))
     return jnp.concatenate(records, axis=1)[None]
 
 

time: 690 us -> 689 us (level)
  waiting for transfers between devices: 345 us -> 450 us
  Pallas kernels: 214 us -> 129 us
  starting transfers between devices: 107 us -> 78.4 us
  other arithmetic: 2.7 us -> 10.3 us
    ppermute x18 -> x9, waiting for transfers between devices: 5.73 us -> 66.3 us  [per_device(): sent = lax.ppermute(own, 'zone', flip)]
    pallas_call x18 -> x9, Pallas kernels: 90.1 us -> 46.1 us  [project(): pl.pallas_call(functools.partial(project_kernel, tick, tiles, tilew, n_y,...]
    pallas_call x18 -> x9, Pallas kernels: 82.8 us -> 41.7 us  [attend(): pl.pallas_call(functools.partial(attend_kernel, steps, brow, kvlocal, gro...]
    ppermute x16 -> x8, waiting for transfers between devices: 18.3 us -> 52.4 us  [per_device(): far = lax.ppermute(after, ('zone', 'spot'), hops[1])]
    ppermute x16 -> x8, waiting for transfers between devices: 30.1 us -> 1.42 us  [per_device(): near = lax.ppermute(after, ('zone', 'spot'), hops[0])]
    ppermute x18 -> x9, waiting for transfers between devices: 32.8 us -> 57.7 us  [per_device(): lax.ppermute(part, 'tensor', [(t, t ^ bit) for t in range(n_tensor)])]
    ppermute x16 -> x8, waiting for transfers between devices: 0.04 us -> 11.4 us  [per_device(): other = lax.ppermute(mine, 'tensor', across)]
    ppermute x16 -> x8, starting transfers between devices: 41.7 us -> 30.9 us  [per_device(): near = lax.ppermute(after, ('zone', 'spot'), hops[0])]
  transfers between devices with their start and end apart: 105 -> 54, of which waited for: 59 -> 47; matrix products, arithmetic and copies ran while one was open for 1% -> 1% of each run, Pallas kernels for 28% -> 9%
where the time goes in v4:
time: 689 us; the launch traced here: 681 us
  waiting for transfers between devices  450 us (65%)
  Pallas kernels  129 us (19%)
  starting transfers between devices  78.4 us (11%)
  other arithmetic  10.3 us (1%)
    ppermute x1, waiting for transfers between devices, per_device(): swapped = lax.ppermute(norm_gain, 'zone', flip)  131 us
    all_to_all x2, waiting for transfers between devices, per_device(): lax.all_to_all(ordered.reshape(tiles, tilew, cdev), ('spot', 'tensor'), s...  117 us
    ppermute x9, waiting for transfers between devices, per_device(): sent = lax.ppermute(own, 'zone', flip)  66.3 us
    ppermute x9, waiting for transfers between devices, per_device(): lax.ppermute(part, 'tensor', [(t, t ^ bit) for t in range(n_tensor)])  57.7 us
    ppermute x8, waiting for transfers between devices, per_device(): far = lax.ppermute(after, ('zone', 'spot'), hops[1])  52.4 us
    pallas_call x9, Pallas kernels, project(): pl.pallas_call(functools.partial(project_kernel, tick, tiles, tilew, n_y,...  46.1 us
    pallas_call x9, Pallas kernels, attend(): pl.pallas_call(functools.partial(attend_kernel, steps, brow, kvlocal, gro...  41.7 us
    pallas_call x2, Pallas kernels, sort_slab(): pl.pallas_call(functools.partial(sort_kernel, phase * kept, layers, kept)...  41.4 us
  transfers between devices with their start and end apart: 54, of which 47 were waited for; matrix products, arithmetic and copies ran while one was open for 1% of the time, Pallas kernels for 9%

profile of v4, /device:TPU:0, one launch (start us, length us, event | category | flops | bytes accessed | tf_op | source)
XLA Modules:
  0.0 681.0 jit_solution(14222284009194248748)
XLA Ops:
  0.0 20.7 %shard_map.82 = bf16[4,4,192,1536]{3,2,1,0:T(8,128)(2,1)} custom-call(bf16[1536,6144]{1,0:T(8,128)(2,1)} %slab.3), custom_call_target="tpu_custom_call" | custom-call | flops 2415919104 | bytes 28311552 | tf_op jit(solution)/shard_map/pallas_call | solution.py:37
  27.0 20.7 %shard_map.91 = bf16[4,4,192,1536]{3,2,1,0:T(8,128)(2,1)} custom-call(bf16[1536,6144]{1,0:T(8,128)(2,1)} %slab.3), custom_call_target="tpu_custom_call" | custom-call | flops 2415919104 | bytes 28311552 | tf_op jit(solution)/shard_map/pallas_call | solution.py:37
  47.7 117.1 %all-to-all-done = bf16[16,192,1536]{2,1,0:T(8,128)(2,1)} async-done(((bf16[16,192,1536]{2,1,0:T(8,128)(2,1)}), bf16[16,192,1536]{2,1,0:T(8,128)(2,1)}, u32[]{:S(2)}, u32[]{:S(2)}) %all-to-all-start) | async-done | bytes 9437216 | tf_op jit(solution)/shard_map/all_to_all | solution.py:285
  178.0 130.8 %collective-permute-done = f32[1,4096]{1,0:T(1,128)S(1)} collective-permute-done((f32[1,4096]{1,0:T(1,128)S(1)}, f32[1,4096]{1,0:T(1,128)S(1)}, u32[]{:S(2)}, u32[]{:S(2)}) %collective-permute-start) | collective-permute-done | bytes 16416 | tf_op jit(solution)/shard_map/ppermute | solution.py:303
  317.6 6.6 collective-permute-done.1.sent
  330.5 6.9 %collective-permute-done.3 = bf16[48,2048]{1,0:T(8,128)(2,1)S(1)} collective-permute-done((bf16[48,2048]{1,0:T(8,128)(2,1)S(1)}, bf16[48,2048]{1,0:T(8,128)(2,1)S(1)}, u32[]{:S(2)}, u32[]{:S(2)}) %collective-permute-start.3) | collective-permute-done | bytes 196640 | tf_op jit(solution)/shard_map/ppermute | solution.py:358
  358.7 7.5 %collective-permute-done.7.sent = bf16[48,1536]{1,0:T(8,128)(2,1)S(1)} collective-permute-done((bf16[48,1536]{1,0:T(8,128)(2,1)S(1)}, bf16[48,1536]{1,0:T(8,128)(2,1)S(1)}, u32[]{:S(2)}, u32[]{:S(2)}) %collective-permute-start.7) | collective-permute-done | bytes 147488 | tf_op jit(solution)/shard_map/ppermute | solution.py:347
  373.0 6.3 collective-permute-done.9
  401.7 8.4 %collective-permute-done.13.sent = bf16[48,1536]{1,0:T(8,128)(2,1)S(1)} collective-permute-done((bf16[48,1536]{1,0:T(8,128)(2,1)S(1)}, bf16[48,1536]{1,0:T(8,128)(2,1)S(1)}, u32[]{:S(2)}, u32[]{:S(2)}) %collective-permute-start.13) | collective-permute-done | bytes 147488 | tf_op jit(solution)/shard_map/ppermute | solution.py:347
  417.0 6.4 collective-permute-done.15
  430.4 6.8 %collective-permute-done.17 = bf16[48,2048]{1,0:T(8,128)(2,1)S(1)} collective-permute-done((bf16[48,2048]{1,0:T(8,128)(2,1)}, bf16[48,2048]{1,0:T(8,128)(2,1)S(1)}, u32[]{:S(2)}, u32[]{:S(2)}) %collective-permute-start.17) | collective-permute-done | bytes 196640 | tf_op jit(solution)/shard_map/ppermute | solution.py:368
  447.0 7.3 %collective-permute-done.19.sent = bf16[48,1536]{1,0:T(8,128)(2,1)S(1)} collective-permute-done((bf16[48,1536]{1,0:T(8,128)(2,1)S(1)}, bf16[48,1536]{1,0:T(8,128)(2,1)S(1)}, u32[]{:S(2)}, u32[]{:S(2)}) %collective-permute-start.19) | collective-permute-done | bytes 147488 | tf_op jit(solution)/shard_map/ppermute | solution.py:347
  471.8 7.1 %collective-permute-done.23 = bf16[48,2048]{1,0:T(8,128)(2,1)S(1)} collective-permute-done((bf16[48,2048]{1,0:T(8,128)(2,1)S(1)}, bf16[48,2048]{1,0:T(8,128)(2,1)S(1)}, u32[]{:S(2)}, u32[]{:S(2)}) %collective-permute-start.23) | collective-permute-done | bytes 196640 | tf_op jit(solution)/shard_map/ppermute | solution.py:368
  488.5 7.3 %collective-permute-done.25.sent = bf16[48,1536]{1,0:T(8,128)(2,1)S(1)} collective-permute-done((bf16[48,1536]{1,0:T(8,128)(2,1)S(1)}, bf16[48,1536]{1,0:T(8,128)(2,1)S(1)}, u32[]{:S(2)}, u32[]{:S(2)}) %collective-permute-start.25) | collective-permute-done | bytes 147488 | tf_op jit(solution)/shard_map/ppermute | solution.py:347
  514.1 7.0 %collective-permute-done.29 = bf16[48,2048]{1,0:T(8,128)(2,1)S(1)} collective-permute-done((bf16[48,2048]{1,0:T(8,128)(2,1)S(1)}, bf16[48,2048]{1,0:T(8,128)(2,1)S(1)}, u32[]{:S(2)}, u32[]{:S(2)}) %collective-permute-start.29) | collective-permute-done | bytes 196640 | tf_op jit(solution)/shard_map/ppermute | solution.py:368
  530.6 7.3 %collective-permute-done.31.sent = bf16[48,1536]{1,0:T(8,128)(2,1)S(1)} collective-permute-done((bf16[48,1536]{1,0:T(8,128)(2,1)S(1)}, bf16[48,1536]{1,0:T(8,128)(2,1)S(1)}, u32[]{:S(2)}, u32[]{:S(2)}) %collective-permute-start.31) | collective-permute-done | bytes 147488 | tf_op jit(solution)/shard_map/ppermute | solution.py:347
  544.8 6.3 collective-permute-done.33
  556.0 7.1 %collective-permute-done.35 = bf16[48,2048]{1,0:T(8,128)(2,1)S(1)} collective-permute-done((bf16[48,2048]{1,0:T(8,128)(2,1)S(1)}, bf16[48,2048]{1,0:T(8,128)(2,1)S(1)}, u32[]{:S(2)}, u32[]{:S(2)}) %collective-permute-start.35) | collective-permute-done | bytes 196640 | tf_op jit(solution)/shard_map/ppermute | solution.py:368
  572.7 7.3 %collective-permute-done.37.sent = bf16[48,1536]{1,0:T(8,128)(2,1)S(1)} collective-permute-done((bf16[48,1536]{1,0:T(8,128)(2,1)S(1)}, bf16[48,1536]{1,0:T(8,128)(2,1)S(1)}, u32[]{:S(2)}, u32[]{:S(2)}) %collective-permute-start.37) | collective-permute-done | bytes 147488 | tf_op jit(solution)/shard_map/ppermute | solution.py:347
  598.1 7.2 %collective-permute-done.41 = bf16[48,2048]{1,0:T(8,128)(2,1)S(1)} collective-permute-done((bf16[48,2048]{1,0:T(8,128)(2,1)S(1)}, bf16[48,2048]{1,0:T(8,128)(2,1)S(1)}, u32[]{:S(2)}, u32[]{:S(2)}) %collective-permute-start.41) | collective-permute-done | bytes 196640 | tf_op jit(solution)/shard_map/ppermute | solution.py:368
  614.7 7.3 %collective-permute-done.43.sent = bf16[48,1536]{1,0:T(8,128)(2,1)S(1)} collective-permute-done((bf16[48,1536]{1,0:T(8,128)(2,1)S(1)}, bf16[48,1536]{1,0:T(8,128)(2,1)S(1)}, u32[]{:S(2)}, u32[]{:S(2)}) %collective-permute-start.43) | collective-permute-done | bytes 147488 | tf_op jit(solution)/shard_map/ppermute | solution.py:347
  628.9 6.3 collective-permute-done.45
  640.2 7.1 %collective-permute-done.47 = bf16[48,2048]{1,0:T(8,128)(2,1)S(1)} collective-permute-done((bf16[48,2048]{1,0:T(8,128)(2,1)S(1)}, bf16[48,2048]{1,0:T(8,128)(2,1)S(1)}, u32[]{:S(2)}, u32[]{:S(2)}) %collective-permute-start.47) | collective-permute-done | bytes 196640 | tf_op jit(solution)/shard_map/ppermute | solution.py:368
  657.8 7.3 %collective-permute-done.49.sent = bf16[48,1536]{1,0:T(8,128)(2,1)S(1)} collective-permute-done((bf16[48,1536]{1,0:T(8,128)(2,1)S(1)}, bf16[48,1536]{1,0:T(8,128)(2,1)S(1)}, u32[]{:S(2)}, u32[]{:S(2)}) %collective-permute-start.49) | collective-permute-done | bytes 147488 | tf_op jit(solution)/shard_map/ppermute | solution.py:347
  (174 shorter events, 244.4 us)
Async XLA Ops:
  20.7 144.2 %all-to-all-start = ((bf16[16,192,1536]{2,1,0:T(8,128)(2,1)}), bf16[16,192,1536]{2,1,0:T(8,128)(2,1)}, u32[]{:S(2)}, u32[]{:S(2)}) async-start(bf16[16,192,1536]{2,1,0:T(8,128)(2,1)} %bitcast.57), calls=%async_computation | async-start | bytes 18874368 | tf_op jit(solution)/shard_map/all_to_all | solution.py:285
  164.9 314.1 %all-to-all-start.1 = ((bf16[16,192,1536]{2,1,0:T(8,128)(2,1)}), bf16[16,192,1536]{2,1,0:T(8,128)(2,1)}, u32[]{:S(2)}, u32[]{:S(2)}) async-start(bf16[16,192,1536]{2,1,0:T(8,128)(2,1)} %bitcast.56), calls=%async_computation.1 | async-start | bytes 18874368 | tf_op jit(solution)/shard_map/all_to_all | solution.py:285
  170.7 138.0 %collective-permute-start = (f32[1,4096]{1,0:T(1,128)S(1)}, f32[1,4096]{1,0:T(1,128)S(1)}, u32[]{:S(2)}, u32[]{:S(2)}) collective-permute-start(f32[1,4096]{1,0:T(1,128)S(1)} %copy-done.6), channel_id=1, source_target_pairs={{0,16},{16,0},{1,17},{17,1},{2,18},{18,2},{3,19},{19,3},{4,20},{20... | collective-permute-start | bytes 49160 | tf_op jit(solution)/shard_map/ppermute | solution.py:303
  313.9 10.2 %collective-permute-start.1 = (bf16[48,1536]{1,0:T(8,128)(2,1)S(1)}, bf16[48,1536]{1,0:T(8,128)(2,1)S(1)}, u32[]{:S(2)}, u32[]{:S(2)}) collective-permute-start(bf16[48,1536]{1,0:T(8,128)(2,1)S(1)} %shard_map.83.own), channel_id=1, source_target_pairs={{0,16},{16,0},{1,17},{17,1},{2,18},{18,2},{3,19},{19,3},{4,20},{20... | collective-permute-start | bytes 442376 | tf_op jit(solution)/shard_map/ppermute | solution.py:347
  338.2 11.3 %collective-permute-start.5 = (bf16[48,2048]{1,0:T(8,128)(2,1)S(1)}, bf16[48,2048]{1,0:T(8,128)(2,1)S(1)}, u32[]{:S(2)}, u32[]{:S(2)}) collective-permute-start(bf16[48,2048]{1,0:T(8,128)(2,1)S(1)} %fusion.10), channel_id=1, source_target_pairs={{0,20},{4,24},{8,28},{12,0},{16,4},{20,8},{24,12},{28,16},{1,21},{... | collective-permute-start | bytes 589832 | tf_op jit(solution)/shard_map/ppermute | solution.py:368
  338.2 11.2 %collective-permute-start.4 = (bf16[48,2048]{1,0:T(8,128)(2,1)S(1)}, bf16[48,2048]{1,0:T(8,128)(2,1)S(1)}, u32[]{:S(2)}, u32[]{:S(2)}) collective-permute-start(bf16[48,2048]{1,0:T(8,128)(2,1)S(1)} %fusion.10), channel_id=1, source_target_pairs={{0,4},{4,8},{8,12},{12,16},{16,20},{20,24},{24,28},{28,0},{1,5},{5... | collective-permute-start | bytes 589832 | tf_op jit(solution)/shard_map/ppermute | solution.py:367
  380.1 11.3 %collective-permute-start.11 = (bf16[48,2048]{1,0:T(8,128)(2,1)S(1)}, bf16[48,2048]{1,0:T(8,128)(2,1)S(1)}, u32[]{:S(2)}, u32[]{:S(2)}) collective-permute-start(bf16[48,2048]{1,0:T(8,128)(2,1)S(1)} %fusion.11), channel_id=1, source_target_pairs={{0,20},{4,24},{8,28},{12,0},{16,4},{20,8},{24,12},{28,16},{1,21},{... | collective-permute-start | bytes 589832 | tf_op jit(solution)/shard_map/ppermute | solution.py:368
  380.6 11.9 %collective-permute-start.10 = (bf16[48,2048]{1,0:T(8,128)(2,1)S(1)}, bf16[48,2048]{1,0:T(8,128)(2,1)}, u32[]{:S(2)}, u32[]{:S(2)}) collective-permute-start(bf16[48,2048]{1,0:T(8,128)(2,1)S(1)} %fusion.11), channel_id=1, source_target_pairs={{0,4},{4,8},{8,12},{12,16},{16,20},{20,24},{24,28},{28,0},{1,5},{5... | collective-permute-start | bytes 589832 | tf_op jit(solution)/shard_map/ppermute | solution.py:367
  425.8 11.4 %collective-permute-start.17 = (bf16[48,2048]{1,0:T(8,128)(2,1)}, bf16[48,2048]{1,0:T(8,128)(2,1)S(1)}, u32[]{:S(2)}, u32[]{:S(2)}) collective-permute-start(bf16[48,2048]{1,0:T(8,128)(2,1)} %get-tuple-element.57), channel_id=1, source_target_pairs={{0,20},{4,24},{8,28},{12,0},{16,4},{20,8},{24,12},{28,16},{1,21},{... | collective-permute-start | bytes 589832 | tf_op jit(solution)/shard_map/ppermute | solution.py:368
  425.8 11.8 %collective-permute-start.16 = (bf16[48,2048]{1,0:T(8,128)(2,1)}, bf16[48,2048]{1,0:T(8,128)(2,1)S(1)}, u32[]{:S(2)}, u32[]{:S(2)}) collective-permute-start(bf16[48,2048]{1,0:T(8,128)(2,1)} %get-tuple-element.57), channel_id=1, source_target_pairs={{0,4},{4,8},{8,12},{12,16},{16,20},{20,24},{24,28},{28,0},{1,5},{5... | collective-permute-start | bytes 589832 | tf_op jit(solution)/shard_map/ppermute | solution.py:367
  467.6 11.3 %collective-permute-start.23 = (bf16[48,2048]{1,0:T(8,128)(2,1)S(1)}, bf16[48,2048]{1,0:T(8,128)(2,1)S(1)}, u32[]{:S(2)}, u32[]{:S(2)}) collective-permute-start(bf16[48,2048]{1,0:T(8,128)(2,1)S(1)} %get-tuple-element.49), channel_id=1, source_target_pairs={{0,20},{4,24},{8,28},{12,0},{16,4},{20,8},{24,12},{28,16},{1,21},{... | collective-permute-start | bytes 589832 | tf_op jit(solution)/shard_map/ppermute | solution.py:368
  467.6 11.2 %collective-permute-start.22 = (bf16[48,2048]{1,0:T(8,128)(2,1)S(1)}, bf16[48,2048]{1,0:T(8,128)(2,1)S(1)}, u32[]{:S(2)}, u32[]{:S(2)}) collective-permute-start(bf16[48,2048]{1,0:T(8,128)(2,1)S(1)} %get-tuple-element.49), channel_id=1, source_target_pairs={{0,4},{4,8},{8,12},{12,16},{16,20},{20,24},{24,28},{28,0},{1,5},{5... | collective-permute-start | bytes 589832 | tf_op jit(solution)/shard_map/ppermute | solution.py:367
  485.5 10.3 %collective-permute-start.25 = (bf16[48,1536]{1,0:T(8,128)(2,1)S(1)}, bf16[48,1536]{1,0:T(8,128)(2,1)S(1)}, u32[]{:S(2)}, u32[]{:S(2)}) collective-permute-start(bf16[48,1536]{1,0:T(8,128)(2,1)S(1)} %shard_map.92.own), channel_id=1, source_target_pairs={{0,16},{16,0},{1,17},{17,1},{2,18},{18,2},{3,19},{19,3},{4,20},{20... | collective-permute-start | bytes 442376 | tf_op jit(solution)/shard_map/ppermute | solution.py:347
  509.9 11.2 %collective-permute-start.29 = (bf16[48,2048]{1,0:T(8,128)(2,1)S(1)}, bf16[48,2048]{1,0:T(8,128)(2,1)S(1)}, u32[]{:S(2)}, u32[]{:S(2)}) collective-permute-start(bf16[48,2048]{1,0:T(8,128)(2,1)S(1)} %get-tuple-element.47), channel_id=1, source_target_pairs={{0,20},{4,24},{8,28},{12,0},{16,4},{20,8},{24,12},{28,16},{1,21},{... | collective-permute-start | bytes 589832 | tf_op jit(solution)/shard_map/ppermute | solution.py:368
  509.9 11.2 %collective-permute-start.28 = (bf16[48,2048]{1,0:T(8,128)(2,1)S(1)}, bf16[48,2048]{1,0:T(8,128)(2,1)S(1)}, u32[]{:S(2)}, u32[]{:S(2)}) collective-permute-start(bf16[48,2048]{1,0:T(8,128)(2,1)S(1)} %get-tuple-element.47), channel_id=1, source_target_pairs={{0,4},{4,8},{8,12},{12,16},{16,20},{20,24},{24,28},{28,0},{1,5},{5... | collective-permute-start | bytes 589832 | tf_op jit(solution)/shard_map/ppermute | solution.py:367
  527.8 10.1 %collective-permute-start.31 = (bf16[48,1536]{1,0:T(8,128)(2,1)S(1)}, bf16[48,1536]{1,0:T(8,128)(2,1)S(1)}, u32[]{:S(2)}, u32[]{:S(2)}) collective-permute-start(bf16[48,1536]{1,0:T(8,128)(2,1)S(1)} %shard_map.94.own), channel_id=1, source_target_pairs={{0,16},{16,0},{1,17},{17,1},{2,18},{18,2},{3,19},{19,3},{4,20},{20... | collective-permute-start | bytes 442376 | tf_op jit(solution)/shard_map/ppermute | solution.py:347
  551.9 11.2 %collective-permute-start.35 = (bf16[48,2048]{1,0:T(8,128)(2,1)S(1)}, bf16[48,2048]{1,0:T(8,128)(2,1)S(1)}, u32[]{:S(2)}, u32[]{:S(2)}) collective-permute-start(bf16[48,2048]{1,0:T(8,128)(2,1)S(1)} %get-tuple-element.45), channel_id=1, source_target_pairs={{0,20},{4,24},{8,28},{12,0},{16,4},{20,8},{24,12},{28,16},{1,21},{... | collective-permute-start | bytes 589832 | tf_op jit(solution)/shard_map/ppermute | solution.py:368
  551.9 11.2 %collective-permute-start.34 = (bf16[48,2048]{1,0:T(8,128)(2,1)S(1)}, bf16[48,2048]{1,0:T(8,128)(2,1)S(1)}, u32[]{:S(2)}, u32[]{:S(2)}) collective-permute-start(bf16[48,2048]{1,0:T(8,128)(2,1)S(1)} %get-tuple-element.45), channel_id=1, source_target_pairs={{0,4},{4,8},{8,12},{12,16},{16,20},{20,24},{24,28},{28,0},{1,5},{5... | collective-permute-start | bytes 589832 | tf_op jit(solution)/shard_map/ppermute | solution.py:367
  569.8 10.2 %collective-permute-start.37 = (bf16[48,1536]{1,0:T(8,128)(2,1)S(1)}, bf16[48,1536]{1,0:T(8,128)(2,1)S(1)}, u32[]{:S(2)}, u32[]{:S(2)}) collective-permute-start(bf16[48,1536]{1,0:T(8,128)(2,1)S(1)} %shard_map.96.own), channel_id=1, source_target_pairs={{0,16},{16,0},{1,17},{17,1},{2,18},{18,2},{3,19},{19,3},{4,20},{20... | collective-permute-start | bytes 442376 | tf_op jit(solution)/shard_map/ppermute | solution.py:347
  594.1 11.2 %collective-permute-start.41 = (bf16[48,2048]{1,0:T(8,128)(2,1)S(1)}, bf16[48,2048]{1,0:T(8,128)(2,1)S(1)}, u32[]{:S(2)}, u32[]{:S(2)}) collective-permute-start(bf16[48,2048]{1,0:T(8,128)(2,1)S(1)} %get-tuple-element.43), channel_id=1, source_target_pairs={{0,20},{4,24},{8,28},{12,0},{16,4},{20,8},{24,12},{28,16},{1,21},{... | collective-permute-start | bytes 589832 | tf_op jit(solution)/shard_map/ppermute | solution.py:368
  594.1 11.2 %collective-permute-start.40 = (bf16[48,2048]{1,0:T(8,128)(2,1)S(1)}, bf16[48,2048]{1,0:T(8,128)(2,1)S(1)}, u32[]{:S(2)}, u32[]{:S(2)}) collective-permute-start(bf16[48,2048]{1,0:T(8,128)(2,1)S(1)} %get-tuple-element.43), channel_id=1, source_target_pairs={{0,4},{4,8},{8,12},{12,16},{16,20},{20,24},{24,28},{28,0},{1,5},{5... | collective-permute-start | bytes 589832 | tf_op jit(solution)/shard_map/ppermute | solution.py:367
  636.0 11.2 %collective-permute-start.47 = (bf16[48,2048]{1,0:T(8,128)(2,1)S(1)}, bf16[48,2048]{1,0:T(8,128)(2,1)S(1)}, u32[]{:S(2)}, u32[]{:S(2)}) collective-permute-start(bf16[48,2048]{1,0:T(8,128)(2,1)S(1)} %get-tuple-element.41), channel_id=1, source_target_pairs={{0,20},{4,24},{8,28},{12,0},{16,4},{20,8},{24,12},{28,16},{1,21},{... | collective-permute-start | bytes 589832 | tf_op jit(solution)/shard_map/ppermute | solution.py:368
  636.0 11.2 %collective-permute-start.46 = (bf16[48,2048]{1,0:T(8,128)(2,1)S(1)}, bf16[48,2048]{1,0:T(8,128)(2,1)}, u32[]{:S(2)}, u32[]{:S(2)}) collective-permute-start(bf16[48,2048]{1,0:T(8,128)(2,1)S(1)} %get-tuple-element.41), channel_id=1, source_target_pairs={{0,4},{4,8},{8,12},{12,16},{16,20},{20,24},{24,28},{28,0},{1,5},{5... | collective-permute-start | bytes 589832 | tf_op jit(solution)/shard_map/ppermute | solution.py:367
  653.9 11.2 %collective-permute-start.49 = (bf16[48,1536]{1,0:T(8,128)(2,1)S(1)}, bf16[48,1536]{1,0:T(8,128)(2,1)S(1)}, u32[]{:S(2)}, u32[]{:S(2)}) collective-permute-start(bf16[48,1536]{1,0:T(8,128)(2,1)S(1)} %shard_map.100.own), channel_id=1, source_target_pairs={{0,16},{16,0},{1,17},{17,1},{2,18},{18,2},{3,19},{19,3},{4,20},{20... | collective-permute-start | bytes 442376 | tf_op jit(solution)/shard_map/ppermute | solution.py:347
  (39 other events, 634.1 us)

commit v5 on v4

--- a/solution.py
+++ b/solution.py
@@ -18,56 +18,62 @@
 VMEM = 48 * 1024 * 1024
 
 
-def sort_kernel(first, layers, kept, slab, out):
+def sort_kernel(first, layers, place, slab, *outs):
     feats = ROWBLOCK // layers
-    row = lax.broadcasted_iota(jnp.int32, (kept * feats, ROWBLOCK), 0)
-    col = lax.broadcasted_iota(jnp.int32, (kept * feats, ROWBLOCK), 1)
-    source = row % feats * layers + first + row // feats
+    shape = (len(outs) * feats, ROWBLOCK)
+    row = lax.broadcasted_iota(jnp.int32, shape, 0)
+    col = lax.broadcasted_iota(jnp.int32, shape, 1)
+    source = row % feats * layers + first + ((row // feats) ^ place[0])
     order = jnp.where(col == source, 1.0, 0.0).astype(jnp.bfloat16)
     moved = jnp.dot(order, slab[...], preferred_element_type=jnp.float32).astype(jnp.bfloat16)
-    for layer in range(kept):
-        out[layer, 0] = moved[layer * feats : (layer + 1) * feats]
-
-
-def sort_slab(slab, phase, layers, n_tensor):
+    for n, out in enumerate(outs):
+        out[...] = moved[n * feats : (n + 1) * feats]
+
+
+def sort_slab(slab, phase, layers, n_tensor, turn, place):
     rows, columns = slab.shape
     kept = layers // 2
     cdev = columns // n_tensor
     feats = ROWBLOCK // layers
     return pl.pallas_call(
-        functools.partial(sort_kernel, phase * kept, layers, kept),
-        grid=(n_tensor, rows // ROWBLOCK),
-        in_specs=[pl.BlockSpec((ROWBLOCK, cdev), lambda t, i: (i, t))],
-        out_specs=pl.BlockSpec((kept, 1, feats, cdev), lambda t, i: (0, t, i, 0)),
-        out_shape=jax.ShapeDtypeStruct((kept, n_tensor, rows // layers, cdev), jnp.bfloat16),
+        functools.partial(sort_kernel, phase * kept, layers),
+        grid_spec=pltpu.PrefetchScalarGridSpec(
+            num_scalar_prefetch=1,
+            grid=(rows // ROWBLOCK,),
+            in_specs=[pl.BlockSpec((ROWBLOCK, cdev), lambda i, s: (i, s[1] ^ turn))],
+            out_specs=[pl.BlockSpec((feats, cdev), lambda i, s: (i, 0))] * kept,
+        ),
+        out_shape=[jax.ShapeDtypeStruct((rows // layers, cdev), jnp.bfloat16)] * kept,
         compiler_params=pltpu.CompilerParams(vmem_limit_bytes=VMEM),
         cost_estimate=pl.CostEstimate(
-            flops=rows * columns * ROWBLOCK, bytes_accessed=3 * rows * columns, transcendentals=0
+            flops=rows * cdev * ROWBLOCK, bytes_accessed=3 * rows * cdev, transcendentals=0
         ),
-    )(slab)
+    )(place, slab)
 
 
 def project_kernel(tick, tiles, tilew, n_y, use, scalars, mine, other, gains, *rest):
-    weights, (out, normed, held, sems) = rest[: len(use)], rest[len(use) :]
+    weights, (out, normed, held, sems) = rest[:-4], rest[-4:]
     rows, half = mine.shape
     width = 2 * half
     shard = half // n_y
     chunks, size, cdev = held.shape
+    per = size // tilew
     core, phase = scalars[0], scalars[1 + tick]
 
-    def fetch(source, j):
-        return pltpu.make_async_copy(source.at[pl.ds(j * size, size)], held.at[j], sems.at[j])
+    def fetch(p, n):
+        target = held.at[n // per, pl.ds(n % per * tilew, tilew)]
+        return pltpu.make_async_copy(weights[p * tiles + n], target, sems.at[n])
 
     if len(use) == 1:
-        for j in range(chunks):
-            fetch(weights[0], j).start()
+        for n in range(tiles):
+            fetch(0, n).start()
     else:
         for p in range(2):
 
             @pl.when(phase == p)
             def _():
-                for j in range(chunks):
-                    fetch(weights[p], j).start()
+                for n in range(tiles):
+                    fetch(p, n).start()
 
     here = mine[...].astype(jnp.float32)
     there = other[...].astype(jnp.float32)
@@ -85,15 +91,15 @@
         normed[:, at : at + shard] = high[:, piece] * gain[:, at : at + shard]
     normed[:, width:] = jnp.zeros((rows, WINDOW), jnp.float32)
 
-    per = CHUNK // tilew
+    along = CHUNK // tilew
     base = scalars.shape[0] - 2 * tiles
     lane = lax.broadcasted_iota(jnp.int32, (rows, CHUNK), 1)
 
     def spread(j):
         value = jnp.zeros((rows, CHUNK), jnp.float32)
-        for a in range(per):
-            start = scalars[base + j * per + a] * FB
-            count = scalars[base + tiles + j * per + a] * FB
+        for a in range(along):
+            start = scalars[base + j * along + a] * FB
+            count = scalars[base + tiles + j * along + a] * FB
             aligned = start // 128 * 128
             window = normed[:, pl.ds(pl.multiple_of(aligned, 128), WINDOW)]
             put = a * tilew
@@ -105,7 +111,8 @@
     acc = jnp.zeros((rows, cdev), jnp.float32)
     for j in range(chunks):
         parts = [spread(j * (size // CHUNK) + i) for i in range(size // CHUNK)]
-        fetch(weights[0], j).wait()
+        for n in range(j * per, (j + 1) * per):
+            fetch(0, n).wait()
         acc = acc + jnp.dot(
             jnp.concatenate(parts, axis=1), held[j], preferred_element_type=jnp.float32
         )
@@ -114,19 +121,20 @@
 
 def project(tick, use, tiles, tilew, n_y, scalars, mine, other, gains, weights):
     rows, half = mine.shape
-    depth, cdev = weights[0].shape
+    cdev = weights[0].shape[1]
+    depth = tiles * tilew
     size = 2 * CHUNK
     vmem = pl.BlockSpec(memory_space=pltpu.VMEM)
     return pl.pallas_call(
         functools.partial(project_kernel, tick, tiles, tilew, n_y, use),
         in_specs=[pl.BlockSpec(memory_space=pltpu.SMEM)]
         + [vmem] * 3
-        + [pl.BlockSpec(memory_space=pl.ANY)] * len(use),
+        + [pl.BlockSpec(memory_space=pl.ANY)] * len(weights),
         out_specs=vmem,
         scratch_shapes=[
             pltpu.VMEM((rows, 2 * half + WINDOW), jnp.float32),
             pltpu.VMEM((depth // size, size, cdev), jnp.bfloat16),
-            pltpu.SemaphoreType.DMA((depth // size,)),
+            pltpu.SemaphoreType.DMA((tiles,)),
         ],
         out_shape=jax.ShapeDtypeStruct((rows, cdev), jnp.bfloat16),
         compiler_params=pltpu.CompilerParams(vmem_limit_bytes=VMEM),
@@ -279,21 +287,30 @@
     core = tpos % 2
     layer = zone * n_spot + spot
 
+    turns = sorted(range(n_tensor), key=lambda kt: (kt < 2, kt))
+    offsets = [(ks, kt) for kt in turns for ks in range(n_spot)]
+    place = jnp.stack([spot, tpos]).astype(jnp.int32)
     weights = []
     for phase in range(2):
-        ordered = sort_slab(trainer_tiles, phase, layers, n_tensor)
-        arrived = lax.all_to_all(
-            ordered.reshape(tiles, tilew, cdev),
-            ("spot", "tensor"),
-            split_axis=0,
-            concat_axis=0,
-            tiled=True,
-        )
-        weights.append(arrived.reshape(tiles * tilew, cdev))
+        pieces = []
+        for kt in turns:
+            sorted_pieces = sort_slab(trainer_tiles, phase, layers, n_tensor, kt, place)
+            for ks, piece in enumerate(sorted_pieces):
+                pairs = [
+                    (s * n_tensor + t, (s ^ ks) * n_tensor + (t ^ kt))
+                    for s in range(n_spot)
+                    for t in range(n_tensor)
+                ]
+                if ks or kt:
+                    piece = lax.ppermute(piece, ("spot", "tensor"), pairs)
+                pieces.append(piece)
+        weights.append(pieces)
 
     ends = jnp.cumsum(tile_lengths)
-    starts = lax.dynamic_slice_in_dim(ends - tile_lengths, zone * tiles, tiles)
-    counts = lax.dynamic_slice_in_dim(tile_lengths, zone * tiles, tiles)
+    offset = np.array(offsets, np.int32)
+    sources = (offset[:, 0] ^ spot) * n_tensor + (offset[:, 1] ^ tpos) + zone * tiles
+    starts = (ends - tile_lengths)[sources]
+    counts = tile_lengths[sources]
     tick_ids = jnp.arange(ticks, dtype=jnp.int32)
     phases = (tick_ids >= spot + n_spot).astype(jnp.int32)
     turns = jnp.clip(tick_ids - layer, 0, ITEMS - 1)
@@ -307,17 +324,21 @@
     spans = jnp.repeat(cache_lengths, length).reshape(n_item, 1, brow * length)
     axes = ("zone", "spot", "tensor")
 
-    flat = [(z, s) for z in range(n_zone) for s in range(n_spot)]
-
-    def shifted(turn):
+    def spots(tick):
+        return sorted({(tick - i) % n_spot for i in range(ITEMS)})
+
+    def hop(tick, turn):
         pairs = []
-        for z, s in flat:
-            nearby = (s + 1) % n_spot
-            ahead = z if s + 1 < n_spot else 1 - z
-            pairs.append((z * n_spot + s, (ahead ^ turn) * n_spot + nearby))
-        return pairs
-
-    hops = [shifted(turn) for turn in range(2)]
+        for s in spots(tick):
+            for z in range(n_zone):
+                ahead = z if s + 1 < n_spot else 1 - z
+                pairs.append((z * n_spot + s, (ahead ^ turn) * n_spot + (s + 1) % n_spot))
+        return sorted(pairs)
+
+    def mirror(tick):
+        return sorted(
+            (z * n_spot + s, (1 - z) * n_spot + s) for s in spots(tick) for z in range(n_zone)
+        )
 
     def active(tick):
         return [l for l in range(layers) if 0 <= tick - l < ITEMS]
@@ -342,9 +363,9 @@
                 other = lax.dynamic_index_in_dim(fresh, 1 - core, 2, False).reshape(rows, half)
             use = sorted({l // n_spot for l in busy})
             own = project(
-                tick, use, tiles, tilew, n_y, scalars, mine, other, gains, [weights[p] for p in use]
+                tick, use, tiles, tilew, n_y, scalars, mine, other, gains, sum([weights[p] for p in use], [])
             )
-            sent = lax.ppermute(own, "zone", flip)
+            sent = lax.ppermute(own, ("zone", "spot"), mirror(tick))
             item_at = 1 + ticks + stream * ticks + tick
             theirs, ours = attend(
                 item_at, steps, brow, n_y, scalars, own, sent, spans, cache_keys[0], cache_values[0], wo_rollout
@@ -364,8 +385,8 @@
             after = wide.astype(jnp.bfloat16)
             if tick + 1 < ticks:
                 at_home = phases[tick + 1] == zone
-                near = lax.ppermute(after, ("zone", "spot"), hops[0])
-                far = lax.ppermute(after, ("zone", "spot"), hops[1])
+                near = lax.ppermute(after, ("zone", "spot"), hop(tick, 0))
+                far = lax.ppermute(after, ("zone", "spot"), hop(tick, 1))
                 arrived = jnp.where(at_home, near, far)
         for value in record:
             value = lax.dynamic_slice_in_dim(value, tpos // 2 * shard, shard, 1)

time: 689 us -> 702 us (1.019)
  waiting for transfers between devices: 450 us -> 306 us
  starting transfers between devices: 78.4 us -> 211 us
  local copies, waits for them, and re-layouts: 6.78 us -> 19.9 us
    ppermute x25 -> x55, starting transfers between devices: 57.1 us -> 193 us  [the longest x30 151 us: per_device(): piece = lax.ppermute(piece, ('spot', 'tensor'), pairs)]
    ppermute x1, waiting for transfers between devices: 131 us -> 0.01 us  [per_device(): swapped = lax.ppermute(norm_gain, 'zone', flip)]
    ppermute x25 -> x55, waiting for transfers between devices: 120 us -> 241 us  [the longest x30 143 us: per_device(): piece = lax.ppermute(piece, ('spot', 'tensor'), pairs)]
    all_to_all x2 -> x0, waiting for transfers between devices: 117 us -> none  [per_device(): lax.all_to_all(ordered.reshape(tiles, tilew, cdev), ('spot', 'tensor'), s...]
    ppermute x9, waiting for transfers between devices: 57.7 us -> 43.8 us  [per_device(): lax.ppermute(part, 'tensor', [(t, t ^ bit) for t in range(n_tensor)])]
    all_to_all x2 -> x0, starting transfers between devices: 12.1 us -> none  [per_device(): lax.all_to_all(ordered.reshape(tiles, tilew, cdev), ('spot', 'tensor'), s...]
    unnamed x21 -> x77, local copies, waits for them, and re-layouts: 1.51 us -> 10.4 us
    ppermute x9, starting transfers between devices: 5.44 us -> 12.5 us  [per_device(): lax.ppermute(part, 'tensor', [(t, t ^ bit) for t in range(n_tensor)])]
  transfers between devices with their start and end apart: 54 -> 82, of which waited for: 47 -> 48; matrix products, arithmetic and copies ran while one was open for 1% -> 2% of each run, Pallas kernels for 9% -> 7%
where the time goes in v5:
time: 702 us; the launch traced here: 693 us
  waiting for transfers between devices  306 us (44%)
  starting transfers between devices  211 us (30%)
  Pallas kernels  133 us (19%)
  local copies, waits for them, and re-layouts  19.9 us (3%)
  other arithmetic  16.6 us (2%)
    ppermute x30, starting transfers between devices, per_device(): piece = lax.ppermute(piece, ('spot', 'tensor'), pairs)  151 us
    ppermute x30, waiting for transfers between devices, per_device(): piece = lax.ppermute(piece, ('spot', 'tensor'), pairs)  143 us
    ppermute x8, waiting for transfers between devices, per_device(): near = lax.ppermute(after, ('zone', 'spot'), hop(tick, 0))  58.1 us
    pallas_call x8, Pallas kernels, sort_slab(): pl.pallas_call(functools.partial(sort_kernel, phase * kept, layers), grid...  46.7 us
    pallas_call x9, Pallas kernels, project(): pl.pallas_call(functools.partial(project_kernel, tick, tiles, tilew, n_y,...  43.9 us
    ppermute x9, waiting for transfers between devices, per_device(): lax.ppermute(part, 'tensor', [(t, t ^ bit) for t in range(n_tensor)])  43.8 us
    pallas_call x9, Pallas kernels, attend(): pl.pallas_call(functools.partial(attend_kernel, steps, brow, kvlocal, gro...  42.2 us
    ppermute x9, waiting for transfers between devices, per_device(): sent = lax.ppermute(own, ('zone', 'spot'), mirror(tick))  29.6 us
  transfers between devices with their start and end apart: 82, of which 48 were waited for; matrix products, arithmetic and copies ran while one was open for 2% of the time, Pallas kernels for 7%

profile of v5, /device:TPU:0, one launch (start us, length us, event | category | flops | bytes accessed | tf_op | source)
XLA Modules:
  0.0 692.5 jit_solution(15606442245169720613)
XLA Ops:
  4.1 6.6 shard_map.100
  16.6 6.6 shard_map.101
  28.6 6.3 shard_map.102
  36.6 28.5 %collective-permute-done.1.rest_0_ = bf16[192,1536]{1,0:T(8,128)(2,1)S(1)} collective-permute-done((bf16[192,1536]{1,0:T(8,128)(2,1)}, bf16[192,1536]{1,0:T(8,128)(2,1)S(1)}, u32[]{:S(2)}, u32[]{:S(2)}) %collective-permute-start.1) | collective-permute-done | bytes 589856 | tf_op jit(solution)/shard_map/ppermute | solution.py:305
  70.3 43.0 %collective-permute-done.5.rest_4_ = bf16[192,1536]{1,0:T(8,128)(2,1)} collective-permute-done((bf16[192,1536]{1,0:T(8,128)(2,1)}, bf16[192,1536]{1,0:T(8,128)(2,1)}, u32[]{:S(2)}, u32[]{:S(2)}) %collective-permute-start.5) | collective-permute-done | bytes 589856 | tf_op jit(solution)/shard_map/ppermute | solution.py:305
  131.8 11.6 %collective-permute-done.11.rest_11_ = bf16[192,1536]{1,0:T(8,128)(2,1)S(1)} collective-permute-done((bf16[192,1536]{1,0:T(8,128)(2,1)S(1)}, bf16[192,1536]{1,0:T(8,128)(2,1)S(1)}, u32[]{:S(2)}, u32[]{:S(2)}) %collective-permute-start.11) | collective-permute-done | bytes 589856 | tf_op jit(solution)/shard_map/ppermute | solution.py:305
  143.4 10.9 %collective-permute-done.13.rest_13_ = bf16[192,1536]{1,0:T(8,128)(2,1)S(1)} collective-permute-done((bf16[192,1536]{1,0:T(8,128)(2,1)S(1)}, bf16[192,1536]{1,0:T(8,128)(2,1)S(1)}, u32[]{:S(2)}, u32[]{:S(2)}) %collective-permute-start.13) | collective-permute-done | bytes 589856 | tf_op jit(solution)/shard_map/ppermute | solution.py:305
  155.2 13.1 %collective-permute-done.15.rest_15_ = bf16[192,1536]{1,0:T(8,128)(2,1)S(1)} collective-permute-done((bf16[192,1536]{1,0:T(8,128)(2,1)S(1)}, bf16[192,1536]{1,0:T(8,128)(2,1)S(1)}, u32[]{:S(2)}, u32[]{:S(2)}) %collective-permute-start.15) | collective-permute-done | bytes 589856 | tf_op jit(solution)/shard_map/ppermute | solution.py:305
  177.0 6.5 collective-permute-done.16.sent
  204.4 6.2 collective-permute-done.19
  224.0 6.2 collective-permute-done.22.sent
  301.9 17.9 %collective-permute-start.41 = (bf16[192,1536]{1,0:T(8,128)(2,1)S(1)}, bf16[192,1536]{1,0:T(8,128)(2,1)}, u32[]{:S(2)}, u32[]{:S(2)}) collective-permute-start(bf16[192,1536]{1,0:T(8,128)(2,1)S(1)} %get-tuple-element.80), channel_id=1, source_target_pairs={{0,6},{1,7},{2,4},{3,5},{4,2},{5,3},{6,0},{7,1},{8,14},{9,15},{10,... | collective-permute-start | bytes 1769480 | tf_op jit(solution)/shard_map/ppermute | solution.py:305
  319.8 10.5 %collective-permute-start.42 = (bf16[192,1536]{1,0:T(8,128)(2,1)S(1)}, bf16[192,1536]{1,0:T(8,128)(2,1)}, u32[]{:S(2)}, u32[]{:S(2)}) collective-permute-start(bf16[192,1536]{1,0:T(8,128)(2,1)S(1)} %get-tuple-element.81), channel_id=1, source_target_pairs={{0,10},{1,11},{2,8},{3,9},{4,14},{5,15},{6,12},{7,13},{8,2},{9,3},... | collective-permute-start | bytes 1769480 | tf_op jit(solution)/shard_map/ppermute | solution.py:305
  339.2 33.1 %collective-permute-start.45 = (bf16[192,1536]{1,0:T(8,128)(2,1)S(1)}, bf16[192,1536]{1,0:T(8,128)(2,1)}, u32[]{:S(2)}, u32[]{:S(2)}) collective-permute-start(bf16[192,1536]{1,0:T(8,128)(2,1)S(1)} %get-tuple-element.84), channel_id=1, source_target_pairs={{0,7},{1,6},{2,5},{3,4},{4,3},{5,2},{6,1},{7,0},{8,15},{9,14},{10,... | collective-permute-start | bytes 1769480 | tf_op jit(solution)/shard_map/ppermute | solution.py:305
  372.3 11.8 %collective-permute-start.46 = (bf16[192,1536]{1,0:T(8,128)(2,1)S(1)}, bf16[192,1536]{1,0:T(8,128)(2,1)}, u32[]{:S(2)}, u32[]{:S(2)}) collective-permute-start(bf16[192,1536]{1,0:T(8,128)(2,1)S(1)} %get-tuple-element.85), channel_id=1, source_target_pairs={{0,11},{1,10},{2,9},{3,8},{4,15},{5,14},{6,13},{7,12},{8,3},{9,2},... | collective-permute-start | bytes 1769480 | tf_op jit(solution)/shard_map/ppermute | solution.py:305
  386.4 6.5 shard_map.114
  393.7 28.2 %collective-permute-start.48 = (bf16[192,1536]{1,0:T(8,128)(2,1)}, bf16[192,1536]{1,0:T(8,128)(2,1)}, u32[]{:S(2)}, u32[]{:S(2)}) collective-permute-start(bf16[192,1536]{1,0:T(8,128)(2,1)} %get-tuple-element.88), channel_id=1, source_target_pairs={{0,4},{1,5},{2,6},{3,7},{4,0},{5,1},{6,2},{7,3},{8,12},{9,13},{10,... | collective-permute-start | bytes 1769480 | tf_op jit(solution)/shard_map/ppermute | solution.py:305
  422.0 15.2 %collective-permute-start.49 = (bf16[192,1536]{1,0:T(8,128)(2,1)}, bf16[192,1536]{1,0:T(8,128)(2,1)}, u32[]{:S(2)}, u32[]{:S(2)}) collective-permute-start(bf16[192,1536]{1,0:T(8,128)(2,1)} %get-tuple-element.89), channel_id=1, source_target_pairs={{0,8},{1,9},{2,10},{3,11},{4,12},{5,13},{6,14},{7,15},{8,0},{9,1},... | collective-permute-start | bytes 1769480 | tf_op jit(solution)/shard_map/ppermute | solution.py:305
  460.6 10.9 %collective-permute-done.50.rest_27_.rest_11_ = bf16[192,1536]{1,0:T(8,128)(2,1)} collective-permute-done((bf16[192,1536]{1,0:T(8,128)(2,1)}, bf16[192,1536]{1,0:T(8,128)(2,1)}, u32[]{:S(2)}, u32[]{:S(2)}) %collective-permute-start.50) | collective-permute-done | bytes 589856 | tf_op jit(solution)/shard_map/ppermute | solution.py:305
  471.5 12.4 %collective-permute-done.52.rest_29_.rest_13_ = bf16[192,1536]{1,0:T(8,128)(2,1)S(1)} collective-permute-done((bf16[192,1536]{1,0:T(8,128)(2,1)S(1)}, bf16[192,1536]{1,0:T(8,128)(2,1)S(1)}, u32[]{:S(2)}, u32[]{:S(2)}) %collective-permute-start.52) | collective-permute-done | bytes 589856 | tf_op jit(solution)/shard_map/ppermute | solution.py:305
  483.9 10.8 %collective-permute-done.54.rest_31_.rest_15_ = bf16[192,1536]{1,0:T(8,128)(2,1)S(1)} collective-permute-done((bf16[192,1536]{1,0:T(8,128)(2,1)S(1)}, bf16[192,1536]{1,0:T(8,128)(2,1)S(1)}, u32[]{:S(2)}, u32[]{:S(2)}) %collective-permute-start.54) | collective-permute-done | bytes 589856 | tf_op jit(solution)/shard_map/ppermute | solution.py:305
  528.9 7.7 %collective-permute-done.58 = bf16[48,2048]{1,0:T(8,128)(2,1)S(1)} collective-permute-done((bf16[48,2048]{1,0:T(8,128)(2,1)S(1)}, bf16[48,2048]{1,0:T(8,128)(2,1)S(1)}, u32[]{:S(2)}, u32[]{:S(2)}) %collective-permute-start.58) | collective-permute-done | bytes 196640 | tf_op jit(solution)/shard_map/ppermute | solution.py:388
  626.2 32.5 %collective-permute-done.76 = bf16[48,2048]{1,0:T(8,128)(2,1)S(1)} collective-permute-done((bf16[48,2048]{1,0:T(8,128)(2,1)S(1)}, bf16[48,2048]{1,0:T(8,128)(2,1)S(1)}, u32[]{:S(2)}, u32[]{:S(2)}) %collective-permute-start.76) | collective-permute-done | bytes 196640 | tf_op jit(solution)/shard_map/ppermute | solution.py:388
  670.3 6.2 collective-permute-done.79.sent
  (295 shorter events, 337.0 us)
Async XLA Ops:
  10.7 54.4 %collective-permute-start.1 = (bf16[192,1536]{1,0:T(8,128)(2,1)}, bf16[192,1536]{1,0:T(8,128)(2,1)S(1)}, u32[]{:S(2)}, u32[]{:S(2)}) collective-permute-start(bf16[192,1536]{1,0:T(8,128)(2,1)} %get-tuple-element.55), channel_id=1, source_target_pairs={{0,2},{1,3},{2,0},{3,1},{4,6},{5,7},{6,4},{7,5},{8,10},{9,11},{10,... | collective-permute-start | bytes 1769480 | tf_op jit(solution)/shard_map/ppermute | solution.py:305
  12.2 52.9 %collective-permute-start.2 = (bf16[192,1536]{1,0:T(8,128)(2,1)}, bf16[192,1536]{1,0:T(8,128)(2,1)S(1)}, u32[]{:S(2)}, u32[]{:S(2)}) collective-permute-start(bf16[192,1536]{1,0:T(8,128)(2,1)} %get-tuple-element.56), channel_id=1, source_target_pairs={{0,6},{1,7},{2,4},{3,5},{4,2},{5,3},{6,0},{7,1},{8,14},{9,15},{10,... | collective-permute-start | bytes 1769480 | tf_op jit(solution)/shard_map/ppermute | solution.py:305
  13.7 55.1 %collective-permute-start.3 = (bf16[192,1536]{1,0:T(8,128)(2,1)}, bf16[192,1536]{1,0:T(8,128)(2,1)}, u32[]{:S(2)}, u32[]{:S(2)}) collective-permute-start(bf16[192,1536]{1,0:T(8,128)(2,1)} %get-tuple-element.57), channel_id=1, source_target_pairs={{0,10},{1,11},{2,8},{3,9},{4,14},{5,15},{6,12},{7,13},{8,2},{9,3},... | collective-permute-start | bytes 1769480 | tf_op jit(solution)/shard_map/ppermute | solution.py:305
  16.2 52.6 %collective-permute-start.4 = (bf16[192,1536]{1,0:T(8,128)(2,1)}, bf16[192,1536]{1,0:T(8,128)(2,1)}, u32[]{:S(2)}, u32[]{:S(2)}) collective-permute-start(bf16[192,1536]{1,0:T(8,128)(2,1)} %get-tuple-element.58), channel_id=1, source_target_pairs={{0,14},{1,15},{2,12},{3,13},{4,10},{5,11},{6,8},{7,9},{8,6},{9,7},... | collective-permute-start | bytes 1769480 | tf_op jit(solution)/shard_map/ppermute | solution.py:305
  23.1 90.2 %collective-permute-start.5 = (bf16[192,1536]{1,0:T(8,128)(2,1)}, bf16[192,1536]{1,0:T(8,128)(2,1)}, u32[]{:S(2)}, u32[]{:S(2)}) collective-permute-start(bf16[192,1536]{1,0:T(8,128)(2,1)} %get-tuple-element.59), channel_id=1, source_target_pairs={{0,3},{1,2},{2,1},{3,0},{4,7},{5,6},{6,5},{7,4},{8,11},{9,10},{10,... | collective-permute-start | bytes 1769480 | tf_op jit(solution)/shard_map/ppermute | solution.py:305
  65.1 59.6 %collective-permute-start.6 = (bf16[192,1536]{1,0:T(8,128)(2,1)}, bf16[192,1536]{1,0:T(8,128)(2,1)}, u32[]{:S(2)}, u32[]{:S(2)}) collective-permute-start(bf16[192,1536]{1,0:T(8,128)(2,1)} %get-tuple-element.60), channel_id=1, source_target_pairs={{0,7},{1,6},{2,5},{3,4},{4,3},{5,2},{6,1},{7,0},{8,15},{9,14},{10,... | collective-permute-start | bytes 1769480 | tf_op jit(solution)/shard_map/ppermute | solution.py:305
  65.1 61.1 %collective-permute-start.7 = (bf16[192,1536]{1,0:T(8,128)(2,1)}, bf16[192,1536]{1,0:T(8,128)(2,1)}, u32[]{:S(2)}, u32[]{:S(2)}) collective-permute-start(bf16[192,1536]{1,0:T(8,128)(2,1)} %get-tuple-element.61), channel_id=1, source_target_pairs={{0,11},{1,10},{2,9},{3,8},{4,15},{5,14},{6,13},{7,12},{8,3},{9,2},... | collective-permute-start | bytes 1769480 | tf_op jit(solution)/shard_map/ppermute | solution.py:305
  68.8 57.6 %collective-permute-start.8 = (bf16[192,1536]{1,0:T(8,128)(2,1)}, bf16[192,1536]{1,0:T(8,128)(2,1)}, u32[]{:S(2)}, u32[]{:S(2)}) collective-permute-start(bf16[192,1536]{1,0:T(8,128)(2,1)} %get-tuple-element.62), channel_id=1, source_target_pairs={{0,15},{1,14},{2,13},{3,12},{4,11},{5,10},{6,9},{7,8},{8,7},{9,6},... | collective-permute-start | bytes 1769480 | tf_op jit(solution)/shard_map/ppermute | solution.py:305
  68.8 58.1 %collective-permute-start.9 = (bf16[192,1536]{1,0:T(8,128)(2,1)}, bf16[192,1536]{1,0:T(8,128)(2,1)}, u32[]{:S(2)}, u32[]{:S(2)}) collective-permute-start(bf16[192,1536]{1,0:T(8,128)(2,1)} %get-tuple-element.64), channel_id=1, source_target_pairs={{0,4},{1,5},{2,6},{3,7},{4,0},{5,1},{6,2},{7,3},{8,12},{9,13},{10,... | collective-permute-start | bytes 1769480 | tf_op jit(solution)/shard_map/ppermute | solution.py:305
  129.7 38.5 %collective-permute-start.15 = (bf16[192,1536]{1,0:T(8,128)(2,1)S(1)}, bf16[192,1536]{1,0:T(8,128)(2,1)S(1)}, u32[]{:S(2)}, u32[]{:S(2)}) collective-permute-start(bf16[192,1536]{1,0:T(8,128)(2,1)S(1)} %get-tuple-element.70), channel_id=1, source_target_pairs={{0,13},{1,12},{2,15},{3,14},{4,9},{5,8},{6,11},{7,10},{8,5},{9,4},... | collective-permute-start | bytes 1769480 | tf_op jit(solution)/shard_map/ppermute | solution.py:305
  295.1 42.6 %collective-permute-start.35 = (bf16[48,2048]{1,0:T(8,128)(2,1)S(1)}, bf16[48,2048]{1,0:T(8,128)(2,1)S(1)}, u32[]{:S(2)}, u32[]{:S(2)}) collective-permute-start(bf16[48,2048]{1,0:T(8,128)(2,1)S(1)} %get-tuple-element.78), channel_id=1, source_target_pairs={{0,1},{1,0},{2,3},{3,2},{4,5},{5,4},{6,7},{7,6},{8,9},{9,8},{10,11... | collective-permute-start | bytes 589832 | tf_op jit(solution)/shard_map/ppermute | solution.py:373
  300.5 37.3 %collective-permute-start.40 = (bf16[192,1536]{1,0:T(8,128)(2,1)S(1)}, bf16[192,1536]{1,0:T(8,128)(2,1)}, u32[]{:S(2)}, u32[]{:S(2)}) collective-permute-start(bf16[192,1536]{1,0:T(8,128)(2,1)S(1)} %get-tuple-element.79), channel_id=1, source_target_pairs={{0,2},{1,3},{2,0},{3,1},{4,6},{5,7},{6,4},{7,5},{8,10},{9,11},{10,... | collective-permute-start | bytes 1769480 | tf_op jit(solution)/shard_map/ppermute | solution.py:305
  301.9 37.2 %collective-permute-start.41 = (bf16[192,1536]{1,0:T(8,128)(2,1)S(1)}, bf16[192,1536]{1,0:T(8,128)(2,1)}, u32[]{:S(2)}, u32[]{:S(2)}) collective-permute-start(bf16[192,1536]{1,0:T(8,128)(2,1)S(1)} %get-tuple-element.80), channel_id=1, source_target_pairs={{0,6},{1,7},{2,4},{3,5},{4,2},{5,3},{6,0},{7,1},{8,14},{9,15},{10,... | collective-permute-start | bytes 1769480 | tf_op jit(solution)/shard_map/ppermute | solution.py:305
  319.8 52.5 %collective-permute-start.42 = (bf16[192,1536]{1,0:T(8,128)(2,1)S(1)}, bf16[192,1536]{1,0:T(8,128)(2,1)}, u32[]{:S(2)}, u32[]{:S(2)}) collective-permute-start(bf16[192,1536]{1,0:T(8,128)(2,1)S(1)} %get-tuple-element.81), channel_id=1, source_target_pairs={{0,10},{1,11},{2,8},{3,9},{4,14},{5,15},{6,12},{7,13},{8,2},{9,3},... | collective-permute-start | bytes 1769480 | tf_op jit(solution)/shard_map/ppermute | solution.py:305
  330.3 53.9 %collective-permute-start.43 = (bf16[192,1536]{1,0:T(8,128)(2,1)S(1)}, bf16[192,1536]{1,0:T(8,128)(2,1)}, u32[]{:S(2)}, u32[]{:S(2)}) collective-permute-start(bf16[192,1536]{1,0:T(8,128)(2,1)S(1)} %get-tuple-element.82), channel_id=1, source_target_pairs={{0,14},{1,15},{2,12},{3,13},{4,10},{5,11},{6,8},{7,9},{8,6},{9,7},... | collective-permute-start | bytes 1769480 | tf_op jit(solution)/shard_map/ppermute | solution.py:305
  337.7 56.0 %collective-permute-start.44 = (bf16[192,1536]{1,0:T(8,128)(2,1)S(1)}, bf16[192,1536]{1,0:T(8,128)(2,1)}, u32[]{:S(2)}, u32[]{:S(2)}) collective-permute-start(bf16[192,1536]{1,0:T(8,128)(2,1)S(1)} %get-tuple-element.83), channel_id=1, source_target_pairs={{0,3},{1,2},{2,1},{3,0},{4,7},{5,6},{6,5},{7,4},{8,11},{9,10},{10,... | collective-permute-start | bytes 1769480 | tf_op jit(solution)/shard_map/ppermute | solution.py:305
  337.9 84.1 %collective-permute-start.36 = (bf16[48,2048]{1,0:T(8,128)(2,1)S(1)}, bf16[48,2048]{1,0:T(8,128)(2,1)S(1)}, u32[]{:S(2)}, u32[]{:S(2)}) collective-permute-start(bf16[48,2048]{1,0:T(8,128)(2,1)S(1)} %add_convert_fusion.5), channel_id=1, source_target_pairs={{0,2},{1,3},{2,0},{3,1},{4,6},{5,7},{6,4},{7,5},{8,10},{9,11},{10,... | collective-permute-start | bytes 589832 | tf_op jit(solution)/shard_map/ppermute | solution.py:379
  339.2 98.9 %collective-permute-start.45 = (bf16[192,1536]{1,0:T(8,128)(2,1)S(1)}, bf16[192,1536]{1,0:T(8,128)(2,1)}, u32[]{:S(2)}, u32[]{:S(2)}) collective-permute-start(bf16[192,1536]{1,0:T(8,128)(2,1)S(1)} %get-tuple-element.84), channel_id=1, source_target_pairs={{0,7},{1,6},{2,5},{3,4},{4,3},{5,2},{6,1},{7,0},{8,15},{9,14},{10,... | collective-permute-start | bytes 1769480 | tf_op jit(solution)/shard_map/ppermute | solution.py:305
  372.3 67.0 %collective-permute-start.46 = (bf16[192,1536]{1,0:T(8,128)(2,1)S(1)}, bf16[192,1536]{1,0:T(8,128)(2,1)}, u32[]{:S(2)}, u32[]{:S(2)}) collective-permute-start(bf16[192,1536]{1,0:T(8,128)(2,1)S(1)} %get-tuple-element.85), channel_id=1, source_target_pairs={{0,11},{1,10},{2,9},{3,8},{4,15},{5,14},{6,13},{7,12},{8,3},{9,2},... | collective-permute-start | bytes 1769480 | tf_op jit(solution)/shard_map/ppermute | solution.py:305
  384.1 56.5 %collective-permute-start.47 = (bf16[192,1536]{1,0:T(8,128)(2,1)S(1)}, bf16[192,1536]{1,0:T(8,128)(2,1)}, u32[]{:S(2)}, u32[]{:S(2)}) collective-permute-start(bf16[192,1536]{1,0:T(8,128)(2,1)S(1)} %get-tuple-element.86), channel_id=1, source_target_pairs={{0,15},{1,14},{2,13},{3,12},{4,11},{5,10},{6,9},{7,8},{8,7},{9,6},... | collective-permute-start | bytes 1769480 | tf_op jit(solution)/shard_map/ppermute | solution.py:305
  393.7 58.2 %collective-permute-start.48 = (bf16[192,1536]{1,0:T(8,128)(2,1)}, bf16[192,1536]{1,0:T(8,128)(2,1)}, u32[]{:S(2)}, u32[]{:S(2)}) collective-permute-start(bf16[192,1536]{1,0:T(8,128)(2,1)} %get-tuple-element.88), channel_id=1, source_target_pairs={{0,4},{1,5},{2,6},{3,7},{4,0},{5,1},{6,2},{7,3},{8,12},{9,13},{10,... | collective-permute-start | bytes 1769480 | tf_op jit(solution)/shard_map/ppermute | solution.py:305
  458.9 35.8 %collective-permute-start.54 = (bf16[192,1536]{1,0:T(8,128)(2,1)S(1)}, bf16[192,1536]{1,0:T(8,128)(2,1)S(1)}, u32[]{:S(2)}, u32[]{:S(2)}) collective-permute-start(bf16[192,1536]{1,0:T(8,128)(2,1)S(1)} %get-tuple-element.94), channel_id=1, source_target_pairs={{0,13},{1,12},{2,15},{3,14},{4,9},{5,8},{6,11},{7,10},{8,5},{9,4},... | collective-permute-start | bytes 1769480 | tf_op jit(solution)/shard_map/ppermute | solution.py:305
  623.0 35.7 %collective-permute-start.76 = (bf16[48,2048]{1,0:T(8,128)(2,1)S(1)}, bf16[48,2048]{1,0:T(8,128)(2,1)S(1)}, u32[]{:S(2)}, u32[]{:S(2)}) collective-permute-start(bf16[48,2048]{1,0:T(8,128)(2,1)S(1)} %get-tuple-element.105), channel_id=1, source_target_pairs={{8,12},{12,16},{24,28},{28,0},{9,13},{13,17},{25,29},{29,1},{10,14... | collective-permute-start | bytes 589832 | tf_op jit(solution)/shard_map/ppermute | solution.py:388
  624.3 37.2 %collective-permute-start.77 = (bf16[48,2048]{1,0:T(8,128)(2,1)S(1)}, bf16[48,2048]{1,0:T(8,128)(2,1)S(1)}, u32[]{:S(2)}, u32[]{:S(2)}) collective-permute-start(bf16[48,2048]{1,0:T(8,128)(2,1)S(1)} %get-tuple-element.105), channel_id=1, source_target_pairs={{8,28},{12,0},{24,12},{28,16},{9,29},{13,1},{25,13},{29,17},{10,30... | collective-permute-start | bytes 589832 | tf_op jit(solution)/shard_map/ppermute | solution.py:389
  (95 other events, 1761.6 us)

commit v6 on v5

--- a/solution.py
+++ b/solution.py
@@ -287,28 +287,49 @@
     core = tpos % 2
     layer = zone * n_spot + spot
 
-    turns = sorted(range(n_tensor), key=lambda kt: (kt < 2, kt))
+    all_s, all_t = n_spot - 1, n_tensor - 2
+    turns = sorted(range(n_tensor), key=lambda kt: (kt % 2, kt))
     offsets = [(ks, kt) for kt in turns for ks in range(n_spot)]
-    place = jnp.stack([spot, tpos]).astype(jnp.int32)
-    weights = []
+    place = jnp.stack([spot ^ core * all_s, tpos ^ core * all_t]).astype(jnp.int32)
+
+    def exchange(offset, piece):
+        pairs = []
+        for s in range(n_spot):
+            for t in range(n_tensor):
+                bits = 1 if offset == (all_s, all_t) else t % 2
+                ks, kt = (0, 0) if offset == (all_s, all_t) else offset
+                target = (s ^ ks ^ bits * all_s) * n_tensor + (t ^ kt ^ bits * all_t)
+                pairs.append((s * n_tensor + t, target))
+        return lax.ppermute(piece, ("spot", "tensor"), pairs)
+
+    ordered, weights = [], []
     for phase in range(2):
-        pieces = []
+        pieces = {}
         for kt in turns:
-            sorted_pieces = sort_slab(trainer_tiles, phase, layers, n_tensor, kt, place)
-            for ks, piece in enumerate(sorted_pieces):
-                pairs = [
-                    (s * n_tensor + t, (s ^ ks) * n_tensor + (t ^ kt))
-                    for s in range(n_spot)
-                    for t in range(n_tensor)
-                ]
-                if ks or kt:
-                    piece = lax.ppermute(piece, ("spot", "tensor"), pairs)
-                pieces.append(piece)
-        weights.append(pieces)
+            for ks, piece in enumerate(
+                sort_slab(trainer_tiles, phase, layers, n_tensor, kt, place)
+            ):
+                pieces[ks, kt] = piece
+        first, last = pieces[0, 0], pieces[all_s, all_t]
+        pieces[0, 0] = jnp.where(core == 0, first, last)
+        pieces[all_s, all_t] = jnp.where(core == 0, last, first)
+        ordered.append(pieces)
+    moving = [offset for offset in offsets if offset != (0, 0)]
+    early = len(moving) - 2 * min(n_spot, 4)
+    got = [{(0, 0): ordered[p][0, 0]} for p in range(2)]
+    for phase in range(2):
+        for n, offset in enumerate(moving):
+            if phase == 0 or n < early:
+                got[phase][offset] = exchange(offset, ordered[phase][offset])
+    late = moving[early:]
 
     ends = jnp.cumsum(tile_lengths)
     offset = np.array(offsets, np.int32)
-    sources = (offset[:, 0] ^ spot) * n_tensor + (offset[:, 1] ^ tpos) + zone * tiles
+    sender = (offset[:, 1] % 2) ^ core
+    fixed = (offset == [0, 0]).all(axis=1) | (offset == [all_s, all_t]).all(axis=1)
+    sender = jnp.where(fixed, 0, sender)
+    sources = (offset[:, 0] ^ spot ^ sender * all_s) * n_tensor
+    sources = sources + (offset[:, 1] ^ tpos ^ sender * all_t) + zone * tiles
     starts = (ends - tile_lengths)[sources]
     counts = tile_lengths[sources]
     tick_ids = jnp.arange(ticks, dtype=jnp.int32)
@@ -362,10 +383,28 @@
             else:
                 other = lax.dynamic_index_in_dim(fresh, 1 - core, 2, False).reshape(rows, half)
             use = sorted({l // n_spot for l in busy})
+            extra = []
+            if late:
+                offset = late.pop(0)
+                if tick == 0:
+                    held = [got[1][k] for k in moving[:early]]
+                    mine, _ = lax.optimization_barrier((mine, held))
+                piece, _ = lax.optimization_barrier((ordered[1][offset], other))
+                got[1][offset] = exchange(offset, piece)
+                extra.append(got[1][offset])
+            weights = [[got[p].get(k) for k in offsets] for p in range(2)]
             own = project(
                 tick, use, tiles, tilew, n_y, scalars, mine, other, gains, sum([weights[p] for p in use], [])
             )
             sent = lax.ppermute(own, ("zone", "spot"), mirror(tick))
+            if extra:
+                sent, _ = lax.optimization_barrier((sent, extra))
+            beside = []
+            if late:
+                offset = late.pop(0)
+                piece, _ = lax.optimization_barrier((ordered[1][offset], sent))
+                got[1][offset] = exchange(offset, piece)
+                beside.append(got[1][offset])
             item_at = 1 + ticks + stream * ticks + tick
             theirs, ours = attend(
                 item_at, steps, brow, n_y, scalars, own, sent, spans, cache_keys[0], cache_values[0], wo_rollout
@@ -388,6 +427,8 @@
                 near = lax.ppermute(after, ("zone", "spot"), hop(tick, 0))
                 far = lax.ppermute(after, ("zone", "spot"), hop(tick, 1))
                 arrived = jnp.where(at_home, near, far)
+                if beside:
+                    arrived, _ = lax.optimization_barrier((arrived, beside))
         for value in record:
             value = lax.dynamic_slice_in_dim(value, tpos // 2 * shard, shard, 1)
             records.append(value.reshape(steps, brow, shard))

time: 702 us -> 620 us (0.88)
  starting transfers between devices: 211 us -> 139 us
  waiting for transfers between devices: 306 us -> 278 us
  local copies, waits for them, and re-layouts: 19.9 us -> 31 us
    ppermute x30, starting transfers between devices: 151 us -> 74.1 us  [exchange(): return lax.ppermute(piece, ('spot', 'tensor'), pairs)]
    ppermute x30, waiting for transfers between devices: 143 us -> 84 us  [exchange(): return lax.ppermute(piece, ('spot', 'tensor'), pairs)]
    ppermute x9, waiting for transfers between devices: 43.8 us -> 60.4 us  [per_device(): lax.ppermute(part, 'tensor', [(t, t ^ bit) for t in range(n_tensor)])]
    unnamed x77 -> x115, local copies, waits for them, and re-layouts: 10.4 us -> 23 us
    ppermute x1, waiting for transfers between devices: 0.01 us -> 8.1 us  [per_device(): swapped = lax.ppermute(norm_gain, 'zone', flip)]
    ppermute x8, waiting for transfers between devices: 58.1 us -> 65.3 us  [per_device(): near = lax.ppermute(after, ('zone', 'spot'), hop(tick, 0))]
  transfers between devices with their start and end apart: 82 -> 82, of which waited for: 48 -> 50; matrix products, arithmetic and copies ran while one was open for 2% -> 2% of each run, Pallas kernels for 7% -> 9%
where the time goes in v6:
time: 620 us; the launch traced here: 611 us
  waiting for transfers between devices  278 us (45%)
  starting transfers between devices  139 us (22%)
  Pallas kernels  135 us (22%)
  local copies, waits for them, and re-layouts  31 us (5%)
  other arithmetic  21 us (3%)
  between operations  6.61 us (1%)
    ppermute x30, waiting for transfers between devices, exchange(): return lax.ppermute(piece, ('spot', 'tensor'), pairs)  84 us
    ppermute x30, starting transfers between devices, exchange(): return lax.ppermute(piece, ('spot', 'tensor'), pairs)  74.1 us
    ppermute x8, waiting for transfers between devices, per_device(): near = lax.ppermute(after, ('zone', 'spot'), hop(tick, 0))  65.3 us
    ppermute x9, waiting for transfers between devices, per_device(): lax.ppermute(part, 'tensor', [(t, t ^ bit) for t in range(n_tensor)])  60.4 us
    pallas_call x8, Pallas kernels, sort_slab(): pl.pallas_call(functools.partial(sort_kernel, phase * kept, layers), grid...  49.5 us
    pallas_call x9, Pallas kernels, project(): pl.pallas_call(functools.partial(project_kernel, tick, tiles, tilew, n_y,...  43.6 us
    pallas_call x9, Pallas kernels, attend(): pl.pallas_call(functools.partial(attend_kernel, steps, brow, kvlocal, gro...  42.2 us
    ppermute x9, waiting for transfers between devices, per_device(): sent = lax.ppermute(own, ('zone', 'spot'), mirror(tick))  27.2 us
  transfers between devices with their start and end apart: 82, of which 50 were waited for; matrix products, arithmetic and copies ran while one was open for 2% of the time, Pallas kernels for 9%

profile of v6, /device:TPU:0, one launch (start us, length us, event | category | flops | bytes accessed | tf_op | source)
XLA Modules:
  0.0 610.5 jit_solution(9804047853081366305)
XLA Ops:
  0.1 6.4 %shard_map.119 = (bf16[192,1536]{1,0:T(8,128)(2,1)}, bf16[192,1536]{1,0:T(8,128)(2,1)}, bf16[192,1536]{1,0:T(8,128)(2,1)}, bf16[192,1536]{1,0:T(8,128)(2,1)S(1)}) custom-call(s32[2]{0:T(128)S(1)} %pad_add_fusion.place, bf16[1536,6144]{1,0:T(8,128)(2,1)} %slab.15), custom_call_target="tpu_custom_call" | custom-call | flops 603979776 | bytes 7077888 | tf_op jit(solution)/shard_map/pallas_call | solution.py:38
  24.6 8.1 %collective-permute-done.7 = f32[1,4096]{1,0:T(1,128)S(1)} collective-permute-done((f32[1,4096]{1,0:T(1,128)S(1)}, f32[1,4096]{1,0:T(1,128)S(1)}, u32[]{:S(2)}, u32[]{:S(2)}) %collective-permute-start.7) | collective-permute-done | bytes 16416 | tf_op jit(solution)/shard_map/ppermute | solution.py:341
  36.8 8.0 %collective-permute-done.rest_17_.rest_1_ = bf16[192,1536]{1,0:T(8,128)(2,1)} collective-permute-done((bf16[192,1536]{1,0:T(8,128)(2,1)S(1)}, bf16[192,1536]{1,0:T(8,128)(2,1)}, u32[]{:S(2)}, u32[]{:S(2)}) %collective-permute-start) | collective-permute-done | bytes 589856 | tf_op jit(solution)/shard_map/ppermute | solution.py:303
  46.2 6.2 %shard_map.120 = (bf16[192,1536]{1,0:T(8,128)(2,1)S(1)}, bf16[192,1536]{1,0:T(8,128)(2,1)S(1)}, bf16[192,1536]{1,0:T(8,128)(2,1)S(1)}, bf16[192,1536]{1,0:T(8,128)(2,1)}) custom-call(s32[2]{0:T(128)S(1)} %pad_add_fusion.place, bf16[1536,6144]{1,0:T(8,128)(2,1)} %slab.15), custom_call_target="tpu_custom_call" | custom-call | flops 603979776 | bytes 7077888 | tf_op jit(solution)/shard_map/pallas_call | solution.py:38
  54.1 6.5 %shard_map.121 = (bf16[192,1536]{1,0:T(8,128)(2,1)}, bf16[192,1536]{1,0:T(8,128)(2,1)}, bf16[192,1536]{1,0:T(8,128)(2,1)}, bf16[192,1536]{1,0:T(8,128)(2,1)S(1)}) custom-call(s32[2]{0:T(128)S(1)} %pad_add_fusion.place, bf16[1536,6144]{1,0:T(8,128)(2,1)} %slab.15), custom_call_target="tpu_custom_call" | custom-call | flops 603979776 | bytes 7077888 | tf_op jit(solution)/shard_map/pallas_call | solution.py:38
  65.4 7.0 %collective-permute-done.3.rest_20_.rest_4_ = bf16[192,1536]{1,0:T(8,128)(2,1)} collective-permute-done((bf16[192,1536]{1,0:T(8,128)(2,1)}, bf16[192,1536]{1,0:T(8,128)(2,1)}, u32[]{:S(2)}, u32[]{:S(2)}) %collective-permute-start.3) | collective-permute-done | bytes 589856 | tf_op jit(solution)/shard_map/ppermute | solution.py:303
  82.5 6.6 %shard_map.122 = (bf16[192,1536]{1,0:T(8,128)(2,1)}, bf16[192,1536]{1,0:T(8,128)(2,1)}, bf16[192,1536]{1,0:T(8,128)(2,1)}, bf16[192,1536]{1,0:T(8,128)(2,1)}) custom-call(s32[2]{0:T(128)S(1)} %pad_add_fusion.place, bf16[1536,6144]{1,0:T(8,128)(2,1)} %slab.15), custom_call_target="tpu_custom_call" | custom-call | flops 603979776 | bytes 7077888 | tf_op jit(solution)/shard_map/pallas_call | solution.py:38
  98.1 11.3 %collective-permute-start.16 = (bf16[192,1536]{1,0:T(8,128)(2,1)}, bf16[192,1536]{1,0:T(8,128)(2,1)}, u32[]{:S(2)}, u32[]{:S(2)}) collective-permute-start(bf16[192,1536]{1,0:T(8,128)(2,1)} %get-tuple-element.90), channel_id=1, source_target_pairs={{0,5},{1,10},{2,7},{3,8},{4,1},{5,14},{6,3},{7,12},{8,13},{9,2},{1... | collective-permute-start | bytes 1769480 | tf_op jit(solution)/shard_map/ppermute | solution.py:303
  109.4 7.7 %collective-permute-start.17 = (bf16[192,1536]{1,0:T(8,128)(2,1)}, bf16[192,1536]{1,0:T(8,128)(2,1)}, u32[]{:S(2)}, u32[]{:S(2)}) collective-permute-start(bf16[192,1536]{1,0:T(8,128)(2,1)} %get-tuple-element.91), channel_id=1, source_target_pairs={{0,9},{1,6},{2,11},{3,4},{4,13},{5,2},{6,15},{7,0},{8,1},{9,14},{1... | collective-permute-start | bytes 1769480 | tf_op jit(solution)/shard_map/ppermute | solution.py:303
  120.2 6.2 %shard_map.125 = (bf16[192,1536]{1,0:T(8,128)(2,1)S(1)}, bf16[192,1536]{1,0:T(8,128)(2,1)S(1)}, bf16[192,1536]{1,0:T(8,128)(2,1)S(1)}, bf16[192,1536]{1,0:T(8,128)(2,1)}) custom-call(s32[2]{0:T(128)S(1)} %pad_add_fusion.place, bf16[1536,6144]{1,0:T(8,128)(2,1)} %slab.15), custom_call_target="tpu_custom_call" | custom-call | flops 603979776 | bytes 7077888 | tf_op jit(solution)/shard_map/pallas_call | solution.py:38
  131.4 9.7 %collective-permute-done.16.rest_9_ = bf16[192,1536]{1,0:T(8,128)(2,1)} collective-permute-done((bf16[192,1536]{1,0:T(8,128)(2,1)}, bf16[192,1536]{1,0:T(8,128)(2,1)}, u32[]{:S(2)}, u32[]{:S(2)}) %collective-permute-start.16) | collective-permute-done | bytes 589856 | tf_op jit(solution)/shard_map/ppermute | solution.py:303
  141.0 24.2 %collective-permute-done.18.rest_11_ = bf16[192,1536]{1,0:T(8,128)(2,1)} collective-permute-done((bf16[192,1536]{1,0:T(8,128)(2,1)}, bf16[192,1536]{1,0:T(8,128)(2,1)}, u32[]{:S(2)}, u32[]{:S(2)}) %collective-permute-start.18) | collective-permute-done | bytes 589856 | tf_op jit(solution)/shard_map/ppermute | solution.py:303
  168.2 20.6 %collective-permute-done.8.rest_1_ = bf16[192,1536]{1,0:T(8,128)(2,1)S(1)} collective-permute-done((bf16[192,1536]{1,0:T(8,128)(2,1)}, bf16[192,1536]{1,0:T(8,128)(2,1)S(1)}, u32[]{:S(2)}, u32[]{:S(2)}) %collective-permute-start.8) | collective-permute-done | bytes 589856 | tf_op jit(solution)/shard_map/ppermute | solution.py:303
  196.6 6.8 %collective-permute-start.23 = (bf16[48,1536]{1,0:T(8,128)(2,1)}, bf16[48,1536]{1,0:T(8,128)(2,1)}, u32[]{:S(2)}, u32[]{:S(2)}) collective-permute-start(bf16[48,1536]{1,0:T(8,128)(2,1)} %shard_map.124.own), channel_id=1, source_target_pairs={{0,16},{12,28},{16,0},{28,12},{1,17},{13,29},{17,1},{29,13},{2,18}... | collective-permute-start | bytes 442376 | tf_op jit(solution)/shard_map/ppermute | solution.py:399
  214.6 13.0 %collective-permute-done.26 = bf16[48,2048]{1,0:T(8,128)(2,1)S(1)} collective-permute-done((bf16[48,2048]{1,0:T(8,128)(2,1)S(1)}, bf16[48,2048]{1,0:T(8,128)(2,1)S(1)}, u32[]{:S(2)}, u32[]{:S(2)}) %collective-permute-start.26) | collective-permute-done | bytes 196640 | tf_op jit(solution)/shard_map/ppermute | solution.py:418
  235.0 6.5 %collective-permute-done.27 = bf16[48,2048]{1,0:T(8,128)(2,1)} collective-permute-done((bf16[48,2048]{1,0:T(8,128)(2,1)}, bf16[48,2048]{1,0:T(8,128)(2,1)}, u32[]{:S(2)}, u32[]{:S(2)}) %collective-permute-start.27) | collective-permute-done | bytes 196640 | tf_op jit(solution)/shard_map/ppermute | solution.py:427
  270.1 6.5 %collective-permute-done.34 = bf16[48,2048]{1,0:T(8,128)(2,1)S(1)} collective-permute-done((bf16[48,2048]{1,0:T(8,128)(2,1)S(1)}, bf16[48,2048]{1,0:T(8,128)(2,1)S(1)}, u32[]{:S(2)}, u32[]{:S(2)}) %collective-permute-start.34) | collective-permute-done | bytes 196640 | tf_op jit(solution)/shard_map/ppermute | solution.py:418
  283.0 11.4 %collective-permute-done.35 = bf16[48,2048]{1,0:T(8,128)(2,1)} collective-permute-done((bf16[48,2048]{1,0:T(8,128)(2,1)}, bf16[48,2048]{1,0:T(8,128)(2,1)}, u32[]{:S(2)}, u32[]{:S(2)}) %collective-permute-start.35) | collective-permute-done | bytes 196640 | tf_op jit(solution)/shard_map/ppermute | solution.py:427
  332.1 9.0 %collective-permute-start.45 = (bf16[192,1536]{1,0:T(8,128)(2,1)}, bf16[192,1536]{1,0:T(8,128)(2,1)}, u32[]{:S(2)}, u32[]{:S(2)}) collective-permute-start(bf16[192,1536]{1,0:T(8,128)(2,1)} %copy-done.36), channel_id=1, source_target_pairs={{0,7},{1,8},{2,5},{3,10},{4,3},{5,12},{6,1},{7,14},{8,15},{9,0},{1... | collective-permute-start | bytes 1769480 | tf_op jit(solution)/shard_map/ppermute | solution.py:303
  341.8 7.0 %collective-permute-done.45.rest_29_.rest_13_ = bf16[192,1536]{1,0:T(8,128)(2,1)} collective-permute-done((bf16[192,1536]{1,0:T(8,128)(2,1)}, bf16[192,1536]{1,0:T(8,128)(2,1)}, u32[]{:S(2)}, u32[]{:S(2)}) %collective-permute-start.45) | collective-permute-done | bytes 589856 | tf_op jit(solution)/shard_map/ppermute | solution.py:303
  351.3 6.8 %collective-permute-start.48 = (bf16[192,1536]{1,0:T(8,128)(2,1)S(1)}, bf16[192,1536]{1,0:T(8,128)(2,1)S(1)}, u32[]{:S(2)}, u32[]{:S(2)}) collective-permute-start(bf16[192,1536]{1,0:T(8,128)(2,1)S(1)} %copy-done.34), channel_id=1, source_target_pairs={{0,11},{1,4},{2,9},{3,6},{4,15},{5,0},{6,13},{7,2},{8,3},{9,12},{1... | collective-permute-start | bytes 1769480 | tf_op jit(solution)/shard_map/ppermute | solution.py:303
  383.3 9.0 %collective-permute-start.53 = (bf16[192,1536]{1,0:T(8,128)(2,1)}, bf16[192,1536]{1,0:T(8,128)(2,1)}, u32[]{:S(2)}, u32[]{:S(2)}) collective-permute-start(bf16[192,1536]{1,0:T(8,128)(2,1)} %copy-done.28), channel_id=1, source_target_pairs={{0,15},{1,0},{2,13},{3,2},{4,11},{5,4},{6,9},{7,6},{8,7},{9,8},{10... | collective-permute-start | bytes 1769480 | tf_op jit(solution)/shard_map/ppermute | solution.py:303
  442.9 8.0 %collective-permute-done.58 = bf16[48,2048]{1,0:T(8,128)(2,1)} collective-permute-done((bf16[48,2048]{1,0:T(8,128)(2,1)S(1)}, bf16[48,2048]{1,0:T(8,128)(2,1)}, u32[]{:S(2)}, u32[]{:S(2)}) %collective-permute-start.58) | collective-permute-done | bytes 196640 | tf_op jit(solution)/shard_map/ppermute | solution.py:427
  544.7 31.0 %collective-permute-done.76 = bf16[48,2048]{1,0:T(8,128)(2,1)} collective-permute-done((bf16[48,2048]{1,0:T(8,128)(2,1)S(1)}, bf16[48,2048]{1,0:T(8,128)(2,1)}, u32[]{:S(2)}, u32[]{:S(2)}) %collective-permute-start.76) | collective-permute-done | bytes 196640 | tf_op jit(solution)/shard_map/ppermute | solution.py:427
  (336 shorter events, 360.4 us)
Async XLA Ops:
  18.6 26.3 %collective-permute-start = (bf16[192,1536]{1,0:T(8,128)(2,1)S(1)}, bf16[192,1536]{1,0:T(8,128)(2,1)}, u32[]{:S(2)}, u32[]{:S(2)}) collective-permute-start(bf16[192,1536]{1,0:T(8,128)(2,1)S(1)} %get-tuple-element.72), channel_id=1, source_target_pairs={{0,4},{1,11},{2,6},{3,9},{4,0},{5,15},{6,2},{7,13},{8,12},{9,3},{1... | collective-permute-start | bytes 1769480 | tf_op jit(solution)/shard_map/ppermute | solution.py:303
  21.7 39.8 %collective-permute-start.1 = (bf16[192,1536]{1,0:T(8,128)(2,1)S(1)}, bf16[192,1536]{1,0:T(8,128)(2,1)}, u32[]{:S(2)}, u32[]{:S(2)}) collective-permute-start(bf16[192,1536]{1,0:T(8,128)(2,1)S(1)} %get-tuple-element.73), channel_id=1, source_target_pairs={{0,8},{1,7},{2,10},{3,5},{4,12},{5,3},{6,14},{7,1},{8,0},{9,15},{1... | collective-permute-start | bytes 1769480 | tf_op jit(solution)/shard_map/ppermute | solution.py:303
  22.1 42.0 %collective-permute-start.2 = (bf16[192,1536]{1,0:T(8,128)(2,1)}, bf16[192,1536]{1,0:T(8,128)(2,1)}, u32[]{:S(2)}, u32[]{:S(2)}) collective-permute-start(bf16[192,1536]{1,0:T(8,128)(2,1)} %get-tuple-element.74), channel_id=1, source_target_pairs={{0,12},{1,3},{2,14},{3,1},{4,8},{5,7},{6,10},{7,5},{8,4},{9,11},{1... | collective-permute-start | bytes 1769480 | tf_op jit(solution)/shard_map/ppermute | solution.py:303
  32.7 39.7 %collective-permute-start.3 = (bf16[192,1536]{1,0:T(8,128)(2,1)}, bf16[192,1536]{1,0:T(8,128)(2,1)}, u32[]{:S(2)}, u32[]{:S(2)}) collective-permute-start(bf16[192,1536]{1,0:T(8,128)(2,1)} %get-tuple-element.75), channel_id=1, source_target_pairs={{0,2},{1,13},{2,0},{3,15},{4,6},{5,9},{6,4},{7,11},{8,10},{9,5},{1... | collective-permute-start | bytes 1769480 | tf_op jit(solution)/shard_map/ppermute | solution.py:303
  33.8 40.2 %collective-permute-start.4 = (bf16[192,1536]{1,0:T(8,128)(2,1)}, bf16[192,1536]{1,0:T(8,128)(2,1)}, u32[]{:S(2)}, u32[]{:S(2)}) collective-permute-start(bf16[192,1536]{1,0:T(8,128)(2,1)} %get-tuple-element.76), channel_id=1, source_target_pairs={{0,6},{1,9},{2,4},{3,11},{4,2},{5,13},{6,0},{7,15},{8,14},{9,1},{1... | collective-permute-start | bytes 1769480 | tf_op jit(solution)/shard_map/ppermute | solution.py:303
  44.8 30.7 %collective-permute-start.5 = (bf16[192,1536]{1,0:T(8,128)(2,1)}, bf16[192,1536]{1,0:T(8,128)(2,1)}, u32[]{:S(2)}, u32[]{:S(2)}) collective-permute-start(bf16[192,1536]{1,0:T(8,128)(2,1)} %get-tuple-element.77), channel_id=1, source_target_pairs={{0,10},{1,5},{2,8},{3,7},{4,14},{5,1},{6,12},{7,3},{8,2},{9,13},{1... | collective-permute-start | bytes 1769480 | tf_op jit(solution)/shard_map/ppermute | solution.py:303
  61.5 36.2 %collective-permute-start.14 = (bf16[192,1536]{1,0:T(8,128)(2,1)}, bf16[192,1536]{1,0:T(8,128)(2,1)S(1)}, u32[]{:S(2)}, u32[]{:S(2)}) collective-permute-start(bf16[192,1536]{1,0:T(8,128)(2,1)} %get-tuple-element.155), channel_id=1, source_target_pairs={{0,14},{1,15},{2,12},{3,13},{4,10},{5,11},{6,8},{7,9},{8,6},{9,7},... | collective-permute-start | bytes 1769480 | tf_op jit(solution)/shard_map/ppermute | solution.py:303
  64.2 33.9 %collective-permute-start.10 = (bf16[192,1536]{1,0:T(8,128)(2,1)}, bf16[192,1536]{1,0:T(8,128)(2,1)}, u32[]{:S(2)}, u32[]{:S(2)}) collective-permute-start(bf16[192,1536]{1,0:T(8,128)(2,1)} %get-tuple-element.85), channel_id=1, source_target_pairs={{0,12},{1,3},{2,14},{3,1},{4,8},{5,7},{6,10},{7,5},{8,4},{9,11},{1... | collective-permute-start | bytes 1769480 | tf_op jit(solution)/shard_map/ppermute | solution.py:303
  72.4 37.0 %collective-permute-start.11 = (bf16[192,1536]{1,0:T(8,128)(2,1)}, bf16[192,1536]{1,0:T(8,128)(2,1)}, u32[]{:S(2)}, u32[]{:S(2)}) collective-permute-start(bf16[192,1536]{1,0:T(8,128)(2,1)} %get-tuple-element.86), channel_id=1, source_target_pairs={{0,2},{1,13},{2,0},{3,15},{4,6},{5,9},{6,4},{7,11},{8,10},{9,5},{1... | collective-permute-start | bytes 1769480 | tf_op jit(solution)/shard_map/ppermute | solution.py:303
  74.0 43.1 %collective-permute-start.12 = (bf16[192,1536]{1,0:T(8,128)(2,1)}, bf16[192,1536]{1,0:T(8,128)(2,1)}, u32[]{:S(2)}, u32[]{:S(2)}) collective-permute-start(bf16[192,1536]{1,0:T(8,128)(2,1)} %get-tuple-element.87), channel_id=1, source_target_pairs={{0,6},{1,9},{2,4},{3,11},{4,2},{5,13},{6,0},{7,15},{8,14},{9,1},{1... | collective-permute-start | bytes 1769480 | tf_op jit(solution)/shard_map/ppermute | solution.py:303
  75.5 43.0 %collective-permute-start.13 = (bf16[192,1536]{1,0:T(8,128)(2,1)}, bf16[192,1536]{1,0:T(8,128)(2,1)}, u32[]{:S(2)}, u32[]{:S(2)}) collective-permute-start(bf16[192,1536]{1,0:T(8,128)(2,1)} %get-tuple-element.88), channel_id=1, source_target_pairs={{0,10},{1,5},{2,8},{3,7},{4,14},{5,1},{6,12},{7,3},{8,2},{9,13},{1... | collective-permute-start | bytes 1769480 | tf_op jit(solution)/shard_map/ppermute | solution.py:303
  97.7 31.2 %collective-permute-start.15 = (bf16[192,1536]{1,0:T(8,128)(2,1)}, bf16[192,1536]{1,0:T(8,128)(2,1)}, u32[]{:S(2)}, u32[]{:S(2)}) collective-permute-start(bf16[192,1536]{1,0:T(8,128)(2,1)} %get-tuple-element.89), channel_id=1, source_target_pairs={{0,1},{1,14},{2,3},{3,12},{4,5},{5,10},{6,7},{7,8},{8,9},{9,6},{10... | collective-permute-start | bytes 1769480 | tf_op jit(solution)/shard_map/ppermute | solution.py:303
  98.1 42.9 %collective-permute-start.16 = (bf16[192,1536]{1,0:T(8,128)(2,1)}, bf16[192,1536]{1,0:T(8,128)(2,1)}, u32[]{:S(2)}, u32[]{:S(2)}) collective-permute-start(bf16[192,1536]{1,0:T(8,128)(2,1)} %get-tuple-element.90), channel_id=1, source_target_pairs={{0,5},{1,10},{2,7},{3,8},{4,1},{5,14},{6,3},{7,12},{8,13},{9,2},{1... | collective-permute-start | bytes 1769480 | tf_op jit(solution)/shard_map/ppermute | solution.py:303
  109.4 31.6 %collective-permute-start.17 = (bf16[192,1536]{1,0:T(8,128)(2,1)}, bf16[192,1536]{1,0:T(8,128)(2,1)}, u32[]{:S(2)}, u32[]{:S(2)}) collective-permute-start(bf16[192,1536]{1,0:T(8,128)(2,1)} %get-tuple-element.91), channel_id=1, source_target_pairs={{0,9},{1,6},{2,11},{3,4},{4,13},{5,2},{6,15},{7,0},{8,1},{9,14},{1... | collective-permute-start | bytes 1769480 | tf_op jit(solution)/shard_map/ppermute | solution.py:303
  117.1 48.2 %collective-permute-start.18 = (bf16[192,1536]{1,0:T(8,128)(2,1)}, bf16[192,1536]{1,0:T(8,128)(2,1)}, u32[]{:S(2)}, u32[]{:S(2)}) collective-permute-start(bf16[192,1536]{1,0:T(8,128)(2,1)} %get-tuple-element.92), channel_id=1, source_target_pairs={{0,13},{1,2},{2,15},{3,0},{4,9},{5,6},{6,11},{7,4},{8,5},{9,10},{1... | collective-permute-start | bytes 1769480 | tf_op jit(solution)/shard_map/ppermute | solution.py:303
  118.6 48.5 %collective-permute-start.19 = (bf16[192,1536]{1,0:T(8,128)(2,1)}, bf16[192,1536]{1,0:T(8,128)(2,1)}, u32[]{:S(2)}, u32[]{:S(2)}) collective-permute-start(bf16[192,1536]{1,0:T(8,128)(2,1)} %get-tuple-element.93), channel_id=1, source_target_pairs={{0,3},{1,12},{2,1},{3,14},{4,7},{5,8},{6,5},{7,10},{8,11},{9,4},{1... | collective-permute-start | bytes 1769480 | tf_op jit(solution)/shard_map/ppermute | solution.py:303
  129.0 38.1 %collective-permute-start.20 = (bf16[192,1536]{1,0:T(8,128)(2,1)}, bf16[192,1536]{1,0:T(8,128)(2,1)S(1)}, u32[]{:S(2)}, u32[]{:S(2)}) collective-permute-start(bf16[192,1536]{1,0:T(8,128)(2,1)} %copy-done.32), channel_id=1, source_target_pairs={{0,7},{1,8},{2,5},{3,10},{4,3},{5,12},{6,1},{7,14},{8,15},{9,0},{1... | collective-permute-start | bytes 1769480 | tf_op jit(solution)/shard_map/ppermute | solution.py:303
  141.0 27.1 %collective-permute-start.21 = (bf16[192,1536]{1,0:T(8,128)(2,1)}, bf16[192,1536]{1,0:T(8,128)(2,1)S(1)}, u32[]{:S(2)}, u32[]{:S(2)}) collective-permute-start(bf16[192,1536]{1,0:T(8,128)(2,1)} %copy-done.31), channel_id=1, source_target_pairs={{0,11},{1,4},{2,9},{3,6},{4,15},{5,0},{6,13},{7,2},{8,3},{9,12},{1... | collective-permute-start | bytes 1769480 | tf_op jit(solution)/shard_map/ppermute | solution.py:303
  141.0 27.2 %collective-permute-start.22 = (bf16[192,1536]{1,0:T(8,128)(2,1)}, bf16[192,1536]{1,0:T(8,128)(2,1)S(1)}, u32[]{:S(2)}, u32[]{:S(2)}) collective-permute-start(bf16[192,1536]{1,0:T(8,128)(2,1)} %copy-done.30), channel_id=1, source_target_pairs={{0,15},{1,0},{2,13},{3,2},{4,11},{5,4},{6,9},{7,6},{8,7},{9,8},{10... | collective-permute-start | bytes 1769480 | tf_op jit(solution)/shard_map/ppermute | solution.py:303
  165.3 23.5 %collective-permute-start.8 = (bf16[192,1536]{1,0:T(8,128)(2,1)}, bf16[192,1536]{1,0:T(8,128)(2,1)S(1)}, u32[]{:S(2)}, u32[]{:S(2)}) collective-permute-start(bf16[192,1536]{1,0:T(8,128)(2,1)} %copy-done.26), channel_id=1, source_target_pairs={{0,4},{1,11},{2,6},{3,9},{4,0},{5,15},{6,2},{7,13},{8,12},{9,3},{1... | collective-permute-start | bytes 1769480 | tf_op jit(solution)/shard_map/ppermute | solution.py:303
  167.1 36.6 %collective-permute-start.24 = (bf16[192,1536]{1,0:T(8,128)(2,1)}, bf16[192,1536]{1,0:T(8,128)(2,1)S(1)}, u32[]{:S(2)}, u32[]{:S(2)}) collective-permute-start(bf16[192,1536]{1,0:T(8,128)(2,1)} %copy-done.35), channel_id=1, source_target_pairs={{0,1},{1,14},{2,3},{3,12},{4,5},{5,10},{6,7},{7,8},{8,9},{9,6},{10... | collective-permute-start | bytes 1769480 | tf_op jit(solution)/shard_map/ppermute | solution.py:303
  214.6 30.7 %collective-permute-start.29 = (bf16[192,1536]{1,0:T(8,128)(2,1)}, bf16[192,1536]{1,0:T(8,128)(2,1)}, u32[]{:S(2)}, u32[]{:S(2)}) collective-permute-start(bf16[192,1536]{1,0:T(8,128)(2,1)} %copy-done.29), channel_id=1, source_target_pairs={{0,5},{1,10},{2,7},{3,8},{4,1},{5,14},{6,3},{7,12},{8,13},{9,2},{1... | collective-permute-start | bytes 1769480 | tf_op jit(solution)/shard_map/ppermute | solution.py:303
  541.5 34.3 %collective-permute-start.76 = (bf16[48,2048]{1,0:T(8,128)(2,1)S(1)}, bf16[48,2048]{1,0:T(8,128)(2,1)}, u32[]{:S(2)}, u32[]{:S(2)}) collective-permute-start(bf16[48,2048]{1,0:T(8,128)(2,1)S(1)} %get-tuple-element.139), channel_id=1, source_target_pairs={{8,12},{12,16},{24,28},{28,0},{9,13},{13,17},{25,29},{29,1},{10,14... | collective-permute-start | bytes 589832 | tf_op jit(solution)/shard_map/ppermute | solution.py:427
  542.7 35.8 %collective-permute-start.77 = (bf16[48,2048]{1,0:T(8,128)(2,1)S(1)}, bf16[48,2048]{1,0:T(8,128)(2,1)}, u32[]{:S(2)}, u32[]{:S(2)}) collective-permute-start(bf16[48,2048]{1,0:T(8,128)(2,1)S(1)} %get-tuple-element.139), channel_id=1, source_target_pairs={{8,28},{12,0},{24,12},{28,16},{9,29},{13,1},{25,13},{29,17},{10,30... | collective-permute-start | bytes 589832 | tf_op jit(solution)/shard_map/ppermute | solution.py:428
  (114 other events, 1760.8 us)

commit v7 on v6

--- a/solution.py
+++ b/solution.py
@@ -11,7 +11,7 @@
 HDIM = 128
 FB = 8
 STREAMS = 1
-ITEMS = 2
+ITEMS = 4
 ROWBLOCK = 256
 CHUNK = 384
 WINDOW = 512
@@ -129,7 +129,7 @@
         functools.partial(project_kernel, tick, tiles, tilew, n_y, use),
         in_specs=[pl.BlockSpec(memory_space=pltpu.SMEM)]
         + [vmem] * 3
-        + [pl.BlockSpec(memory_space=pl.ANY)] * len(weights),
+        + [pl.BlockSpec(memory_space=pltpu.HBM)] * len(weights),
         out_specs=vmem,
         scratch_shapes=[
             pltpu.VMEM((rows, 2 * half + WINDOW), jnp.float32),
@@ -144,7 +144,7 @@
     )(scalars, mine, other, gains, *weights)
 
 
-def attend_kernel(steps, brow, kvlocal, groups, n_y, item_at, scalars, own, sent, spans, ckeys, cvals, wo, theirs, ours, attn, kheld, vheld, held, sems):
+def attend_kernel(steps, brow, kvlocal, groups, n_y, item_at, scalars, own, sent, spans, ckeys, cvals, wo, theirs, attn, kheld, vheld, held, sems):
     rows = steps * brow
     length = ckeys.shape[1]
     scale = 1.0 / HDIM**0.5
@@ -155,15 +155,10 @@
     item = scalars[item_at]
     first = pl.multiple_of(item * brow, brow)
     gets = [
-        pltpu.make_async_copy(ckeys.at[pl.ds(first, brow)], kheld, sems.at[2 * n_y]),
-        pltpu.make_async_copy(cvals.at[pl.ds(first, brow)], vheld, sems.at[2 * n_y + 1]),
+        pltpu.make_async_copy(ckeys.at[pl.ds(first, brow)], kheld, sems.at[n_y]),
+        pltpu.make_async_copy(cvals.at[pl.ds(first, brow)], vheld, sems.at[n_y + 1]),
     ]
-    for k in range(2 * n_y):
-        side = 1 - core if k < n_y else core
-        at = pl.multiple_of((k % n_y * 2 + side) * shard, shard)
-        gets.append(
-            pltpu.make_async_copy(wo.at[0, :, pl.ds(at, shard)], held.at[k], sems.at[k])
-        )
+    gets = gets + wo_copies(1 - core, wo, held, sems)
     for get in gets:
         get.start()
     gets[0].wait()
@@ -216,12 +211,58 @@
                 g * rows : (g + 1) * rows
             ].astype(jnp.bfloat16)
 
-    for k in range(2 * n_y):
-        gets[2 + k].wait()
-        product = jnp.dot(attn[...], held[k], preferred_element_type=jnp.float32)
-        target = theirs if k < n_y else ours
-        at = k % n_y * shard
-        target[:, at : at + shard] = product.astype(jnp.bfloat16)
+    multiply(attn, gets[2:], held, theirs)
+
+
+def wo_copies(side, wo, held, sems):
+    n_y, _, shard = held.shape
+    copies = []
+    for y in range(n_y):
+        at = pl.multiple_of((2 * y + side) * shard, shard)
+        copies.append(
+            pltpu.make_async_copy(wo.at[0, :, pl.ds(at, shard)], held.at[y], sems.at[y])
+        )
+    return copies
+
+
+def multiply(attn, copies, held, out):
+    shard = held.shape[2]
+    for y, copy in enumerate(copies):
+        copy.wait()
+        product = jnp.dot(attn[...], held[y], preferred_element_type=jnp.float32)
+        out[:, y * shard : (y + 1) * shard] = product.astype(jnp.bfloat16)
+
+
+def finish_kernel(scalars, attn, wo, ours, held, sems):
+    copies = wo_copies(scalars[0], wo, held, sems)
+    for copy in copies:
+        copy.start()
+    multiply(attn, copies, held, ours)
+
+
+def finish(n_y, scalars, attn, wo):
+    rows, qdim = attn.shape
+    width = wo.shape[2]
+    shard = width // (2 * n_y)
+    vmem = pl.BlockSpec(memory_space=pltpu.VMEM)
+    return pl.pallas_call(
+        finish_kernel,
+        in_specs=[
+            pl.BlockSpec(memory_space=pltpu.SMEM),
+            vmem,
+            pl.BlockSpec(memory_space=pltpu.HBM),
+        ],
+        out_specs=vmem,
+        scratch_shapes=[
+            pltpu.VMEM((n_y, qdim, shard), jnp.bfloat16),
+            pltpu.SemaphoreType.DMA((n_y,)),
+        ],
+        out_shape=jax.ShapeDtypeStruct((rows, shard * n_y), jnp.bfloat16),
+        compiler_params=pltpu.CompilerParams(vmem_limit_bytes=VMEM),
+        cost_estimate=pl.CostEstimate(
+            flops=rows * qdim * width, bytes_accessed=qdim * width, transcendentals=0
+        ),
+    )(scalars, attn, wo)
 
 
 def attend(item_at, steps, brow, n_y, scalars, own, sent, spans, keys, values, wo):
@@ -236,19 +277,21 @@
         functools.partial(attend_kernel, steps, brow, kvlocal, groups, n_y, item_at),
         in_specs=[pl.BlockSpec(memory_space=pltpu.SMEM)]
         + [vmem] * 3
-        + [pl.BlockSpec(memory_space=pl.ANY)] * 3,
+        + [pl.BlockSpec(memory_space=pltpu.HBM)] * 3,
         out_specs=[vmem] * 2,
         scratch_shapes=[
-            pltpu.VMEM((rows, qdim), jnp.bfloat16),
             pltpu.VMEM((brow, length, kvdim), jnp.bfloat16),
             pltpu.VMEM((brow, length, kvdim), jnp.bfloat16),
-            pltpu.VMEM((2 * n_y, qdim, shard), jnp.bfloat16),
-            pltpu.SemaphoreType.DMA((2 * n_y + 2,)),
+            pltpu.VMEM((n_y, qdim, shard), jnp.bfloat16),
+            pltpu.SemaphoreType.DMA((n_y + 2,)),
         ],
-        out_shape=[jax.ShapeDtypeStruct((rows, shard * n_y), jnp.bfloat16)] * 2,
+        out_shape=[
+            jax.ShapeDtypeStruct((rows, shard * n_y), jnp.bfloat16),
+            jax.ShapeDtypeStruct((rows, qdim), jnp.bfloat16),
+        ],
         compiler_params=pltpu.CompilerParams(vmem_limit_bytes=VMEM),
         cost_estimate=pl.CostEstimate(
-            flops=2 * rows * qdim * width, bytes_accessed=2 * qdim * width, transcendentals=0
+            flops=rows * qdim * width, bytes_accessed=qdim * width, transcendentals=0
         ),
     )(scalars, own, sent, spans, keys, values, wo)
 
@@ -406,12 +449,12 @@
                 got[1][offset] = exchange(offset, piece)
                 beside.append(got[1][offset])
             item_at = 1 + ticks + stream * ticks + tick
-            theirs, ours = attend(
+            theirs, attn = attend(
                 item_at, steps, brow, n_y, scalars, own, sent, spans, cache_keys[0], cache_values[0], wo_rollout
             )
-            part = ours.astype(jnp.float32) + lax.ppermute(theirs, "tensor", across).astype(
-                jnp.float32
-            )
+            moved = lax.ppermute(theirs, "tensor", across)
+            ours = finish(n_y, scalars, attn, wo_rollout)
+            part = ours.astype(jnp.float32) + moved.astype(jnp.float32)
             bit = 2
             while bit < n_tensor:
                 part = part.astype(jnp.bfloat16)

time: 620 us -> 652 us (1.052)
  waiting for transfers between devices: 278 us -> 199 us
  local copies, waits for them, and re-layouts: 31 us -> 80.6 us
  Pallas kernels: 135 us -> 172 us
  starting transfers between devices: 139 us -> 156 us
    unnamed x115 -> x259, local copies, waits for them, and re-layouts: 23 us -> 73.5 us
    ppermute x8 -> x10, waiting for transfers between devices: 65.3 us -> 20.1 us  [per_device(): near = lax.ppermute(after, ('zone', 'spot'), hop(tick, 0))]
    pallas_call x0 -> x11, Pallas kernels: none -> 35.9 us  [finish(): pl.pallas_call(finish_kernel, in_specs=[pl.BlockSpec(memory_space=pltpu.S...]
    ppermute x9 -> x11, waiting for transfers between devices: 60.4 us -> 31.1 us  [per_device(): lax.ppermute(part, 'tensor', [(t, t ^ bit) for t in range(n_tensor)])]
    ppermute x30, waiting for transfers between devices: 84 us -> 57.5 us  [exchange(): return lax.ppermute(piece, ('spot', 'tensor'), pairs)]
    ppermute x8 -> x10, waiting for transfers between devices: 11.1 us -> 33.1 us  [per_device(): far = lax.ppermute(after, ('zone', 'spot'), hop(tick, 1))]
    ppermute x9 -> x11, waiting for transfers between devices: 27.2 us -> 47.2 us  [per_device(): sent = lax.ppermute(own, ('zone', 'spot'), mirror(tick))]
    ppermute x8 -> x10, starting transfers between devices: 13.3 us -> 28.8 us  [per_device(): near = lax.ppermute(after, ('zone', 'spot'), hop(tick, 0))]
  transfers between devices with their start and end apart: 82 -> 94, of which waited for: 50 -> 47; matrix products, arithmetic and copies ran while one was open for 2% -> 3% of each run, Pallas kernels for 9% -> 15%
where the time goes in v7:
time: 652 us; the launch traced here: 641 us
  waiting for transfers between devices  199 us (31%)
  Pallas kernels  172 us (26%)
  starting transfers between devices  156 us (24%)
  local copies, waits for them, and re-layouts  80.6 us (12%)
  other arithmetic  25.8 us (4%)
  between operations  8.54 us (1%)
    unnamed x259, local copies, waits for them, and re-layouts  73.5 us
    ppermute x30, starting transfers between devices, exchange(): return lax.ppermute(piece, ('spot', 'tensor'), pairs)  72 us
    ppermute x30, waiting for transfers between devices, exchange(): return lax.ppermute(piece, ('spot', 'tensor'), pairs)  57.5 us
    pallas_call x11, Pallas kernels, project(): pl.pallas_call(functools.partial(project_kernel, tick, tiles, tilew, n_y,...  50.7 us
    pallas_call x8, Pallas kernels, sort_slab(): pl.pallas_call(functools.partial(sort_kernel, phase * kept, layers), grid...  48.4 us
    ppermute x11, waiting for transfers between devices, per_device(): sent = lax.ppermute(own, ('zone', 'spot'), mirror(tick))  47.2 us
    pallas_call x11, Pallas kernels, attend(): pl.pallas_call(functools.partial(attend_kernel, steps, brow, kvlocal, gro...  36.9 us
    pallas_call x11, Pallas kernels, finish(): pl.pallas_call(finish_kernel, in_specs=[pl.BlockSpec(memory_space=pltpu.S...  35.9 us
  transfers between devices with their start and end apart: 94, of which 47 were waited for; matrix products, arithmetic and copies ran while one was open for 3% of the time, Pallas kernels for 15%

profile of v7, /device:TPU:0, one launch (start us, length us, event | category | flops | bytes accessed | tf_op | source)
XLA Modules:
  0.0 641.2 jit_solution(16494309891348816688)
XLA Ops:
  0.1 5.2 shard_map.123
  14.4 6.5 %shard_map.122 = (bf16[192,1536]{1,0:T(8,128)(2,1)S(1)}, bf16[192,1536]{1,0:T(8,128)(2,1)}, bf16[192,1536]{1,0:T(8,128)(2,1)}, bf16[192,1536]{1,0:T(8,128)(2,1)}) custom-call(s32[2]{0:T(128)S(1)} %pad_add_fusion.place, bf16[1536,6144]{1,0:T(8,128)(2,1)} %slab.15), custom_call_target="tpu_custom_call" | custom-call | flops 603979776 | bytes 7077888 | tf_op jit(solution)/shard_map/pallas_call | solution.py:38
  21.7 6.4 %shard_map.121 = (bf16[192,1536]{1,0:T(8,128)(2,1)}, bf16[192,1536]{1,0:T(8,128)(2,1)}, bf16[192,1536]{1,0:T(8,128)(2,1)}, bf16[192,1536]{1,0:T(8,128)(2,1)S(1)}) custom-call(s32[2]{0:T(128)S(1)} %pad_add_fusion.place, bf16[1536,6144]{1,0:T(8,128)(2,1)} %slab.15), custom_call_target="tpu_custom_call" | custom-call | flops 603979776 | bytes 7077888 | tf_op jit(solution)/shard_map/pallas_call | solution.py:38
  39.4 6.2 shard_map.119
  52.3 10.6 %collective-permute-done.16.rest_9_ = bf16[192,1536]{1,0:T(8,128)(2,1)S(1)} collective-permute-done((bf16[192,1536]{1,0:T(8,128)(2,1)}, bf16[192,1536]{1,0:T(8,128)(2,1)S(1)}, u32[]{:S(2)}, u32[]{:S(2)}) %collective-permute-start.16) | collective-permute-done | bytes 589856 | tf_op jit(solution)/shard_map/ppermute | solution.py:346
  66.3 16.2 %collective-permute-start.4 = (bf16[192,1536]{1,0:T(8,128)(2,1)}, bf16[192,1536]{1,0:T(8,128)(2,1)S(1)}, u32[]{:S(2)}, u32[]{:S(2)}) collective-permute-start(bf16[192,1536]{1,0:T(8,128)(2,1)} %copy-done.90), channel_id=1, source_target_pairs={{0,6},{1,9},{2,4},{3,11},{4,2},{5,13},{6,0},{7,15},{8,14},{9,1},{1... | collective-permute-start | bytes 1769480 | tf_op jit(solution)/shard_map/ppermute | solution.py:346
  82.5 6.5 %shard_map.118 = (bf16[192,1536]{1,0:T(8,128)(2,1)S(1)}, bf16[192,1536]{1,0:T(8,128)(2,1)}, bf16[192,1536]{1,0:T(8,128)(2,1)}, bf16[192,1536]{1,0:T(8,128)(2,1)}) custom-call(s32[2]{0:T(128)S(1)} %pad_add_fusion.place, bf16[1536,6144]{1,0:T(8,128)(2,1)} %slab.15), custom_call_target="tpu_custom_call" | custom-call | flops 603979776 | bytes 7077888 | tf_op jit(solution)/shard_map/pallas_call | solution.py:38
  96.2 25.7 %collective-permute-done.4.rest_21_.rest_5_ = bf16[192,1536]{1,0:T(8,128)(2,1)S(1)} collective-permute-done((bf16[192,1536]{1,0:T(8,128)(2,1)}, bf16[192,1536]{1,0:T(8,128)(2,1)S(1)}, u32[]{:S(2)}, u32[]{:S(2)}) %collective-permute-start.4) | collective-permute-done | bytes 589856 | tf_op jit(solution)/shard_map/ppermute | solution.py:346
  123.9 6.2 shard_map.125
  134.9 5.2 shard_map.120
  147.5 13.6 %collective-permute-start.24 = (bf16[192,1536]{1,0:T(8,128)(2,1)}, bf16[192,1536]{1,0:T(8,128)(2,1)S(1)}, u32[]{:S(2)}, u32[]{:S(2)}) collective-permute-start(bf16[192,1536]{1,0:T(8,128)(2,1)} %get-tuple-element.102), channel_id=1, source_target_pairs={{0,1},{1,14},{2,3},{3,12},{4,5},{5,10},{6,7},{7,8},{8,9},{9,6},{10... | collective-permute-start | bytes 1769480 | tf_op jit(solution)/shard_map/ppermute | solution.py:346
  162.0 17.8 %collective-permute-done.8.rest_1_ = bf16[192,1536]{1,0:T(8,128)(2,1)S(1)} collective-permute-done((bf16[192,1536]{1,0:T(8,128)(2,1)S(1)}, bf16[192,1536]{1,0:T(8,128)(2,1)S(1)}, u32[]{:S(2)}, u32[]{:S(2)}) %collective-permute-start.8) | collective-permute-done | bytes 589856 | tf_op jit(solution)/shard_map/ppermute | solution.py:346
  213.4 5.1 collective-permute-start.28
  221.6 5.4 collective-permute-done.27
  243.7 5.4 collective-permute-done.31.sent
  266.9 5.7 collective-permute-done.36
  276.8 6.2 shard_map.132
  298.4 5.6 collective-permute-done.39.sent
  366.7 5.9 collective-permute-done.52
  384.2 5.1 shard_map.138.own
  389.3 5.6 collective-permute-done.55.sent
  425.3 5.1 shard_map.141.own
  467.3 5.1 shard_map.144.own
  511.7 5.0 collective-permute-done.73.sent
  (535 shorter events, 441.4 us)
Async XLA Ops:
  5.3 28.4 %collective-permute-start.19 = (bf16[192,1536]{1,0:T(8,128)(2,1)S(1)}, bf16[192,1536]{1,0:T(8,128)(2,1)S(1)}, u32[]{:S(2)}, u32[]{:S(2)}) collective-permute-start(bf16[192,1536]{1,0:T(8,128)(2,1)S(1)} %get-tuple-element.97), channel_id=1, source_target_pairs={{0,3},{1,12},{2,1},{3,14},{4,7},{5,8},{6,5},{7,10},{8,11},{9,4},{1... | collective-permute-start | bytes 1769480 | tf_op jit(solution)/shard_map/ppermute | solution.py:346
  7.7 26.0 %collective-permute-start.20 = (bf16[192,1536]{1,0:T(8,128)(2,1)S(1)}, bf16[192,1536]{1,0:T(8,128)(2,1)S(1)}, u32[]{:S(2)}, u32[]{:S(2)}) collective-permute-start(bf16[192,1536]{1,0:T(8,128)(2,1)S(1)} %get-tuple-element.98), channel_id=1, source_target_pairs={{0,7},{1,8},{2,5},{3,10},{4,3},{5,12},{6,1},{7,14},{8,15},{9,0},{1... | collective-permute-start | bytes 1769480 | tf_op jit(solution)/shard_map/ppermute | solution.py:346
  10.5 27.0 %collective-permute-start.21 = (bf16[192,1536]{1,0:T(8,128)(2,1)S(1)}, bf16[192,1536]{1,0:T(8,128)(2,1)S(1)}, u32[]{:S(2)}, u32[]{:S(2)}) collective-permute-start(bf16[192,1536]{1,0:T(8,128)(2,1)S(1)} %get-tuple-element.99), channel_id=1, source_target_pairs={{0,11},{1,4},{2,9},{3,6},{4,15},{5,0},{6,13},{7,2},{8,3},{9,12},{1... | collective-permute-start | bytes 1769480 | tf_op jit(solution)/shard_map/ppermute | solution.py:346
  13.1 35.3 %collective-permute-start.22 = (bf16[192,1536]{1,0:T(8,128)(2,1)S(1)}, bf16[192,1536]{1,0:T(8,128)(2,1)}, u32[]{:S(2)}, u32[]{:S(2)}) collective-permute-start(bf16[192,1536]{1,0:T(8,128)(2,1)S(1)} %get-tuple-element.100), channel_id=1, source_target_pairs={{0,15},{1,0},{2,13},{3,2},{4,11},{5,4},{6,9},{7,6},{8,7},{9,8},{10... | collective-permute-start | bytes 1769480 | tf_op jit(solution)/shard_map/ppermute | solution.py:346
  29.0 19.4 %collective-permute-start.15 = (bf16[192,1536]{1,0:T(8,128)(2,1)S(1)}, bf16[192,1536]{1,0:T(8,128)(2,1)S(1)}, u32[]{:S(2)}, u32[]{:S(2)}) collective-permute-start(bf16[192,1536]{1,0:T(8,128)(2,1)S(1)} %get-tuple-element.93), channel_id=1, source_target_pairs={{0,1},{1,14},{2,3},{3,12},{4,5},{5,10},{6,7},{7,8},{8,9},{9,6},{10... | collective-permute-start | bytes 1769480 | tf_op jit(solution)/shard_map/ppermute | solution.py:346
  33.7 29.2 %collective-permute-start.16 = (bf16[192,1536]{1,0:T(8,128)(2,1)}, bf16[192,1536]{1,0:T(8,128)(2,1)S(1)}, u32[]{:S(2)}, u32[]{:S(2)}) collective-permute-start(bf16[192,1536]{1,0:T(8,128)(2,1)} %get-tuple-element.94), channel_id=1, source_target_pairs={{0,5},{1,10},{2,7},{3,8},{4,1},{5,14},{6,3},{7,12},{8,13},{9,2},{1... | collective-permute-start | bytes 1769480 | tf_op jit(solution)/shard_map/ppermute | solution.py:346
  33.7 29.2 %collective-permute-start.17 = (bf16[192,1536]{1,0:T(8,128)(2,1)}, bf16[192,1536]{1,0:T(8,128)(2,1)}, u32[]{:S(2)}, u32[]{:S(2)}) collective-permute-start(bf16[192,1536]{1,0:T(8,128)(2,1)} %get-tuple-element.95), channel_id=1, source_target_pairs={{0,9},{1,6},{2,11},{3,4},{4,13},{5,2},{6,15},{7,0},{8,1},{9,14},{1... | collective-permute-start | bytes 1769480 | tf_op jit(solution)/shard_map/ppermute | solution.py:346
  37.5 28.7 %collective-permute-start.18 = (bf16[192,1536]{1,0:T(8,128)(2,1)}, bf16[192,1536]{1,0:T(8,128)(2,1)}, u32[]{:S(2)}, u32[]{:S(2)}) collective-permute-start(bf16[192,1536]{1,0:T(8,128)(2,1)} %get-tuple-element.96), channel_id=1, source_target_pairs={{0,13},{1,2},{2,15},{3,0},{4,9},{5,6},{6,11},{7,4},{8,5},{9,10},{1... | collective-permute-start | bytes 1769480 | tf_op jit(solution)/shard_map/ppermute | solution.py:346
  48.4 41.7 %collective-permute-start.11 = (bf16[192,1536]{1,0:T(8,128)(2,1)}, bf16[192,1536]{1,0:T(8,128)(2,1)S(1)}, u32[]{:S(2)}, u32[]{:S(2)}) collective-permute-start(bf16[192,1536]{1,0:T(8,128)(2,1)} %get-tuple-element.90), channel_id=1, source_target_pairs={{0,2},{1,13},{2,0},{3,15},{4,6},{5,9},{6,4},{7,11},{8,10},{9,5},{1... | collective-permute-start | bytes 1769480 | tf_op jit(solution)/shard_map/ppermute | solution.py:346
  49.2 41.7 %collective-permute-start.12 = (bf16[192,1536]{1,0:T(8,128)(2,1)}, bf16[192,1536]{1,0:T(8,128)(2,1)S(1)}, u32[]{:S(2)}, u32[]{:S(2)}) collective-permute-start(bf16[192,1536]{1,0:T(8,128)(2,1)} %get-tuple-element.91), channel_id=1, source_target_pairs={{0,6},{1,9},{2,4},{3,11},{4,2},{5,13},{6,0},{7,15},{8,14},{9,1},{1... | collective-permute-start | bytes 1769480 | tf_op jit(solution)/shard_map/ppermute | solution.py:346
  63.0 30.6 %collective-permute-start.13 = (bf16[192,1536]{1,0:T(8,128)(2,1)}, bf16[192,1536]{1,0:T(8,128)(2,1)}, u32[]{:S(2)}, u32[]{:S(2)}) collective-permute-start(bf16[192,1536]{1,0:T(8,128)(2,1)} %get-tuple-element.92), channel_id=1, source_target_pairs={{0,10},{1,5},{2,8},{3,7},{4,14},{5,1},{6,12},{7,3},{8,2},{9,13},{1... | collective-permute-start | bytes 1769480 | tf_op jit(solution)/shard_map/ppermute | solution.py:346
  63.0 33.2 %collective-permute-start.3 = (bf16[192,1536]{1,0:T(8,128)(2,1)}, bf16[192,1536]{1,0:T(8,128)(2,1)S(1)}, u32[]{:S(2)}, u32[]{:S(2)}) collective-permute-start(bf16[192,1536]{1,0:T(8,128)(2,1)} %copy-done.91), channel_id=1, source_target_pairs={{0,2},{1,13},{2,0},{3,15},{4,6},{5,9},{6,4},{7,11},{8,10},{9,5},{1... | collective-permute-start | bytes 1769480 | tf_op jit(solution)/shard_map/ppermute | solution.py:346
  66.3 55.7 %collective-permute-start.4 = (bf16[192,1536]{1,0:T(8,128)(2,1)}, bf16[192,1536]{1,0:T(8,128)(2,1)S(1)}, u32[]{:S(2)}, u32[]{:S(2)}) collective-permute-start(bf16[192,1536]{1,0:T(8,128)(2,1)} %copy-done.90), channel_id=1, source_target_pairs={{0,6},{1,9},{2,4},{3,11},{4,2},{5,13},{6,0},{7,15},{8,14},{9,1},{1... | collective-permute-start | bytes 1769480 | tf_op jit(solution)/shard_map/ppermute | solution.py:346
  91.0 49.3 %collective-permute-start.5 = (bf16[192,1536]{1,0:T(8,128)(2,1)}, bf16[192,1536]{1,0:T(8,128)(2,1)}, u32[]{:S(2)}, u32[]{:S(2)}) collective-permute-start(bf16[192,1536]{1,0:T(8,128)(2,1)} %get-tuple-element.81), channel_id=1, source_target_pairs={{0,10},{1,5},{2,8},{3,7},{4,14},{5,1},{6,12},{7,3},{8,2},{9,13},{1... | collective-permute-start | bytes 1769480 | tf_op jit(solution)/shard_map/ppermute | solution.py:346
  91.8 51.1 %collective-permute-start.6 = (bf16[192,1536]{1,0:T(8,128)(2,1)}, bf16[192,1536]{1,0:T(8,128)(2,1)}, u32[]{:S(2)}, u32[]{:S(2)}) collective-permute-start(bf16[192,1536]{1,0:T(8,128)(2,1)} %get-tuple-element.161), channel_id=1, source_target_pairs={{0,14},{1,15},{2,12},{3,13},{4,10},{5,11},{6,8},{7,9},{8,6},{9,7},... | collective-permute-start | bytes 1769480 | tf_op jit(solution)/shard_map/ppermute | solution.py:346
  93.6 49.6 %collective-permute-start = (bf16[192,1536]{1,0:T(8,128)(2,1)}, bf16[192,1536]{1,0:T(8,128)(2,1)}, u32[]{:S(2)}, u32[]{:S(2)}) collective-permute-start(bf16[192,1536]{1,0:T(8,128)(2,1)} %get-tuple-element.76), channel_id=1, source_target_pairs={{0,4},{1,11},{2,6},{3,9},{4,0},{5,15},{6,2},{7,13},{8,12},{9,3},{1... | collective-permute-start | bytes 1769480 | tf_op jit(solution)/shard_map/ppermute | solution.py:346
  96.2 49.4 %collective-permute-start.1 = (bf16[192,1536]{1,0:T(8,128)(2,1)}, bf16[192,1536]{1,0:T(8,128)(2,1)}, u32[]{:S(2)}, u32[]{:S(2)}) collective-permute-start(bf16[192,1536]{1,0:T(8,128)(2,1)} %get-tuple-element.77), channel_id=1, source_target_pairs={{0,8},{1,7},{2,10},{3,5},{4,12},{5,3},{6,14},{7,1},{8,0},{9,15},{1... | collective-permute-start | bytes 1769480 | tf_op jit(solution)/shard_map/ppermute | solution.py:346
  121.9 25.6 %collective-permute-start.2 = (bf16[192,1536]{1,0:T(8,128)(2,1)}, bf16[192,1536]{1,0:T(8,128)(2,1)}, u32[]{:S(2)}, u32[]{:S(2)}) collective-permute-start(bf16[192,1536]{1,0:T(8,128)(2,1)} %get-tuple-element.78), channel_id=1, source_target_pairs={{0,12},{1,3},{2,14},{3,1},{4,8},{5,7},{6,10},{7,5},{8,4},{9,11},{1... | collective-permute-start | bytes 1769480 | tf_op jit(solution)/shard_map/ppermute | solution.py:346
  140.3 21.7 %collective-permute-start.14 = (bf16[192,1536]{1,0:T(8,128)(2,1)S(1)}, bf16[192,1536]{1,0:T(8,128)(2,1)S(1)}, u32[]{:S(2)}, u32[]{:S(2)}) collective-permute-start(bf16[192,1536]{1,0:T(8,128)(2,1)S(1)} %get-tuple-element.162), channel_id=1, source_target_pairs={{0,14},{1,15},{2,12},{3,13},{4,10},{5,11},{6,8},{7,9},{8,6},{9,7},... | collective-permute-start | bytes 1769480 | tf_op jit(solution)/shard_map/ppermute | solution.py:346
  142.8 36.9 %collective-permute-start.8 = (bf16[192,1536]{1,0:T(8,128)(2,1)S(1)}, bf16[192,1536]{1,0:T(8,128)(2,1)S(1)}, u32[]{:S(2)}, u32[]{:S(2)}) collective-permute-start(bf16[192,1536]{1,0:T(8,128)(2,1)S(1)} %get-tuple-element.87), channel_id=1, source_target_pairs={{0,4},{1,11},{2,6},{3,9},{4,0},{5,15},{6,2},{7,13},{8,12},{9,3},{1... | collective-permute-start | bytes 1769480 | tf_op jit(solution)/shard_map/ppermute | solution.py:346
  143.2 36.6 %collective-permute-start.9 = (bf16[192,1536]{1,0:T(8,128)(2,1)S(1)}, bf16[192,1536]{1,0:T(8,128)(2,1)S(1)}, u32[]{:S(2)}, u32[]{:S(2)}) collective-permute-start(bf16[192,1536]{1,0:T(8,128)(2,1)S(1)} %get-tuple-element.88), channel_id=1, source_target_pairs={{0,8},{1,7},{2,10},{3,5},{4,12},{5,3},{6,14},{7,1},{8,0},{9,15},{1... | collective-permute-start | bytes 1769480 | tf_op jit(solution)/shard_map/ppermute | solution.py:346
  145.6 34.2 %collective-permute-start.10 = (bf16[192,1536]{1,0:T(8,128)(2,1)S(1)}, bf16[192,1536]{1,0:T(8,128)(2,1)S(1)}, u32[]{:S(2)}, u32[]{:S(2)}) collective-permute-start(bf16[192,1536]{1,0:T(8,128)(2,1)S(1)} %get-tuple-element.89), channel_id=1, source_target_pairs={{0,12},{1,3},{2,14},{3,1},{4,8},{5,7},{6,10},{7,5},{8,4},{9,11},{1... | collective-permute-start | bytes 1769480 | tf_op jit(solution)/shard_map/ppermute | solution.py:346
  147.5 41.8 %collective-permute-start.24 = (bf16[192,1536]{1,0:T(8,128)(2,1)}, bf16[192,1536]{1,0:T(8,128)(2,1)S(1)}, u32[]{:S(2)}, u32[]{:S(2)}) collective-permute-start(bf16[192,1536]{1,0:T(8,128)(2,1)} %get-tuple-element.102), channel_id=1, source_target_pairs={{0,1},{1,14},{2,3},{3,12},{4,5},{5,10},{6,7},{7,8},{8,9},{9,6},{10... | collective-permute-start | bytes 1769480 | tf_op jit(solution)/shard_map/ppermute | solution.py:346
  284.7 19.3 %collective-permute-start.40 = (bf16[192,1536]{1,0:T(8,128)(2,1)S(1)}, bf16[192,1536]{1,0:T(8,128)(2,1)S(1)}, u32[]{:S(2)}, u32[]{:S(2)}) collective-permute-start(bf16[192,1536]{1,0:T(8,128)(2,1)S(1)} %get-tuple-element.118), channel_id=1, source_target_pairs={{0,3},{1,12},{2,1},{3,14},{4,7},{5,8},{6,5},{7,10},{8,11},{9,4},{1... | collective-permute-start | bytes 1769480 | tf_op jit(solution)/shard_map/ppermute | solution.py:346
  (197 other events, 2016.0 us)

commit v8 on v5

--- a/solution.py
+++ b/solution.py
@@ -18,40 +18,42 @@
 VMEM = 48 * 1024 * 1024
 
 
-def sort_kernel(first, layers, place, slab, *outs):
+def sort_kernel(layers, place, slab, *outs):
     feats = ROWBLOCK // layers
-    shape = (len(outs) * feats, ROWBLOCK)
-    row = lax.broadcasted_iota(jnp.int32, shape, 0)
-    col = lax.broadcasted_iota(jnp.int32, shape, 1)
-    source = row % feats * layers + first + ((row // feats) ^ place[0])
-    order = jnp.where(col == source, 1.0, 0.0).astype(jnp.bfloat16)
+    kept = len(outs)
+    row = lax.broadcasted_iota(jnp.int32, (ROWBLOCK, ROWBLOCK), 0)
+    col = lax.broadcasted_iota(jnp.int32, (ROWBLOCK, ROWBLOCK), 1)
+    layer = row // feats % 2 * kept + ((row // (2 * feats)) ^ place[0])
+    order = jnp.where(col == row % feats * layers + layer, 1.0, 0.0).astype(jnp.bfloat16)
     moved = jnp.dot(order, slab[...], preferred_element_type=jnp.float32).astype(jnp.bfloat16)
     for n, out in enumerate(outs):
-        out[...] = moved[n * feats : (n + 1) * feats]
-
-
-def sort_slab(slab, phase, layers, n_tensor, turn, place):
+        for phase in range(2):
+            at = (2 * n + phase) * feats
+            out[phase] = moved[at : at + feats]
+
+
+def sort_slab(slab, layers, n_tensor, turn, place):
     rows, columns = slab.shape
     kept = layers // 2
     cdev = columns // n_tensor
     feats = ROWBLOCK // layers
     return pl.pallas_call(
-        functools.partial(sort_kernel, phase * kept, layers),
+        functools.partial(sort_kernel, layers),
         grid_spec=pltpu.PrefetchScalarGridSpec(
             num_scalar_prefetch=1,
             grid=(rows // ROWBLOCK,),
             in_specs=[pl.BlockSpec((ROWBLOCK, cdev), lambda i, s: (i, s[1] ^ turn))],
-            out_specs=[pl.BlockSpec((feats, cdev), lambda i, s: (i, 0))] * kept,
+            out_specs=[pl.BlockSpec((2, feats, cdev), lambda i, s: (0, i, 0))] * kept,
         ),
-        out_shape=[jax.ShapeDtypeStruct((rows // layers, cdev), jnp.bfloat16)] * kept,
+        out_shape=[jax.ShapeDtypeStruct((2, rows // layers, cdev), jnp.bfloat16)] * kept,
         compiler_params=pltpu.CompilerParams(vmem_limit_bytes=VMEM),
         cost_estimate=pl.CostEstimate(
-            flops=rows * cdev * ROWBLOCK, bytes_accessed=3 * rows * cdev, transcendentals=0
+            flops=2 * rows * cdev * ROWBLOCK, bytes_accessed=4 * rows * cdev, transcendentals=0
         ),
     )(place, slab)
 
 
-def project_kernel(tick, tiles, tilew, n_y, use, scalars, mine, other, gains, *rest):
+def project_kernel(tick, tiles, tilew, n_y, scalars, mine, other, gains, *rest):
     weights, (out, normed, held, sems) = rest[:-4], rest[-4:]
     rows, half = mine.shape
     width = 2 * half
@@ -60,20 +62,12 @@
     per = size // tilew
     core, phase = scalars[0], scalars[1 + tick]
 
-    def fetch(p, n):
+    def fetch(n):
         target = held.at[n // per, pl.ds(n % per * tilew, tilew)]
-        return pltpu.make_async_copy(weights[p * tiles + n], target, sems.at[n])
-
-    if len(use) == 1:
-        for n in range(tiles):
-            fetch(0, n).start()
-    else:
-        for p in range(2):
-
-            @pl.when(phase == p)
-            def _():
-                for n in range(tiles):
-                    fetch(p, n).start()
+        return pltpu.make_async_copy(weights[n].at[phase], target, sems.at[n])
+
+    for n in range(tiles):
+        fetch(n).start()
 
     here = mine[...].astype(jnp.float32)
     there = other[...].astype(jnp.float32)
@@ -112,24 +106,24 @@
     for j in range(chunks):
         parts = [spread(j * (size // CHUNK) + i) for i in range(size // CHUNK)]
         for n in range(j * per, (j + 1) * per):
-            fetch(0, n).wait()
+            fetch(n).wait()
         acc = acc + jnp.dot(
             jnp.concatenate(parts, axis=1), held[j], preferred_element_type=jnp.float32
         )
     out[...] = acc.astype(jnp.bfloat16)
 
 
-def project(tick, use, tiles, tilew, n_y, scalars, mine, other, gains, weights):
+def project(tick, tiles, tilew, n_y, scalars, mine, other, gains, weights):
     rows, half = mine.shape
-    cdev = weights[0].shape[1]
+    cdev = weights[0].shape[2]
     depth = tiles * tilew
     size = 2 * CHUNK
     vmem = pl.BlockSpec(memory_space=pltpu.VMEM)
     return pl.pallas_call(
-        functools.partial(project_kernel, tick, tiles, tilew, n_y, use),
+        functools.partial(project_kernel, tick, tiles, tilew, n_y),
         in_specs=[pl.BlockSpec(memory_space=pltpu.SMEM)]
         + [vmem] * 3
-        + [pl.BlockSpec(memory_space=pl.ANY)] * len(weights),
+        + [pl.BlockSpec(memory_space=pltpu.HBM)] * len(weights),
         out_specs=vmem,
         scratch_shapes=[
             pltpu.VMEM((rows, 2 * half + WINDOW), jnp.float32),
@@ -236,7 +230,7 @@
         functools.partial(attend_kernel, steps, brow, kvlocal, groups, n_y, item_at),
         in_specs=[pl.BlockSpec(memory_space=pltpu.SMEM)]
         + [vmem] * 3
-        + [pl.BlockSpec(memory_space=pl.ANY)] * 3,
+        + [pl.BlockSpec(memory_space=pltpu.HBM)] * 3,
         out_specs=[vmem] * 2,
         scratch_shapes=[
             pltpu.VMEM((rows, qdim), jnp.bfloat16),
@@ -287,28 +281,41 @@
     core = tpos % 2
     layer = zone * n_spot + spot
 
-    turns = sorted(range(n_tensor), key=lambda kt: (kt < 2, kt))
+    all_s, all_t = n_spot - 1, n_tensor - 2
+    turns = sorted(range(n_tensor), key=lambda kt: (kt % 2, kt))
     offsets = [(ks, kt) for kt in turns for ks in range(n_spot)]
-    place = jnp.stack([spot, tpos]).astype(jnp.int32)
-    weights = []
-    for phase in range(2):
-        pieces = []
-        for kt in turns:
-            sorted_pieces = sort_slab(trainer_tiles, phase, layers, n_tensor, kt, place)
-            for ks, piece in enumerate(sorted_pieces):
-                pairs = [
-                    (s * n_tensor + t, (s ^ ks) * n_tensor + (t ^ kt))
-                    for s in range(n_spot)
-                    for t in range(n_tensor)
-                ]
-                if ks or kt:
-                    piece = lax.ppermute(piece, ("spot", "tensor"), pairs)
-                pieces.append(piece)
-        weights.append(pieces)
+    place = jnp.stack([spot ^ core * all_s, tpos ^ core * all_t]).astype(jnp.int32)
+
+    def exchange(offset, piece):
+        pairs = []
+        for s in range(n_spot):
+            for t in range(n_tensor):
+                bits = 1 if offset == (all_s, all_t) else t % 2
+                ks, kt = (0, 0) if offset == (all_s, all_t) else offset
+                target = (s ^ ks ^ bits * all_s) * n_tensor + (t ^ kt ^ bits * all_t)
+                pairs.append((s * n_tensor + t, target))
+        return lax.ppermute(piece, ("spot", "tensor"), pairs)
+
+    pieces = {}
+    for kt in turns:
+        for ks, piece in enumerate(sort_slab(trainer_tiles, layers, n_tensor, kt, place)):
+            pieces[ks, kt] = piece
+        place, _ = lax.optimization_barrier((place, piece))
+    first, last = pieces[0, 0], pieces[all_s, all_t]
+    pieces[0, 0] = jnp.where(core == 0, first, last)
+    pieces[all_s, all_t] = jnp.where(core == 0, last, first)
+    weights = [
+        exchange(offset, pieces[offset]) if offset != (0, 0) else pieces[offset]
+        for offset in offsets
+    ]
 
     ends = jnp.cumsum(tile_lengths)
     offset = np.array(offsets, np.int32)
-    sources = (offset[:, 0] ^ spot) * n_tensor + (offset[:, 1] ^ tpos) + zone * tiles
+    sender = (offset[:, 1] % 2) ^ core
+    fixed = (offset == [0, 0]).all(axis=1) | (offset == [all_s, all_t]).all(axis=1)
+    sender = jnp.where(fixed, 0, sender)
+    sources = (offset[:, 0] ^ spot ^ sender * all_s) * n_tensor
+    sources = sources + (offset[:, 1] ^ tpos ^ sender * all_t) + zone * tiles
     starts = (ends - tile_lengths)[sources]
     counts = tile_lengths[sources]
     tick_ids = jnp.arange(ticks, dtype=jnp.int32)
@@ -340,16 +347,12 @@
             (z * n_spot + s, (1 - z) * n_spot + s) for s in spots(tick) for z in range(n_zone)
         )
 
-    def active(tick):
-        return [l for l in range(layers) if 0 <= tick - l < ITEMS]
-
     across = [(t, t ^ 1) for t in range(n_tensor)]
     shown = step_inputs.reshape(steps, n_item, brow, n_y, 2, shard)
     records = []
     for stream in range(STREAMS):
         arrived, record = None, [jnp.zeros((rows, half), jnp.float32)] * ITEMS
         for tick in range(ticks):
-            busy = active(tick)
             if tick < ITEMS:
                 item = stream * ITEMS + tick
                 fresh = shown[:, item].reshape(rows, n_y, 2, shard)
@@ -361,10 +364,7 @@
                 other = lax.ppermute(mine, "tensor", across)
             else:
                 other = lax.dynamic_index_in_dim(fresh, 1 - core, 2, False).reshape(rows, half)
-            use = sorted({l // n_spot for l in busy})
-            own = project(
-                tick, use, tiles, tilew, n_y, scalars, mine, other, gains, sum([weights[p] for p in use], [])
-            )
+            own = project(tick, tiles, tilew, n_y, scalars, mine, other, gains, weights)
             sent = lax.ppermute(own, ("zone", "spot"), mirror(tick))
             item_at = 1 + ticks + stream * ticks + tick
             theirs, ours = attend(

time: 702 us -> 622 us (0.89)
  starting transfers between devices: 211 us -> 107 us
  waiting for transfers between devices: 306 us -> 327 us
  Pallas kernels: 133 us -> 116 us
  other arithmetic: 16.6 us -> 27.7 us
  local copies, waits for them, and re-layouts: 19.9 us -> 28 us
    ppermute x30 -> x15, starting transfers between devices: 151 us -> 45.2 us  [exchange(): return lax.ppermute(piece, ('spot', 'tensor'), pairs)]
    ppermute x8, waiting for transfers between devices: 58.1 us -> 89.1 us  [per_device(): near = lax.ppermute(after, ('zone', 'spot'), hop(tick, 0))]
    ppermute x30 -> x15, waiting for transfers between devices: 143 us -> 124 us  [exchange(): return lax.ppermute(piece, ('spot', 'tensor'), pairs)]
    pallas_call x17 -> x13, Pallas kernels: 90.6 us -> 73.3 us  [the longest x9 46 us: project(): pl.pallas_call(functools.partial(project_kernel, tick, tiles, tilew, n_y)...]
    ppermute x9, waiting for transfers between devices: 43.8 us -> 51.2 us  [per_device(): lax.ppermute(part, 'tensor', [(t, t ^ bit) for t in range(n_tensor)])]
    unnamed x77 -> x127, local copies, waits for them, and re-layouts: 10.4 us -> 14.7 us
  transfers between devices with their start and end apart: 82 -> 67, of which waited for: 48 -> 46; matrix products, arithmetic and copies ran while one was open for 2% -> 4% of each run, Pallas kernels for 7% -> 4%
where the time goes in v8:
time: 622 us; the launch traced here: 612 us
  waiting for transfers between devices  327 us (53%)
  Pallas kernels  116 us (19%)
  starting transfers between devices  107 us (17%)
  local copies, waits for them, and re-layouts  28 us (5%)
  other arithmetic  27.7 us (4%)
  between operations  6.46 us (1%)
    ppermute x15, waiting for transfers between devices, exchange(): return lax.ppermute(piece, ('spot', 'tensor'), pairs)  124 us
    ppermute x8, waiting for transfers between devices, per_device(): near = lax.ppermute(after, ('zone', 'spot'), hop(tick, 0))  89.1 us
    ppermute x9, waiting for transfers between devices, per_device(): lax.ppermute(part, 'tensor', [(t, t ^ bit) for t in range(n_tensor)])  51.2 us
    pallas_call x9, Pallas kernels, project(): pl.pallas_call(functools.partial(project_kernel, tick, tiles, tilew, n_y)...  46 us
    ppermute x15, starting transfers between devices, exchange(): return lax.ppermute(piece, ('spot', 'tensor'), pairs)  45.2 us
    pallas_call x9, Pallas kernels, attend(): pl.pallas_call(functools.partial(attend_kernel, steps, brow, kvlocal, gro...  42.2 us
    ppermute x9, waiting for transfers between devices, per_device(): sent = lax.ppermute(own, ('zone', 'spot'), mirror(tick))  28.7 us
    pallas_call x4, Pallas kernels, sort_slab(): pl.pallas_call(functools.partial(sort_kernel, layers), grid_spec=pltpu.Pr...  27.3 us
  transfers between devices with their start and end apart: 67, of which 46 were waited for; matrix products, arithmetic and copies ran while one was open for 4% of the time, Pallas kernels for 4%

profile of v8, /device:TPU:0, one launch (start us, length us, event | category | flops | bytes accessed | tf_op | source)
XLA Modules:
  0.0 612.0 jit_solution(12531927113823443492)
XLA Ops:
  4.1 7.1 %shard_map.118 = (bf16[2,192,1536]{2,1,0:T(8,128)(2,1)S(1)}, bf16[2,192,1536]{2,1,0:T(8,128)(2,1)}, bf16[2,192,1536]{2,1,0:T(8,128)(2,1)}, bf16[2,192,1536]{2,1,0:T(8,128)(2,1)}) custom-call(s32[2]{0:T(128)S(1)} %pad_add_fusion.place, bf16[1536,6144]{1,0:T(8,128)(2,1)} %slab.7), custom_call_target="tpu_custom_call" | custom-call | flops 1207959552 | bytes 9437184 | tf_op jit(solution)/shard_map/pallas_call | solution.py:40
  15.8 7.1 %shard_map.119 = (bf16[2,192,1536]{2,1,0:T(8,128)(2,1)}, bf16[2,192,1536]{2,1,0:T(8,128)(2,1)}, bf16[2,192,1536]{2,1,0:T(8,128)(2,1)}, bf16[2,192,1536]{2,1,0:T(8,128)(2,1)S(1)}) custom-call(s32[2]{0:T(128)S(1)} %pad_add_fusion.place, bf16[1536,6144]{1,0:T(8,128)(2,1)} %slab.7), custom_call_target="tpu_custom_call" | custom-call | flops 1207959552 | bytes 9437184 | tf_op jit(solution)/shard_map/pallas_call | solution.py:40
  26.9 7.3 %shard_map.120 = (bf16[2,192,1536]{2,1,0:T(8,128)(2,1)}, bf16[2,192,1536]{2,1,0:T(8,128)(2,1)}, bf16[2,192,1536]{2,1,0:T(8,128)(2,1)}, bf16[2,192,1536]{2,1,0:T(8,128)(2,1)S(1)}) custom-call(s32[2]{0:T(128)S(1)} %pad_add_fusion.place, bf16[1536,6144]{1,0:T(8,128)(2,1)} %slab.7), custom_call_target="tpu_custom_call" | custom-call | flops 1207959552 | bytes 9437184 | tf_op jit(solution)/shard_map/pallas_call | solution.py:40
  40.9 26.0 %collective-permute-start.6 = (bf16[2,192,1536]{2,1,0:T(8,128)(2,1)}, bf16[2,192,1536]{2,1,0:T(8,128)(2,1)}, u32[]{:S(2)}, u32[]{:S(2)}) collective-permute-start(bf16[2,192,1536]{2,1,0:T(8,128)(2,1)} %get-tuple-element.50), channel_id=1, source_target_pairs={{0,10},{1,5},{2,8},{3,7},{4,14},{5,1},{6,12},{7,3},{8,2},{9,13},{1... | collective-permute-start | bytes 3538952 | tf_op jit(solution)/shard_map/ppermute | solution.py:297
  72.4 60.1 %collective-permute-done.5.rest_5_ = bf16[2,192,1536]{2,1,0:T(8,128)(2,1)} collective-permute-done((bf16[2,192,1536]{2,1,0:T(8,128)(2,1)}, bf16[2,192,1536]{2,1,0:T(8,128)(2,1)}, u32[]{:S(2)}, u32[]{:S(2)}) %collective-permute-start.5) | collective-permute-done | bytes 1179680 | tf_op jit(solution)/shard_map/ppermute | solution.py:297
  150.5 5.8 shard_map.121
  164.5 19.9 %collective-permute-done.11.rest_11_ = bf16[2,192,1536]{2,1,0:T(8,128)(2,1)S(1)} collective-permute-done((bf16[2,192,1536]{2,1,0:T(8,128)(2,1)S(1)}, bf16[2,192,1536]{2,1,0:T(8,128)(2,1)S(1)}, u32[]{:S(2)}, u32[]{:S(2)}) %collective-permute-start.11) | collective-permute-done | bytes 1179680 | tf_op jit(solution)/shard_map/ppermute | solution.py:297
  184.4 21.3 %collective-permute-done.12.rest_12_ = bf16[2,192,1536]{2,1,0:T(8,128)(2,1)S(1)} collective-permute-done((bf16[2,192,1536]{2,1,0:T(8,128)(2,1)S(1)}, bf16[2,192,1536]{2,1,0:T(8,128)(2,1)S(1)}, u32[]{:S(2)}, u32[]{:S(2)}) %collective-permute-start.12) | collective-permute-done | bytes 1179680 | tf_op jit(solution)/shard_map/ppermute | solution.py:297
  205.8 17.7 %collective-permute-done.13.rest_13_ = bf16[2,192,1536]{2,1,0:T(8,128)(2,1)S(1)} collective-permute-done((bf16[2,192,1536]{2,1,0:T(8,128)(2,1)S(1)}, bf16[2,192,1536]{2,1,0:T(8,128)(2,1)S(1)}, u32[]{:S(2)}, u32[]{:S(2)}) %collective-permute-start.13) | collective-permute-done | bytes 1179680 | tf_op jit(solution)/shard_map/ppermute | solution.py:297
  225.2 5.7 shard_map.122.own
  263.9 6.2 %collective-permute-done.19 = bf16[48,2048]{1,0:T(8,128)(2,1)} collective-permute-done((bf16[48,2048]{1,0:T(8,128)(2,1)}, bf16[48,2048]{1,0:T(8,128)(2,1)}, u32[]{:S(2)}, u32[]{:S(2)}) %collective-permute-start.19) | collective-permute-done | bytes 196640 | tf_op jit(solution)/shard_map/ppermute | solution.py:388
  283.7 6.2 %collective-permute-done.22.sent = bf16[48,1536]{1,0:T(8,128)(2,1)S(1)} collective-permute-done((bf16[48,1536]{1,0:T(8,128)(2,1)S(1)}, bf16[48,1536]{1,0:T(8,128)(2,1)S(1)}, u32[]{:S(2)}, u32[]{:S(2)}) %collective-permute-start.22) | collective-permute-done | bytes 147488 | tf_op jit(solution)/shard_map/ppermute | solution.py:368
  297.4 5.7 collective-permute-done.24
  330.8 6.0 collective-permute-done.30
  359.6 5.7 collective-permute-done.36
  369.4 32.3 %collective-permute-done.37 = bf16[48,2048]{1,0:T(8,128)(2,1)} collective-permute-done((bf16[48,2048]{1,0:T(8,128)(2,1)}, bf16[48,2048]{1,0:T(8,128)(2,1)}, u32[]{:S(2)}, u32[]{:S(2)}) %collective-permute-start.37) | collective-permute-done | bytes 196640 | tf_op jit(solution)/shard_map/ppermute | solution.py:388
  415.2 6.1 collective-permute-done.40.sent
  439.8 8.3 %collective-permute-done.43 = bf16[48,2048]{1,0:T(8,128)(2,1)} collective-permute-done((bf16[48,2048]{1,0:T(8,128)(2,1)}, bf16[48,2048]{1,0:T(8,128)(2,1)}, u32[]{:S(2)}, u32[]{:S(2)}) %collective-permute-start.43) | collective-permute-done | bytes 196640 | tf_op jit(solution)/shard_map/ppermute | solution.py:388
  461.6 6.0 collective-permute-done.46.sent
  508.0 5.7 collective-permute-done.54
  534.7 5.7 collective-permute-done.60
  544.5 32.0 %collective-permute-done.61 = bf16[48,2048]{1,0:T(8,128)(2,1)} collective-permute-done((bf16[48,2048]{1,0:T(8,128)(2,1)}, bf16[48,2048]{1,0:T(8,128)(2,1)}, u32[]{:S(2)}, u32[]{:S(2)}) %collective-permute-start.61) | collective-permute-done | bytes 196640 | tf_op jit(solution)/shard_map/ppermute | solution.py:388
  590.1 6.1 collective-permute-done.64.sent
  603.7 5.8 collective-permute-done.66
  (312 shorter events, 289.7 us)
Async XLA Ops:
  0.0 25.4 %collective-permute-start = (f32[1,4096]{1,0:T(1,128)}, f32[1,4096]{1,0:T(1,128)}, u32[]{:S(2)}, u32[]{:S(2)}) collective-permute-start(f32[1,4096]{1,0:T(1,128)} %param.18), channel_id=1, source_target_pairs={{0,16},{16,0},{1,17},{17,1},{2,18},{18,2},{3,19},{19,3},{4,20},{20... | collective-permute-start | bytes 49160 | tf_op jit(solution)/shard_map/ppermute | solution.py:327
  12.3 28.7 %collective-permute-start.1 = (bf16[2,192,1536]{2,1,0:T(8,128)(2,1)}, bf16[2,192,1536]{2,1,0:T(8,128)(2,1)S(1)}, u32[]{:S(2)}, u32[]{:S(2)}) collective-permute-start(bf16[2,192,1536]{2,1,0:T(8,128)(2,1)} %get-tuple-element.46), channel_id=1, source_target_pairs={{0,4},{1,11},{2,6},{3,9},{4,0},{5,15},{6,2},{7,13},{8,12},{9,3},{1... | collective-permute-start | bytes 3538952 | tf_op jit(solution)/shard_map/ppermute | solution.py:297
  13.8 53.2 %collective-permute-start.2 = (bf16[2,192,1536]{2,1,0:T(8,128)(2,1)}, bf16[2,192,1536]{2,1,0:T(8,128)(2,1)S(1)}, u32[]{:S(2)}, u32[]{:S(2)}) collective-permute-start(bf16[2,192,1536]{2,1,0:T(8,128)(2,1)} %get-tuple-element.47), channel_id=1, source_target_pairs={{0,8},{1,7},{2,10},{3,5},{4,12},{5,3},{6,14},{7,1},{8,0},{9,15},{1... | collective-permute-start | bytes 3538952 | tf_op jit(solution)/shard_map/ppermute | solution.py:297
  15.3 52.9 %collective-permute-start.3 = (bf16[2,192,1536]{2,1,0:T(8,128)(2,1)}, bf16[2,192,1536]{2,1,0:T(8,128)(2,1)}, u32[]{:S(2)}, u32[]{:S(2)}) collective-permute-start(bf16[2,192,1536]{2,1,0:T(8,128)(2,1)} %get-tuple-element.43), channel_id=1, source_target_pairs={{0,12},{1,3},{2,14},{3,1},{4,8},{5,7},{6,10},{7,5},{8,4},{9,11},{1... | collective-permute-start | bytes 3538952 | tf_op jit(solution)/shard_map/ppermute | solution.py:297
  23.9 44.4 %collective-permute-start.4 = (bf16[2,192,1536]{2,1,0:T(8,128)(2,1)}, bf16[2,192,1536]{2,1,0:T(8,128)(2,1)}, u32[]{:S(2)}, u32[]{:S(2)}) collective-permute-start(bf16[2,192,1536]{2,1,0:T(8,128)(2,1)} %get-tuple-element.48), channel_id=1, source_target_pairs={{0,2},{1,13},{2,0},{3,15},{4,6},{5,9},{6,4},{7,11},{8,10},{9,5},{1... | collective-permute-start | bytes 3538952 | tf_op jit(solution)/shard_map/ppermute | solution.py:297
  25.4 107.0 %collective-permute-start.5 = (bf16[2,192,1536]{2,1,0:T(8,128)(2,1)}, bf16[2,192,1536]{2,1,0:T(8,128)(2,1)}, u32[]{:S(2)}, u32[]{:S(2)}) collective-permute-start(bf16[2,192,1536]{2,1,0:T(8,128)(2,1)} %get-tuple-element.49), channel_id=1, source_target_pairs={{0,6},{1,9},{2,4},{3,11},{4,2},{5,13},{6,0},{7,15},{8,14},{9,1},{1... | collective-permute-start | bytes 3538952 | tf_op jit(solution)/shard_map/ppermute | solution.py:297
  40.9 115.4 %collective-permute-start.6 = (bf16[2,192,1536]{2,1,0:T(8,128)(2,1)}, bf16[2,192,1536]{2,1,0:T(8,128)(2,1)}, u32[]{:S(2)}, u32[]{:S(2)}) collective-permute-start(bf16[2,192,1536]{2,1,0:T(8,128)(2,1)} %get-tuple-element.50), channel_id=1, source_target_pairs={{0,10},{1,5},{2,8},{3,7},{4,14},{5,1},{6,12},{7,3},{8,2},{9,13},{1... | collective-permute-start | bytes 3538952 | tf_op jit(solution)/shard_map/ppermute | solution.py:297
  66.9 91.5 %collective-permute-start.7 = (bf16[2,192,1536]{2,1,0:T(8,128)(2,1)}, bf16[2,192,1536]{2,1,0:T(8,128)(2,1)}, u32[]{:S(2)}, u32[]{:S(2)}) collective-permute-start(bf16[2,192,1536]{2,1,0:T(8,128)(2,1)} %get-tuple-element.91), channel_id=1, source_target_pairs={{0,14},{1,15},{2,12},{3,13},{4,10},{5,11},{6,8},{7,9},{8,6},{9,7},... | collective-permute-start | bytes 3538952 | tf_op jit(solution)/shard_map/ppermute | solution.py:297
  68.3 91.4 %collective-permute-start.8 = (bf16[2,192,1536]{2,1,0:T(8,128)(2,1)}, bf16[2,192,1536]{2,1,0:T(8,128)(2,1)}, u32[]{:S(2)}, u32[]{:S(2)}) collective-permute-start(bf16[2,192,1536]{2,1,0:T(8,128)(2,1)} %get-tuple-element.52), channel_id=1, source_target_pairs={{0,1},{1,14},{2,3},{3,12},{4,5},{5,10},{6,7},{7,8},{8,9},{9,6},{10... | collective-permute-start | bytes 3538952 | tf_op jit(solution)/shard_map/ppermute | solution.py:297
  68.3 93.4 %collective-permute-start.9 = (bf16[2,192,1536]{2,1,0:T(8,128)(2,1)}, bf16[2,192,1536]{2,1,0:T(8,128)(2,1)}, u32[]{:S(2)}, u32[]{:S(2)}) collective-permute-start(bf16[2,192,1536]{2,1,0:T(8,128)(2,1)} %get-tuple-element.53), channel_id=1, source_target_pairs={{0,5},{1,10},{2,7},{3,8},{4,1},{5,14},{6,3},{7,12},{8,13},{9,2},{1... | collective-permute-start | bytes 3538952 | tf_op jit(solution)/shard_map/ppermute | solution.py:297
  132.5 30.3 %collective-permute-start.10 = (bf16[2,192,1536]{2,1,0:T(8,128)(2,1)}, bf16[2,192,1536]{2,1,0:T(8,128)(2,1)}, u32[]{:S(2)}, u32[]{:S(2)}) collective-permute-start(bf16[2,192,1536]{2,1,0:T(8,128)(2,1)} %get-tuple-element.54), channel_id=1, source_target_pairs={{0,9},{1,6},{2,11},{3,4},{4,13},{5,2},{6,15},{7,0},{8,1},{9,14},{1... | collective-permute-start | bytes 3538952 | tf_op jit(solution)/shard_map/ppermute | solution.py:297
  156.3 28.1 %collective-permute-start.11 = (bf16[2,192,1536]{2,1,0:T(8,128)(2,1)S(1)}, bf16[2,192,1536]{2,1,0:T(8,128)(2,1)S(1)}, u32[]{:S(2)}, u32[]{:S(2)}) collective-permute-start(bf16[2,192,1536]{2,1,0:T(8,128)(2,1)S(1)} %copy-done.39), channel_id=1, source_target_pairs={{0,13},{1,2},{2,15},{3,0},{4,9},{5,6},{6,11},{7,4},{8,5},{9,10},{1... | collective-permute-start | bytes 3538952 | tf_op jit(solution)/shard_map/ppermute | solution.py:297
  158.4 47.4 %collective-permute-start.12 = (bf16[2,192,1536]{2,1,0:T(8,128)(2,1)S(1)}, bf16[2,192,1536]{2,1,0:T(8,128)(2,1)S(1)}, u32[]{:S(2)}, u32[]{:S(2)}) collective-permute-start(bf16[2,192,1536]{2,1,0:T(8,128)(2,1)S(1)} %get-tuple-element.57), channel_id=1, source_target_pairs={{0,3},{1,12},{2,1},{3,14},{4,7},{5,8},{6,5},{7,10},{8,11},{9,4},{1... | collective-permute-start | bytes 3538952 | tf_op jit(solution)/shard_map/ppermute | solution.py:297
  159.7 63.7 %collective-permute-start.13 = (bf16[2,192,1536]{2,1,0:T(8,128)(2,1)S(1)}, bf16[2,192,1536]{2,1,0:T(8,128)(2,1)S(1)}, u32[]{:S(2)}, u32[]{:S(2)}) collective-permute-start(bf16[2,192,1536]{2,1,0:T(8,128)(2,1)S(1)} %get-tuple-element.58), channel_id=1, source_target_pairs={{0,7},{1,8},{2,5},{3,10},{4,3},{5,12},{6,1},{7,14},{8,15},{9,0},{1... | collective-permute-start | bytes 3538952 | tf_op jit(solution)/shard_map/ppermute | solution.py:297
  161.7 61.7 %collective-permute-start.14 = (bf16[2,192,1536]{2,1,0:T(8,128)(2,1)S(1)}, bf16[2,192,1536]{2,1,0:T(8,128)(2,1)S(1)}, u32[]{:S(2)}, u32[]{:S(2)}) collective-permute-start(bf16[2,192,1536]{2,1,0:T(8,128)(2,1)S(1)} %get-tuple-element.59), channel_id=1, source_target_pairs={{0,11},{1,4},{2,9},{3,6},{4,15},{5,0},{6,13},{7,2},{8,3},{9,12},{1... | collective-permute-start | bytes 3538952 | tf_op jit(solution)/shard_map/ppermute | solution.py:297
  162.8 60.6 %collective-permute-start.15 = (bf16[2,192,1536]{2,1,0:T(8,128)(2,1)S(1)}, bf16[2,192,1536]{2,1,0:T(8,128)(2,1)S(1)}, u32[]{:S(2)}, u32[]{:S(2)}) collective-permute-start(bf16[2,192,1536]{2,1,0:T(8,128)(2,1)S(1)} %get-tuple-element.60), channel_id=1, source_target_pairs={{0,15},{1,0},{2,13},{3,2},{4,11},{5,4},{6,9},{7,6},{8,7},{9,8},{10... | collective-permute-start | bytes 3538952 | tf_op jit(solution)/shard_map/ppermute | solution.py:297
  257.4 12.7 %collective-permute-start.19 = (bf16[48,2048]{1,0:T(8,128)(2,1)}, bf16[48,2048]{1,0:T(8,128)(2,1)}, u32[]{:S(2)}, u32[]{:S(2)}) collective-permute-start(bf16[48,2048]{1,0:T(8,128)(2,1)} %fusion.10), channel_id=1, source_target_pairs={{0,4},{12,16},{16,20},{28,0},{1,5},{13,17},{17,21},{29,1},{2,6},{1... | collective-permute-start | bytes 589832 | tf_op jit(solution)/shard_map/ppermute | solution.py:388
  259.3 13.6 %collective-permute-start.20 = (bf16[48,2048]{1,0:T(8,128)(2,1)}, bf16[48,2048]{1,0:T(8,128)(2,1)}, u32[]{:S(2)}, u32[]{:S(2)}) collective-permute-start(bf16[48,2048]{1,0:T(8,128)(2,1)} %fusion.10), channel_id=1, source_target_pairs={{0,20},{12,0},{16,4},{28,16},{1,21},{13,1},{17,5},{29,17},{2,22},{... | collective-permute-start | bytes 589832 | tf_op jit(solution)/shard_map/ppermute | solution.py:389
  366.2 35.5 %collective-permute-start.37 = (bf16[48,2048]{1,0:T(8,128)(2,1)}, bf16[48,2048]{1,0:T(8,128)(2,1)}, u32[]{:S(2)}, u32[]{:S(2)}) collective-permute-start(bf16[48,2048]{1,0:T(8,128)(2,1)} %get-tuple-element.87), channel_id=1, source_target_pairs={{8,12},{12,16},{24,28},{28,0},{9,13},{13,17},{25,29},{29,1},{10,14... | collective-permute-start | bytes 589832 | tf_op jit(solution)/shard_map/ppermute | solution.py:388
  367.5 36.8 %collective-permute-start.38 = (bf16[48,2048]{1,0:T(8,128)(2,1)}, bf16[48,2048]{1,0:T(8,128)(2,1)}, u32[]{:S(2)}, u32[]{:S(2)}) collective-permute-start(bf16[48,2048]{1,0:T(8,128)(2,1)} %get-tuple-element.87), channel_id=1, source_target_pairs={{8,28},{12,0},{24,12},{28,16},{9,29},{13,1},{25,13},{29,17},{10,30... | collective-permute-start | bytes 589832 | tf_op jit(solution)/shard_map/ppermute | solution.py:389
  435.4 12.7 %collective-permute-start.43 = (bf16[48,2048]{1,0:T(8,128)(2,1)}, bf16[48,2048]{1,0:T(8,128)(2,1)}, u32[]{:S(2)}, u32[]{:S(2)}) collective-permute-start(bf16[48,2048]{1,0:T(8,128)(2,1)} %get-tuple-element.85), channel_id=1, source_target_pairs={{0,4},{12,16},{16,20},{28,0},{1,5},{13,17},{17,21},{29,1},{2,6},{1... | collective-permute-start | bytes 589832 | tf_op jit(solution)/shard_map/ppermute | solution.py:388
  437.4 13.3 %collective-permute-start.44 = (bf16[48,2048]{1,0:T(8,128)(2,1)}, bf16[48,2048]{1,0:T(8,128)(2,1)}, u32[]{:S(2)}, u32[]{:S(2)}) collective-permute-start(bf16[48,2048]{1,0:T(8,128)(2,1)} %get-tuple-element.85), channel_id=1, source_target_pairs={{0,20},{12,0},{16,4},{28,16},{1,21},{13,1},{17,5},{29,17},{2,22},{... | collective-permute-start | bytes 589832 | tf_op jit(solution)/shard_map/ppermute | solution.py:389
  541.3 35.2 %collective-permute-start.61 = (bf16[48,2048]{1,0:T(8,128)(2,1)}, bf16[48,2048]{1,0:T(8,128)(2,1)}, u32[]{:S(2)}, u32[]{:S(2)}) collective-permute-start(bf16[48,2048]{1,0:T(8,128)(2,1)} %get-tuple-element.79), channel_id=1, source_target_pairs={{8,12},{12,16},{24,28},{28,0},{9,13},{13,17},{25,29},{29,1},{10,14... | collective-permute-start | bytes 589832 | tf_op jit(solution)/shard_map/ppermute | solution.py:388
  542.6 36.6 %collective-permute-start.62 = (bf16[48,2048]{1,0:T(8,128)(2,1)}, bf16[48,2048]{1,0:T(8,128)(2,1)}, u32[]{:S(2)}, u32[]{:S(2)}) collective-permute-start(bf16[48,2048]{1,0:T(8,128)(2,1)} %get-tuple-element.79), channel_id=1, source_target_pairs={{8,28},{12,0},{24,12},{28,16},{9,29},{13,1},{25,13},{29,17},{10,30... | collective-permute-start | bytes 589832 | tf_op jit(solution)/shard_map/ppermute | solution.py:389
  (105 other events, 1107.6 us)

commit v9 on v8

--- a/solution.py
+++ b/solution.py
@@ -16,6 +16,7 @@
 CHUNK = 384
 WINDOW = 512
 VMEM = 48 * 1024 * 1024
+WHOLE_VMEM = 62 * 1024 * 1024
 
 
 def sort_kernel(layers, place, slab, *outs):
@@ -46,7 +47,7 @@
             out_specs=[pl.BlockSpec((2, feats, cdev), lambda i, s: (0, i, 0))] * kept,
         ),
         out_shape=[jax.ShapeDtypeStruct((2, rows // layers, cdev), jnp.bfloat16)] * kept,
-        compiler_params=pltpu.CompilerParams(vmem_limit_bytes=VMEM),
+        compiler_params=pltpu.CompilerParams(vmem_limit_bytes=WHOLE_VMEM),
         cost_estimate=pl.CostEstimate(
             flops=2 * rows * cdev * ROWBLOCK, bytes_accessed=4 * rows * cdev, transcendentals=0
         ),
@@ -131,7 +132,7 @@
             pltpu.SemaphoreType.DMA((tiles,)),
         ],
         out_shape=jax.ShapeDtypeStruct((rows, cdev), jnp.bfloat16),
-        compiler_params=pltpu.CompilerParams(vmem_limit_bytes=VMEM),
+        compiler_params=pltpu.CompilerParams(vmem_limit_bytes=VMEM if tick else WHOLE_VMEM),
         cost_estimate=pl.CostEstimate(
             flops=2 * rows * depth * cdev, bytes_accessed=2 * depth * cdev, transcendentals=0
         ),

time: 622 us -> 610 us (0.981)
  local copies, waits for them, and re-layouts: 28 us -> 11.1 us
  waiting for transfers between devices: 327 us -> 336 us
    unnamed x127 -> x93, local copies, waits for them, and re-layouts: 14.7 us -> 5.46 us
  transfers between devices with their start and end apart: 67 -> 67, of which waited for: 46 -> 48; matrix products, arithmetic and copies ran while one was open for 4% -> 2% of each run, Pallas kernels for 4% -> 5%
where the time goes in v9:
time: 610 us; the launch traced here: 601 us
  waiting for transfers between devices  336 us (55%)
  Pallas kernels  119 us (20%)
  starting transfers between devices  103 us (17%)
  other arithmetic  24.6 us (4%)
  local copies, waits for them, and re-layouts  11.1 us (2%)
  between operations  6.38 us (1%)
    ppermute x15, waiting for transfers between devices, exchange(): return lax.ppermute(piece, ('spot', 'tensor'), pairs)  130 us
    ppermute x8, waiting for transfers between devices, per_device(): near = lax.ppermute(after, ('zone', 'spot'), hop(tick, 0))  89.2 us
    ppermute x9, waiting for transfers between devices, per_device(): lax.ppermute(part, 'tensor', [(t, t ^ bit) for t in range(n_tensor)])  52.9 us
    pallas_call x9, Pallas kernels, project(): pl.pallas_call(functools.partial(project_kernel, tick, tiles, tilew, n_y)...  46.9 us
    ppermute x15, starting transfers between devices, exchange(): return lax.ppermute(piece, ('spot', 'tensor'), pairs)  43.6 us
    pallas_call x9, Pallas kernels, attend(): pl.pallas_call(functools.partial(attend_kernel, steps, brow, kvlocal, gro...  41.7 us
    pallas_call x4, Pallas kernels, sort_slab(): pl.pallas_call(functools.partial(sort_kernel, layers), grid_spec=pltpu.Pr...  30.8 us
    ppermute x9, waiting for transfers between devices, per_device(): sent = lax.ppermute(own, ('zone', 'spot'), mirror(tick))  29.9 us
  transfers between devices with their start and end apart: 67, of which 48 were waited for; matrix products, arithmetic and copies ran while one was open for 2% of the time, Pallas kernels for 5%

profile of v9, /device:TPU:0, one launch (start us, length us, event | category | flops | bytes accessed | tf_op | source)
XLA Modules:
  0.0 601.0 jit_solution(11303079943587928262)
XLA Ops:
  4.6 7.7 %shard_map.118 = (bf16[2,192,1536]{2,1,0:T(8,128)(2,1)}, bf16[2,192,1536]{2,1,0:T(8,128)(2,1)}, bf16[2,192,1536]{2,1,0:T(8,128)(2,1)}, bf16[2,192,1536]{2,1,0:T(8,128)(2,1)}) custom-call(s32[2]{0:T(128)} %pad_add_fusion.place, bf16[1536,6144]{1,0:T(8,128)(2,1)} %slab.7), custom_call_target="tpu_custom_call" | custom-call | flops 1207959552 | bytes 9437184 | tf_op jit(solution)/shard_map/pallas_call | solution.py:41
  15.8 7.7 %shard_map.119 = (bf16[2,192,1536]{2,1,0:T(8,128)(2,1)}, bf16[2,192,1536]{2,1,0:T(8,128)(2,1)}, bf16[2,192,1536]{2,1,0:T(8,128)(2,1)}, bf16[2,192,1536]{2,1,0:T(8,128)(2,1)}) custom-call(s32[2]{0:T(128)} %pad_add_fusion.place, bf16[1536,6144]{1,0:T(8,128)(2,1)} %slab.7), custom_call_target="tpu_custom_call" | custom-call | flops 1207959552 | bytes 9437184 | tf_op jit(solution)/shard_map/pallas_call | solution.py:41
  26.4 7.7 %shard_map.120 = (bf16[2,192,1536]{2,1,0:T(8,128)(2,1)}, bf16[2,192,1536]{2,1,0:T(8,128)(2,1)}, bf16[2,192,1536]{2,1,0:T(8,128)(2,1)}, bf16[2,192,1536]{2,1,0:T(8,128)(2,1)}) custom-call(s32[2]{0:T(128)} %pad_add_fusion.place, bf16[1536,6144]{1,0:T(8,128)(2,1)} %slab.7), custom_call_target="tpu_custom_call" | custom-call | flops 1207959552 | bytes 9437184 | tf_op jit(solution)/shard_map/pallas_call | solution.py:41
  41.0 25.9 %collective-permute-start.6 = (bf16[2,192,1536]{2,1,0:T(8,128)(2,1)}, bf16[2,192,1536]{2,1,0:T(8,128)(2,1)}, u32[]{:S(2)}, u32[]{:S(2)}) collective-permute-start(bf16[2,192,1536]{2,1,0:T(8,128)(2,1)} %get-tuple-element.50), channel_id=1, source_target_pairs={{0,10},{1,5},{2,8},{3,7},{4,14},{5,1},{6,12},{7,3},{8,2},{9,13},{1... | collective-permute-start | bytes 3538952 | tf_op jit(solution)/shard_map/ppermute | solution.py:298
  72.4 60.1 %collective-permute-done.5.rest_5_ = bf16[2,192,1536]{2,1,0:T(8,128)(2,1)} collective-permute-done((bf16[2,192,1536]{2,1,0:T(8,128)(2,1)}, bf16[2,192,1536]{2,1,0:T(8,128)(2,1)}, u32[]{:S(2)}, u32[]{:S(2)}) %collective-permute-start.5) | collective-permute-done | bytes 1179680 | tf_op jit(solution)/shard_map/ppermute | solution.py:298
  138.8 7.8 %shard_map.121 = (bf16[2,192,1536]{2,1,0:T(8,128)(2,1)}, bf16[2,192,1536]{2,1,0:T(8,128)(2,1)}, bf16[2,192,1536]{2,1,0:T(8,128)(2,1)}, bf16[2,192,1536]{2,1,0:T(8,128)(2,1)}) custom-call(s32[2]{0:T(128)} %pad_add_fusion.place, bf16[1536,6144]{1,0:T(8,128)(2,1)} %slab.7), custom_call_target="tpu_custom_call" | custom-call | flops 1207959552 | bytes 9437184 | tf_op jit(solution)/shard_map/pallas_call | solution.py:41
  153.1 32.9 %collective-permute-done.10.rest_10_ = bf16[2,192,1536]{2,1,0:T(8,128)(2,1)} collective-permute-done((bf16[2,192,1536]{2,1,0:T(8,128)(2,1)}, bf16[2,192,1536]{2,1,0:T(8,128)(2,1)}, u32[]{:S(2)}, u32[]{:S(2)}) %collective-permute-start.10) | collective-permute-done | bytes 1179680 | tf_op jit(solution)/shard_map/ppermute | solution.py:298
  186.7 18.8 %collective-permute-done.13.rest_13_ = bf16[2,192,1536]{2,1,0:T(8,128)(2,1)S(1)} collective-permute-done((bf16[2,192,1536]{2,1,0:T(8,128)(2,1)}, bf16[2,192,1536]{2,1,0:T(8,128)(2,1)S(1)}, u32[]{:S(2)}, u32[]{:S(2)}) %collective-permute-start.13) | collective-permute-done | bytes 1179680 | tf_op jit(solution)/shard_map/ppermute | solution.py:298
  206.8 12.6 %collective-permute-done.15.rest_15_ = bf16[2,192,1536]{2,1,0:T(8,128)(2,1)S(1)} collective-permute-done((bf16[2,192,1536]{2,1,0:T(8,128)(2,1)}, bf16[2,192,1536]{2,1,0:T(8,128)(2,1)S(1)}, u32[]{:S(2)}, u32[]{:S(2)}) %collective-permute-start.15) | collective-permute-done | bytes 1179680 | tf_op jit(solution)/shard_map/ppermute | solution.py:298
  220.5 6.4 %shard_map.122.own = bf16[48,1536]{1,0:T(8,128)(2,1)} custom-call(s32[51]{0:T(128)} %concatenate.9.scalars, bf16[48,2048]{1,0:T(8,128)(2,1)} %bitcast.51, bf16[48,2048]{1,0:T(8,128)(2,1)} %bitcast.56, f32[2,4096]{1,0:T(2,128)} %pad_maximum_fusion.gains, bf16[2,192,1536]{2,1,0:T(8,128)(2,1)} %get-tuple-element.92.rest_0_, bf16[2,192,1536]{2,1,0:T(8,128)(2,1)} %copy-done.1, ...), custom_call_target="tpu_custom_call" | custom-call | flops 452984832 | bytes 9437184 | tf_op jit(solution)/shard_map/pallas_call | solution.py:123
  258.9 6.3 %collective-permute-done.19 = bf16[48,2048]{1,0:T(8,128)(2,1)} collective-permute-done((bf16[48,2048]{1,0:T(8,128)(2,1)}, bf16[48,2048]{1,0:T(8,128)(2,1)}, u32[]{:S(2)}, u32[]{:S(2)}) %collective-permute-start.19) | collective-permute-done | bytes 196640 | tf_op jit(solution)/shard_map/ppermute | solution.py:389
  278.1 6.2 %collective-permute-done.22.sent = bf16[48,1536]{1,0:T(8,128)(2,1)S(1)} collective-permute-done((bf16[48,1536]{1,0:T(8,128)(2,1)S(1)}, bf16[48,1536]{1,0:T(8,128)(2,1)S(1)}, u32[]{:S(2)}, u32[]{:S(2)}) %collective-permute-start.22) | collective-permute-done | bytes 147488 | tf_op jit(solution)/shard_map/ppermute | solution.py:369
  324.3 6.1 %collective-permute-done.30 = bf16[48,2048]{1,0:T(8,128)(2,1)} collective-permute-done((bf16[48,2048]{1,0:T(8,128)(2,1)}, bf16[48,2048]{1,0:T(8,128)(2,1)}, u32[]{:S(2)}, u32[]{:S(2)}) %collective-permute-start.30) | collective-permute-done | bytes 196640 | tf_op jit(solution)/shard_map/ppermute | solution.py:380
  362.1 32.4 %collective-permute-done.37 = bf16[48,2048]{1,0:T(8,128)(2,1)} collective-permute-done((bf16[48,2048]{1,0:T(8,128)(2,1)}, bf16[48,2048]{1,0:T(8,128)(2,1)}, u32[]{:S(2)}, u32[]{:S(2)}) %collective-permute-start.37) | collective-permute-done | bytes 196640 | tf_op jit(solution)/shard_map/ppermute | solution.py:389
  407.3 6.1 %collective-permute-done.40.sent = bf16[48,1536]{1,0:T(8,128)(2,1)S(1)} collective-permute-done((bf16[48,1536]{1,0:T(8,128)(2,1)S(1)}, bf16[48,1536]{1,0:T(8,128)(2,1)S(1)}, u32[]{:S(2)}, u32[]{:S(2)}) %collective-permute-start.40) | collective-permute-done | bytes 147488 | tf_op jit(solution)/shard_map/ppermute | solution.py:369
  420.7 5.9 collective-permute-done.42
  432.0 8.3 %collective-permute-done.43 = bf16[48,2048]{1,0:T(8,128)(2,1)} collective-permute-done((bf16[48,2048]{1,0:T(8,128)(2,1)}, bf16[48,2048]{1,0:T(8,128)(2,1)}, u32[]{:S(2)}, u32[]{:S(2)}) %collective-permute-start.43) | collective-permute-done | bytes 196640 | tf_op jit(solution)/shard_map/ppermute | solution.py:389
  453.0 6.0 collective-permute-done.46.sent
  466.3 5.9 collective-permute-done.48
  498.4 5.9 collective-permute-done.54
  524.4 5.9 collective-permute-done.60
  534.3 32.0 %collective-permute-done.61 = bf16[48,2048]{1,0:T(8,128)(2,1)} collective-permute-done((bf16[48,2048]{1,0:T(8,128)(2,1)}, bf16[48,2048]{1,0:T(8,128)(2,1)}, u32[]{:S(2)}, u32[]{:S(2)}) %collective-permute-start.61) | collective-permute-done | bytes 196640 | tf_op jit(solution)/shard_map/ppermute | solution.py:389
  579.2 6.0 %collective-permute-done.64.sent = bf16[48,1536]{1,0:T(8,128)(2,1)S(1)} collective-permute-done((bf16[48,1536]{1,0:T(8,128)(2,1)S(1)}, bf16[48,1536]{1,0:T(8,128)(2,1)S(1)}, u32[]{:S(2)}, u32[]{:S(2)}) %collective-permute-start.64) | collective-permute-done | bytes 147488 | tf_op jit(solution)/shard_map/ppermute | solution.py:369
  592.6 5.9 collective-permute-done.66
  (278 shorter events, 268.2 us)
Async XLA Ops:
  0.0 25.0 %collective-permute-start = (f32[1,4096]{1,0:T(1,128)}, f32[1,4096]{1,0:T(1,128)S(1)}, u32[]{:S(2)}, u32[]{:S(2)}) collective-permute-start(f32[1,4096]{1,0:T(1,128)} %param.18), channel_id=1, source_target_pairs={{0,16},{16,0},{1,17},{17,1},{2,18},{18,2},{3,19},{19,3},{4,20},{20... | collective-permute-start | bytes 49160 | tf_op jit(solution)/shard_map/ppermute | solution.py:328
  12.3 28.7 %collective-permute-start.1 = (bf16[2,192,1536]{2,1,0:T(8,128)(2,1)}, bf16[2,192,1536]{2,1,0:T(8,128)(2,1)S(1)}, u32[]{:S(2)}, u32[]{:S(2)}) collective-permute-start(bf16[2,192,1536]{2,1,0:T(8,128)(2,1)} %get-tuple-element.46), channel_id=1, source_target_pairs={{0,4},{1,11},{2,6},{3,9},{4,0},{5,15},{6,2},{7,13},{8,12},{9,3},{1... | collective-permute-start | bytes 3538952 | tf_op jit(solution)/shard_map/ppermute | solution.py:298
  13.8 53.1 %collective-permute-start.2 = (bf16[2,192,1536]{2,1,0:T(8,128)(2,1)}, bf16[2,192,1536]{2,1,0:T(8,128)(2,1)}, u32[]{:S(2)}, u32[]{:S(2)}) collective-permute-start(bf16[2,192,1536]{2,1,0:T(8,128)(2,1)} %get-tuple-element.47), channel_id=1, source_target_pairs={{0,8},{1,7},{2,10},{3,5},{4,12},{5,3},{6,14},{7,1},{8,0},{9,15},{1... | collective-permute-start | bytes 3538952 | tf_op jit(solution)/shard_map/ppermute | solution.py:298
  15.3 53.0 %collective-permute-start.3 = (bf16[2,192,1536]{2,1,0:T(8,128)(2,1)}, bf16[2,192,1536]{2,1,0:T(8,128)(2,1)}, u32[]{:S(2)}, u32[]{:S(2)}) collective-permute-start(bf16[2,192,1536]{2,1,0:T(8,128)(2,1)} %get-tuple-element.43), channel_id=1, source_target_pairs={{0,12},{1,3},{2,14},{3,1},{4,8},{5,7},{6,10},{7,5},{8,4},{9,11},{1... | collective-permute-start | bytes 3538952 | tf_op jit(solution)/shard_map/ppermute | solution.py:298
  23.4 44.9 %collective-permute-start.4 = (bf16[2,192,1536]{2,1,0:T(8,128)(2,1)}, bf16[2,192,1536]{2,1,0:T(8,128)(2,1)}, u32[]{:S(2)}, u32[]{:S(2)}) collective-permute-start(bf16[2,192,1536]{2,1,0:T(8,128)(2,1)} %get-tuple-element.48), channel_id=1, source_target_pairs={{0,2},{1,13},{2,0},{3,15},{4,6},{5,9},{6,4},{7,11},{8,10},{9,5},{1... | collective-permute-start | bytes 3538952 | tf_op jit(solution)/shard_map/ppermute | solution.py:298
  25.0 107.5 %collective-permute-start.5 = (bf16[2,192,1536]{2,1,0:T(8,128)(2,1)}, bf16[2,192,1536]{2,1,0:T(8,128)(2,1)}, u32[]{:S(2)}, u32[]{:S(2)}) collective-permute-start(bf16[2,192,1536]{2,1,0:T(8,128)(2,1)} %get-tuple-element.49), channel_id=1, source_target_pairs={{0,6},{1,9},{2,4},{3,11},{4,2},{5,13},{6,0},{7,15},{8,14},{9,1},{1... | collective-permute-start | bytes 3538952 | tf_op jit(solution)/shard_map/ppermute | solution.py:298
  41.0 105.7 %collective-permute-start.6 = (bf16[2,192,1536]{2,1,0:T(8,128)(2,1)}, bf16[2,192,1536]{2,1,0:T(8,128)(2,1)}, u32[]{:S(2)}, u32[]{:S(2)}) collective-permute-start(bf16[2,192,1536]{2,1,0:T(8,128)(2,1)} %get-tuple-element.50), channel_id=1, source_target_pairs={{0,10},{1,5},{2,8},{3,7},{4,14},{5,1},{6,12},{7,3},{8,2},{9,13},{1... | collective-permute-start | bytes 3538952 | tf_op jit(solution)/shard_map/ppermute | solution.py:298
  66.9 81.8 %collective-permute-start.7 = (bf16[2,192,1536]{2,1,0:T(8,128)(2,1)}, bf16[2,192,1536]{2,1,0:T(8,128)(2,1)}, u32[]{:S(2)}, u32[]{:S(2)}) collective-permute-start(bf16[2,192,1536]{2,1,0:T(8,128)(2,1)} %get-tuple-element.91), channel_id=1, source_target_pairs={{0,14},{1,15},{2,12},{3,13},{4,10},{5,11},{6,8},{7,9},{8,6},{9,7},... | collective-permute-start | bytes 3538952 | tf_op jit(solution)/shard_map/ppermute | solution.py:298
  68.3 81.6 %collective-permute-start.8 = (bf16[2,192,1536]{2,1,0:T(8,128)(2,1)}, bf16[2,192,1536]{2,1,0:T(8,128)(2,1)}, u32[]{:S(2)}, u32[]{:S(2)}) collective-permute-start(bf16[2,192,1536]{2,1,0:T(8,128)(2,1)} %get-tuple-element.52), channel_id=1, source_target_pairs={{0,1},{1,14},{2,3},{3,12},{4,5},{5,10},{6,7},{7,8},{8,9},{9,6},{10... | collective-permute-start | bytes 3538952 | tf_op jit(solution)/shard_map/ppermute | solution.py:298
  68.4 84.3 %collective-permute-start.9 = (bf16[2,192,1536]{2,1,0:T(8,128)(2,1)}, bf16[2,192,1536]{2,1,0:T(8,128)(2,1)}, u32[]{:S(2)}, u32[]{:S(2)}) collective-permute-start(bf16[2,192,1536]{2,1,0:T(8,128)(2,1)} %get-tuple-element.53), channel_id=1, source_target_pairs={{0,5},{1,10},{2,7},{3,8},{4,1},{5,14},{6,3},{7,12},{8,13},{9,2},{1... | collective-permute-start | bytes 3538952 | tf_op jit(solution)/shard_map/ppermute | solution.py:298
  132.5 53.5 %collective-permute-start.10 = (bf16[2,192,1536]{2,1,0:T(8,128)(2,1)}, bf16[2,192,1536]{2,1,0:T(8,128)(2,1)}, u32[]{:S(2)}, u32[]{:S(2)}) collective-permute-start(bf16[2,192,1536]{2,1,0:T(8,128)(2,1)} %get-tuple-element.54), channel_id=1, source_target_pairs={{0,9},{1,6},{2,11},{3,4},{4,13},{5,2},{6,15},{7,0},{8,1},{9,14},{1... | collective-permute-start | bytes 3538952 | tf_op jit(solution)/shard_map/ppermute | solution.py:298
  146.7 40.0 %collective-permute-start.11 = (bf16[2,192,1536]{2,1,0:T(8,128)(2,1)S(1)}, bf16[2,192,1536]{2,1,0:T(8,128)(2,1)S(1)}, u32[]{:S(2)}, u32[]{:S(2)}) collective-permute-start(bf16[2,192,1536]{2,1,0:T(8,128)(2,1)S(1)} %copy-done.43), channel_id=1, source_target_pairs={{0,13},{1,2},{2,15},{3,0},{4,9},{5,6},{6,11},{7,4},{8,5},{9,10},{1... | collective-permute-start | bytes 3538952 | tf_op jit(solution)/shard_map/ppermute | solution.py:298
  148.7 38.0 %collective-permute-start.12 = (bf16[2,192,1536]{2,1,0:T(8,128)(2,1)}, bf16[2,192,1536]{2,1,0:T(8,128)(2,1)S(1)}, u32[]{:S(2)}, u32[]{:S(2)}) collective-permute-start(bf16[2,192,1536]{2,1,0:T(8,128)(2,1)} %get-tuple-element.57), channel_id=1, source_target_pairs={{0,3},{1,12},{2,1},{3,14},{4,7},{5,8},{6,5},{7,10},{8,11},{9,4},{1... | collective-permute-start | bytes 3538952 | tf_op jit(solution)/shard_map/ppermute | solution.py:298
  150.0 55.5 %collective-permute-start.13 = (bf16[2,192,1536]{2,1,0:T(8,128)(2,1)}, bf16[2,192,1536]{2,1,0:T(8,128)(2,1)S(1)}, u32[]{:S(2)}, u32[]{:S(2)}) collective-permute-start(bf16[2,192,1536]{2,1,0:T(8,128)(2,1)} %get-tuple-element.58), channel_id=1, source_target_pairs={{0,7},{1,8},{2,5},{3,10},{4,3},{5,12},{6,1},{7,14},{8,15},{9,0},{1... | collective-permute-start | bytes 3538952 | tf_op jit(solution)/shard_map/ppermute | solution.py:298
  152.7 54.2 %collective-permute-start.14 = (bf16[2,192,1536]{2,1,0:T(8,128)(2,1)}, bf16[2,192,1536]{2,1,0:T(8,128)(2,1)S(1)}, u32[]{:S(2)}, u32[]{:S(2)}) collective-permute-start(bf16[2,192,1536]{2,1,0:T(8,128)(2,1)} %get-tuple-element.59), channel_id=1, source_target_pairs={{0,11},{1,4},{2,9},{3,6},{4,15},{5,0},{6,13},{7,2},{8,3},{9,12},{1... | collective-permute-start | bytes 3538952 | tf_op jit(solution)/shard_map/ppermute | solution.py:298
  186.0 33.5 %collective-permute-start.15 = (bf16[2,192,1536]{2,1,0:T(8,128)(2,1)}, bf16[2,192,1536]{2,1,0:T(8,128)(2,1)S(1)}, u32[]{:S(2)}, u32[]{:S(2)}) collective-permute-start(bf16[2,192,1536]{2,1,0:T(8,128)(2,1)} %get-tuple-element.60), channel_id=1, source_target_pairs={{0,15},{1,0},{2,13},{3,2},{4,11},{5,4},{6,9},{7,6},{8,7},{9,8},{10... | collective-permute-start | bytes 3538952 | tf_op jit(solution)/shard_map/ppermute | solution.py:298
  252.4 12.7 %collective-permute-start.19 = (bf16[48,2048]{1,0:T(8,128)(2,1)}, bf16[48,2048]{1,0:T(8,128)(2,1)}, u32[]{:S(2)}, u32[]{:S(2)}) collective-permute-start(bf16[48,2048]{1,0:T(8,128)(2,1)} %fusion.10), channel_id=1, source_target_pairs={{0,4},{12,16},{16,20},{28,0},{1,5},{13,17},{17,21},{29,1},{2,6},{1... | collective-permute-start | bytes 589832 | tf_op jit(solution)/shard_map/ppermute | solution.py:389
  254.4 13.6 %collective-permute-start.20 = (bf16[48,2048]{1,0:T(8,128)(2,1)}, bf16[48,2048]{1,0:T(8,128)(2,1)}, u32[]{:S(2)}, u32[]{:S(2)}) collective-permute-start(bf16[48,2048]{1,0:T(8,128)(2,1)} %fusion.10), channel_id=1, source_target_pairs={{0,20},{12,0},{16,4},{28,16},{1,21},{13,1},{17,5},{29,17},{2,22},{... | collective-permute-start | bytes 589832 | tf_op jit(solution)/shard_map/ppermute | solution.py:390
  358.9 35.6 %collective-permute-start.37 = (bf16[48,2048]{1,0:T(8,128)(2,1)}, bf16[48,2048]{1,0:T(8,128)(2,1)}, u32[]{:S(2)}, u32[]{:S(2)}) collective-permute-start(bf16[48,2048]{1,0:T(8,128)(2,1)} %get-tuple-element.87), channel_id=1, source_target_pairs={{8,12},{12,16},{24,28},{28,0},{9,13},{13,17},{25,29},{29,1},{10,14... | collective-permute-start | bytes 589832 | tf_op jit(solution)/shard_map/ppermute | solution.py:389
  360.2 37.0 %collective-permute-start.38 = (bf16[48,2048]{1,0:T(8,128)(2,1)}, bf16[48,2048]{1,0:T(8,128)(2,1)}, u32[]{:S(2)}, u32[]{:S(2)}) collective-permute-start(bf16[48,2048]{1,0:T(8,128)(2,1)} %get-tuple-element.87), channel_id=1, source_target_pairs={{8,28},{12,0},{24,12},{28,16},{9,29},{13,1},{25,13},{29,17},{10,30... | collective-permute-start | bytes 589832 | tf_op jit(solution)/shard_map/ppermute | solution.py:390
  427.5 12.7 %collective-permute-start.43 = (bf16[48,2048]{1,0:T(8,128)(2,1)}, bf16[48,2048]{1,0:T(8,128)(2,1)}, u32[]{:S(2)}, u32[]{:S(2)}) collective-permute-start(bf16[48,2048]{1,0:T(8,128)(2,1)} %get-tuple-element.85), channel_id=1, source_target_pairs={{0,4},{12,16},{16,20},{28,0},{1,5},{13,17},{17,21},{29,1},{2,6},{1... | collective-permute-start | bytes 589832 | tf_op jit(solution)/shard_map/ppermute | solution.py:389
  429.4 13.3 %collective-permute-start.44 = (bf16[48,2048]{1,0:T(8,128)(2,1)}, bf16[48,2048]{1,0:T(8,128)(2,1)}, u32[]{:S(2)}, u32[]{:S(2)}) collective-permute-start(bf16[48,2048]{1,0:T(8,128)(2,1)} %get-tuple-element.85), channel_id=1, source_target_pairs={{0,20},{12,0},{16,4},{28,16},{1,21},{13,1},{17,5},{29,17},{2,22},{... | collective-permute-start | bytes 589832 | tf_op jit(solution)/shard_map/ppermute | solution.py:390
  531.1 35.2 %collective-permute-start.61 = (bf16[48,2048]{1,0:T(8,128)(2,1)}, bf16[48,2048]{1,0:T(8,128)(2,1)}, u32[]{:S(2)}, u32[]{:S(2)}) collective-permute-start(bf16[48,2048]{1,0:T(8,128)(2,1)} %get-tuple-element.79), channel_id=1, source_target_pairs={{8,12},{12,16},{24,28},{28,0},{9,13},{13,17},{25,29},{29,1},{10,14... | collective-permute-start | bytes 589832 | tf_op jit(solution)/shard_map/ppermute | solution.py:389
  532.4 36.5 %collective-permute-start.62 = (bf16[48,2048]{1,0:T(8,128)(2,1)}, bf16[48,2048]{1,0:T(8,128)(2,1)}, u32[]{:S(2)}, u32[]{:S(2)}) collective-permute-start(bf16[48,2048]{1,0:T(8,128)(2,1)} %get-tuple-element.79), channel_id=1, source_target_pairs={{8,28},{12,0},{24,12},{28,16},{9,29},{13,1},{25,13},{29,17},{10,30... | collective-permute-start | bytes 589832 | tf_op jit(solution)/shard_map/ppermute | solution.py:390
  (88 other events, 1376.1 us)

commit v10 on v9

--- a/solution.py
+++ b/solution.py
@@ -246,6 +246,27 @@
             flops=2 * rows * qdim * width, bytes_accessed=2 * qdim * width, transcendentals=0
         ),
     )(scalars, own, sent, spans, keys, values, wo)
+
+
+def join_kernel(part, moved, mine, out):
+    total = part[...].astype(jnp.float32) + moved[...].astype(jnp.float32)
+    out[...] = (mine[...].astype(jnp.float32) + total).astype(jnp.bfloat16)
+
+
+def choose_kernel(flag, near, far, out):
+    out[...] = jnp.where(flag[0] == 1, near[...], far[...])
+
+
+def in_vmem(kernel, arrays, flag=None):
+    vmem = pl.BlockSpec(memory_space=pltpu.VMEM)
+    scalar = [] if flag is None else [flag.astype(jnp.int32)[None]]
+    return pl.pallas_call(
+        kernel,
+        in_specs=[pl.BlockSpec(memory_space=pltpu.SMEM)] * len(scalar) + [vmem] * len(arrays),
+        out_specs=vmem,
+        out_shape=jax.ShapeDtypeStruct(arrays[0].shape, jnp.bfloat16),
+        compiler_params=pltpu.CompilerParams(vmem_limit_bytes=VMEM),
+    )(*scalar, *arrays)
 
 
 def per_device(
@@ -352,7 +373,7 @@
     shown = step_inputs.reshape(steps, n_item, brow, n_y, 2, shard)
     records = []
     for stream in range(STREAMS):
-        arrived, record = None, [jnp.zeros((rows, half), jnp.float32)] * ITEMS
+        arrived, record = None, []
         for tick in range(ticks):
             if tick < ITEMS:
                 item = stream * ITEMS + tick
@@ -371,27 +392,28 @@
             theirs, ours = attend(
                 item_at, steps, brow, n_y, scalars, own, sent, spans, cache_keys[0], cache_values[0], wo_rollout
             )
-            part = ours.astype(jnp.float32) + lax.ppermute(theirs, "tensor", across).astype(
-                jnp.float32
-            )
+            moved = lax.ppermute(theirs, "tensor", across)
+            part = (ours.astype(jnp.float32) + moved.astype(jnp.float32)).astype(jnp.bfloat16)
             bit = 2
             while bit < n_tensor:
-                part = part.astype(jnp.bfloat16)
                 moved = lax.ppermute(part, "tensor", [(t, t ^ bit) for t in range(n_tensor)])
-                part = part.astype(jnp.float32) + moved.astype(jnp.float32)
                 bit = bit * 2
-            wide = mine.astype(jnp.float32) + part
-            for item in range(ITEMS):
-                record[item] = jnp.where(layer == tick - item, wide, record[item])
-            after = wide.astype(jnp.bfloat16)
+                if bit < n_tensor:
+                    part = part.astype(jnp.float32) + moved.astype(jnp.float32)
+                    part = part.astype(jnp.bfloat16)
+            after = in_vmem(join_kernel, [part, moved, mine])
+            record.append(after)
             if tick + 1 < ticks:
                 at_home = phases[tick + 1] == zone
+                far = lax.ppermute(after, ("zone", "spot"), hop(tick, 1))
                 near = lax.ppermute(after, ("zone", "spot"), hop(tick, 0))
-                far = lax.ppermute(after, ("zone", "spot"), hop(tick, 1))
-                arrived = jnp.where(at_home, near, far)
-        for value in record:
+                arrived = in_vmem(choose_kernel, [near, far], at_home)
+        for item in range(ITEMS):
+            value = jnp.zeros((rows, half), jnp.bfloat16)
+            for tick in range(item, ticks):
+                value = jnp.where(layer == tick - item, record[tick], value)
             value = lax.dynamic_slice_in_dim(value, tpos // 2 * shard, shard, 1)
-            records.append(value.reshape(steps, brow, shard))
+            records.append(value.astype(jnp.float32).reshape(steps, brow, shard))
     return jnp.concatenate(records, axis=1)[None]
 
 

time: 610 us -> 597 us (0.979)
  starting transfers between devices: 103 us -> 124 us
  other arithmetic: 24.6 us -> 6.41 us
  waiting for transfers between devices: 336 us -> 320 us
    ppermute x8, waiting for transfers between devices: 10.5 us -> 73.7 us  [per_device(): far = lax.ppermute(after, ('zone', 'spot'), hop(tick, 1))]
    ppermute x8, waiting for transfers between devices: 89.2 us -> 26.2 us  [per_device(): near = lax.ppermute(after, ('zone', 'spot'), hop(tick, 0))]
    ppermute x15, starting transfers between devices: 43.6 us -> 74.5 us  [exchange(): return lax.ppermute(piece, ('spot', 'tensor'), pairs)]
    ppermute x15, waiting for transfers between devices: 130 us -> 105 us  [exchange(): return lax.ppermute(piece, ('spot', 'tensor'), pairs)]
    select_n x9 -> x2, other arithmetic: 10.6 us -> 0.2 us  [per_device(): value = jnp.where(layer == tick - item, record[tick], value)]
    convert_element_type x16 -> x9, other arithmetic: 7.12 us -> 0.43 us  [per_device(): (ours.astype(jnp.float32) + moved.astype(jnp.float32)).astype(jnp.bfloat16)]
    ppermute x9, starting transfers between devices: 10.3 us -> 4.08 us  [per_device(): lax.ppermute(part, 'tensor', [(t, t ^ bit) for t in range(n_tensor)])]
  transfers between devices with their start and end apart: 67 -> 67, of which waited for: 48 -> 50; matrix products, arithmetic and copies ran while one was open for 2% -> 2% of each run, Pallas kernels for 5% -> 5%
where the time goes in v10:
time: 597 us; the launch traced here: 589 us
  waiting for transfers between devices  320 us (54%)
  starting transfers between devices  124 us (21%)
  Pallas kernels  122 us (20%)
  local copies, waits for them, and re-layouts  9.87 us (2%)
  between operations  6.72 us (1%)
  other arithmetic  6.41 us (1%)
    ppermute x15, waiting for transfers between devices, exchange(): return lax.ppermute(piece, ('spot', 'tensor'), pairs)  105 us
    ppermute x15, starting transfers between devices, exchange(): return lax.ppermute(piece, ('spot', 'tensor'), pairs)  74.5 us
    ppermute x8, waiting for transfers between devices, per_device(): far = lax.ppermute(after, ('zone', 'spot'), hop(tick, 1))  73.7 us
    ppermute x9, waiting for transfers between devices, per_device(): lax.ppermute(part, 'tensor', [(t, t ^ bit) for t in range(n_tensor)])  59 us
    pallas_call x9, Pallas kernels, project(): pl.pallas_call(functools.partial(project_kernel, tick, tiles, tilew, n_y)...  46.9 us
    pallas_call x9, Pallas kernels, attend(): pl.pallas_call(functools.partial(attend_kernel, steps, brow, kvlocal, gro...  41.7 us
    ppermute x9, waiting for transfers between devices, per_device(): sent = lax.ppermute(own, ('zone', 'spot'), mirror(tick))  32 us
    pallas_call x4, Pallas kernels, sort_slab(): pl.pallas_call(functools.partial(sort_kernel, layers), grid_spec=pltpu.Pr...  30.8 us
  transfers between devices with their start and end apart: 67, of which 50 were waited for; matrix products, arithmetic and copies ran while one was open for 2% of the time, Pallas kernels for 5%

profile of v10, /device:TPU:0, one launch (start us, length us, event | category | flops | bytes accessed | tf_op | source)
XLA Modules:
  0.0 588.7 jit_solution(17649589677109463925)
XLA Ops:
  4.6 7.7 %shard_map.118 = (bf16[2,192,1536]{2,1,0:T(8,128)(2,1)}, bf16[2,192,1536]{2,1,0:T(8,128)(2,1)}, bf16[2,192,1536]{2,1,0:T(8,128)(2,1)}, bf16[2,192,1536]{2,1,0:T(8,128)(2,1)}) custom-call(s32[2]{0:T(128)} %pad_add_fusion.place, bf16[1536,6144]{1,0:T(8,128)(2,1)} %slab.7), custom_call_target="tpu_custom_call" | custom-call | flops 1207959552 | bytes 9437184 | tf_op jit(solution)/shard_map/pallas_call | solution.py:41
  15.8 7.7 %shard_map.119 = (bf16[2,192,1536]{2,1,0:T(8,128)(2,1)}, bf16[2,192,1536]{2,1,0:T(8,128)(2,1)}, bf16[2,192,1536]{2,1,0:T(8,128)(2,1)}, bf16[2,192,1536]{2,1,0:T(8,128)(2,1)}) custom-call(s32[2]{0:T(128)} %pad_add_fusion.place, bf16[1536,6144]{1,0:T(8,128)(2,1)} %slab.7), custom_call_target="tpu_custom_call" | custom-call | flops 1207959552 | bytes 9437184 | tf_op jit(solution)/shard_map/pallas_call | solution.py:41
  30.7 7.7 %shard_map.120 = (bf16[2,192,1536]{2,1,0:T(8,128)(2,1)}, bf16[2,192,1536]{2,1,0:T(8,128)(2,1)}, bf16[2,192,1536]{2,1,0:T(8,128)(2,1)}, bf16[2,192,1536]{2,1,0:T(8,128)(2,1)}) custom-call(s32[2]{0:T(128)} %pad_add_fusion.place, bf16[1536,6144]{1,0:T(8,128)(2,1)} %slab.7), custom_call_target="tpu_custom_call" | custom-call | flops 1207959552 | bytes 9437184 | tf_op jit(solution)/shard_map/pallas_call | solution.py:41
  41.0 50.3 %collective-permute-start.5 = (bf16[2,192,1536]{2,1,0:T(8,128)(2,1)}, bf16[2,192,1536]{2,1,0:T(8,128)(2,1)}, u32[]{:S(2)}, u32[]{:S(2)}) collective-permute-start(bf16[2,192,1536]{2,1,0:T(8,128)(2,1)} %get-tuple-element.49), channel_id=1, source_target_pairs={{0,6},{1,9},{2,4},{3,11},{4,2},{5,13},{6,0},{7,15},{8,14},{9,1},{1... | collective-permute-start | bytes 3538952 | tf_op jit(solution)/shard_map/ppermute | solution.py:319
  103.1 7.8 %shard_map.121 = (bf16[2,192,1536]{2,1,0:T(8,128)(2,1)}, bf16[2,192,1536]{2,1,0:T(8,128)(2,1)}, bf16[2,192,1536]{2,1,0:T(8,128)(2,1)}, bf16[2,192,1536]{2,1,0:T(8,128)(2,1)}) custom-call(s32[2]{0:T(128)} %pad_add_fusion.place, bf16[1536,6144]{1,0:T(8,128)(2,1)} %slab.7), custom_call_target="tpu_custom_call" | custom-call | flops 1207959552 | bytes 9437184 | tf_op jit(solution)/shard_map/pallas_call | solution.py:41
  111.0 18.0 %collective-permute-done.5.rest_5_ = bf16[2,192,1536]{2,1,0:T(8,128)(2,1)} collective-permute-done((bf16[2,192,1536]{2,1,0:T(8,128)(2,1)}, bf16[2,192,1536]{2,1,0:T(8,128)(2,1)}, u32[]{:S(2)}, u32[]{:S(2)}) %collective-permute-start.5) | collective-permute-done | bytes 1179680 | tf_op jit(solution)/shard_map/ppermute | solution.py:319
  140.0 43.2 %collective-permute-done.9.rest_9_ = bf16[2,192,1536]{2,1,0:T(8,128)(2,1)} collective-permute-done((bf16[2,192,1536]{2,1,0:T(8,128)(2,1)}, bf16[2,192,1536]{2,1,0:T(8,128)(2,1)}, u32[]{:S(2)}, u32[]{:S(2)}) %collective-permute-start.9) | collective-permute-done | bytes 1179680 | tf_op jit(solution)/shard_map/ppermute | solution.py:319
  189.7 19.0 %collective-permute-done.12.rest_12_ = bf16[2,192,1536]{2,1,0:T(8,128)(2,1)S(1)} collective-permute-done((bf16[2,192,1536]{2,1,0:T(8,128)(2,1)}, bf16[2,192,1536]{2,1,0:T(8,128)(2,1)S(1)}, u32[]{:S(2)}, u32[]{:S(2)}) %collective-permute-start.12) | collective-permute-done | bytes 1179680 | tf_op jit(solution)/shard_map/ppermute | solution.py:319
  208.7 14.7 %collective-permute-done.13.rest_13_ = bf16[2,192,1536]{2,1,0:T(8,128)(2,1)S(1)} collective-permute-done((bf16[2,192,1536]{2,1,0:T(8,128)(2,1)}, bf16[2,192,1536]{2,1,0:T(8,128)(2,1)S(1)}, u32[]{:S(2)}, u32[]{:S(2)}) %collective-permute-start.13) | collective-permute-done | bytes 1179680 | tf_op jit(solution)/shard_map/ppermute | solution.py:319
  225.6 6.4 %shard_map.122.own = bf16[48,1536]{1,0:T(8,128)(2,1)} custom-call(s32[51]{0:T(128)} %concatenate.10.scalars, bf16[48,2048]{1,0:T(8,128)(2,1)} %bitcast.61, bf16[48,2048]{1,0:T(8,128)(2,1)} %bitcast.66, f32[2,4096]{1,0:T(2,128)} %pad_maximum_fusion.gains, bf16[2,192,1536]{2,1,0:T(8,128)(2,1)} %get-tuple-element.80.rest_0_, bf16[2,192,1536]{2,1,0:T(8,128)(2,1)} %copy-done.1, ...), custom_call_target="tpu_custom_call" | custom-call | flops 452984832 | bytes 9437184 | tf_op jit(solution)/shard_map/pallas_call | solution.py:123
  234.5 6.8 %collective-permute-done.16.sent = bf16[48,1536]{1,0:T(8,128)(2,1)S(1)} collective-permute-done((bf16[48,1536]{1,0:T(8,128)(2,1)}, bf16[48,1536]{1,0:T(8,128)(2,1)S(1)}, u32[]{:S(2)}, u32[]{:S(2)}) %collective-permute-start.16) | collective-permute-done | bytes 147488 | tf_op jit(solution)/shard_map/ppermute | solution.py:390
  250.1 6.5 %collective-permute-done.18.moved = bf16[48,2048]{1,0:T(8,128)(2,1)S(1)} collective-permute-done((bf16[48,2048]{1,0:T(8,128)(2,1)S(1)}, bf16[48,2048]{1,0:T(8,128)(2,1)S(1)}, u32[]{:S(2)}, u32[]{:S(2)}) %collective-permute-start.18) | collective-permute-done | bytes 196640 | tf_op jit(solution)/shard_map/ppermute | solution.py:399
  279.2 6.5 %collective-permute-done.22.sent = bf16[48,1536]{1,0:T(8,128)(2,1)S(1)} collective-permute-done((bf16[48,1536]{1,0:T(8,128)(2,1)S(1)}, bf16[48,1536]{1,0:T(8,128)(2,1)S(1)}, u32[]{:S(2)}, u32[]{:S(2)}) %collective-permute-start.22) | collective-permute-done | bytes 147488 | tf_op jit(solution)/shard_map/ppermute | solution.py:390
  292.4 6.6 %collective-permute-done.24.moved = bf16[48,2048]{1,0:T(8,128)(2,1)S(1)} collective-permute-done((bf16[48,2048]{1,0:T(8,128)(2,1)S(1)}, bf16[48,2048]{1,0:T(8,128)(2,1)S(1)}, u32[]{:S(2)}, u32[]{:S(2)}) %collective-permute-start.24) | collective-permute-done | bytes 196640 | tf_op jit(solution)/shard_map/ppermute | solution.py:399
  323.6 6.6 %collective-permute-done.30.moved = bf16[48,2048]{1,0:T(8,128)(2,1)S(1)} collective-permute-done((bf16[48,2048]{1,0:T(8,128)(2,1)S(1)}, bf16[48,2048]{1,0:T(8,128)(2,1)S(1)}, u32[]{:S(2)}, u32[]{:S(2)}) %collective-permute-start.30) | collective-permute-done | bytes 196640 | tf_op jit(solution)/shard_map/ppermute | solution.py:399
  346.5 6.6 %collective-permute-done.36.moved = bf16[48,2048]{1,0:T(8,128)(2,1)S(1)} collective-permute-done((bf16[48,2048]{1,0:T(8,128)(2,1)S(1)}, bf16[48,2048]{1,0:T(8,128)(2,1)S(1)}, u32[]{:S(2)}, u32[]{:S(2)}) %collective-permute-start.36) | collective-permute-done | bytes 196640 | tf_op jit(solution)/shard_map/ppermute | solution.py:399
  356.4 31.6 %collective-permute-done.38.far = bf16[48,2048]{1,0:T(8,128)(2,1)S(1)} collective-permute-done((bf16[48,2048]{1,0:T(8,128)(2,1)S(1)}, bf16[48,2048]{1,0:T(8,128)(2,1)S(1)}, u32[]{:S(2)}, u32[]{:S(2)}) %collective-permute-start.38) | collective-permute-done | bytes 196640 | tf_op jit(solution)/shard_map/ppermute | solution.py:408
  414.3 6.5 %collective-permute-done.42.moved = bf16[48,2048]{1,0:T(8,128)(2,1)S(1)} collective-permute-done((bf16[48,2048]{1,0:T(8,128)(2,1)S(1)}, bf16[48,2048]{1,0:T(8,128)(2,1)S(1)}, u32[]{:S(2)}, u32[]{:S(2)}) %collective-permute-start.42) | collective-permute-done | bytes 196640 | tf_op jit(solution)/shard_map/ppermute | solution.py:399
  443.6 6.3 %collective-permute-done.46.sent = bf16[48,1536]{1,0:T(8,128)(2,1)S(1)} collective-permute-done((bf16[48,1536]{1,0:T(8,128)(2,1)S(1)}, bf16[48,1536]{1,0:T(8,128)(2,1)S(1)}, u32[]{:S(2)}, u32[]{:S(2)}) %collective-permute-start.46) | collective-permute-done | bytes 147488 | tf_op jit(solution)/shard_map/ppermute | solution.py:390
  456.6 6.5 %collective-permute-done.48.moved = bf16[48,2048]{1,0:T(8,128)(2,1)S(1)} collective-permute-done((bf16[48,2048]{1,0:T(8,128)(2,1)S(1)}, bf16[48,2048]{1,0:T(8,128)(2,1)S(1)}, u32[]{:S(2)}, u32[]{:S(2)}) %collective-permute-start.48) | collective-permute-done | bytes 196640 | tf_op jit(solution)/shard_map/ppermute | solution.py:399
  487.6 6.5 %collective-permute-done.54.moved = bf16[48,2048]{1,0:T(8,128)(2,1)S(1)} collective-permute-done((bf16[48,2048]{1,0:T(8,128)(2,1)S(1)}, bf16[48,2048]{1,0:T(8,128)(2,1)S(1)}, u32[]{:S(2)}, u32[]{:S(2)}) %collective-permute-start.54) | collective-permute-done | bytes 196640 | tf_op jit(solution)/shard_map/ppermute | solution.py:399
  512.2 6.5 %collective-permute-done.60.moved = bf16[48,2048]{1,0:T(8,128)(2,1)S(1)} collective-permute-done((bf16[48,2048]{1,0:T(8,128)(2,1)S(1)}, bf16[48,2048]{1,0:T(8,128)(2,1)S(1)}, u32[]{:S(2)}, u32[]{:S(2)}) %collective-permute-start.60) | collective-permute-done | bytes 196640 | tf_op jit(solution)/shard_map/ppermute | solution.py:399
  522.1 30.9 %collective-permute-done.62.far = bf16[48,2048]{1,0:T(8,128)(2,1)} collective-permute-done((bf16[48,2048]{1,0:T(8,128)(2,1)S(1)}, bf16[48,2048]{1,0:T(8,128)(2,1)}, u32[]{:S(2)}, u32[]{:S(2)}) %collective-permute-start.62) | collective-permute-done | bytes 196640 | tf_op jit(solution)/shard_map/ppermute | solution.py:408
  580.8 6.5 %collective-permute-done.66.moved = bf16[48,2048]{1,0:T(8,128)(2,1)S(1)} collective-permute-done((bf16[48,2048]{1,0:T(8,128)(2,1)S(1)}, bf16[48,2048]{1,0:T(8,128)(2,1)S(1)}, u32[]{:S(2)}, u32[]{:S(2)}) %collective-permute-start.66) | collective-permute-done | bytes 196640 | tf_op jit(solution)/shard_map/ppermute | solution.py:399
  (284 shorter events, 258.5 us)
Async XLA Ops:
  0.0 30.1 %collective-permute-start = (f32[1,4096]{1,0:T(1,128)}, f32[1,4096]{1,0:T(1,128)S(1)}, u32[]{:S(2)}, u32[]{:S(2)}) collective-permute-start(f32[1,4096]{1,0:T(1,128)} %param.18), channel_id=1, source_target_pairs={{0,16},{16,0},{1,17},{17,1},{2,18},{18,2},{3,19},{19,3},{4,20},{20... | collective-permute-start | bytes 49160 | tf_op jit(solution)/shard_map/ppermute | solution.py:349
  12.3 28.7 %collective-permute-start.1 = (bf16[2,192,1536]{2,1,0:T(8,128)(2,1)}, bf16[2,192,1536]{2,1,0:T(8,128)(2,1)S(1)}, u32[]{:S(2)}, u32[]{:S(2)}) collective-permute-start(bf16[2,192,1536]{2,1,0:T(8,128)(2,1)} %get-tuple-element.46), channel_id=1, source_target_pairs={{0,4},{1,11},{2,6},{3,9},{4,0},{5,15},{6,2},{7,13},{8,12},{9,3},{1... | collective-permute-start | bytes 3538952 | tf_op jit(solution)/shard_map/ppermute | solution.py:319
  13.8 77.5 %collective-permute-start.2 = (bf16[2,192,1536]{2,1,0:T(8,128)(2,1)}, bf16[2,192,1536]{2,1,0:T(8,128)(2,1)}, u32[]{:S(2)}, u32[]{:S(2)}) collective-permute-start(bf16[2,192,1536]{2,1,0:T(8,128)(2,1)} %get-tuple-element.47), channel_id=1, source_target_pairs={{0,8},{1,7},{2,10},{3,5},{4,12},{5,3},{6,14},{7,1},{8,0},{9,15},{1... | collective-permute-start | bytes 3538952 | tf_op jit(solution)/shard_map/ppermute | solution.py:319
  15.3 79.5 %collective-permute-start.3 = (bf16[2,192,1536]{2,1,0:T(8,128)(2,1)}, bf16[2,192,1536]{2,1,0:T(8,128)(2,1)}, u32[]{:S(2)}, u32[]{:S(2)}) collective-permute-start(bf16[2,192,1536]{2,1,0:T(8,128)(2,1)} %get-tuple-element.43), channel_id=1, source_target_pairs={{0,12},{1,3},{2,14},{3,1},{4,8},{5,7},{6,10},{7,5},{8,4},{9,11},{1... | collective-permute-start | bytes 3538952 | tf_op jit(solution)/shard_map/ppermute | solution.py:319
  26.7 68.2 %collective-permute-start.7 = (bf16[2,192,1536]{2,1,0:T(8,128)(2,1)}, bf16[2,192,1536]{2,1,0:T(8,128)(2,1)}, u32[]{:S(2)}, u32[]{:S(2)}) collective-permute-start(bf16[2,192,1536]{2,1,0:T(8,128)(2,1)} %get-tuple-element.79), channel_id=1, source_target_pairs={{0,14},{1,15},{2,12},{3,13},{4,10},{5,11},{6,8},{7,9},{8,6},{9,7},... | collective-permute-start | bytes 3538952 | tf_op jit(solution)/shard_map/ppermute | solution.py:319
  30.2 65.9 %collective-permute-start.4 = (bf16[2,192,1536]{2,1,0:T(8,128)(2,1)}, bf16[2,192,1536]{2,1,0:T(8,128)(2,1)}, u32[]{:S(2)}, u32[]{:S(2)}) collective-permute-start(bf16[2,192,1536]{2,1,0:T(8,128)(2,1)} %get-tuple-element.48), channel_id=1, source_target_pairs={{0,2},{1,13},{2,0},{3,15},{4,6},{5,9},{6,4},{7,11},{8,10},{9,5},{1... | collective-permute-start | bytes 3538952 | tf_op jit(solution)/shard_map/ppermute | solution.py:319
  41.0 88.0 %collective-permute-start.5 = (bf16[2,192,1536]{2,1,0:T(8,128)(2,1)}, bf16[2,192,1536]{2,1,0:T(8,128)(2,1)}, u32[]{:S(2)}, u32[]{:S(2)}) collective-permute-start(bf16[2,192,1536]{2,1,0:T(8,128)(2,1)} %get-tuple-element.49), channel_id=1, source_target_pairs={{0,6},{1,9},{2,4},{3,11},{4,2},{5,13},{6,0},{7,15},{8,14},{9,1},{1... | collective-permute-start | bytes 3538952 | tf_op jit(solution)/shard_map/ppermute | solution.py:319
  91.3 37.7 %collective-permute-start.6 = (bf16[2,192,1536]{2,1,0:T(8,128)(2,1)}, bf16[2,192,1536]{2,1,0:T(8,128)(2,1)}, u32[]{:S(2)}, u32[]{:S(2)}) collective-permute-start(bf16[2,192,1536]{2,1,0:T(8,128)(2,1)} %get-tuple-element.50), channel_id=1, source_target_pairs={{0,10},{1,5},{2,8},{3,7},{4,14},{5,1},{6,12},{7,3},{8,2},{9,13},{1... | collective-permute-start | bytes 3538952 | tf_op jit(solution)/shard_map/ppermute | solution.py:319
  94.9 45.1 %collective-permute-start.8 = (bf16[2,192,1536]{2,1,0:T(8,128)(2,1)}, bf16[2,192,1536]{2,1,0:T(8,128)(2,1)}, u32[]{:S(2)}, u32[]{:S(2)}) collective-permute-start(bf16[2,192,1536]{2,1,0:T(8,128)(2,1)} %get-tuple-element.52), channel_id=1, source_target_pairs={{0,1},{1,14},{2,3},{3,12},{4,5},{5,10},{6,7},{7,8},{8,9},{9,6},{10... | collective-permute-start | bytes 3538952 | tf_op jit(solution)/shard_map/ppermute | solution.py:319
  94.9 88.3 %collective-permute-start.9 = (bf16[2,192,1536]{2,1,0:T(8,128)(2,1)}, bf16[2,192,1536]{2,1,0:T(8,128)(2,1)}, u32[]{:S(2)}, u32[]{:S(2)}) collective-permute-start(bf16[2,192,1536]{2,1,0:T(8,128)(2,1)} %get-tuple-element.53), channel_id=1, source_target_pairs={{0,5},{1,10},{2,7},{3,8},{4,1},{5,14},{6,3},{7,12},{8,13},{9,2},{1... | collective-permute-start | bytes 3538952 | tf_op jit(solution)/shard_map/ppermute | solution.py:319
  96.1 91.8 %collective-permute-start.10 = (bf16[2,192,1536]{2,1,0:T(8,128)(2,1)}, bf16[2,192,1536]{2,1,0:T(8,128)(2,1)}, u32[]{:S(2)}, u32[]{:S(2)}) collective-permute-start(bf16[2,192,1536]{2,1,0:T(8,128)(2,1)} %get-tuple-element.54), channel_id=1, source_target_pairs={{0,9},{1,6},{2,11},{3,4},{4,13},{5,2},{6,15},{7,0},{8,1},{9,14},{1... | collective-permute-start | bytes 3538952 | tf_op jit(solution)/shard_map/ppermute | solution.py:319
  129.0 60.7 %collective-permute-start.11 = (bf16[2,192,1536]{2,1,0:T(8,128)(2,1)S(1)}, bf16[2,192,1536]{2,1,0:T(8,128)(2,1)S(1)}, u32[]{:S(2)}, u32[]{:S(2)}) collective-permute-start(bf16[2,192,1536]{2,1,0:T(8,128)(2,1)S(1)} %copy-done.45), channel_id=1, source_target_pairs={{0,13},{1,2},{2,15},{3,0},{4,9},{5,6},{6,11},{7,4},{8,5},{9,10},{1... | collective-permute-start | bytes 3538952 | tf_op jit(solution)/shard_map/ppermute | solution.py:319
  129.0 79.7 %collective-permute-start.12 = (bf16[2,192,1536]{2,1,0:T(8,128)(2,1)}, bf16[2,192,1536]{2,1,0:T(8,128)(2,1)S(1)}, u32[]{:S(2)}, u32[]{:S(2)}) collective-permute-start(bf16[2,192,1536]{2,1,0:T(8,128)(2,1)} %get-tuple-element.57), channel_id=1, source_target_pairs={{0,3},{1,12},{2,1},{3,14},{4,7},{5,8},{6,5},{7,10},{8,11},{9,4},{1... | collective-permute-start | bytes 3538952 | tf_op jit(solution)/shard_map/ppermute | solution.py:319
  140.0 83.4 %collective-permute-start.13 = (bf16[2,192,1536]{2,1,0:T(8,128)(2,1)}, bf16[2,192,1536]{2,1,0:T(8,128)(2,1)S(1)}, u32[]{:S(2)}, u32[]{:S(2)}) collective-permute-start(bf16[2,192,1536]{2,1,0:T(8,128)(2,1)} %get-tuple-element.58), channel_id=1, source_target_pairs={{0,7},{1,8},{2,5},{3,10},{4,3},{5,12},{6,1},{7,14},{8,15},{9,0},{1... | collective-permute-start | bytes 3538952 | tf_op jit(solution)/shard_map/ppermute | solution.py:319
  183.2 40.2 %collective-permute-start.14 = (bf16[2,192,1536]{2,1,0:T(8,128)(2,1)}, bf16[2,192,1536]{2,1,0:T(8,128)(2,1)S(1)}, u32[]{:S(2)}, u32[]{:S(2)}) collective-permute-start(bf16[2,192,1536]{2,1,0:T(8,128)(2,1)} %get-tuple-element.59), channel_id=1, source_target_pairs={{0,11},{1,4},{2,9},{3,6},{4,15},{5,0},{6,13},{7,2},{8,3},{9,12},{1... | collective-permute-start | bytes 3538952 | tf_op jit(solution)/shard_map/ppermute | solution.py:319
  187.9 36.7 %collective-permute-start.15 = (bf16[2,192,1536]{2,1,0:T(8,128)(2,1)}, bf16[2,192,1536]{2,1,0:T(8,128)(2,1)S(1)}, u32[]{:S(2)}, u32[]{:S(2)}) collective-permute-start(bf16[2,192,1536]{2,1,0:T(8,128)(2,1)} %get-tuple-element.60), channel_id=1, source_target_pairs={{0,15},{1,0},{2,13},{3,2},{4,11},{5,4},{6,9},{7,6},{8,7},{9,8},{10... | collective-permute-start | bytes 3538952 | tf_op jit(solution)/shard_map/ppermute | solution.py:319
  231.9 9.4 %collective-permute-start.16 = (bf16[48,1536]{1,0:T(8,128)(2,1)}, bf16[48,1536]{1,0:T(8,128)(2,1)S(1)}, u32[]{:S(2)}, u32[]{:S(2)}) collective-permute-start(bf16[48,1536]{1,0:T(8,128)(2,1)} %shard_map.122.own), channel_id=1, source_target_pairs={{0,16},{12,28},{16,0},{28,12},{1,17},{13,29},{17,1},{29,13},{2,18}... | collective-permute-start | bytes 442376 | tf_op jit(solution)/shard_map/ppermute | solution.py:390
  256.8 9.3 %collective-permute-start.20 = (bf16[48,2048]{1,0:T(8,128)(2,1)S(1)}, bf16[48,2048]{1,0:T(8,128)(2,1)S(1)}, u32[]{:S(2)}, u32[]{:S(2)}) collective-permute-start(bf16[48,2048]{1,0:T(8,128)(2,1)S(1)} %shard_map.124), channel_id=1, source_target_pairs={{0,20},{12,0},{16,4},{28,16},{1,21},{13,1},{17,5},{29,17},{2,22},{... | collective-permute-start | bytes 589832 | tf_op jit(solution)/shard_map/ppermute | solution.py:408
  258.7 11.7 %collective-permute-start.19 = (bf16[48,2048]{1,0:T(8,128)(2,1)S(1)}, bf16[48,2048]{1,0:T(8,128)(2,1)S(1)}, u32[]{:S(2)}, u32[]{:S(2)}) collective-permute-start(bf16[48,2048]{1,0:T(8,128)(2,1)S(1)} %shard_map.124), channel_id=1, source_target_pairs={{0,4},{12,16},{16,20},{28,0},{1,5},{13,17},{17,21},{29,1},{2,6},{1... | collective-permute-start | bytes 589832 | tf_op jit(solution)/shard_map/ppermute | solution.py:409
  353.1 34.9 %collective-permute-start.38 = (bf16[48,2048]{1,0:T(8,128)(2,1)S(1)}, bf16[48,2048]{1,0:T(8,128)(2,1)S(1)}, u32[]{:S(2)}, u32[]{:S(2)}) collective-permute-start(bf16[48,2048]{1,0:T(8,128)(2,1)S(1)} %shard_map.136), channel_id=1, source_target_pairs={{8,28},{12,0},{24,12},{28,16},{9,29},{13,1},{25,13},{29,17},{10,30... | collective-permute-start | bytes 589832 | tf_op jit(solution)/shard_map/ppermute | solution.py:408
  354.4 37.8 %collective-permute-start.37 = (bf16[48,2048]{1,0:T(8,128)(2,1)S(1)}, bf16[48,2048]{1,0:T(8,128)(2,1)S(1)}, u32[]{:S(2)}, u32[]{:S(2)}) collective-permute-start(bf16[48,2048]{1,0:T(8,128)(2,1)S(1)} %shard_map.136), channel_id=1, source_target_pairs={{8,12},{12,16},{24,28},{28,0},{9,13},{13,17},{25,29},{29,1},{10,14... | collective-permute-start | bytes 589832 | tf_op jit(solution)/shard_map/ppermute | solution.py:409
  422.8 11.8 %collective-permute-start.43 = (bf16[48,2048]{1,0:T(8,128)(2,1)S(1)}, bf16[48,2048]{1,0:T(8,128)(2,1)S(1)}, u32[]{:S(2)}, u32[]{:S(2)}) collective-permute-start(bf16[48,2048]{1,0:T(8,128)(2,1)S(1)} %shard_map.140), channel_id=1, source_target_pairs={{0,4},{12,16},{16,20},{28,0},{1,5},{13,17},{17,21},{29,1},{2,6},{1... | collective-permute-start | bytes 589832 | tf_op jit(solution)/shard_map/ppermute | solution.py:409
  518.8 34.1 %collective-permute-start.62 = (bf16[48,2048]{1,0:T(8,128)(2,1)S(1)}, bf16[48,2048]{1,0:T(8,128)(2,1)}, u32[]{:S(2)}, u32[]{:S(2)}) collective-permute-start(bf16[48,2048]{1,0:T(8,128)(2,1)S(1)} %shard_map.152), channel_id=1, source_target_pairs={{8,28},{12,0},{24,12},{28,16},{9,29},{13,1},{25,13},{29,17},{10,30... | collective-permute-start | bytes 589832 | tf_op jit(solution)/shard_map/ppermute | solution.py:408
  520.1 37.4 %collective-permute-start.61 = (bf16[48,2048]{1,0:T(8,128)(2,1)S(1)}, bf16[48,2048]{1,0:T(8,128)(2,1)}, u32[]{:S(2)}, u32[]{:S(2)}) collective-permute-start(bf16[48,2048]{1,0:T(8,128)(2,1)S(1)} %shard_map.152), channel_id=1, source_target_pairs={{8,12},{12,16},{24,28},{28,0},{9,13},{13,17},{25,29},{29,1},{10,14... | collective-permute-start | bytes 589832 | tf_op jit(solution)/shard_map/ppermute | solution.py:409
  (90 other events, 1178.2 us)

commit v11 on v10

--- a/solution.py
+++ b/solution.py
@@ -10,8 +10,7 @@
 
 HDIM = 128
 FB = 8
-STREAMS = 1
-ITEMS = 2
+ITEMS = 4
 ROWBLOCK = 256
 CHUNK = 384
 WINDOW = 512
@@ -54,14 +53,29 @@
     )(place, slab)
 
 
-def project_kernel(tick, tiles, tilew, n_y, scalars, mine, other, gains, *rest):
-    weights, (out, normed, held, sems) = rest[:-4], rest[-4:]
+def core_here():
+    return lax.axis_index("tensor") % 2
+
+
+def phase_at(tick):
+    n_spot = lax.axis_size("spot")
+    return (tick >= lax.axis_index("spot") + n_spot).astype(jnp.int32)
+
+
+def item_at(tick):
+    layer = lax.axis_index("zone") * lax.axis_size("spot") + lax.axis_index("spot")
+    return jnp.clip(tick - layer, 0, ITEMS - 1)
+
+
+def project_kernel(tick, tiles, tilew, n_y, table, mine, other, gains, *rest):
+    weights, (out, normed, held, scalars, sems) = rest[:-5], rest[-5:]
     rows, half = mine.shape
     width = 2 * half
     shard = half // n_y
     chunks, size, cdev = held.shape
     per = size // tilew
-    core, phase = scalars[0], scalars[1 + tick]
+    core, phase = core_here(), phase_at(tick)
+    lookup = pltpu.make_async_copy(table, scalars, sems.at[tiles])
 
     def fetch(n):
         target = held.at[n // per, pl.ds(n % per * tilew, tilew)]
@@ -69,6 +83,8 @@
 
     for n in range(tiles):
         fetch(n).start()
+        if n == 0:
+            lookup.start()
 
     here = mine[...].astype(jnp.float32)
     there = other[...].astype(jnp.float32)
@@ -87,14 +103,14 @@
     normed[:, width:] = jnp.zeros((rows, WINDOW), jnp.float32)
 
     along = CHUNK // tilew
-    base = scalars.shape[0] - 2 * tiles
+    lookup.wait()
     lane = lax.broadcasted_iota(jnp.int32, (rows, CHUNK), 1)
 
     def spread(j):
         value = jnp.zeros((rows, CHUNK), jnp.float32)
         for a in range(along):
-            start = scalars[base + j * along + a] * FB
-            count = scalars[base + tiles + j * along + a] * FB
+            start = scalars[j * along + a] * FB
+            count = scalars[tiles + j * along + a] * FB
             aligned = start // 128 * 128
             window = normed[:, pl.ds(pl.multiple_of(aligned, 128), WINDOW)]
             put = a * tilew
@@ -114,7 +130,7 @@
     out[...] = acc.astype(jnp.bfloat16)
 
 
-def project(tick, tiles, tilew, n_y, scalars, mine, other, gains, weights):
+def project(tick, tiles, tilew, n_y, table, mine, other, gains, weights):
     rows, half = mine.shape
     cdev = weights[0].shape[2]
     depth = tiles * tilew
@@ -122,32 +138,33 @@
     vmem = pl.BlockSpec(memory_space=pltpu.VMEM)
     return pl.pallas_call(
         functools.partial(project_kernel, tick, tiles, tilew, n_y),
-        in_specs=[pl.BlockSpec(memory_space=pltpu.SMEM)]
+        in_specs=[pl.BlockSpec(memory_space=pltpu.HBM)]
         + [vmem] * 3
         + [pl.BlockSpec(memory_space=pltpu.HBM)] * len(weights),
         out_specs=vmem,
         scratch_shapes=[
             pltpu.VMEM((rows, 2 * half + WINDOW), jnp.float32),
             pltpu.VMEM((depth // size, size, cdev), jnp.bfloat16),
-            pltpu.SemaphoreType.DMA((tiles,)),
+            pltpu.SMEM(table.shape, jnp.int32),
+            pltpu.SemaphoreType.DMA((tiles + 1,)),
         ],
         out_shape=jax.ShapeDtypeStruct((rows, cdev), jnp.bfloat16),
         compiler_params=pltpu.CompilerParams(vmem_limit_bytes=VMEM if tick else WHOLE_VMEM),
         cost_estimate=pl.CostEstimate(
             flops=2 * rows * depth * cdev, bytes_accessed=2 * depth * cdev, transcendentals=0
         ),
-    )(scalars, mine, other, gains, *weights)
-
-
-def attend_kernel(steps, brow, kvlocal, groups, n_y, item_at, scalars, own, sent, spans, ckeys, cvals, wo, theirs, ours, attn, kheld, vheld, held, sems):
+    )(table, mine, other, gains, *weights)
+
+
+def attend_kernel(steps, brow, kvlocal, groups, n_y, tick, own, sent, spans, ckeys, cvals, wo, theirs, ours, attn, kheld, vheld, held, sems):
     rows = steps * brow
     length = ckeys.shape[1]
     scale = 1.0 / HDIM**0.5
     qdim = kvlocal * groups * HDIM
     kvdim = kvlocal * HDIM
     shard = held.shape[2]
-    core = scalars[0]
-    item = scalars[item_at]
+    core = core_here()
+    item = item_at(tick)
     first = pl.multiple_of(item * brow, brow)
     gets = [
         pltpu.make_async_copy(ckeys.at[pl.ds(first, brow)], kheld, sems.at[2 * n_y]),
@@ -219,7 +236,7 @@
         target[:, at : at + shard] = product.astype(jnp.bfloat16)
 
 
-def attend(item_at, steps, brow, n_y, scalars, own, sent, spans, keys, values, wo):
+def attend(tick, steps, brow, n_y, own, sent, spans, keys, values, wo):
     rows, cdev = own.shape
     _, qdim, width = wo.shape
     length, kvdim = keys.shape[1:]
@@ -228,9 +245,8 @@
     shard = width // (2 * n_y)
     vmem = pl.BlockSpec(memory_space=pltpu.VMEM)
     return pl.pallas_call(
-        functools.partial(attend_kernel, steps, brow, kvlocal, groups, n_y, item_at),
-        in_specs=[pl.BlockSpec(memory_space=pltpu.SMEM)]
-        + [vmem] * 3
+        functools.partial(attend_kernel, steps, brow, kvlocal, groups, n_y, tick),
+        in_specs=[vmem] * 3
         + [pl.BlockSpec(memory_space=pltpu.HBM)] * 3,
         out_specs=[vmem] * 2,
         scratch_shapes=[
@@ -245,7 +261,7 @@
         cost_estimate=pl.CostEstimate(
             flops=2 * rows * qdim * width, bytes_accessed=2 * qdim * width, transcendentals=0
         ),
-    )(scalars, own, sent, spans, keys, values, wo)
+    )(own, sent, spans, keys, values, wo)
 
 
 def join_kernel(part, moved, mine, out):
@@ -253,20 +269,20 @@
     out[...] = (mine[...].astype(jnp.float32) + total).astype(jnp.bfloat16)
 
 
-def choose_kernel(flag, near, far, out):
-    out[...] = jnp.where(flag[0] == 1, near[...], far[...])
-
-
-def in_vmem(kernel, arrays, flag=None):
+def choose_kernel(tick, near, far, out):
+    at_home = phase_at(tick) == lax.axis_index("zone")
+    out[...] = jnp.where(at_home, near[...], far[...])
+
+
+def in_vmem(kernel, *arrays):
     vmem = pl.BlockSpec(memory_space=pltpu.VMEM)
-    scalar = [] if flag is None else [flag.astype(jnp.int32)[None]]
     return pl.pallas_call(
         kernel,
-        in_specs=[pl.BlockSpec(memory_space=pltpu.SMEM)] * len(scalar) + [vmem] * len(arrays),
+        in_specs=[vmem] * len(arrays),
         out_specs=vmem,
         out_shape=jax.ShapeDtypeStruct(arrays[0].shape, jnp.bfloat16),
         compiler_params=pltpu.CompilerParams(vmem_limit_bytes=VMEM),
-    )(*scalar, *arrays)
+    )(*arrays)
 
 
 def per_device(
@@ -293,8 +309,7 @@
     half = n_y * shard
     steps = step_inputs.shape[0]
     seqs, length = cache_keys.shape[1:3]
-    n_item = STREAMS * ITEMS
-    brow = seqs // n_item
+    brow = seqs // ITEMS
     rows = steps * brow
     ticks = layers + ITEMS - 1
     zone = lax.axis_index("zone")
@@ -340,17 +355,13 @@
     sources = sources + (offset[:, 1] ^ tpos ^ sender * all_t) + zone * tiles
     starts = (ends - tile_lengths)[sources]
     counts = tile_lengths[sources]
-    tick_ids = jnp.arange(ticks, dtype=jnp.int32)
-    phases = (tick_ids >= spot + n_spot).astype(jnp.int32)
-    turns = jnp.clip(tick_ids - layer, 0, ITEMS - 1)
-    turns = jnp.concatenate([turns + stream * ITEMS for stream in range(STREAMS)])
-    scalars = jnp.concatenate([core[None], phases, turns, starts, counts]).astype(jnp.int32)
+    table = jnp.concatenate([starts, counts]).astype(jnp.int32)
     flip = [(z, 1 - z) for z in range(2)]
     swapped = lax.ppermute(norm_gain, "zone", flip)
     gains = jnp.concatenate(
         [jnp.where(zone == 0, norm_gain, swapped), jnp.where(zone == 0, swapped, norm_gain)]
     )
-    spans = jnp.repeat(cache_lengths, length).reshape(n_item, 1, brow * length)
+    spans = jnp.repeat(cache_lengths, length).reshape(ITEMS, 1, brow * length)
     axes = ("zone", "spot", "tensor")
 
     def spots(tick):
@@ -370,50 +381,46 @@
         )
 
     across = [(t, t ^ 1) for t in range(n_tensor)]
-    shown = step_inputs.reshape(steps, n_item, brow, n_y, 2, shard)
+    shown = step_inputs.reshape(steps, ITEMS, brow, n_y, 2, shard)
     records = []
-    for stream in range(STREAMS):
-        arrived, record = None, []
-        for tick in range(ticks):
-            if tick < ITEMS:
-                item = stream * ITEMS + tick
-                fresh = shown[:, item].reshape(rows, n_y, 2, shard)
-                mine = lax.dynamic_index_in_dim(fresh, core, 2, False).reshape(rows, half)
-                mine = jnp.where(spot == 0, mine, arrived if tick else 0)
-            else:
-                mine = arrived
-            if tick:
-                other = lax.ppermute(mine, "tensor", across)
-            else:
-                other = lax.dynamic_index_in_dim(fresh, 1 - core, 2, False).reshape(rows, half)
-            own = project(tick, tiles, tilew, n_y, scalars, mine, other, gains, weights)
-            sent = lax.ppermute(own, ("zone", "spot"), mirror(tick))
-            item_at = 1 + ticks + stream * ticks + tick
-            theirs, ours = attend(
-                item_at, steps, brow, n_y, scalars, own, sent, spans, cache_keys[0], cache_values[0], wo_rollout
-            )
-            moved = lax.ppermute(theirs, "tensor", across)
-            part = (ours.astype(jnp.float32) + moved.astype(jnp.float32)).astype(jnp.bfloat16)
-            bit = 2
-            while bit < n_tensor:
-                moved = lax.ppermute(part, "tensor", [(t, t ^ bit) for t in range(n_tensor)])
-                bit = bit * 2
-                if bit < n_tensor:
-                    part = part.astype(jnp.float32) + moved.astype(jnp.float32)
-                    part = part.astype(jnp.bfloat16)
-            after = in_vmem(join_kernel, [part, moved, mine])
-            record.append(after)
-            if tick + 1 < ticks:
-                at_home = phases[tick + 1] == zone
-                far = lax.ppermute(after, ("zone", "spot"), hop(tick, 1))
-                near = lax.ppermute(after, ("zone", "spot"), hop(tick, 0))
-                arrived = in_vmem(choose_kernel, [near, far], at_home)
-        for item in range(ITEMS):
-            value = jnp.zeros((rows, half), jnp.bfloat16)
-            for tick in range(item, ticks):
-                value = jnp.where(layer == tick - item, record[tick], value)
-            value = lax.dynamic_slice_in_dim(value, tpos // 2 * shard, shard, 1)
-            records.append(value.astype(jnp.float32).reshape(steps, brow, shard))
+    arrived, record = None, []
+    for tick in range(ticks):
+        if tick < ITEMS:
+            fresh = shown[:, tick].reshape(rows, n_y, 2, shard)
+            mine = lax.dynamic_index_in_dim(fresh, core, 2, False).reshape(rows, half)
+            mine = jnp.where(spot == 0, mine, arrived if tick else 0)
+        else:
+            mine = arrived
+        if tick:
+            other = lax.ppermute(mine, "tensor", across)
+        else:
+            other = lax.dynamic_index_in_dim(fresh, 1 - core, 2, False).reshape(rows, half)
+        own = project(tick, tiles, tilew, n_y, table, mine, other, gains, weights)
+        sent = lax.ppermute(own, ("zone", "spot"), mirror(tick))
+        theirs, ours = attend(
+            tick, steps, brow, n_y, own, sent, spans, cache_keys[0], cache_values[0], wo_rollout
+        )
+        moved = lax.ppermute(theirs, "tensor", across)
+        part = (ours.astype(jnp.float32) + moved.astype(jnp.float32)).astype(jnp.bfloat16)
+        bit = 2
+        while bit < n_tensor:
+            moved = lax.ppermute(part, "tensor", [(t, t ^ bit) for t in range(n_tensor)])
+            bit = bit * 2
+            if bit < n_tensor:
+                part = part.astype(jnp.float32) + moved.astype(jnp.float32)
+                part = part.astype(jnp.bfloat16)
+        after = in_vmem(join_kernel, part, moved, mine)
+        record.append(after)
+        if tick + 1 < ticks:
+            far = lax.ppermute(after, ("zone", "spot"), hop(tick, 1))
+            near = lax.ppermute(after, ("zone", "spot"), hop(tick, 0))
+            arrived = in_vmem(functools.partial(choose_kernel, tick + 1), near, far)
+    for item in range(ITEMS):
+        value = jnp.zeros((rows, half), jnp.bfloat16)
+        for tick in range(item, ticks):
+            value = jnp.where(layer == tick - item, record[tick], value)
+        value = lax.dynamic_slice_in_dim(value, tpos // 2 * shard, shard, 1)
+        records.append(value.astype(jnp.float32).reshape(steps, brow, shard))
     return jnp.concatenate(records, axis=1)[None]
 
 

time: 597 us -> 566 us (0.948)
  waiting for transfers between devices: 320 us -> 307 us
  starting transfers between devices: 124 us -> 112 us
    ppermute x8 -> x10, waiting for transfers between devices: 73.7 us -> 1.76 us  [per_device(): far = lax.ppermute(after, ('zone', 'spot'), hop(tick, 1))]
    ppermute x15, starting transfers between devices: 74.5 us -> 43.6 us  [exchange(): return lax.ppermute(piece, ('spot', 'tensor'), pairs)]
    ppermute x9 -> x11, waiting for transfers between devices: 32 us -> 59.6 us  [per_device(): sent = lax.ppermute(own, ('zone', 'spot'), mirror(tick))]
    ppermute x15, waiting for transfers between devices: 105 us -> 132 us  [exchange(): return lax.ppermute(piece, ('spot', 'tensor'), pairs)]
    ppermute x8 -> x10, waiting for transfers between devices: 26.2 us -> 43.3 us  [per_device(): near = lax.ppermute(after, ('zone', 'spot'), hop(tick, 0))]
    ppermute x9 -> x11, waiting for transfers between devices: 59 us -> 43.9 us  [per_device(): lax.ppermute(part, 'tensor', [(t, t ^ bit) for t in range(n_tensor)])]
    ppermute x8 -> x10, starting transfers between devices: 12.9 us -> 23.7 us  [per_device(): far = lax.ppermute(after, ('zone', 'spot'), hop(tick, 1))]
    pallas_call x9 -> x11, Pallas kernels: 41.7 us -> 44.6 us  [attend(): pl.pallas_call(functools.partial(attend_kernel, steps, brow, kvlocal, gro...]
  transfers between devices with their start and end apart: 67 -> 79, of which waited for: 50 -> 67; matrix products, arithmetic and copies ran while one was open for 2% -> 2% of each run, Pallas kernels for 5% -> 6%
where the time goes in v11:
time: 566 us; the launch traced here: 559 us
  waiting for transfers between devices  307 us (54%)
  Pallas kernels  125 us (22%)
  starting transfers between devices  112 us (20%)
  local copies, waits for them, and re-layouts  7.35 us (1%)
  other arithmetic  6.87 us (1%)
    ppermute x15, waiting for transfers between devices, exchange(): return lax.ppermute(piece, ('spot', 'tensor'), pairs)  132 us
    ppermute x11, waiting for transfers between devices, per_device(): sent = lax.ppermute(own, ('zone', 'spot'), mirror(tick))  59.6 us
    pallas_call x11, Pallas kernels, project(): pl.pallas_call(functools.partial(project_kernel, tick, tiles, tilew, n_y)...  48.9 us
    pallas_call x11, Pallas kernels, attend(): pl.pallas_call(functools.partial(attend_kernel, steps, brow, kvlocal, gro...  44.6 us
    ppermute x11, waiting for transfers between devices, per_device(): lax.ppermute(part, 'tensor', [(t, t ^ bit) for t in range(n_tensor)])  43.9 us
    ppermute x15, starting transfers between devices, exchange(): return lax.ppermute(piece, ('spot', 'tensor'), pairs)  43.6 us
    ppermute x10, waiting for transfers between devices, per_device(): near = lax.ppermute(after, ('zone', 'spot'), hop(tick, 0))  43.3 us
    pallas_call x4, Pallas kernels, sort_slab(): pl.pallas_call(functools.partial(sort_kernel, layers), grid_spec=pltpu.Pr...  30.8 us
  transfers between devices with their start and end apart: 79, of which 67 were waited for; matrix products, arithmetic and copies ran while one was open for 2% of the time, Pallas kernels for 6%

profile of v11, /device:TPU:0, one launch (start us, length us, event | category | flops | bytes accessed | tf_op | source)
XLA Modules:
  0.0 559.3 jit_solution(14782953113486480501)
XLA Ops:
  4.7 7.7 %shard_map.118 = (bf16[2,192,1536]{2,1,0:T(8,128)(2,1)}, bf16[2,192,1536]{2,1,0:T(8,128)(2,1)}, bf16[2,192,1536]{2,1,0:T(8,128)(2,1)}, bf16[2,192,1536]{2,1,0:T(8,128)(2,1)}) custom-call(s32[2]{0:T(128)} %pad_add_fusion.1.place, bf16[1536,6144]{1,0:T(8,128)(2,1)} %slab.7), custom_call_target="tpu_custom_call" | custom-call | flops 1207959552 | bytes 9437184 | tf_op jit(solution)/shard_map/pallas_call | solution.py:40
  15.9 7.7 %shard_map.119 = (bf16[2,192,1536]{2,1,0:T(8,128)(2,1)}, bf16[2,192,1536]{2,1,0:T(8,128)(2,1)}, bf16[2,192,1536]{2,1,0:T(8,128)(2,1)}, bf16[2,192,1536]{2,1,0:T(8,128)(2,1)}) custom-call(s32[2]{0:T(128)} %pad_add_fusion.1.place, bf16[1536,6144]{1,0:T(8,128)(2,1)} %slab.7), custom_call_target="tpu_custom_call" | custom-call | flops 1207959552 | bytes 9437184 | tf_op jit(solution)/shard_map/pallas_call | solution.py:40
  26.5 7.7 %shard_map.120 = (bf16[2,192,1536]{2,1,0:T(8,128)(2,1)}, bf16[2,192,1536]{2,1,0:T(8,128)(2,1)}, bf16[2,192,1536]{2,1,0:T(8,128)(2,1)}, bf16[2,192,1536]{2,1,0:T(8,128)(2,1)}) custom-call(s32[2]{0:T(128)} %pad_add_fusion.1.place, bf16[1536,6144]{1,0:T(8,128)(2,1)} %slab.7), custom_call_target="tpu_custom_call" | custom-call | flops 1207959552 | bytes 9437184 | tf_op jit(solution)/shard_map/pallas_call | solution.py:40
  41.1 25.9 %collective-permute-start.6 = (bf16[2,192,1536]{2,1,0:T(8,128)(2,1)}, bf16[2,192,1536]{2,1,0:T(8,128)(2,1)}, u32[]{:S(2)}, u32[]{:S(2)}) collective-permute-start(bf16[2,192,1536]{2,1,0:T(8,128)(2,1)} %get-tuple-element.54), channel_id=1, source_target_pairs={{0,10},{1,5},{2,8},{3,7},{4,14},{5,1},{6,12},{7,3},{8,2},{9,13},{1... | collective-permute-start | bytes 3538952 | tf_op jit(solution)/shard_map/ppermute | solution.py:334
  72.5 60.1 %collective-permute-done.5.rest_5_ = bf16[2,192,1536]{2,1,0:T(8,128)(2,1)} collective-permute-done((bf16[2,192,1536]{2,1,0:T(8,128)(2,1)}, bf16[2,192,1536]{2,1,0:T(8,128)(2,1)}, u32[]{:S(2)}, u32[]{:S(2)}) %collective-permute-start.5) | collective-permute-done | bytes 1179680 | tf_op jit(solution)/shard_map/ppermute | solution.py:334
  136.9 7.8 %shard_map.121 = (bf16[2,192,1536]{2,1,0:T(8,128)(2,1)}, bf16[2,192,1536]{2,1,0:T(8,128)(2,1)}, bf16[2,192,1536]{2,1,0:T(8,128)(2,1)}, bf16[2,192,1536]{2,1,0:T(8,128)(2,1)}) custom-call(s32[2]{0:T(128)} %pad_add_fusion.1.place, bf16[1536,6144]{1,0:T(8,128)(2,1)} %slab.7), custom_call_target="tpu_custom_call" | custom-call | flops 1207959552 | bytes 9437184 | tf_op jit(solution)/shard_map/pallas_call | solution.py:40
  153.2 34.3 %collective-permute-done.10.rest_10_ = bf16[2,192,1536]{2,1,0:T(8,128)(2,1)} collective-permute-done((bf16[2,192,1536]{2,1,0:T(8,128)(2,1)}, bf16[2,192,1536]{2,1,0:T(8,128)(2,1)}, u32[]{:S(2)}, u32[]{:S(2)}) %collective-permute-start.10) | collective-permute-done | bytes 1179680 | tf_op jit(solution)/shard_map/ppermute | solution.py:334
  188.2 19.6 %collective-permute-done.11.rest_11_ = bf16[2,192,1536]{2,1,0:T(8,128)(2,1)S(1)} collective-permute-done((bf16[2,192,1536]{2,1,0:T(8,128)(2,1)S(1)}, bf16[2,192,1536]{2,1,0:T(8,128)(2,1)S(1)}, u32[]{:S(2)}, u32[]{:S(2)}) %collective-permute-start.11) | collective-permute-done | bytes 1179680 | tf_op jit(solution)/shard_map/ppermute | solution.py:334
  207.8 11.7 %collective-permute-done.15.rest_15_ = bf16[2,192,1536]{2,1,0:T(8,128)(2,1)S(1)} collective-permute-done((bf16[2,192,1536]{2,1,0:T(8,128)(2,1)}, bf16[2,192,1536]{2,1,0:T(8,128)(2,1)S(1)}, u32[]{:S(2)}, u32[]{:S(2)}) %collective-permute-start.15) | collective-permute-done | bytes 1179680 | tf_op jit(solution)/shard_map/ppermute | solution.py:334
  220.5 6.0 %shard_map.122.own = bf16[24,1536]{1,0:T(8,128)(2,1)} custom-call(s32[32]{0:T(128)} %pad_add_fusion.table, bf16[24,2048]{1,0:T(8,128)(2,1)} %bitcast.65, bf16[24,2048]{1,0:T(8,128)(2,1)} %bitcast.73, f32[2,4096]{1,0:T(2,128)} %pad_maximum_fusion.gains, bf16[2,192,1536]{2,1,0:T(8,128)(2,1)} %get-tuple-element.88.rest_0_, bf16[2,192,1536]{2,1,0:T(8,128)(2,1)} %copy-done.1, ...), custom_call_target="tpu_custom_call" | custom-call | flops 226492416 | bytes 9437184 | tf_op jit(solution)/shard_map/pallas_call | solution.py:139
  227.2 5.2 collective-permute-done.16.sent
  248.5 6.4 %collective-permute-done.19.near = bf16[24,2048]{1,0:T(8,128)(2,1)S(1)} collective-permute-done((bf16[24,2048]{1,0:T(8,128)(2,1)S(1)}, bf16[24,2048]{1,0:T(8,128)(2,1)S(1)}, u32[]{:S(2)}, u32[]{:S(2)}) %collective-permute-start.19) | collective-permute-done | bytes 98336 | tf_op jit(solution)/shard_map/ppermute | solution.py:416
  262.4 5.7 %collective-permute-done.22.sent = bf16[24,1536]{1,0:T(8,128)(2,1)S(1)} collective-permute-done((bf16[24,1536]{1,0:T(8,128)(2,1)S(1)}, bf16[24,1536]{1,0:T(8,128)(2,1)S(1)}, u32[]{:S(2)}, u32[]{:S(2)}) %collective-permute-start.22) | collective-permute-done | bytes 73760 | tf_op jit(solution)/shard_map/ppermute | solution.py:399
  293.7 5.2 collective-permute-done.28.sent
  324.5 5.2 collective-permute-done.34.sent
  355.4 5.6 collective-permute-done.40.sent
  386.6 5.5 collective-permute-done.46.sent
  417.7 5.4 collective-permute-done.52.sent
  448.8 5.7 %collective-permute-done.58.sent = bf16[24,1536]{1,0:T(8,128)(2,1)S(1)} collective-permute-done((bf16[24,1536]{1,0:T(8,128)(2,1)S(1)}, bf16[24,1536]{1,0:T(8,128)(2,1)S(1)}, u32[]{:S(2)}, u32[]{:S(2)}) %collective-permute-start.58) | collective-permute-done | bytes 73760 | tf_op jit(solution)/shard_map/ppermute | solution.py:399
  468.5 4.4 collective-permute-done.61.near
  480.2 5.5 collective-permute-done.64.sent
  511.3 5.4 collective-permute-done.70.sent
  536.6 4.3 shard_map.162.own
  542.4 5.3 collective-permute-done.76.sent
  (307 shorter events, 295.0 us)
Async XLA Ops:
  0.0 25.0 %collective-permute-start = (f32[1,4096]{1,0:T(1,128)}, f32[1,4096]{1,0:T(1,128)S(1)}, u32[]{:S(2)}, u32[]{:S(2)}) collective-permute-start(f32[1,4096]{1,0:T(1,128)} %param.18), channel_id=1, source_target_pairs={{0,16},{16,0},{1,17},{17,1},{2,18},{18,2},{3,19},{19,3},{4,20},{20... | collective-permute-start | bytes 49160 | tf_op jit(solution)/shard_map/ppermute | solution.py:360
  12.4 28.7 %collective-permute-start.1 = (bf16[2,192,1536]{2,1,0:T(8,128)(2,1)}, bf16[2,192,1536]{2,1,0:T(8,128)(2,1)S(1)}, u32[]{:S(2)}, u32[]{:S(2)}) collective-permute-start(bf16[2,192,1536]{2,1,0:T(8,128)(2,1)} %get-tuple-element.50), channel_id=1, source_target_pairs={{0,4},{1,11},{2,6},{3,9},{4,0},{5,15},{6,2},{7,13},{8,12},{9,3},{1... | collective-permute-start | bytes 3538952 | tf_op jit(solution)/shard_map/ppermute | solution.py:334
  13.9 53.1 %collective-permute-start.2 = (bf16[2,192,1536]{2,1,0:T(8,128)(2,1)}, bf16[2,192,1536]{2,1,0:T(8,128)(2,1)}, u32[]{:S(2)}, u32[]{:S(2)}) collective-permute-start(bf16[2,192,1536]{2,1,0:T(8,128)(2,1)} %get-tuple-element.51), channel_id=1, source_target_pairs={{0,8},{1,7},{2,10},{3,5},{4,12},{5,3},{6,14},{7,1},{8,0},{9,15},{1... | collective-permute-start | bytes 3538952 | tf_op jit(solution)/shard_map/ppermute | solution.py:334
  15.4 53.0 %collective-permute-start.3 = (bf16[2,192,1536]{2,1,0:T(8,128)(2,1)}, bf16[2,192,1536]{2,1,0:T(8,128)(2,1)}, u32[]{:S(2)}, u32[]{:S(2)}) collective-permute-start(bf16[2,192,1536]{2,1,0:T(8,128)(2,1)} %get-tuple-element.47), channel_id=1, source_target_pairs={{0,12},{1,3},{2,14},{3,1},{4,8},{5,7},{6,10},{7,5},{8,4},{9,11},{1... | collective-permute-start | bytes 3538952 | tf_op jit(solution)/shard_map/ppermute | solution.py:334
  23.5 44.9 %collective-permute-start.4 = (bf16[2,192,1536]{2,1,0:T(8,128)(2,1)}, bf16[2,192,1536]{2,1,0:T(8,128)(2,1)}, u32[]{:S(2)}, u32[]{:S(2)}) collective-permute-start(bf16[2,192,1536]{2,1,0:T(8,128)(2,1)} %get-tuple-element.52), channel_id=1, source_target_pairs={{0,2},{1,13},{2,0},{3,15},{4,6},{5,9},{6,4},{7,11},{8,10},{9,5},{1... | collective-permute-start | bytes 3538952 | tf_op jit(solution)/shard_map/ppermute | solution.py:334
  25.0 107.5 %collective-permute-start.5 = (bf16[2,192,1536]{2,1,0:T(8,128)(2,1)}, bf16[2,192,1536]{2,1,0:T(8,128)(2,1)}, u32[]{:S(2)}, u32[]{:S(2)}) collective-permute-start(bf16[2,192,1536]{2,1,0:T(8,128)(2,1)} %get-tuple-element.53), channel_id=1, source_target_pairs={{0,6},{1,9},{2,4},{3,11},{4,2},{5,13},{6,0},{7,15},{8,14},{9,1},{1... | collective-permute-start | bytes 3538952 | tf_op jit(solution)/shard_map/ppermute | solution.py:334
  41.1 103.6 %collective-permute-start.6 = (bf16[2,192,1536]{2,1,0:T(8,128)(2,1)}, bf16[2,192,1536]{2,1,0:T(8,128)(2,1)}, u32[]{:S(2)}, u32[]{:S(2)}) collective-permute-start(bf16[2,192,1536]{2,1,0:T(8,128)(2,1)} %get-tuple-element.54), channel_id=1, source_target_pairs={{0,10},{1,5},{2,8},{3,7},{4,14},{5,1},{6,12},{7,3},{8,2},{9,13},{1... | collective-permute-start | bytes 3538952 | tf_op jit(solution)/shard_map/ppermute | solution.py:334
  67.0 79.7 %collective-permute-start.7 = (bf16[2,192,1536]{2,1,0:T(8,128)(2,1)}, bf16[2,192,1536]{2,1,0:T(8,128)(2,1)}, u32[]{:S(2)}, u32[]{:S(2)}) collective-permute-start(bf16[2,192,1536]{2,1,0:T(8,128)(2,1)} %get-tuple-element.87), channel_id=1, source_target_pairs={{0,14},{1,15},{2,12},{3,13},{4,10},{5,11},{6,8},{7,9},{8,6},{9,7},... | collective-permute-start | bytes 3538952 | tf_op jit(solution)/shard_map/ppermute | solution.py:334
  68.4 79.6 %collective-permute-start.8 = (bf16[2,192,1536]{2,1,0:T(8,128)(2,1)}, bf16[2,192,1536]{2,1,0:T(8,128)(2,1)}, u32[]{:S(2)}, u32[]{:S(2)}) collective-permute-start(bf16[2,192,1536]{2,1,0:T(8,128)(2,1)} %get-tuple-element.56), channel_id=1, source_target_pairs={{0,1},{1,14},{2,3},{3,12},{4,5},{5,10},{6,7},{7,8},{8,9},{9,6},{10... | collective-permute-start | bytes 3538952 | tf_op jit(solution)/shard_map/ppermute | solution.py:334
  68.4 84.3 %collective-permute-start.9 = (bf16[2,192,1536]{2,1,0:T(8,128)(2,1)}, bf16[2,192,1536]{2,1,0:T(8,128)(2,1)}, u32[]{:S(2)}, u32[]{:S(2)}) collective-permute-start(bf16[2,192,1536]{2,1,0:T(8,128)(2,1)} %get-tuple-element.57), channel_id=1, source_target_pairs={{0,5},{1,10},{2,7},{3,8},{4,1},{5,14},{6,3},{7,12},{8,13},{9,2},{1... | collective-permute-start | bytes 3538952 | tf_op jit(solution)/shard_map/ppermute | solution.py:334
  132.6 54.9 %collective-permute-start.10 = (bf16[2,192,1536]{2,1,0:T(8,128)(2,1)}, bf16[2,192,1536]{2,1,0:T(8,128)(2,1)}, u32[]{:S(2)}, u32[]{:S(2)}) collective-permute-start(bf16[2,192,1536]{2,1,0:T(8,128)(2,1)} %get-tuple-element.58), channel_id=1, source_target_pairs={{0,9},{1,6},{2,11},{3,4},{4,13},{5,2},{6,15},{7,0},{8,1},{9,14},{1... | collective-permute-start | bytes 3538952 | tf_op jit(solution)/shard_map/ppermute | solution.py:334
  144.7 63.1 %collective-permute-start.11 = (bf16[2,192,1536]{2,1,0:T(8,128)(2,1)S(1)}, bf16[2,192,1536]{2,1,0:T(8,128)(2,1)S(1)}, u32[]{:S(2)}, u32[]{:S(2)}) collective-permute-start(bf16[2,192,1536]{2,1,0:T(8,128)(2,1)S(1)} %copy-done.39), channel_id=1, source_target_pairs={{0,13},{1,2},{2,15},{3,0},{4,9},{5,6},{6,11},{7,4},{8,5},{9,10},{1... | collective-permute-start | bytes 3538952 | tf_op jit(solution)/shard_map/ppermute | solution.py:334
  146.7 61.1 %collective-permute-start.12 = (bf16[2,192,1536]{2,1,0:T(8,128)(2,1)}, bf16[2,192,1536]{2,1,0:T(8,128)(2,1)S(1)}, u32[]{:S(2)}, u32[]{:S(2)}) collective-permute-start(bf16[2,192,1536]{2,1,0:T(8,128)(2,1)} %get-tuple-element.61), channel_id=1, source_target_pairs={{0,3},{1,12},{2,1},{3,14},{4,7},{5,8},{6,5},{7,10},{8,11},{9,4},{1... | collective-permute-start | bytes 3538952 | tf_op jit(solution)/shard_map/ppermute | solution.py:334
  148.0 59.7 %collective-permute-start.13 = (bf16[2,192,1536]{2,1,0:T(8,128)(2,1)}, bf16[2,192,1536]{2,1,0:T(8,128)(2,1)S(1)}, u32[]{:S(2)}, u32[]{:S(2)}) collective-permute-start(bf16[2,192,1536]{2,1,0:T(8,128)(2,1)} %get-tuple-element.62), channel_id=1, source_target_pairs={{0,7},{1,8},{2,5},{3,10},{4,3},{5,12},{6,1},{7,14},{8,15},{9,0},{1... | collective-permute-start | bytes 3538952 | tf_op jit(solution)/shard_map/ppermute | solution.py:334
  152.8 55.0 %collective-permute-start.14 = (bf16[2,192,1536]{2,1,0:T(8,128)(2,1)}, bf16[2,192,1536]{2,1,0:T(8,128)(2,1)S(1)}, u32[]{:S(2)}, u32[]{:S(2)}) collective-permute-start(bf16[2,192,1536]{2,1,0:T(8,128)(2,1)} %get-tuple-element.63), channel_id=1, source_target_pairs={{0,11},{1,4},{2,9},{3,6},{4,15},{5,0},{6,13},{7,2},{8,3},{9,12},{1... | collective-permute-start | bytes 3538952 | tf_op jit(solution)/shard_map/ppermute | solution.py:334
  187.5 32.0 %collective-permute-start.15 = (bf16[2,192,1536]{2,1,0:T(8,128)(2,1)}, bf16[2,192,1536]{2,1,0:T(8,128)(2,1)S(1)}, u32[]{:S(2)}, u32[]{:S(2)}) collective-permute-start(bf16[2,192,1536]{2,1,0:T(8,128)(2,1)} %get-tuple-element.64), channel_id=1, source_target_pairs={{0,15},{1,0},{2,13},{3,2},{4,11},{5,4},{6,9},{7,6},{8,7},{9,8},{10... | collective-permute-start | bytes 3538952 | tf_op jit(solution)/shard_map/ppermute | solution.py:334
  246.9 8.0 %collective-permute-start.19 = (bf16[24,2048]{1,0:T(8,128)(2,1)S(1)}, bf16[24,2048]{1,0:T(8,128)(2,1)S(1)}, u32[]{:S(2)}, u32[]{:S(2)}) collective-permute-start(bf16[24,2048]{1,0:T(8,128)(2,1)S(1)} %shard_map.124), channel_id=1, source_target_pairs={{0,4},{4,8},{8,12},{12,16},{16,20},{20,24},{24,28},{28,0},{1,5},{5... | collective-permute-start | bytes 294920 | tf_op jit(solution)/shard_map/ppermute | solution.py:416
  340.2 8.0 %collective-permute-start.37 = (bf16[24,2048]{1,0:T(8,128)(2,1)S(1)}, bf16[24,2048]{1,0:T(8,128)(2,1)S(1)}, u32[]{:S(2)}, u32[]{:S(2)}) collective-permute-start(bf16[24,2048]{1,0:T(8,128)(2,1)S(1)} %shard_map.136), channel_id=1, source_target_pairs={{0,4},{4,8},{8,12},{12,16},{16,20},{20,24},{24,28},{28,0},{1,5},{5... | collective-permute-start | bytes 294920 | tf_op jit(solution)/shard_map/ppermute | solution.py:416
  371.4 7.9 %collective-permute-start.43 = (bf16[24,2048]{1,0:T(8,128)(2,1)S(1)}, bf16[24,2048]{1,0:T(8,128)(2,1)S(1)}, u32[]{:S(2)}, u32[]{:S(2)}) collective-permute-start(bf16[24,2048]{1,0:T(8,128)(2,1)S(1)} %shard_map.140), channel_id=1, source_target_pairs={{0,4},{4,8},{8,12},{12,16},{16,20},{20,24},{24,28},{28,0},{1,5},{5... | collective-permute-start | bytes 294920 | tf_op jit(solution)/shard_map/ppermute | solution.py:416
  402.5 7.9 %collective-permute-start.49 = (bf16[24,2048]{1,0:T(8,128)(2,1)S(1)}, bf16[24,2048]{1,0:T(8,128)(2,1)S(1)}, u32[]{:S(2)}, u32[]{:S(2)}) collective-permute-start(bf16[24,2048]{1,0:T(8,128)(2,1)S(1)} %shard_map.144), channel_id=1, source_target_pairs={{0,4},{4,8},{8,12},{12,16},{16,20},{20,24},{24,28},{28,0},{1,5},{5... | collective-permute-start | bytes 294920 | tf_op jit(solution)/shard_map/ppermute | solution.py:416
  433.5 8.0 %collective-permute-start.55 = (bf16[24,2048]{1,0:T(8,128)(2,1)S(1)}, bf16[24,2048]{1,0:T(8,128)(2,1)S(1)}, u32[]{:S(2)}, u32[]{:S(2)}) collective-permute-start(bf16[24,2048]{1,0:T(8,128)(2,1)S(1)} %shard_map.148), channel_id=1, source_target_pairs={{0,4},{4,8},{8,12},{12,16},{16,20},{20,24},{24,28},{28,0},{1,5},{5... | collective-permute-start | bytes 294920 | tf_op jit(solution)/shard_map/ppermute | solution.py:416
  464.9 7.9 %collective-permute-start.61 = (bf16[24,2048]{1,0:T(8,128)(2,1)S(1)}, bf16[24,2048]{1,0:T(8,128)(2,1)S(1)}, u32[]{:S(2)}, u32[]{:S(2)}) collective-permute-start(bf16[24,2048]{1,0:T(8,128)(2,1)S(1)} %shard_map.152), channel_id=1, source_target_pairs={{0,4},{4,8},{8,12},{12,16},{16,20},{20,24},{24,28},{28,0},{1,5},{5... | collective-permute-start | bytes 294920 | tf_op jit(solution)/shard_map/ppermute | solution.py:416
  496.0 7.9 %collective-permute-start.67 = (bf16[24,2048]{1,0:T(8,128)(2,1)S(1)}, bf16[24,2048]{1,0:T(8,128)(2,1)S(1)}, u32[]{:S(2)}, u32[]{:S(2)}) collective-permute-start(bf16[24,2048]{1,0:T(8,128)(2,1)S(1)} %shard_map.156), channel_id=1, source_target_pairs={{0,4},{4,8},{8,12},{12,16},{16,20},{20,24},{24,28},{28,0},{1,5},{5... | collective-permute-start | bytes 294920 | tf_op jit(solution)/shard_map/ppermute | solution.py:416
  527.1 8.0 %collective-permute-start.73 = (bf16[24,2048]{1,0:T(8,128)(2,1)S(1)}, bf16[24,2048]{1,0:T(8,128)(2,1)S(1)}, u32[]{:S(2)}, u32[]{:S(2)}) collective-permute-start(bf16[24,2048]{1,0:T(8,128)(2,1)S(1)} %shard_map.160), channel_id=1, source_target_pairs={{0,4},{4,8},{8,12},{12,16},{16,20},{20,24},{24,28},{28,0},{1,5},{5... | collective-permute-start | bytes 294920 | tf_op jit(solution)/shard_map/ppermute | solution.py:416
  (95 other events, 1356.1 us)

commit v12 on v11

--- a/solution.py
+++ b/solution.py
@@ -269,7 +269,11 @@
     out[...] = (mine[...].astype(jnp.float32) + total).astype(jnp.bfloat16)
 
 
-def choose_kernel(tick, near, far, out):
+def copy_kernel(value, out):
+    out[...] = value[...]
+
+
+def choose_kernel(tick, far, near, out):
     at_home = phase_at(tick) == lax.axis_index("zone")
     out[...] = jnp.where(at_home, near[...], far[...])
 
@@ -364,21 +368,19 @@
     spans = jnp.repeat(cache_lengths, length).reshape(ITEMS, 1, brow * length)
     axes = ("zone", "spot", "tensor")
 
-    def spots(tick):
-        return sorted({(tick - i) % n_spot for i in range(ITEMS)})
+    def actives(tick):
+        held = {(tick - i) % n_spot for i in range(ITEMS)}
+        return [(s, int(tick >= s + n_spot)) for s in sorted(held)]
 
     def hop(tick, turn):
         pairs = []
-        for s in spots(tick):
-            for z in range(n_zone):
-                ahead = z if s + 1 < n_spot else 1 - z
-                pairs.append((z * n_spot + s, (ahead ^ turn) * n_spot + (s + 1) % n_spot))
+        for s, z in actives(tick):
+            ahead = z if s + 1 < n_spot else 1 - z
+            pairs.append((z * n_spot + s, (ahead ^ turn) * n_spot + (s + 1) % n_spot))
         return sorted(pairs)
 
     def mirror(tick):
-        return sorted(
-            (z * n_spot + s, (1 - z) * n_spot + s) for s in spots(tick) for z in range(n_zone)
-        )
+        return sorted(((1 - z) * n_spot + s, z * n_spot + s) for s, z in actives(tick))
 
     across = [(t, t ^ 1) for t in range(n_tensor)]
     shown = step_inputs.reshape(steps, ITEMS, brow, n_y, 2, shard)
@@ -413,8 +415,9 @@
         record.append(after)
         if tick + 1 < ticks:
             far = lax.ppermute(after, ("zone", "spot"), hop(tick, 1))
-            near = lax.ppermute(after, ("zone", "spot"), hop(tick, 0))
-            arrived = in_vmem(functools.partial(choose_kernel, tick + 1), near, far)
+            behind = in_vmem(copy_kernel, after)
+            near = lax.ppermute(behind, ("zone", "spot"), hop(tick, 0))
+            arrived = in_vmem(functools.partial(choose_kernel, tick + 1), far, near)
     for item in range(ITEMS):
         value = jnp.zeros((rows, half), jnp.bfloat16)
         for tick in range(item, ticks):

time: 566 us -> 586 us (1.035)
  starting transfers between devices: 112 us -> 140 us
  waiting for transfers between devices: 307 us -> 295 us
    ppermute x11, starting transfers between devices: 14.7 us -> 38.7 us  [per_device(): sent = lax.ppermute(own, ('zone', 'spot'), mirror(tick))]
    ppermute x11, waiting for transfers between devices: 59.6 us -> 36.8 us  [per_device(): sent = lax.ppermute(own, ('zone', 'spot'), mirror(tick))]
    ppermute x10, waiting for transfers between devices: 1.76 us -> 19.9 us  [per_device(): far = lax.ppermute(after, ('zone', 'spot'), hop(tick, 1))]
  transfers between devices with their start and end apart: 79 -> 79, of which waited for: 67 -> 61; matrix products, arithmetic and copies ran while one was open for 2% -> 2% of each run, Pallas kernels for 6% -> 5%
where the time goes in v12:
time: 586 us; the launch traced here: 576 us
  waiting for transfers between devices  295 us (50%)
  starting transfers between devices  140 us (24%)
  Pallas kernels  125 us (21%)
  local copies, waits for them, and re-layouts  7.36 us (1%)
  other arithmetic  6.89 us (1%)
    ppermute x15, waiting for transfers between devices, exchange(): return lax.ppermute(piece, ('spot', 'tensor'), pairs)  132 us
    pallas_call x11, Pallas kernels, project(): pl.pallas_call(functools.partial(project_kernel, tick, tiles, tilew, n_y)...  48.9 us
    pallas_call x11, Pallas kernels, attend(): pl.pallas_call(functools.partial(attend_kernel, steps, brow, kvlocal, gro...  44.6 us
    ppermute x15, starting transfers between devices, exchange(): return lax.ppermute(piece, ('spot', 'tensor'), pairs)  43.8 us
    ppermute x11, waiting for transfers between devices, per_device(): lax.ppermute(part, 'tensor', [(t, t ^ bit) for t in range(n_tensor)])  41.7 us
    ppermute x11, starting transfers between devices, per_device(): sent = lax.ppermute(own, ('zone', 'spot'), mirror(tick))  38.7 us
    ppermute x10, waiting for transfers between devices, per_device(): near = lax.ppermute(behind, ('zone', 'spot'), hop(tick, 0))  37.9 us
    ppermute x11, waiting for transfers between devices, per_device(): sent = lax.ppermute(own, ('zone', 'spot'), mirror(tick))  36.8 us
  transfers between devices with their start and end apart: 79, of which 61 were waited for; matrix products, arithmetic and copies ran while one was open for 2% of the time, Pallas kernels for 5%

profile of v12, /device:TPU:0, one launch (start us, length us, event | category | flops | bytes accessed | tf_op | source)
XLA Modules:
  0.0 576.5 jit_solution(7636056686803514274)
XLA Ops:
  4.6 7.7 %shard_map.118 = (bf16[2,192,1536]{2,1,0:T(8,128)(2,1)}, bf16[2,192,1536]{2,1,0:T(8,128)(2,1)}, bf16[2,192,1536]{2,1,0:T(8,128)(2,1)}, bf16[2,192,1536]{2,1,0:T(8,128)(2,1)}) custom-call(s32[2]{0:T(128)} %pad_add_fusion.1.place, bf16[1536,6144]{1,0:T(8,128)(2,1)} %slab.7), custom_call_target="tpu_custom_call" | custom-call | flops 1207959552 | bytes 9437184 | tf_op jit(solution)/shard_map/pallas_call | solution.py:40
  15.8 7.7 %shard_map.119 = (bf16[2,192,1536]{2,1,0:T(8,128)(2,1)}, bf16[2,192,1536]{2,1,0:T(8,128)(2,1)}, bf16[2,192,1536]{2,1,0:T(8,128)(2,1)}, bf16[2,192,1536]{2,1,0:T(8,128)(2,1)}) custom-call(s32[2]{0:T(128)} %pad_add_fusion.1.place, bf16[1536,6144]{1,0:T(8,128)(2,1)} %slab.7), custom_call_target="tpu_custom_call" | custom-call | flops 1207959552 | bytes 9437184 | tf_op jit(solution)/shard_map/pallas_call | solution.py:40
  26.4 7.7 %shard_map.120 = (bf16[2,192,1536]{2,1,0:T(8,128)(2,1)}, bf16[2,192,1536]{2,1,0:T(8,128)(2,1)}, bf16[2,192,1536]{2,1,0:T(8,128)(2,1)}, bf16[2,192,1536]{2,1,0:T(8,128)(2,1)}) custom-call(s32[2]{0:T(128)} %pad_add_fusion.1.place, bf16[1536,6144]{1,0:T(8,128)(2,1)} %slab.7), custom_call_target="tpu_custom_call" | custom-call | flops 1207959552 | bytes 9437184 | tf_op jit(solution)/shard_map/pallas_call | solution.py:40
  41.0 25.9 %collective-permute-start.6 = (bf16[2,192,1536]{2,1,0:T(8,128)(2,1)}, bf16[2,192,1536]{2,1,0:T(8,128)(2,1)}, u32[]{:S(2)}, u32[]{:S(2)}) collective-permute-start(bf16[2,192,1536]{2,1,0:T(8,128)(2,1)} %get-tuple-element.54), channel_id=1, source_target_pairs={{0,10},{1,5},{2,8},{3,7},{4,14},{5,1},{6,12},{7,3},{8,2},{9,13},{1... | collective-permute-start | bytes 3538952 | tf_op jit(solution)/shard_map/ppermute | solution.py:338
  72.6 59.9 %collective-permute-done.5.rest_5_ = bf16[2,192,1536]{2,1,0:T(8,128)(2,1)} collective-permute-done((bf16[2,192,1536]{2,1,0:T(8,128)(2,1)}, bf16[2,192,1536]{2,1,0:T(8,128)(2,1)}, u32[]{:S(2)}, u32[]{:S(2)}) %collective-permute-start.5) | collective-permute-done | bytes 1179680 | tf_op jit(solution)/shard_map/ppermute | solution.py:338
  136.9 7.8 %shard_map.121 = (bf16[2,192,1536]{2,1,0:T(8,128)(2,1)}, bf16[2,192,1536]{2,1,0:T(8,128)(2,1)}, bf16[2,192,1536]{2,1,0:T(8,128)(2,1)}, bf16[2,192,1536]{2,1,0:T(8,128)(2,1)}) custom-call(s32[2]{0:T(128)} %pad_add_fusion.1.place, bf16[1536,6144]{1,0:T(8,128)(2,1)} %slab.7), custom_call_target="tpu_custom_call" | custom-call | flops 1207959552 | bytes 9437184 | tf_op jit(solution)/shard_map/pallas_call | solution.py:40
  153.1 34.2 %collective-permute-done.10.rest_10_ = bf16[2,192,1536]{2,1,0:T(8,128)(2,1)} collective-permute-done((bf16[2,192,1536]{2,1,0:T(8,128)(2,1)}, bf16[2,192,1536]{2,1,0:T(8,128)(2,1)}, u32[]{:S(2)}, u32[]{:S(2)}) %collective-permute-start.10) | collective-permute-done | bytes 1179680 | tf_op jit(solution)/shard_map/ppermute | solution.py:338
  187.9 19.8 %collective-permute-done.11.rest_11_ = bf16[2,192,1536]{2,1,0:T(8,128)(2,1)S(1)} collective-permute-done((bf16[2,192,1536]{2,1,0:T(8,128)(2,1)}, bf16[2,192,1536]{2,1,0:T(8,128)(2,1)S(1)}, u32[]{:S(2)}, u32[]{:S(2)}) %collective-permute-start.11) | collective-permute-done | bytes 1179680 | tf_op jit(solution)/shard_map/ppermute | solution.py:338
  207.7 12.0 %collective-permute-done.15.rest_15_ = bf16[2,192,1536]{2,1,0:T(8,128)(2,1)S(1)} collective-permute-done((bf16[2,192,1536]{2,1,0:T(8,128)(2,1)}, bf16[2,192,1536]{2,1,0:T(8,128)(2,1)S(1)}, u32[]{:S(2)}, u32[]{:S(2)}) %collective-permute-start.15) | collective-permute-done | bytes 1179680 | tf_op jit(solution)/shard_map/ppermute | solution.py:338
  220.7 6.0 %shard_map.122.own = bf16[24,1536]{1,0:T(8,128)(2,1)} custom-call(s32[32]{0:T(128)} %pad_add_fusion.table, bf16[24,2048]{1,0:T(8,128)(2,1)} %bitcast.65, bf16[24,2048]{1,0:T(8,128)(2,1)} %bitcast.73, f32[2,4096]{1,0:T(2,128)} %pad_maximum_fusion.gains, bf16[2,192,1536]{2,1,0:T(8,128)(2,1)} %get-tuple-element.88.rest_0_, bf16[2,192,1536]{2,1,0:T(8,128)(2,1)} %copy-done.1, ...), custom_call_target="tpu_custom_call" | custom-call | flops 226492416 | bytes 9437184 | tf_op jit(solution)/shard_map/pallas_call | solution.py:139
  228.3 5.9 %collective-permute-done.16.sent = bf16[24,1536]{1,0:T(8,128)(2,1)S(1)} collective-permute-done((bf16[24,1536]{1,0:T(8,128)(2,1)}, bf16[24,1536]{1,0:T(8,128)(2,1)S(1)}, u32[]{:S(2)}, u32[]{:S(2)}) %collective-permute-start.16) | collective-permute-done | bytes 73760 | tf_op jit(solution)/shard_map/ppermute | solution.py:401
  243.9 5.0 collective-permute-done.18.moved
  263.6 5.8 %collective-permute-done.22.sent = bf16[24,1536]{1,0:T(8,128)(2,1)S(1)} collective-permute-done((bf16[24,1536]{1,0:T(8,128)(2,1)S(1)}, bf16[24,1536]{1,0:T(8,128)(2,1)S(1)}, u32[]{:S(2)}, u32[]{:S(2)}) %collective-permute-start.22) | collective-permute-done | bytes 73760 | tf_op jit(solution)/shard_map/ppermute | solution.py:401
  296.8 5.8 %collective-permute-done.28.sent = bf16[24,1536]{1,0:T(8,128)(2,1)S(1)} collective-permute-done((bf16[24,1536]{1,0:T(8,128)(2,1)S(1)}, bf16[24,1536]{1,0:T(8,128)(2,1)S(1)}, u32[]{:S(2)}, u32[]{:S(2)}) %collective-permute-start.28) | collective-permute-done | bytes 73760 | tf_op jit(solution)/shard_map/ppermute | solution.py:401
  329.5 5.9 %collective-permute-done.34.sent = bf16[24,1536]{1,0:T(8,128)(2,1)S(1)} collective-permute-done((bf16[24,1536]{1,0:T(8,128)(2,1)S(1)}, bf16[24,1536]{1,0:T(8,128)(2,1)S(1)}, u32[]{:S(2)}, u32[]{:S(2)}) %collective-permute-start.34) | collective-permute-done | bytes 73760 | tf_op jit(solution)/shard_map/ppermute | solution.py:401
  379.3 5.4 collective-permute-done.43.far
  390.4 10.8 %collective-permute-start.46 = (bf16[24,1536]{1,0:T(8,128)(2,1)S(1)}, bf16[24,1536]{1,0:T(8,128)(2,1)S(1)}, u32[]{:S(2)}, u32[]{:S(2)}) collective-permute-start(bf16[24,1536]{1,0:T(8,128)(2,1)S(1)} %shard_map.147.own), channel_id=1, source_target_pairs={{0,16},{4,20},{24,8},{28,12},{1,17},{5,21},{25,9},{29,13},{2,18},{... | collective-permute-start | bytes 221192 | tf_op jit(solution)/shard_map/ppermute | solution.py:401
  415.6 5.4 collective-permute-done.49.far
  426.8 6.5 %collective-permute-start.52 = (bf16[24,1536]{1,0:T(8,128)(2,1)S(1)}, bf16[24,1536]{1,0:T(8,128)(2,1)S(1)}, u32[]{:S(2)}, u32[]{:S(2)}) collective-permute-start(bf16[24,1536]{1,0:T(8,128)(2,1)S(1)} %shard_map.152.own), channel_id=1, source_target_pairs={{0,16},{4,20},{8,24},{28,12},{1,17},{5,21},{9,25},{29,13},{2,18},{... | collective-permute-start | bytes 221192 | tf_op jit(solution)/shard_map/ppermute | solution.py:401
  447.6 5.4 collective-permute-done.55.far
  458.8 6.7 %collective-permute-start.58 = (bf16[24,1536]{1,0:T(8,128)(2,1)S(1)}, bf16[24,1536]{1,0:T(8,128)(2,1)S(1)}, u32[]{:S(2)}, u32[]{:S(2)}) collective-permute-start(bf16[24,1536]{1,0:T(8,128)(2,1)S(1)} %shard_map.157.own), channel_id=1, source_target_pairs={{0,16},{4,20},{8,24},{12,28},{1,17},{5,21},{9,25},{13,29},{2,18},{... | collective-permute-start | bytes 221192 | tf_op jit(solution)/shard_map/ppermute | solution.py:401
  479.7 10.2 %collective-permute-done.62.near = bf16[24,2048]{1,0:T(8,128)(2,1)S(1)} collective-permute-done((bf16[24,2048]{1,0:T(8,128)(2,1)S(1)}, bf16[24,2048]{1,0:T(8,128)(2,1)S(1)}, u32[]{:S(2)}, u32[]{:S(2)}) %collective-permute-start.62) | collective-permute-done | bytes 98336 | tf_op jit(solution)/shard_map/ppermute | solution.py:419
  511.6 11.0 %collective-permute-done.68.near = bf16[24,2048]{1,0:T(8,128)(2,1)S(1)} collective-permute-done((bf16[24,2048]{1,0:T(8,128)(2,1)S(1)}, bf16[24,2048]{1,0:T(8,128)(2,1)S(1)}, u32[]{:S(2)}, u32[]{:S(2)}) %collective-permute-start.68) | collective-permute-done | bytes 98336 | tf_op jit(solution)/shard_map/ppermute | solution.py:419
  544.1 11.1 %collective-permute-done.74.near = bf16[24,2048]{1,0:T(8,128)(2,1)S(1)} collective-permute-done((bf16[24,2048]{1,0:T(8,128)(2,1)S(1)}, bf16[24,2048]{1,0:T(8,128)(2,1)S(1)}, u32[]{:S(2)}, u32[]{:S(2)}) %collective-permute-start.74) | collective-permute-done | bytes 98336 | tf_op jit(solution)/shard_map/ppermute | solution.py:419
  (315 shorter events, 285.0 us)
Async XLA Ops:
  0.0 25.0 %collective-permute-start = (f32[1,4096]{1,0:T(1,128)}, f32[1,4096]{1,0:T(1,128)S(1)}, u32[]{:S(2)}, u32[]{:S(2)}) collective-permute-start(f32[1,4096]{1,0:T(1,128)} %param.18), channel_id=1, source_target_pairs={{0,16},{16,0},{1,17},{17,1},{2,18},{18,2},{3,19},{19,3},{4,20},{20... | collective-permute-start | bytes 49160 | tf_op jit(solution)/shard_map/ppermute | solution.py:364
  12.3 28.7 %collective-permute-start.1 = (bf16[2,192,1536]{2,1,0:T(8,128)(2,1)}, bf16[2,192,1536]{2,1,0:T(8,128)(2,1)S(1)}, u32[]{:S(2)}, u32[]{:S(2)}) collective-permute-start(bf16[2,192,1536]{2,1,0:T(8,128)(2,1)} %get-tuple-element.50), channel_id=1, source_target_pairs={{0,4},{1,11},{2,6},{3,9},{4,0},{5,15},{6,2},{7,13},{8,12},{9,3},{1... | collective-permute-start | bytes 3538952 | tf_op jit(solution)/shard_map/ppermute | solution.py:338
  13.8 53.1 %collective-permute-start.2 = (bf16[2,192,1536]{2,1,0:T(8,128)(2,1)}, bf16[2,192,1536]{2,1,0:T(8,128)(2,1)}, u32[]{:S(2)}, u32[]{:S(2)}) collective-permute-start(bf16[2,192,1536]{2,1,0:T(8,128)(2,1)} %get-tuple-element.51), channel_id=1, source_target_pairs={{0,8},{1,7},{2,10},{3,5},{4,12},{5,3},{6,14},{7,1},{8,0},{9,15},{1... | collective-permute-start | bytes 3538952 | tf_op jit(solution)/shard_map/ppermute | solution.py:338
  15.4 53.2 %collective-permute-start.3 = (bf16[2,192,1536]{2,1,0:T(8,128)(2,1)}, bf16[2,192,1536]{2,1,0:T(8,128)(2,1)}, u32[]{:S(2)}, u32[]{:S(2)}) collective-permute-start(bf16[2,192,1536]{2,1,0:T(8,128)(2,1)} %get-tuple-element.47), channel_id=1, source_target_pairs={{0,12},{1,3},{2,14},{3,1},{4,8},{5,7},{6,10},{7,5},{8,4},{9,11},{1... | collective-permute-start | bytes 3538952 | tf_op jit(solution)/shard_map/ppermute | solution.py:338
  23.5 45.1 %collective-permute-start.4 = (bf16[2,192,1536]{2,1,0:T(8,128)(2,1)}, bf16[2,192,1536]{2,1,0:T(8,128)(2,1)}, u32[]{:S(2)}, u32[]{:S(2)}) collective-permute-start(bf16[2,192,1536]{2,1,0:T(8,128)(2,1)} %get-tuple-element.52), channel_id=1, source_target_pairs={{0,2},{1,13},{2,0},{3,15},{4,6},{5,9},{6,4},{7,11},{8,10},{9,5},{1... | collective-permute-start | bytes 3538952 | tf_op jit(solution)/shard_map/ppermute | solution.py:338
  25.0 107.5 %collective-permute-start.5 = (bf16[2,192,1536]{2,1,0:T(8,128)(2,1)}, bf16[2,192,1536]{2,1,0:T(8,128)(2,1)}, u32[]{:S(2)}, u32[]{:S(2)}) collective-permute-start(bf16[2,192,1536]{2,1,0:T(8,128)(2,1)} %get-tuple-element.53), channel_id=1, source_target_pairs={{0,6},{1,9},{2,4},{3,11},{4,2},{5,13},{6,0},{7,15},{8,14},{9,1},{1... | collective-permute-start | bytes 3538952 | tf_op jit(solution)/shard_map/ppermute | solution.py:338
  41.0 103.7 %collective-permute-start.6 = (bf16[2,192,1536]{2,1,0:T(8,128)(2,1)}, bf16[2,192,1536]{2,1,0:T(8,128)(2,1)}, u32[]{:S(2)}, u32[]{:S(2)}) collective-permute-start(bf16[2,192,1536]{2,1,0:T(8,128)(2,1)} %get-tuple-element.54), channel_id=1, source_target_pairs={{0,10},{1,5},{2,8},{3,7},{4,14},{5,1},{6,12},{7,3},{8,2},{9,13},{1... | collective-permute-start | bytes 3538952 | tf_op jit(solution)/shard_map/ppermute | solution.py:338
  66.9 79.8 %collective-permute-start.7 = (bf16[2,192,1536]{2,1,0:T(8,128)(2,1)}, bf16[2,192,1536]{2,1,0:T(8,128)(2,1)}, u32[]{:S(2)}, u32[]{:S(2)}) collective-permute-start(bf16[2,192,1536]{2,1,0:T(8,128)(2,1)} %get-tuple-element.87), channel_id=1, source_target_pairs={{0,14},{1,15},{2,12},{3,13},{4,10},{5,11},{6,8},{7,9},{8,6},{9,7},... | collective-permute-start | bytes 3538952 | tf_op jit(solution)/shard_map/ppermute | solution.py:338
  68.6 79.6 %collective-permute-start.8 = (bf16[2,192,1536]{2,1,0:T(8,128)(2,1)}, bf16[2,192,1536]{2,1,0:T(8,128)(2,1)}, u32[]{:S(2)}, u32[]{:S(2)}) collective-permute-start(bf16[2,192,1536]{2,1,0:T(8,128)(2,1)} %get-tuple-element.56), channel_id=1, source_target_pairs={{0,1},{1,14},{2,3},{3,12},{4,5},{5,10},{6,7},{7,8},{8,9},{9,6},{10... | collective-permute-start | bytes 3538952 | tf_op jit(solution)/shard_map/ppermute | solution.py:338
  68.6 84.1 %collective-permute-start.9 = (bf16[2,192,1536]{2,1,0:T(8,128)(2,1)}, bf16[2,192,1536]{2,1,0:T(8,128)(2,1)}, u32[]{:S(2)}, u32[]{:S(2)}) collective-permute-start(bf16[2,192,1536]{2,1,0:T(8,128)(2,1)} %get-tuple-element.57), channel_id=1, source_target_pairs={{0,5},{1,10},{2,7},{3,8},{4,1},{5,14},{6,3},{7,12},{8,13},{9,2},{1... | collective-permute-start | bytes 3538952 | tf_op jit(solution)/shard_map/ppermute | solution.py:338
  132.5 54.7 %collective-permute-start.10 = (bf16[2,192,1536]{2,1,0:T(8,128)(2,1)}, bf16[2,192,1536]{2,1,0:T(8,128)(2,1)}, u32[]{:S(2)}, u32[]{:S(2)}) collective-permute-start(bf16[2,192,1536]{2,1,0:T(8,128)(2,1)} %get-tuple-element.58), channel_id=1, source_target_pairs={{0,9},{1,6},{2,11},{3,4},{4,13},{5,2},{6,15},{7,0},{8,1},{9,14},{1... | collective-permute-start | bytes 3538952 | tf_op jit(solution)/shard_map/ppermute | solution.py:338
  144.8 62.9 %collective-permute-start.11 = (bf16[2,192,1536]{2,1,0:T(8,128)(2,1)}, bf16[2,192,1536]{2,1,0:T(8,128)(2,1)S(1)}, u32[]{:S(2)}, u32[]{:S(2)}) collective-permute-start(bf16[2,192,1536]{2,1,0:T(8,128)(2,1)} %get-tuple-element.59), channel_id=1, source_target_pairs={{0,13},{1,2},{2,15},{3,0},{4,9},{5,6},{6,11},{7,4},{8,5},{9,10},{1... | collective-permute-start | bytes 3538952 | tf_op jit(solution)/shard_map/ppermute | solution.py:338
  146.8 60.9 %collective-permute-start.12 = (bf16[2,192,1536]{2,1,0:T(8,128)(2,1)}, bf16[2,192,1536]{2,1,0:T(8,128)(2,1)S(1)}, u32[]{:S(2)}, u32[]{:S(2)}) collective-permute-start(bf16[2,192,1536]{2,1,0:T(8,128)(2,1)} %get-tuple-element.61), channel_id=1, source_target_pairs={{0,3},{1,12},{2,1},{3,14},{4,7},{5,8},{6,5},{7,10},{8,11},{9,4},{1... | collective-permute-start | bytes 3538952 | tf_op jit(solution)/shard_map/ppermute | solution.py:338
  148.2 59.5 %collective-permute-start.13 = (bf16[2,192,1536]{2,1,0:T(8,128)(2,1)}, bf16[2,192,1536]{2,1,0:T(8,128)(2,1)S(1)}, u32[]{:S(2)}, u32[]{:S(2)}) collective-permute-start(bf16[2,192,1536]{2,1,0:T(8,128)(2,1)} %get-tuple-element.62), channel_id=1, source_target_pairs={{0,7},{1,8},{2,5},{3,10},{4,3},{5,12},{6,1},{7,14},{8,15},{9,0},{1... | collective-permute-start | bytes 3538952 | tf_op jit(solution)/shard_map/ppermute | solution.py:338
  152.7 55.0 %collective-permute-start.14 = (bf16[2,192,1536]{2,1,0:T(8,128)(2,1)}, bf16[2,192,1536]{2,1,0:T(8,128)(2,1)S(1)}, u32[]{:S(2)}, u32[]{:S(2)}) collective-permute-start(bf16[2,192,1536]{2,1,0:T(8,128)(2,1)} %get-tuple-element.63), channel_id=1, source_target_pairs={{0,11},{1,4},{2,9},{3,6},{4,15},{5,0},{6,13},{7,2},{8,3},{9,12},{1... | collective-permute-start | bytes 3538952 | tf_op jit(solution)/shard_map/ppermute | solution.py:338
  187.3 32.4 %collective-permute-start.15 = (bf16[2,192,1536]{2,1,0:T(8,128)(2,1)}, bf16[2,192,1536]{2,1,0:T(8,128)(2,1)S(1)}, u32[]{:S(2)}, u32[]{:S(2)}) collective-permute-start(bf16[2,192,1536]{2,1,0:T(8,128)(2,1)} %get-tuple-element.64), channel_id=1, source_target_pairs={{0,15},{1,0},{2,13},{3,2},{4,11},{5,4},{6,9},{7,6},{8,7},{9,8},{10... | collective-permute-start | bytes 3538952 | tf_op jit(solution)/shard_map/ppermute | solution.py:338
  226.7 7.4 %collective-permute-start.16 = (bf16[24,1536]{1,0:T(8,128)(2,1)}, bf16[24,1536]{1,0:T(8,128)(2,1)S(1)}, u32[]{:S(2)}, u32[]{:S(2)}) collective-permute-start(bf16[24,1536]{1,0:T(8,128)(2,1)} %shard_map.122.own), channel_id=1, source_target_pairs={{16,0},{20,4},{24,8},{28,12},{17,1},{21,5},{25,9},{29,13},{18,2},{... | collective-permute-start | bytes 221192 | tf_op jit(solution)/shard_map/ppermute | solution.py:401
  279.8 8.0 %collective-permute-start.25 = (bf16[24,2048]{1,0:T(8,128)(2,1)S(1)}, bf16[24,2048]{1,0:T(8,128)(2,1)S(1)}, u32[]{:S(2)}, u32[]{:S(2)}) collective-permute-start(bf16[24,2048]{1,0:T(8,128)(2,1)S(1)} %shard_map.129.value), channel_id=1, source_target_pairs={{0,20},{4,24},{8,28},{12,0},{1,21},{5,25},{9,29},{13,1},{2,22},{6,... | collective-permute-start | bytes 294920 | tf_op jit(solution)/shard_map/ppermute | solution.py:417
  390.4 12.8 %collective-permute-start.46 = (bf16[24,1536]{1,0:T(8,128)(2,1)S(1)}, bf16[24,1536]{1,0:T(8,128)(2,1)S(1)}, u32[]{:S(2)}, u32[]{:S(2)}) collective-permute-start(bf16[24,1536]{1,0:T(8,128)(2,1)S(1)} %shard_map.147.own), channel_id=1, source_target_pairs={{0,16},{4,20},{24,8},{28,12},{1,17},{5,21},{25,9},{29,13},{2,18},{... | collective-permute-start | bytes 221192 | tf_op jit(solution)/shard_map/ppermute | solution.py:401
  426.8 8.5 %collective-permute-start.52 = (bf16[24,1536]{1,0:T(8,128)(2,1)S(1)}, bf16[24,1536]{1,0:T(8,128)(2,1)S(1)}, u32[]{:S(2)}, u32[]{:S(2)}) collective-permute-start(bf16[24,1536]{1,0:T(8,128)(2,1)S(1)} %shard_map.152.own), channel_id=1, source_target_pairs={{0,16},{4,20},{8,24},{28,12},{1,17},{5,21},{9,25},{29,13},{2,18},{... | collective-permute-start | bytes 221192 | tf_op jit(solution)/shard_map/ppermute | solution.py:401
  458.8 8.5 %collective-permute-start.58 = (bf16[24,1536]{1,0:T(8,128)(2,1)S(1)}, bf16[24,1536]{1,0:T(8,128)(2,1)S(1)}, u32[]{:S(2)}, u32[]{:S(2)}) collective-permute-start(bf16[24,1536]{1,0:T(8,128)(2,1)S(1)} %shard_map.157.own), channel_id=1, source_target_pairs={{0,16},{4,20},{8,24},{12,28},{1,17},{5,21},{9,25},{13,29},{2,18},{... | collective-permute-start | bytes 221192 | tf_op jit(solution)/shard_map/ppermute | solution.py:401
  478.4 11.5 %collective-permute-start.62 = (bf16[24,2048]{1,0:T(8,128)(2,1)S(1)}, bf16[24,2048]{1,0:T(8,128)(2,1)S(1)}, u32[]{:S(2)}, u32[]{:S(2)}) collective-permute-start(bf16[24,2048]{1,0:T(8,128)(2,1)S(1)} %shard_map.160), channel_id=1, source_target_pairs={{16,20},{20,24},{24,28},{28,0},{17,21},{21,25},{25,29},{29,1},{18,... | collective-permute-start | bytes 294920 | tf_op jit(solution)/shard_map/ppermute | solution.py:419
  510.3 12.3 %collective-permute-start.68 = (bf16[24,2048]{1,0:T(8,128)(2,1)S(1)}, bf16[24,2048]{1,0:T(8,128)(2,1)S(1)}, u32[]{:S(2)}, u32[]{:S(2)}) collective-permute-start(bf16[24,2048]{1,0:T(8,128)(2,1)S(1)} %shard_map.165), channel_id=1, source_target_pairs={{16,20},{20,24},{24,28},{28,0},{17,21},{21,25},{25,29},{29,1},{18,... | collective-permute-start | bytes 294920 | tf_op jit(solution)/shard_map/ppermute | solution.py:419
  542.8 12.4 %collective-permute-start.74 = (bf16[24,2048]{1,0:T(8,128)(2,1)S(1)}, bf16[24,2048]{1,0:T(8,128)(2,1)S(1)}, u32[]{:S(2)}, u32[]{:S(2)}) collective-permute-start(bf16[24,2048]{1,0:T(8,128)(2,1)S(1)} %shard_map.170), channel_id=1, source_target_pairs={{16,20},{20,24},{24,28},{28,0},{17,21},{21,25},{25,29},{29,1},{18,... | collective-permute-start | bytes 294920 | tf_op jit(solution)/shard_map/ppermute | solution.py:419
  (94 other events, 1316.0 us)

commit v13 on v11

--- a/solution.py
+++ b/solution.py
@@ -269,7 +269,11 @@
     out[...] = (mine[...].astype(jnp.float32) + total).astype(jnp.bfloat16)
 
 
-def choose_kernel(tick, near, far, out):
+def copy_kernel(value, out):
+    out[...] = value[...]
+
+
+def choose_kernel(tick, far, near, out):
     at_home = phase_at(tick) == lax.axis_index("zone")
     out[...] = jnp.where(at_home, near[...], far[...])
 
@@ -357,6 +361,7 @@
     counts = tile_lengths[sources]
     table = jnp.concatenate([starts, counts]).astype(jnp.int32)
     flip = [(z, 1 - z) for z in range(2)]
+    norm_gain, _ = lax.optimization_barrier((norm_gain, place))
     swapped = lax.ppermute(norm_gain, "zone", flip)
     gains = jnp.concatenate(
         [jnp.where(zone == 0, norm_gain, swapped), jnp.where(zone == 0, swapped, norm_gain)]
@@ -413,8 +418,9 @@
         record.append(after)
         if tick + 1 < ticks:
             far = lax.ppermute(after, ("zone", "spot"), hop(tick, 1))
-            near = lax.ppermute(after, ("zone", "spot"), hop(tick, 0))
-            arrived = in_vmem(functools.partial(choose_kernel, tick + 1), near, far)
+            behind = in_vmem(copy_kernel, after)
+            near = lax.ppermute(behind, ("zone", "spot"), hop(tick, 0))
+            arrived = in_vmem(functools.partial(choose_kernel, tick + 1), far, near)
     for item in range(ITEMS):
         value = jnp.zeros((rows, half), jnp.bfloat16)
         for tick in range(item, ticks):

time: 566 us -> 563 us (level)
  waiting for transfers between devices: 307 us -> 283 us
  starting transfers between devices: 112 us -> 132 us
    ppermute x10, waiting for transfers between devices: 43.3 us -> 13.6 us  [per_device(): near = lax.ppermute(behind, ('zone', 'spot'), hop(tick, 0))]
    ppermute x10, starting transfers between devices: 12.3 us -> 36.3 us  [per_device(): near = lax.ppermute(behind, ('zone', 'spot'), hop(tick, 0))]
    ppermute x10, waiting for transfers between devices: 1.76 us -> 25.2 us  [per_device(): far = lax.ppermute(after, ('zone', 'spot'), hop(tick, 1))]
    ppermute x10, starting transfers between devices: 23.7 us -> 6.18 us  [per_device(): far = lax.ppermute(after, ('zone', 'spot'), hop(tick, 1))]
    ppermute x11, waiting for transfers between devices: 59.6 us -> 48.5 us  [per_device(): sent = lax.ppermute(own, ('zone', 'spot'), mirror(tick))]
    ppermute x11, starting transfers between devices: 9.97 us -> 16.8 us  [per_device(): lax.ppermute(part, 'tensor', [(t, t ^ bit) for t in range(n_tensor)])]
    ppermute x11, waiting for transfers between devices: 43.9 us -> 37 us  [per_device(): lax.ppermute(part, 'tensor', [(t, t ^ bit) for t in range(n_tensor)])]
    ppermute x11, starting transfers between devices: 14.7 us -> 21.4 us  [per_device(): sent = lax.ppermute(own, ('zone', 'spot'), mirror(tick))]
  transfers between devices with their start and end apart: 79 -> 79, of which waited for: 67 -> 64; matrix products, arithmetic and copies ran while one was open for 2% -> 2% of each run, Pallas kernels for 6% -> 6%
where the time goes in v13:
time: 563 us; the launch traced here: 555 us
  waiting for transfers between devices  283 us (50%)
  starting transfers between devices  132 us (23%)
  Pallas kernels  125 us (22%)
  local copies, waits for them, and re-layouts  7.35 us (1%)
  other arithmetic  6.89 us (1%)
    ppermute x15, waiting for transfers between devices, exchange(): return lax.ppermute(piece, ('spot', 'tensor'), pairs)  132 us
    pallas_call x11, Pallas kernels, project(): pl.pallas_call(functools.partial(project_kernel, tick, tiles, tilew, n_y)...  48.9 us
    ppermute x11, waiting for transfers between devices, per_device(): sent = lax.ppermute(own, ('zone', 'spot'), mirror(tick))  48.5 us
    pallas_call x11, Pallas kernels, attend(): pl.pallas_call(functools.partial(attend_kernel, steps, brow, kvlocal, gro...  44.6 us
    ppermute x15, starting transfers between devices, exchange(): return lax.ppermute(piece, ('spot', 'tensor'), pairs)  43.5 us
    ppermute x11, waiting for transfers between devices, per_device(): lax.ppermute(part, 'tensor', [(t, t ^ bit) for t in range(n_tensor)])  37 us
    ppermute x10, starting transfers between devices, per_device(): near = lax.ppermute(behind, ('zone', 'spot'), hop(tick, 0))  36.3 us
    pallas_call x4, Pallas kernels, sort_slab(): pl.pallas_call(functools.partial(sort_kernel, layers), grid_spec=pltpu.Pr...  30.8 us
  transfers between devices with their start and end apart: 79, of which 64 were waited for; matrix products, arithmetic and copies ran while one was open for 2% of the time, Pallas kernels for 6%

profile of v13, /device:TPU:0, one launch (start us, length us, event | category | flops | bytes accessed | tf_op | source)
XLA Modules:
  0.0 555.3 jit_solution(11328053816475194430)
XLA Ops:
  4.6 7.7 %shard_map.118 = (bf16[2,192,1536]{2,1,0:T(8,128)(2,1)}, bf16[2,192,1536]{2,1,0:T(8,128)(2,1)}, bf16[2,192,1536]{2,1,0:T(8,128)(2,1)}, bf16[2,192,1536]{2,1,0:T(8,128)(2,1)}) custom-call(s32[2]{0:T(128)} %pad_add_fusion.1.place, bf16[1536,6144]{1,0:T(8,128)(2,1)} %slab.7), custom_call_target="tpu_custom_call" | custom-call | flops 1207959552 | bytes 9437184 | tf_op jit(solution)/shard_map/pallas_call | solution.py:40
  15.8 7.7 %shard_map.119 = (bf16[2,192,1536]{2,1,0:T(8,128)(2,1)}, bf16[2,192,1536]{2,1,0:T(8,128)(2,1)}, bf16[2,192,1536]{2,1,0:T(8,128)(2,1)}, bf16[2,192,1536]{2,1,0:T(8,128)(2,1)}) custom-call(s32[2]{0:T(128)} %pad_add_fusion.1.place, bf16[1536,6144]{1,0:T(8,128)(2,1)} %slab.7), custom_call_target="tpu_custom_call" | custom-call | flops 1207959552 | bytes 9437184 | tf_op jit(solution)/shard_map/pallas_call | solution.py:40
  26.5 7.7 %shard_map.120 = (bf16[2,192,1536]{2,1,0:T(8,128)(2,1)}, bf16[2,192,1536]{2,1,0:T(8,128)(2,1)}, bf16[2,192,1536]{2,1,0:T(8,128)(2,1)}, bf16[2,192,1536]{2,1,0:T(8,128)(2,1)}) custom-call(s32[2]{0:T(128)} %pad_add_fusion.1.place, bf16[1536,6144]{1,0:T(8,128)(2,1)} %slab.7), custom_call_target="tpu_custom_call" | custom-call | flops 1207959552 | bytes 9437184 | tf_op jit(solution)/shard_map/pallas_call | solution.py:40
  41.0 25.9 %collective-permute-start.6 = (bf16[2,192,1536]{2,1,0:T(8,128)(2,1)}, bf16[2,192,1536]{2,1,0:T(8,128)(2,1)}, u32[]{:S(2)}, u32[]{:S(2)}) collective-permute-start(bf16[2,192,1536]{2,1,0:T(8,128)(2,1)} %get-tuple-element.54), channel_id=1, source_target_pairs={{0,10},{1,5},{2,8},{3,7},{4,14},{5,1},{6,12},{7,3},{8,2},{9,13},{1... | collective-permute-start | bytes 3538952 | tf_op jit(solution)/shard_map/ppermute | solution.py:338
  72.4 60.1 %collective-permute-done.5.rest_5_ = bf16[2,192,1536]{2,1,0:T(8,128)(2,1)} collective-permute-done((bf16[2,192,1536]{2,1,0:T(8,128)(2,1)}, bf16[2,192,1536]{2,1,0:T(8,128)(2,1)}, u32[]{:S(2)}, u32[]{:S(2)}) %collective-permute-start.5) | collective-permute-done | bytes 1179680 | tf_op jit(solution)/shard_map/ppermute | solution.py:338
  136.9 7.8 %shard_map.121 = (bf16[2,192,1536]{2,1,0:T(8,128)(2,1)}, bf16[2,192,1536]{2,1,0:T(8,128)(2,1)}, bf16[2,192,1536]{2,1,0:T(8,128)(2,1)}, bf16[2,192,1536]{2,1,0:T(8,128)(2,1)}) custom-call(s32[2]{0:T(128)} %pad_add_fusion.1.place, bf16[1536,6144]{1,0:T(8,128)(2,1)} %slab.7), custom_call_target="tpu_custom_call" | custom-call | flops 1207959552 | bytes 9437184 | tf_op jit(solution)/shard_map/pallas_call | solution.py:40
  153.1 34.4 %collective-permute-done.10.rest_10_ = bf16[2,192,1536]{2,1,0:T(8,128)(2,1)} collective-permute-done((bf16[2,192,1536]{2,1,0:T(8,128)(2,1)}, bf16[2,192,1536]{2,1,0:T(8,128)(2,1)}, u32[]{:S(2)}, u32[]{:S(2)}) %collective-permute-start.10) | collective-permute-done | bytes 1179680 | tf_op jit(solution)/shard_map/ppermute | solution.py:338
  188.1 19.6 %collective-permute-done.11.rest_11_ = bf16[2,192,1536]{2,1,0:T(8,128)(2,1)S(1)} collective-permute-done((bf16[2,192,1536]{2,1,0:T(8,128)(2,1)}, bf16[2,192,1536]{2,1,0:T(8,128)(2,1)S(1)}, u32[]{:S(2)}, u32[]{:S(2)}) %collective-permute-start.11) | collective-permute-done | bytes 1179680 | tf_op jit(solution)/shard_map/ppermute | solution.py:338
  207.8 11.7 %collective-permute-done.15.rest_15_ = bf16[2,192,1536]{2,1,0:T(8,128)(2,1)S(1)} collective-permute-done((bf16[2,192,1536]{2,1,0:T(8,128)(2,1)}, bf16[2,192,1536]{2,1,0:T(8,128)(2,1)S(1)}, u32[]{:S(2)}, u32[]{:S(2)}) %collective-permute-start.15) | collective-permute-done | bytes 1179680 | tf_op jit(solution)/shard_map/ppermute | solution.py:338
  220.5 6.0 %shard_map.122.own = bf16[24,1536]{1,0:T(8,128)(2,1)} custom-call(s32[32]{0:T(128)} %pad_add_fusion.table, bf16[24,2048]{1,0:T(8,128)(2,1)} %bitcast.65, bf16[24,2048]{1,0:T(8,128)(2,1)} %bitcast.73, f32[2,4096]{1,0:T(2,128)} %pad_maximum_fusion.gains, bf16[2,192,1536]{2,1,0:T(8,128)(2,1)} %get-tuple-element.88.rest_0_, bf16[2,192,1536]{2,1,0:T(8,128)(2,1)} %copy-done.1, ...), custom_call_target="tpu_custom_call" | custom-call | flops 226492416 | bytes 9437184 | tf_op jit(solution)/shard_map/pallas_call | solution.py:139
  227.2 5.2 collective-permute-done.16.sent
  242.5 4.3 collective-permute-done.18.moved
  248.6 5.0 collective-permute-done.19.far
  261.8 5.8 %collective-permute-done.22.sent = bf16[24,1536]{1,0:T(8,128)(2,1)S(1)} collective-permute-done((bf16[24,1536]{1,0:T(8,128)(2,1)S(1)}, bf16[24,1536]{1,0:T(8,128)(2,1)S(1)}, u32[]{:S(2)}, u32[]{:S(2)}) %collective-permute-start.22) | collective-permute-done | bytes 73760 | tf_op jit(solution)/shard_map/ppermute | solution.py:404
  293.7 4.7 collective-permute-done.28.sent
  324.2 4.9 collective-permute-done.34.sent
  355.0 4.8 collective-permute-done.40.sent
  385.8 4.7 collective-permute-done.46.sent
  432.1 4.5 collective-permute-start.56
  441.3 4.3 shard_map.157.own
  448.1 4.4 collective-permute-done.58.sent
  472.4 4.3 shard_map.162.own
  478.7 4.9 collective-permute-done.64.sent
  503.1 4.3 shard_map.167.own
  (315 shorter events, 299.2 us)
Async XLA Ops:
  0.0 25.0 %collective-permute-start = (f32[1,4096]{1,0:T(1,128)}, f32[1,4096]{1,0:T(1,128)S(1)}, u32[]{:S(2)}, u32[]{:S(2)}) collective-permute-start(f32[1,4096]{1,0:T(1,128)} %param.18), channel_id=1, source_target_pairs={{0,16},{16,0},{1,17},{17,1},{2,18},{18,2},{3,19},{19,3},{4,20},{20... | collective-permute-start | bytes 49160 | tf_op jit(solution)/shard_map/ppermute | solution.py:365
  12.3 28.7 %collective-permute-start.1 = (bf16[2,192,1536]{2,1,0:T(8,128)(2,1)}, bf16[2,192,1536]{2,1,0:T(8,128)(2,1)S(1)}, u32[]{:S(2)}, u32[]{:S(2)}) collective-permute-start(bf16[2,192,1536]{2,1,0:T(8,128)(2,1)} %get-tuple-element.50), channel_id=1, source_target_pairs={{0,4},{1,11},{2,6},{3,9},{4,0},{5,15},{6,2},{7,13},{8,12},{9,3},{1... | collective-permute-start | bytes 3538952 | tf_op jit(solution)/shard_map/ppermute | solution.py:338
  13.8 53.1 %collective-permute-start.2 = (bf16[2,192,1536]{2,1,0:T(8,128)(2,1)}, bf16[2,192,1536]{2,1,0:T(8,128)(2,1)}, u32[]{:S(2)}, u32[]{:S(2)}) collective-permute-start(bf16[2,192,1536]{2,1,0:T(8,128)(2,1)} %get-tuple-element.51), channel_id=1, source_target_pairs={{0,8},{1,7},{2,10},{3,5},{4,12},{5,3},{6,14},{7,1},{8,0},{9,15},{1... | collective-permute-start | bytes 3538952 | tf_op jit(solution)/shard_map/ppermute | solution.py:338
  15.4 53.0 %collective-permute-start.3 = (bf16[2,192,1536]{2,1,0:T(8,128)(2,1)}, bf16[2,192,1536]{2,1,0:T(8,128)(2,1)}, u32[]{:S(2)}, u32[]{:S(2)}) collective-permute-start(bf16[2,192,1536]{2,1,0:T(8,128)(2,1)} %get-tuple-element.47), channel_id=1, source_target_pairs={{0,12},{1,3},{2,14},{3,1},{4,8},{5,7},{6,10},{7,5},{8,4},{9,11},{1... | collective-permute-start | bytes 3538952 | tf_op jit(solution)/shard_map/ppermute | solution.py:338
  23.5 44.9 %collective-permute-start.4 = (bf16[2,192,1536]{2,1,0:T(8,128)(2,1)}, bf16[2,192,1536]{2,1,0:T(8,128)(2,1)}, u32[]{:S(2)}, u32[]{:S(2)}) collective-permute-start(bf16[2,192,1536]{2,1,0:T(8,128)(2,1)} %get-tuple-element.52), channel_id=1, source_target_pairs={{0,2},{1,13},{2,0},{3,15},{4,6},{5,9},{6,4},{7,11},{8,10},{9,5},{1... | collective-permute-start | bytes 3538952 | tf_op jit(solution)/shard_map/ppermute | solution.py:338
  25.0 107.5 %collective-permute-start.5 = (bf16[2,192,1536]{2,1,0:T(8,128)(2,1)}, bf16[2,192,1536]{2,1,0:T(8,128)(2,1)}, u32[]{:S(2)}, u32[]{:S(2)}) collective-permute-start(bf16[2,192,1536]{2,1,0:T(8,128)(2,1)} %get-tuple-element.53), channel_id=1, source_target_pairs={{0,6},{1,9},{2,4},{3,11},{4,2},{5,13},{6,0},{7,15},{8,14},{9,1},{1... | collective-permute-start | bytes 3538952 | tf_op jit(solution)/shard_map/ppermute | solution.py:338
  41.0 103.7 %collective-permute-start.6 = (bf16[2,192,1536]{2,1,0:T(8,128)(2,1)}, bf16[2,192,1536]{2,1,0:T(8,128)(2,1)}, u32[]{:S(2)}, u32[]{:S(2)}) collective-permute-start(bf16[2,192,1536]{2,1,0:T(8,128)(2,1)} %get-tuple-element.54), channel_id=1, source_target_pairs={{0,10},{1,5},{2,8},{3,7},{4,14},{5,1},{6,12},{7,3},{8,2},{9,13},{1... | collective-permute-start | bytes 3538952 | tf_op jit(solution)/shard_map/ppermute | solution.py:338
  66.9 79.8 %collective-permute-start.7 = (bf16[2,192,1536]{2,1,0:T(8,128)(2,1)}, bf16[2,192,1536]{2,1,0:T(8,128)(2,1)}, u32[]{:S(2)}, u32[]{:S(2)}) collective-permute-start(bf16[2,192,1536]{2,1,0:T(8,128)(2,1)} %get-tuple-element.87), channel_id=1, source_target_pairs={{0,14},{1,15},{2,12},{3,13},{4,10},{5,11},{6,8},{7,9},{8,6},{9,7},... | collective-permute-start | bytes 3538952 | tf_op jit(solution)/shard_map/ppermute | solution.py:338
  68.4 79.7 %collective-permute-start.8 = (bf16[2,192,1536]{2,1,0:T(8,128)(2,1)}, bf16[2,192,1536]{2,1,0:T(8,128)(2,1)}, u32[]{:S(2)}, u32[]{:S(2)}) collective-permute-start(bf16[2,192,1536]{2,1,0:T(8,128)(2,1)} %get-tuple-element.56), channel_id=1, source_target_pairs={{0,1},{1,14},{2,3},{3,12},{4,5},{5,10},{6,7},{7,8},{8,9},{9,6},{10... | collective-permute-start | bytes 3538952 | tf_op jit(solution)/shard_map/ppermute | solution.py:338
  68.4 84.4 %collective-permute-start.9 = (bf16[2,192,1536]{2,1,0:T(8,128)(2,1)}, bf16[2,192,1536]{2,1,0:T(8,128)(2,1)}, u32[]{:S(2)}, u32[]{:S(2)}) collective-permute-start(bf16[2,192,1536]{2,1,0:T(8,128)(2,1)} %get-tuple-element.57), channel_id=1, source_target_pairs={{0,5},{1,10},{2,7},{3,8},{4,1},{5,14},{6,3},{7,12},{8,13},{9,2},{1... | collective-permute-start | bytes 3538952 | tf_op jit(solution)/shard_map/ppermute | solution.py:338
  132.5 54.9 %collective-permute-start.10 = (bf16[2,192,1536]{2,1,0:T(8,128)(2,1)}, bf16[2,192,1536]{2,1,0:T(8,128)(2,1)}, u32[]{:S(2)}, u32[]{:S(2)}) collective-permute-start(bf16[2,192,1536]{2,1,0:T(8,128)(2,1)} %get-tuple-element.58), channel_id=1, source_target_pairs={{0,9},{1,6},{2,11},{3,4},{4,13},{5,2},{6,15},{7,0},{8,1},{9,14},{1... | collective-permute-start | bytes 3538952 | tf_op jit(solution)/shard_map/ppermute | solution.py:338
  144.8 63.0 %collective-permute-start.11 = (bf16[2,192,1536]{2,1,0:T(8,128)(2,1)}, bf16[2,192,1536]{2,1,0:T(8,128)(2,1)S(1)}, u32[]{:S(2)}, u32[]{:S(2)}) collective-permute-start(bf16[2,192,1536]{2,1,0:T(8,128)(2,1)} %get-tuple-element.59), channel_id=1, source_target_pairs={{0,13},{1,2},{2,15},{3,0},{4,9},{5,6},{6,11},{7,4},{8,5},{9,10},{1... | collective-permute-start | bytes 3538952 | tf_op jit(solution)/shard_map/ppermute | solution.py:338
  146.7 61.1 %collective-permute-start.12 = (bf16[2,192,1536]{2,1,0:T(8,128)(2,1)}, bf16[2,192,1536]{2,1,0:T(8,128)(2,1)S(1)}, u32[]{:S(2)}, u32[]{:S(2)}) collective-permute-start(bf16[2,192,1536]{2,1,0:T(8,128)(2,1)} %get-tuple-element.61), channel_id=1, source_target_pairs={{0,3},{1,12},{2,1},{3,14},{4,7},{5,8},{6,5},{7,10},{8,11},{9,4},{1... | collective-permute-start | bytes 3538952 | tf_op jit(solution)/shard_map/ppermute | solution.py:338
  148.0 59.7 %collective-permute-start.13 = (bf16[2,192,1536]{2,1,0:T(8,128)(2,1)}, bf16[2,192,1536]{2,1,0:T(8,128)(2,1)S(1)}, u32[]{:S(2)}, u32[]{:S(2)}) collective-permute-start(bf16[2,192,1536]{2,1,0:T(8,128)(2,1)} %get-tuple-element.62), channel_id=1, source_target_pairs={{0,7},{1,8},{2,5},{3,10},{4,3},{5,12},{6,1},{7,14},{8,15},{9,0},{1... | collective-permute-start | bytes 3538952 | tf_op jit(solution)/shard_map/ppermute | solution.py:338
  152.8 55.0 %collective-permute-start.14 = (bf16[2,192,1536]{2,1,0:T(8,128)(2,1)}, bf16[2,192,1536]{2,1,0:T(8,128)(2,1)S(1)}, u32[]{:S(2)}, u32[]{:S(2)}) collective-permute-start(bf16[2,192,1536]{2,1,0:T(8,128)(2,1)} %get-tuple-element.63), channel_id=1, source_target_pairs={{0,11},{1,4},{2,9},{3,6},{4,15},{5,0},{6,13},{7,2},{8,3},{9,12},{1... | collective-permute-start | bytes 3538952 | tf_op jit(solution)/shard_map/ppermute | solution.py:338
  187.5 32.0 %collective-permute-start.15 = (bf16[2,192,1536]{2,1,0:T(8,128)(2,1)}, bf16[2,192,1536]{2,1,0:T(8,128)(2,1)S(1)}, u32[]{:S(2)}, u32[]{:S(2)}) collective-permute-start(bf16[2,192,1536]{2,1,0:T(8,128)(2,1)} %get-tuple-element.64), channel_id=1, source_target_pairs={{0,15},{1,0},{2,13},{3,2},{4,11},{5,4},{6,9},{7,6},{8,7},{9,8},{10... | collective-permute-start | bytes 3538952 | tf_op jit(solution)/shard_map/ppermute | solution.py:338
  247.5 7.5 %collective-permute-start.20 = (bf16[24,2048]{1,0:T(8,128)(2,1)S(1)}, bf16[24,2048]{1,0:T(8,128)(2,1)S(1)}, u32[]{:S(2)}, u32[]{:S(2)}) collective-permute-start(bf16[24,2048]{1,0:T(8,128)(2,1)S(1)} %shard_map.125), channel_id=1, source_target_pairs={{0,4},{4,8},{8,12},{12,16},{16,20},{20,24},{24,28},{28,0},{1,5},{5... | collective-permute-start | bytes 294920 | tf_op jit(solution)/shard_map/ppermute | solution.py:422
  308.9 7.6 %collective-permute-start.32 = (bf16[24,2048]{1,0:T(8,128)(2,1)S(1)}, bf16[24,2048]{1,0:T(8,128)(2,1)S(1)}, u32[]{:S(2)}, u32[]{:S(2)}) collective-permute-start(bf16[24,2048]{1,0:T(8,128)(2,1)S(1)} %shard_map.135), channel_id=1, source_target_pairs={{0,4},{4,8},{8,12},{12,16},{16,20},{20,24},{24,28},{28,0},{1,5},{5... | collective-permute-start | bytes 294920 | tf_op jit(solution)/shard_map/ppermute | solution.py:422
  339.6 7.7 %collective-permute-start.37 = (bf16[24,2048]{1,0:T(8,128)(2,1)S(1)}, bf16[24,2048]{1,0:T(8,128)(2,1)S(1)}, u32[]{:S(2)}, u32[]{:S(2)}) collective-permute-start(bf16[24,2048]{1,0:T(8,128)(2,1)S(1)} %shard_map.139.value), channel_id=1, source_target_pairs={{0,20},{4,24},{8,28},{12,0},{16,4},{20,8},{24,12},{28,16},{1,21},{... | collective-permute-start | bytes 294920 | tf_op jit(solution)/shard_map/ppermute | solution.py:420
  339.6 7.6 %collective-permute-start.38 = (bf16[24,2048]{1,0:T(8,128)(2,1)S(1)}, bf16[24,2048]{1,0:T(8,128)(2,1)S(1)}, u32[]{:S(2)}, u32[]{:S(2)}) collective-permute-start(bf16[24,2048]{1,0:T(8,128)(2,1)S(1)} %shard_map.140), channel_id=1, source_target_pairs={{0,4},{4,8},{8,12},{12,16},{16,20},{20,24},{24,28},{28,0},{1,5},{5... | collective-permute-start | bytes 294920 | tf_op jit(solution)/shard_map/ppermute | solution.py:422
  370.2 7.7 %collective-permute-start.43 = (bf16[24,2048]{1,0:T(8,128)(2,1)S(1)}, bf16[24,2048]{1,0:T(8,128)(2,1)S(1)}, u32[]{:S(2)}, u32[]{:S(2)}) collective-permute-start(bf16[24,2048]{1,0:T(8,128)(2,1)S(1)} %shard_map.144.value), channel_id=1, source_target_pairs={{0,20},{4,24},{8,28},{12,0},{16,4},{20,8},{24,12},{28,16},{1,21},{... | collective-permute-start | bytes 294920 | tf_op jit(solution)/shard_map/ppermute | solution.py:420
  432.1 7.8 %collective-permute-start.56 = (bf16[24,2048]{1,0:T(8,128)(2,1)S(1)}, bf16[24,2048]{1,0:T(8,128)(2,1)S(1)}, u32[]{:S(2)}, u32[]{:S(2)}) collective-permute-start(bf16[24,2048]{1,0:T(8,128)(2,1)S(1)} %shard_map.155), channel_id=1, source_target_pairs={{0,4},{4,8},{8,12},{12,16},{16,20},{20,24},{24,28},{28,0},{1,5},{5... | collective-permute-start | bytes 294920 | tf_op jit(solution)/shard_map/ppermute | solution.py:422
  494.0 7.7 %collective-permute-start.67 = (bf16[24,2048]{1,0:T(8,128)(2,1)S(1)}, bf16[24,2048]{1,0:T(8,128)(2,1)S(1)}, u32[]{:S(2)}, u32[]{:S(2)}) collective-permute-start(bf16[24,2048]{1,0:T(8,128)(2,1)S(1)} %shard_map.164.value), channel_id=1, source_target_pairs={{0,20},{4,24},{8,28},{12,0},{16,4},{20,8},{24,12},{28,16},{1,21},{... | collective-permute-start | bytes 294920 | tf_op jit(solution)/shard_map/ppermute | solution.py:420
  494.1 7.5 %collective-permute-start.68 = (bf16[24,2048]{1,0:T(8,128)(2,1)S(1)}, bf16[24,2048]{1,0:T(8,128)(2,1)S(1)}, u32[]{:S(2)}, u32[]{:S(2)}) collective-permute-start(bf16[24,2048]{1,0:T(8,128)(2,1)S(1)} %shard_map.165), channel_id=1, source_target_pairs={{0,4},{4,8},{8,12},{12,16},{16,20},{20,24},{24,28},{28,0},{1,5},{5... | collective-permute-start | bytes 294920 | tf_op jit(solution)/shard_map/ppermute | solution.py:422
  (94 other events, 1330.3 us)

commit v14 on v13

--- a/solution.py
+++ b/solution.py
@@ -25,24 +25,28 @@
     col = lax.broadcasted_iota(jnp.int32, (ROWBLOCK, ROWBLOCK), 1)
     layer = row // feats % 2 * kept + ((row // (2 * feats)) ^ place[0])
     order = jnp.where(col == row % feats * layers + layer, 1.0, 0.0).astype(jnp.bfloat16)
-    moved = jnp.dot(order, slab[...], preferred_element_type=jnp.float32).astype(jnp.bfloat16)
-    for n, out in enumerate(outs):
-        for phase in range(2):
-            at = (2 * n + phase) * feats
-            out[phase] = moved[at : at + feats]
+    for block in range(slab.shape[0] // ROWBLOCK):
+        piece = slab[block * ROWBLOCK : (block + 1) * ROWBLOCK]
+        moved = jnp.dot(order, piece, preferred_element_type=jnp.float32).astype(jnp.bfloat16)
+        for n, out in enumerate(outs):
+            for phase in range(2):
+                at = (2 * n + phase) * feats
+                out[phase, block * feats : (block + 1) * feats] = moved[at : at + feats]
 
 
 def sort_slab(slab, layers, n_tensor, turn, place):
     rows, columns = slab.shape
     kept = layers // 2
     cdev = columns // n_tensor
-    feats = ROWBLOCK // layers
+    blocks = rows // ROWBLOCK
+    taken = next(n for n in (3, 2, 1) if blocks % n == 0) * ROWBLOCK
+    feats = taken // layers
     return pl.pallas_call(
         functools.partial(sort_kernel, layers),
         grid_spec=pltpu.PrefetchScalarGridSpec(
             num_scalar_prefetch=1,
-            grid=(rows // ROWBLOCK,),
-            in_specs=[pl.BlockSpec((ROWBLOCK, cdev), lambda i, s: (i, s[1] ^ turn))],
+            grid=(rows // taken,),
+            in_specs=[pl.BlockSpec((taken, cdev), lambda i, s: (i, s[1] ^ turn))],
             out_specs=[pl.BlockSpec((2, feats, cdev), lambda i, s: (0, i, 0))] * kept,
         ),
         out_shape=[jax.ShapeDtypeStruct((2, rows // layers, cdev), jnp.bfloat16)] * kept,
@@ -276,6 +280,21 @@
 def choose_kernel(tick, far, near, out):
     at_home = phase_at(tick) == lax.axis_index("zone")
     out[...] = jnp.where(at_home, near[...], far[...])
+
+
+def late_kernel(value, piece, out):
+    out[...] = value[...]
+
+
+def after_piece(value, piece):
+    vmem = pl.BlockSpec(memory_space=pltpu.VMEM)
+    return pl.pallas_call(
+        late_kernel,
+        in_specs=[vmem, pl.BlockSpec(memory_space=pltpu.HBM)],
+        out_specs=vmem,
+        out_shape=jax.ShapeDtypeStruct(value.shape, value.dtype),
+        compiler_params=pltpu.CompilerParams(vmem_limit_bytes=VMEM),
+    )(value, piece)
 
 
 def in_vmem(kernel, *arrays):
@@ -361,8 +380,7 @@
     counts = tile_lengths[sources]
     table = jnp.concatenate([starts, counts]).astype(jnp.int32)
     flip = [(z, 1 - z) for z in range(2)]
-    norm_gain, _ = lax.optimization_barrier((norm_gain, place))
-    swapped = lax.ppermute(norm_gain, "zone", flip)
+    swapped = lax.ppermute(after_piece(norm_gain, piece), "zone", flip)
     gains = jnp.concatenate(
         [jnp.where(zone == 0, norm_gain, swapped), jnp.where(zone == 0, swapped, norm_gain)]
     )

time: 563 us -> 571 us (1.014)
  starting transfers between devices: 132 us -> 160 us
  waiting for transfers between devices: 283 us -> 270 us
  Pallas kernels: 125 us -> 116 us
    ppermute x15, waiting for transfers between devices: 132 us -> 77.1 us  [exchange(): return lax.ppermute(piece, ('spot', 'tensor'), pairs)]
    ppermute x15, starting transfers between devices: 43.5 us -> 85.7 us  [exchange(): return lax.ppermute(piece, ('spot', 'tensor'), pairs)]
    ppermute x10, waiting for transfers between devices: 13.6 us -> 41.6 us  [per_device(): near = lax.ppermute(behind, ('zone', 'spot'), hop(tick, 0))]
    ppermute x1, waiting for transfers between devices: 0.01 us -> 25 us  [per_device(): swapped = lax.ppermute(after_piece(norm_gain, piece), 'zone', flip)]
    ppermute x10, starting transfers between devices: 36.3 us -> 12.1 us  [per_device(): near = lax.ppermute(behind, ('zone', 'spot'), hop(tick, 0))]
    ppermute x10, waiting for transfers between devices: 25.2 us -> 1.31 us  [per_device(): far = lax.ppermute(after, ('zone', 'spot'), hop(tick, 1))]
    ppermute x10, starting transfers between devices: 6.18 us -> 26.2 us  [per_device(): far = lax.ppermute(after, ('zone', 'spot'), hop(tick, 1))]
    ppermute x11, waiting for transfers between devices: 48.5 us -> 58.4 us  [per_device(): sent = lax.ppermute(own, ('zone', 'spot'), mirror(tick))]
  transfers between devices with their start and end apart: 79 -> 79, of which waited for: 64 -> 68; matrix products, arithmetic and copies ran while one was open for 2% -> 2% of each run, Pallas kernels for 6% -> 3%
where the time goes in v14:
time: 571 us; the launch traced here: 564 us
  waiting for transfers between devices  270 us (47%)
  starting transfers between devices  160 us (28%)
  Pallas kernels  116 us (20%)
  local copies, waits for them, and re-layouts  10.2 us (2%)
  other arithmetic  6.35 us (1%)
    ppermute x15, starting transfers between devices, exchange(): return lax.ppermute(piece, ('spot', 'tensor'), pairs)  85.7 us
    ppermute x15, waiting for transfers between devices, exchange(): return lax.ppermute(piece, ('spot', 'tensor'), pairs)  77.1 us
    ppermute x11, waiting for transfers between devices, per_device(): sent = lax.ppermute(own, ('zone', 'spot'), mirror(tick))  58.4 us
    pallas_call x11, Pallas kernels, project(): pl.pallas_call(functools.partial(project_kernel, tick, tiles, tilew, n_y)...  48.9 us
    pallas_call x11, Pallas kernels, attend(): pl.pallas_call(functools.partial(attend_kernel, steps, brow, kvlocal, gro...  44.6 us
    ppermute x10, waiting for transfers between devices, per_device(): near = lax.ppermute(behind, ('zone', 'spot'), hop(tick, 0))  41.6 us
    ppermute x11, waiting for transfers between devices, per_device(): lax.ppermute(part, 'tensor', [(t, t ^ bit) for t in range(n_tensor)])  40.1 us
    ppermute x10, starting transfers between devices, per_device(): far = lax.ppermute(after, ('zone', 'spot'), hop(tick, 1))  26.2 us
  transfers between devices with their start and end apart: 79, of which 68 were waited for; matrix products, arithmetic and copies ran while one was open for 2% of the time, Pallas kernels for 3%

profile of v14, /device:TPU:0, one launch (start us, length us, event | category | flops | bytes accessed | tf_op | source)
XLA Modules:
  0.0 564.2 jit_solution(3493180401168668944)
XLA Ops:
  0.6 5.4 shard_map.118
  10.5 5.4 shard_map.119
  15.9 5.4 shard_map.120
  21.3 5.5 shard_map.121
  37.3 25.0 %collective-permute-done = f32[1,4096]{1,0:T(1,128)S(1)} collective-permute-done((f32[1,4096]{1,0:T(1,128)S(1)}, f32[1,4096]{1,0:T(1,128)S(1)}, u32[]{:S(2)}, u32[]{:S(2)}) %collective-permute-start) | collective-permute-done | bytes 16416 | tf_op jit(solution)/shard_map/ppermute | solution.py:383
  64.7 24.1 %collective-permute-start.6 = (bf16[2,192,1536]{2,1,0:T(8,128)(2,1)}, bf16[2,192,1536]{2,1,0:T(8,128)(2,1)}, u32[]{:S(2)}, u32[]{:S(2)}) collective-permute-start(bf16[2,192,1536]{2,1,0:T(8,128)(2,1)} %get-tuple-element.58), channel_id=1, source_target_pairs={{0,10},{1,5},{2,8},{3,7},{4,14},{5,1},{6,12},{7,3},{8,2},{9,13},{1... | collective-permute-start | bytes 3538952 | tf_op jit(solution)/shard_map/ppermute | solution.py:357
  90.3 28.9 %collective-permute-done.4.rest_4_ = bf16[2,192,1536]{2,1,0:T(8,128)(2,1)} collective-permute-done((bf16[2,192,1536]{2,1,0:T(8,128)(2,1)S(1)}, bf16[2,192,1536]{2,1,0:T(8,128)(2,1)}, u32[]{:S(2)}, u32[]{:S(2)}) %collective-permute-start.4) | collective-permute-done | bytes 1179680 | tf_op jit(solution)/shard_map/ppermute | solution.py:357
  124.9 12.0 %collective-permute-start.15 = (bf16[2,192,1536]{2,1,0:T(8,128)(2,1)S(1)}, bf16[2,192,1536]{2,1,0:T(8,128)(2,1)S(1)}, u32[]{:S(2)}, u32[]{:S(2)}) collective-permute-start(bf16[2,192,1536]{2,1,0:T(8,128)(2,1)S(1)} %copy-done.24), channel_id=1, source_target_pairs={{0,15},{1,0},{2,13},{3,2},{4,11},{5,4},{6,9},{7,6},{8,7},{9,8},{10... | collective-permute-start | bytes 3538952 | tf_op jit(solution)/shard_map/ppermute | solution.py:357
  136.9 22.8 %collective-permute-done.9.rest_9_ = bf16[2,192,1536]{2,1,0:T(8,128)(2,1)} collective-permute-done((bf16[2,192,1536]{2,1,0:T(8,128)(2,1)}, bf16[2,192,1536]{2,1,0:T(8,128)(2,1)}, u32[]{:S(2)}, u32[]{:S(2)}) %collective-permute-start.9) | collective-permute-done | bytes 1179680 | tf_op jit(solution)/shard_map/ppermute | solution.py:357
  159.7 32.0 %collective-permute-start.13 = (bf16[2,192,1536]{2,1,0:T(8,128)(2,1)}, bf16[2,192,1536]{2,1,0:T(8,128)(2,1)S(1)}, u32[]{:S(2)}, u32[]{:S(2)}) collective-permute-start(bf16[2,192,1536]{2,1,0:T(8,128)(2,1)} %get-tuple-element.63), channel_id=1, source_target_pairs={{0,7},{1,8},{2,5},{3,10},{4,3},{5,12},{6,1},{7,14},{8,15},{9,0},{1... | collective-permute-start | bytes 3538952 | tf_op jit(solution)/shard_map/ppermute | solution.py:357
  192.3 5.8 %collective-permute-start.14 = (bf16[2,192,1536]{2,1,0:T(8,128)(2,1)}, bf16[2,192,1536]{2,1,0:T(8,128)(2,1)S(1)}, u32[]{:S(2)}, u32[]{:S(2)}) collective-permute-start(bf16[2,192,1536]{2,1,0:T(8,128)(2,1)} %get-tuple-element.64), channel_id=1, source_target_pairs={{0,11},{1,4},{2,9},{3,6},{4,15},{5,0},{6,13},{7,2},{8,3},{9,12},{1... | collective-permute-start | bytes 3538952 | tf_op jit(solution)/shard_map/ppermute | solution.py:357
  198.7 10.2 %collective-permute-done.11.rest_11_ = bf16[2,192,1536]{2,1,0:T(8,128)(2,1)S(1)} collective-permute-done((bf16[2,192,1536]{2,1,0:T(8,128)(2,1)}, bf16[2,192,1536]{2,1,0:T(8,128)(2,1)S(1)}, u32[]{:S(2)}, u32[]{:S(2)}) %collective-permute-start.11) | collective-permute-done | bytes 1179680 | tf_op jit(solution)/shard_map/ppermute | solution.py:357
  212.9 7.0 %collective-permute-done.13.rest_13_ = bf16[2,192,1536]{2,1,0:T(8,128)(2,1)S(1)} collective-permute-done((bf16[2,192,1536]{2,1,0:T(8,128)(2,1)}, bf16[2,192,1536]{2,1,0:T(8,128)(2,1)S(1)}, u32[]{:S(2)}, u32[]{:S(2)}) %collective-permute-start.13) | collective-permute-done | bytes 1179680 | tf_op jit(solution)/shard_map/ppermute | solution.py:357
  224.9 6.0 %shard_map.123.own = bf16[24,1536]{1,0:T(8,128)(2,1)} custom-call(s32[32]{0:T(128)} %pad_add_fusion.table, bf16[24,2048]{1,0:T(8,128)(2,1)} %bitcast.65, bf16[24,2048]{1,0:T(8,128)(2,1)} %bitcast.73, f32[2,4096]{1,0:T(2,128)} %pad_maximum_fusion.gains, bf16[2,192,1536]{2,1,0:T(8,128)(2,1)} %get-tuple-element.88.rest_0_, bf16[2,192,1536]{2,1,0:T(8,128)(2,1)} %copy-done.1, ...), custom_call_target="tpu_custom_call" | custom-call | flops 226492416 | bytes 9437184 | tf_op jit(solution)/shard_map/pallas_call | solution.py:143
  266.5 5.5 collective-permute-done.22.sent
  298.8 5.0 collective-permute-done.28.sent
  329.4 5.1 collective-permute-done.34.sent
  360.1 5.5 collective-permute-done.40.sent
  391.3 5.4 collective-permute-done.46.sent
  422.4 5.3 collective-permute-done.52.sent
  453.4 5.6 collective-permute-done.58.sent
  484.6 5.5 collective-permute-done.64.sent
  515.8 5.4 collective-permute-done.70.sent
  546.9 5.5 collective-permute-done.76.sent
  (324 shorter events, 313.6 us)
Async XLA Ops:
  6.0 56.3 %collective-permute-start.1 = (bf16[2,192,1536]{2,1,0:T(8,128)(2,1)}, bf16[2,192,1536]{2,1,0:T(8,128)(2,1)S(1)}, u32[]{:S(2)}, u32[]{:S(2)}) collective-permute-start(bf16[2,192,1536]{2,1,0:T(8,128)(2,1)} %get-tuple-element.54), channel_id=1, source_target_pairs={{0,4},{1,11},{2,6},{3,9},{4,0},{5,15},{6,2},{7,13},{8,12},{9,3},{1... | collective-permute-start | bytes 3538952 | tf_op jit(solution)/shard_map/ppermute | solution.py:357
  8.9 55.7 %collective-permute-start.2 = (bf16[2,192,1536]{2,1,0:T(8,128)(2,1)}, bf16[2,192,1536]{2,1,0:T(8,128)(2,1)}, u32[]{:S(2)}, u32[]{:S(2)}) collective-permute-start(bf16[2,192,1536]{2,1,0:T(8,128)(2,1)} %get-tuple-element.55), channel_id=1, source_target_pairs={{0,8},{1,7},{2,10},{3,5},{4,12},{5,3},{6,14},{7,1},{8,0},{9,15},{1... | collective-permute-start | bytes 3538952 | tf_op jit(solution)/shard_map/ppermute | solution.py:357
  10.5 78.2 %collective-permute-start.3 = (bf16[2,192,1536]{2,1,0:T(8,128)(2,1)}, bf16[2,192,1536]{2,1,0:T(8,128)(2,1)}, u32[]{:S(2)}, u32[]{:S(2)}) collective-permute-start(bf16[2,192,1536]{2,1,0:T(8,128)(2,1)} %get-tuple-element.46), channel_id=1, source_target_pairs={{0,12},{1,3},{2,14},{3,1},{4,8},{5,7},{6,10},{7,5},{8,4},{9,11},{1... | collective-permute-start | bytes 3538952 | tf_op jit(solution)/shard_map/ppermute | solution.py:357
  28.1 34.2 %collective-permute-start = (f32[1,4096]{1,0:T(1,128)S(1)}, f32[1,4096]{1,0:T(1,128)S(1)}, u32[]{:S(2)}, u32[]{:S(2)}) collective-permute-start(f32[1,4096]{1,0:T(1,128)S(1)} %shard_map.122), channel_id=1, source_target_pairs={{0,16},{16,0},{1,17},{17,1},{2,18},{18,2},{3,19},{19,3},{4,20},{20... | collective-permute-start | bytes 49160 | tf_op jit(solution)/shard_map/ppermute | solution.py:383
  33.8 56.5 %collective-permute-start.7 = (bf16[2,192,1536]{2,1,0:T(8,128)(2,1)S(1)}, bf16[2,192,1536]{2,1,0:T(8,128)(2,1)S(1)}, u32[]{:S(2)}, u32[]{:S(2)}) collective-permute-start(bf16[2,192,1536]{2,1,0:T(8,128)(2,1)S(1)} %get-tuple-element.87), channel_id=1, source_target_pairs={{0,14},{1,15},{2,12},{3,13},{4,10},{5,11},{6,8},{7,9},{8,6},{9,7},... | collective-permute-start | bytes 3538952 | tf_op jit(solution)/shard_map/ppermute | solution.py:357
  62.3 56.9 %collective-permute-start.4 = (bf16[2,192,1536]{2,1,0:T(8,128)(2,1)S(1)}, bf16[2,192,1536]{2,1,0:T(8,128)(2,1)}, u32[]{:S(2)}, u32[]{:S(2)}) collective-permute-start(bf16[2,192,1536]{2,1,0:T(8,128)(2,1)S(1)} %copy-done.42), channel_id=1, source_target_pairs={{0,2},{1,13},{2,0},{3,15},{4,6},{5,9},{6,4},{7,11},{8,10},{9,5},{1... | collective-permute-start | bytes 3538952 | tf_op jit(solution)/shard_map/ppermute | solution.py:357
  62.3 62.6 %collective-permute-start.5 = (bf16[2,192,1536]{2,1,0:T(8,128)(2,1)}, bf16[2,192,1536]{2,1,0:T(8,128)(2,1)}, u32[]{:S(2)}, u32[]{:S(2)}) collective-permute-start(bf16[2,192,1536]{2,1,0:T(8,128)(2,1)} %get-tuple-element.57), channel_id=1, source_target_pairs={{0,6},{1,9},{2,4},{3,11},{4,2},{5,13},{6,0},{7,15},{8,14},{9,1},{1... | collective-permute-start | bytes 3538952 | tf_op jit(solution)/shard_map/ppermute | solution.py:357
  64.7 60.2 %collective-permute-start.6 = (bf16[2,192,1536]{2,1,0:T(8,128)(2,1)}, bf16[2,192,1536]{2,1,0:T(8,128)(2,1)}, u32[]{:S(2)}, u32[]{:S(2)}) collective-permute-start(bf16[2,192,1536]{2,1,0:T(8,128)(2,1)} %get-tuple-element.58), channel_id=1, source_target_pairs={{0,10},{1,5},{2,8},{3,7},{4,14},{5,1},{6,12},{7,3},{8,2},{9,13},{1... | collective-permute-start | bytes 3538952 | tf_op jit(solution)/shard_map/ppermute | solution.py:357
  88.7 48.2 %collective-permute-start.8 = (bf16[2,192,1536]{2,1,0:T(8,128)(2,1)}, bf16[2,192,1536]{2,1,0:T(8,128)(2,1)}, u32[]{:S(2)}, u32[]{:S(2)}) collective-permute-start(bf16[2,192,1536]{2,1,0:T(8,128)(2,1)} %get-tuple-element.59), channel_id=1, source_target_pairs={{0,1},{1,14},{2,3},{3,12},{4,5},{5,10},{6,7},{7,8},{8,9},{9,6},{10... | collective-permute-start | bytes 3538952 | tf_op jit(solution)/shard_map/ppermute | solution.py:357
  90.3 69.3 %collective-permute-start.9 = (bf16[2,192,1536]{2,1,0:T(8,128)(2,1)}, bf16[2,192,1536]{2,1,0:T(8,128)(2,1)}, u32[]{:S(2)}, u32[]{:S(2)}) collective-permute-start(bf16[2,192,1536]{2,1,0:T(8,128)(2,1)} %get-tuple-element.60), channel_id=1, source_target_pairs={{0,5},{1,10},{2,7},{3,8},{4,1},{5,14},{6,3},{7,12},{8,13},{9,2},{1... | collective-permute-start | bytes 3538952 | tf_op jit(solution)/shard_map/ppermute | solution.py:357
  119.3 73.0 %collective-permute-start.10 = (bf16[2,192,1536]{2,1,0:T(8,128)(2,1)}, bf16[2,192,1536]{2,1,0:T(8,128)(2,1)}, u32[]{:S(2)}, u32[]{:S(2)}) collective-permute-start(bf16[2,192,1536]{2,1,0:T(8,128)(2,1)} %get-tuple-element.61), channel_id=1, source_target_pairs={{0,9},{1,6},{2,11},{3,4},{4,13},{5,2},{6,15},{7,0},{8,1},{9,14},{1... | collective-permute-start | bytes 3538952 | tf_op jit(solution)/shard_map/ppermute | solution.py:357
  124.9 84.0 %collective-permute-start.11 = (bf16[2,192,1536]{2,1,0:T(8,128)(2,1)}, bf16[2,192,1536]{2,1,0:T(8,128)(2,1)S(1)}, u32[]{:S(2)}, u32[]{:S(2)}) collective-permute-start(bf16[2,192,1536]{2,1,0:T(8,128)(2,1)} %get-tuple-element.50), channel_id=1, source_target_pairs={{0,13},{1,2},{2,15},{3,0},{4,9},{5,6},{6,11},{7,4},{8,5},{9,10},{1... | collective-permute-start | bytes 3538952 | tf_op jit(solution)/shard_map/ppermute | solution.py:357
  124.9 98.5 %collective-permute-start.15 = (bf16[2,192,1536]{2,1,0:T(8,128)(2,1)S(1)}, bf16[2,192,1536]{2,1,0:T(8,128)(2,1)S(1)}, u32[]{:S(2)}, u32[]{:S(2)}) collective-permute-start(bf16[2,192,1536]{2,1,0:T(8,128)(2,1)S(1)} %copy-done.24), channel_id=1, source_target_pairs={{0,15},{1,0},{2,13},{3,2},{4,11},{5,4},{6,9},{7,6},{8,7},{9,8},{10... | collective-permute-start | bytes 3538952 | tf_op jit(solution)/shard_map/ppermute | solution.py:357
  136.9 76.0 %collective-permute-start.12 = (bf16[2,192,1536]{2,1,0:T(8,128)(2,1)}, bf16[2,192,1536]{2,1,0:T(8,128)(2,1)S(1)}, u32[]{:S(2)}, u32[]{:S(2)}) collective-permute-start(bf16[2,192,1536]{2,1,0:T(8,128)(2,1)} %get-tuple-element.62), channel_id=1, source_target_pairs={{0,3},{1,12},{2,1},{3,14},{4,7},{5,8},{6,5},{7,10},{8,11},{9,4},{1... | collective-permute-start | bytes 3538952 | tf_op jit(solution)/shard_map/ppermute | solution.py:357
  159.7 60.2 %collective-permute-start.13 = (bf16[2,192,1536]{2,1,0:T(8,128)(2,1)}, bf16[2,192,1536]{2,1,0:T(8,128)(2,1)S(1)}, u32[]{:S(2)}, u32[]{:S(2)}) collective-permute-start(bf16[2,192,1536]{2,1,0:T(8,128)(2,1)} %get-tuple-element.63), channel_id=1, source_target_pairs={{0,7},{1,8},{2,5},{3,10},{4,3},{5,12},{6,1},{7,14},{8,15},{9,0},{1... | collective-permute-start | bytes 3538952 | tf_op jit(solution)/shard_map/ppermute | solution.py:357
  192.3 31.2 %collective-permute-start.14 = (bf16[2,192,1536]{2,1,0:T(8,128)(2,1)}, bf16[2,192,1536]{2,1,0:T(8,128)(2,1)S(1)}, u32[]{:S(2)}, u32[]{:S(2)}) collective-permute-start(bf16[2,192,1536]{2,1,0:T(8,128)(2,1)} %get-tuple-element.64), channel_id=1, source_target_pairs={{0,11},{1,4},{2,9},{3,6},{4,15},{5,0},{6,13},{7,2},{8,3},{9,12},{1... | collective-permute-start | bytes 3538952 | tf_op jit(solution)/shard_map/ppermute | solution.py:357
  251.3 7.9 %collective-permute-start.20 = (bf16[24,2048]{1,0:T(8,128)(2,1)S(1)}, bf16[24,2048]{1,0:T(8,128)(2,1)S(1)}, u32[]{:S(2)}, u32[]{:S(2)}) collective-permute-start(bf16[24,2048]{1,0:T(8,128)(2,1)S(1)} %shard_map.126), channel_id=1, source_target_pairs={{0,4},{4,8},{8,12},{12,16},{16,20},{20,24},{24,28},{28,0},{1,5},{5... | collective-permute-start | bytes 294920 | tf_op jit(solution)/shard_map/ppermute | solution.py:440
  282.4 8.8 %collective-permute-start.25 = (bf16[24,2048]{1,0:T(8,128)(2,1)S(1)}, bf16[24,2048]{1,0:T(8,128)(2,1)S(1)}, u32[]{:S(2)}, u32[]{:S(2)}) collective-permute-start(bf16[24,2048]{1,0:T(8,128)(2,1)S(1)} %shard_map.130.value), channel_id=1, source_target_pairs={{0,20},{4,24},{8,28},{12,0},{16,4},{20,8},{24,12},{28,16},{1,21},{... | collective-permute-start | bytes 294920 | tf_op jit(solution)/shard_map/ppermute | solution.py:438
  344.9 7.9 %collective-permute-start.38 = (bf16[24,2048]{1,0:T(8,128)(2,1)S(1)}, bf16[24,2048]{1,0:T(8,128)(2,1)S(1)}, u32[]{:S(2)}, u32[]{:S(2)}) collective-permute-start(bf16[24,2048]{1,0:T(8,128)(2,1)S(1)} %shard_map.141), channel_id=1, source_target_pairs={{0,4},{4,8},{8,12},{12,16},{16,20},{20,24},{24,28},{28,0},{1,5},{5... | collective-permute-start | bytes 294920 | tf_op jit(solution)/shard_map/ppermute | solution.py:440
  376.1 7.9 %collective-permute-start.44 = (bf16[24,2048]{1,0:T(8,128)(2,1)S(1)}, bf16[24,2048]{1,0:T(8,128)(2,1)S(1)}, u32[]{:S(2)}, u32[]{:S(2)}) collective-permute-start(bf16[24,2048]{1,0:T(8,128)(2,1)S(1)} %shard_map.146), channel_id=1, source_target_pairs={{0,4},{4,8},{8,12},{12,16},{16,20},{20,24},{24,28},{28,0},{1,5},{5... | collective-permute-start | bytes 294920 | tf_op jit(solution)/shard_map/ppermute | solution.py:440
  438.1 8.0 %collective-permute-start.56 = (bf16[24,2048]{1,0:T(8,128)(2,1)S(1)}, bf16[24,2048]{1,0:T(8,128)(2,1)S(1)}, u32[]{:S(2)}, u32[]{:S(2)}) collective-permute-start(bf16[24,2048]{1,0:T(8,128)(2,1)S(1)} %shard_map.156), channel_id=1, source_target_pairs={{0,4},{4,8},{8,12},{12,16},{16,20},{20,24},{24,28},{28,0},{1,5},{5... | collective-permute-start | bytes 294920 | tf_op jit(solution)/shard_map/ppermute | solution.py:440
  469.4 7.9 %collective-permute-start.62 = (bf16[24,2048]{1,0:T(8,128)(2,1)S(1)}, bf16[24,2048]{1,0:T(8,128)(2,1)S(1)}, u32[]{:S(2)}, u32[]{:S(2)}) collective-permute-start(bf16[24,2048]{1,0:T(8,128)(2,1)S(1)} %shard_map.161), channel_id=1, source_target_pairs={{0,4},{4,8},{8,12},{12,16},{16,20},{20,24},{24,28},{28,0},{1,5},{5... | collective-permute-start | bytes 294920 | tf_op jit(solution)/shard_map/ppermute | solution.py:440
  500.5 7.9 %collective-permute-start.68 = (bf16[24,2048]{1,0:T(8,128)(2,1)S(1)}, bf16[24,2048]{1,0:T(8,128)(2,1)S(1)}, u32[]{:S(2)}, u32[]{:S(2)}) collective-permute-start(bf16[24,2048]{1,0:T(8,128)(2,1)S(1)} %shard_map.166), channel_id=1, source_target_pairs={{0,4},{4,8},{8,12},{12,16},{16,20},{20,24},{24,28},{28,0},{1,5},{5... | collective-permute-start | bytes 294920 | tf_op jit(solution)/shard_map/ppermute | solution.py:440
  531.6 8.0 %collective-permute-start.74 = (bf16[24,2048]{1,0:T(8,128)(2,1)S(1)}, bf16[24,2048]{1,0:T(8,128)(2,1)S(1)}, u32[]{:S(2)}, u32[]{:S(2)}) collective-permute-start(bf16[24,2048]{1,0:T(8,128)(2,1)S(1)} %shard_map.171), channel_id=1, source_target_pairs={{0,4},{4,8},{8,12},{12,16},{16,20},{20,24},{24,28},{28,0},{1,5},{5... | collective-permute-start | bytes 294920 | tf_op jit(solution)/shard_map/ppermute | solution.py:440
  (98 other events, 1167.7 us)
